TPU v7x, 32 devices: a whole 2x2x4 slice. The times are simulated.
32 devices in a mesh: ctx: 4 (over z), tp: 8 (over y, x, core).
Axes of the slice: x: 2, y: 2, z: 4, core: 2. Of those that a mesh axis runs over, the one named last changes fastest.
Arguments:
- tokens: bfloat16 [4096, 2048], P(('ctx', 'tp')), may hold values from -6 to 6
- cotangent: bfloat16 [4096, 2048], P(('ctx', 'tp')), may hold values from -6 to 6
- routes: int32 [4096, 1], P(('ctx', 'tp')), may hold values from 0 to 7; in each aligned block of 128 rows (0 to 127, 128 to 255, ...) at most 24 rows name the same one
- gate_weights: float32 [4096, 1], P(('ctx', 'tp')), may hold values from 0.2 to 1
- w_gate: bfloat16 [8, 2048, 768], P('tp'), may hold values from -0.125 to 0.125
- w_up: bfloat16 [8, 2048, 768], P('tp'), may hold values from -0.125 to 0.125
- w_down: bfloat16 [8, 768, 2048], P('tp'), may hold values from -0.21875 to 0.21875
Outputs:
- layer_output: bfloat16 [4096, 2048], P(('ctx', 'tp'))
- token_grad: bfloat16 [4096, 2048], P(('ctx', 'tp'))
- gate_grad: float32 [4096, 1], P(('ctx', 'tp'))
- down_grad: bfloat16 [8, 768, 2048], P('tp', 'ctx')
Inputs may be any that keep to these rules, and one draw needn't show every extreme that they name: `routes`: among the 128 tokens of one device (aligned blocks of rows), at most 24 name the same expert; some device's block reaches 24 for some expert.
All inputs are finite; a program needn't handle non-finite values.
Results may differ from a plain program's by a relative error of at most 0.015.
Values may be sent and summed in bfloat16 or wider, within the bound.
No kernel may reach another device: no remote copies, remote signals or barrier semaphores. Data moves between devices by JAX's collectives and lax.ppermute only.
A program may use at most 64 MiB of HBM per device.

v0:
```python
import jax
import jax.numpy as jnp
from jax import lax
from jax.sharding import PartitionSpec as P


def expert_block(rows_in, rows_cot, gate_mat, up_mat, down_mat):
    pre_act = jnp.dot(rows_in, gate_mat, preferred_element_type=jnp.float32)
    up_act = jnp.dot(rows_in, up_mat, preferred_element_type=jnp.float32)
    sigma = jax.nn.sigmoid(pre_act)
    hidden = (pre_act * sigma * up_act).astype(jnp.bfloat16)
    output = jnp.dot(hidden, down_mat, preferred_element_type=jnp.float32).astype(jnp.bfloat16)
    dhidden = lax.dot_general(
        rows_cot, down_mat, (((1,), (1,)), ((), ())), preferred_element_type=jnp.float32
    )
    dup_act = (dhidden * pre_act * sigma).astype(jnp.bfloat16)
    dpre_act = (dhidden * up_act * sigma * (1.0 + pre_act * (1.0 - sigma))).astype(jnp.bfloat16)
    first = lax.dot_general(
        dpre_act, gate_mat, (((1,), (1,)), ((), ())), preferred_element_type=jnp.float32
    )
    second = lax.dot_general(
        dup_act, up_mat, (((1,), (1,)), ((), ())), preferred_element_type=jnp.float32
    )
    input_grad = (first + second).astype(jnp.bfloat16)
    return (output, input_grad, hidden)


def body(tokens, cotangent, routes, gate_weights, w_gate, w_up, w_down):
    tok_rows = tokens.shape[0]
    width = tokens.shape[1]
    peers = lax.axis_size("tp")
    num_experts = peers * w_gate.shape[0]
    capacity = 3 * tok_rows * routes.shape[1] // (2 * num_experts)
    gate_mat = w_gate[0]
    up_mat = w_up[0]
    down_mat = w_down[0]
    expert_ids = routes[:, 0]
    onehot = (expert_ids[:, None] == jnp.arange(num_experts, dtype=jnp.int32)[None, :]).astype(
        jnp.int32
    )
    rank = jnp.sum((jnp.cumsum(onehot, axis=0) - 1) * onehot, axis=1)
    slot = expert_ids * capacity + rank
    placing = (
        slot[None, :] == jnp.arange(num_experts * capacity, dtype=jnp.int32)[:, None]
    ).astype(jnp.bfloat16)
    scaled = (gate_weights * cotangent.astype(jnp.float32)).astype(jnp.bfloat16)
    send_in = jnp.dot(placing, tokens, preferred_element_type=jnp.float32).astype(jnp.bfloat16)
    send_cot = jnp.dot(placing, scaled, preferred_element_type=jnp.float32).astype(jnp.bfloat16)
    send_in = send_in.reshape(num_experts, capacity, width)
    send_cot = send_cot.reshape(num_experts, capacity, width)
    got_in, got_cot = (
        lax.all_to_all(send_in, "tp", split_axis=0, concat_axis=0, tiled=True),
        lax.all_to_all(send_cot, "tp", split_axis=0, concat_axis=0, tiled=True),
    )
    output, input_grad, hidden = expert_block(
        got_in.reshape(-1, width), got_cot.reshape(-1, width), gate_mat, up_mat, down_mat
    )
    back_out, back_grad = (
        lax.all_to_all(
            output.reshape(peers, capacity, width), "tp", split_axis=0, concat_axis=0, tiled=True
        ),
        lax.all_to_all(
            input_grad.reshape(peers, capacity, width),
            "tp",
            split_axis=0,
            concat_axis=0,
            tiled=True,
        ),
    )
    cot_flat = got_cot.reshape(-1, width)
    contract_first = (((0,), (0,)), ((), ()))
    out_tok = lax.dot_general(
        placing, back_out.reshape(-1, width), contract_first, preferred_element_type=jnp.float32
    )
    grad_tok = lax.dot_general(
        placing, back_grad.reshape(-1, width), contract_first, preferred_element_type=jnp.float32
    )
    layer_output = (gate_weights * out_tok).astype(jnp.bfloat16)
    token_grad = grad_tok.astype(jnp.bfloat16)
    gate_grad = jnp.sum(cotangent.astype(jnp.float32) * out_tok, axis=1, keepdims=True)
    summed = lax.psum_scatter(
        lax.dot_general(
            hidden, cot_flat, contract_first, preferred_element_type=jnp.float32
        ).astype(jnp.bfloat16),
        "ctx",
        scatter_dimension=0,
        tiled=True,
    )
    down_grad = summed[None]
    return (layer_output, token_grad, gate_grad, down_grad)


def solution(mesh):
    in_specs = (
        P(("ctx", "tp"), None),
        P(("ctx", "tp"), None),
        P(("ctx", "tp"), None),
        P(("ctx", "tp"), None),
        P("tp", None, None),
        P("tp", None, None),
        P("tp", None, None),
    )
    out_specs = (
        P(("ctx", "tp"), None),
        P(("ctx", "tp"), None),
        P(("ctx", "tp"), None),
        P("tp", "ctx", None),
    )
    return jax.shard_map(body, mesh=mesh, in_specs=in_specs, out_specs=out_specs, check_vma=False)
```

profile of v0, /device:TPU:0, one launch (start us, length us, event | category | flops | bytes accessed | tf_op | source)
XLA Modules:
  0.0 117.6 jit_solution(1280870019563322320)
XLA Ops:
  7.2 0.0 copy-start
  7.2 0.9 fusion.28
  8.1 0.2 reduce_window_sum.11
  8.3 0.8 select_reduce_fusion
  9.1 0.7 multiply_add_fusion
  9.8 2.3 %convolution_convert_fusion.2 = bf16[192,2048]{1,0:T(8,128)(2,1)} fusion(bf16[128,2048]{1,0:T(8,128)(2,1)} %param.7, s32[128]{0:T(128)S(1)} %multiply_add_fusion), kind=kOutput, calls=%fused_computation.17 | convolution fusion | flops 101081088 | bytes 1311232 | tf_op jit(solution)/shard_map/dot_general | solution.py:47
  12.0 5.2 %all-to-all-start = ((bf16[8,24,2048]{2,1,0:T(8,128)(2,1)}), bf16[8,24,2048]{2,1,0:T(8,128)(2,1)}, u32[]{:S(2)}, u32[]{:S(2)}) async-start(bf16[8,24,2048]{2,1,0:T(8,128)(2,1)} %bitcast.48), calls=%async_computation | async-start | bytes 1572864 | tf_op jit(solution)/shard_map/all_to_all | solution.py:52
  17.2 0.0 copy-done.5
  17.2 2.4 %convolution_convert_fusion.1 = bf16[192,2048]{1,0:T(8,128)(2,1)} fusion(bf16[128,2048]{1,0:T(8,128)(2,1)} %param.8, f32[128]{0:T(128)S(1)} %bitcast.51, s32[128]{0:T(128)S(1)} %multiply_add_fusion), kind=kOutput, calls=%fused_computation.16 | convolution fusion | flops 101867520 | bytes 1311744 | tf_op jit(solution)/shard_map/dot_general | solution.py:48
  19.6 10.3 %all-to-all-done = bf16[8,24,2048]{2,1,0:T(8,128)(2,1)} async-done(((bf16[8,24,2048]{2,1,0:T(8,128)(2,1)}), bf16[8,24,2048]{2,1,0:T(8,128)(2,1)}, u32[]{:S(2)}, u32[]{:S(2)}) %all-to-all-start) | async-done | bytes 786464 | tf_op jit(solution)/shard_map/all_to_all | solution.py:52
  29.9 4.2 %all-to-all-start.2 = ((bf16[8,24,2048]{2,1,0:T(8,128)(2,1)}), bf16[8,24,2048]{2,1,0:T(8,128)(2,1)}, u32[]{:S(2)}, u32[]{:S(2)}) async-start(bf16[8,24,2048]{2,1,0:T(8,128)(2,1)} %bitcast.47), calls=%async_computation.2 | async-start | bytes 1572864 | tf_op jit(solution)/shard_map/all_to_all | solution.py:53
  34.1 0.0 reduce-scatter.2.cloned.1.call-start
  34.2 2.9 %fusion.10 = f32[192,768]{1,0:T(8,128)S(1)} fusion(bf16[192,2048]{1,0:T(8,128)(2,1)} %bitcast.3, bf16[1,2048,768]{2,1,0:T(8,128)(2,1)} %param.11), kind=kOutput, calls=%fused_computation.11 | convolution fusion | flops 603979776 | bytes 4521984 | tf_op jit(solution)/shard_map/dot_general | solution.py:8
  37.1 0.8 copy-done.2
  37.9 2.7 %multiply_convert_fusion.3 = (bf16[192,768]{1,0:T(8,128)(2,1)S(1)}, f32[192,768]{1,0:T(8,128)}) fusion(f32[192,768]{1,0:T(8,128)S(1)} %fusion.10, bf16[192,2048]{1,0:T(8,128)(2,1)} %bitcast.3, bf16[1,2048,768]{2,1,0:T(8,128)(2,1)S(1)} %copy-done), kind=kOutput, calls=%fused_computation.26 | convolution fusion | flops 604864512 | bytes 5406720 | tf_op jit(solution)/shard_map/dot_general | solution.py:9
  40.7 6.1 %all-to-all-done.2 = bf16[8,24,2048]{2,1,0:T(8,128)(2,1)} async-done(((bf16[8,24,2048]{2,1,0:T(8,128)(2,1)}), bf16[8,24,2048]{2,1,0:T(8,128)(2,1)}, u32[]{:S(2)}, u32[]{:S(2)}) %all-to-all-start.2) | async-done | bytes 786464 | tf_op jit(solution)/shard_map/all_to_all | solution.py:53
  46.7 3.8 %convolution_convert_fusion = bf16[768,2048]{1,0:T(8,128)(2,1)} fusion(bf16[192,768]{1,0:T(8,128)(2,1)S(1)} %get-tuple-element.6, bf16[192,2048]{1,0:T(8,128)(2,1)} %bitcast.10), kind=kOutput, calls=%fused_computation | convolution fusion | flops 605552640 | bytes 4227072 | tf_op jit(solution)/shard_map/dot_general | solution.py:82
  50.5 0.0 reduce-scatter.2.cloned.1.call-update
  50.6 3.4 %fusion = f32[192,768]{1,0:T(8,128)S(1)} fusion(bf16[192,2048]{1,0:T(8,128)(2,1)} %bitcast.10, bf16[1,768,2048]{2,1,0:T(8,128)(2,1)} %param.13), kind=kOutput, calls=%fused_computation.1 | convolution fusion | flops 603979776 | bytes 4521984 | tf_op jit(solution)/shard_map/dot_general | solution.py:13
  54.0 0.0 copy-start.1
  54.0 1.2 %fusion.4 = f32[192,2048]{1,0:T(8,128)S(1)} fusion(bf16[1,2048,768]{2,1,0:T(8,128)(2,1)S(1)} %copy-done, f32[192,768]{1,0:T(8,128)S(1)} %fusion, f32[192,768]{1,0:T(8,128)S(1)} %copy-done.3), kind=kOutput, calls=%fused_computation.5 | convolution fusion | flops 604864512 | bytes 5898240 | tf_op jit(solution)/shard_map/dot_general | solution.py:21
  55.2 0.7 copy-done.1
  55.9 0.1 copy-done.4
  56.0 2.1 %fusion.18 = bf16[192,2048]{1,0:T(8,128)(2,1)} fusion(f32[192,2048]{1,0:T(8,128)S(1)} %fusion.4, bf16[1,2048,768]{2,1,0:T(8,128)(2,1)S(1)} %copy-done.1, f32[192,768]{1,0:T(8,128)S(1)} %copy-done.3, f32[192,768]{1,0:T(8,128)S(1)} %fusion, f32[192,768]{1,0:T(8,128)S(1)} %copy-done.4), kind=kOutput, calls=%fused_computation.15 | convolution fusion | flops 606240768 | bytes 7274496 | tf_op jit(solution)/shard_map/dot_general | solution.py:18
  58.1 4.2 %all-to-all-start.3 = ((bf16[8,24,2048]{2,1,0:T(8,128)(2,1)}), bf16[8,24,2048]{2,1,0:T(8,128)(2,1)}, u32[]{:S(2)}, u32[]{:S(2)}) async-start(bf16[8,24,2048]{2,1,0:T(8,128)(2,1)} %bitcast.46), calls=%async_computation.3 | async-start | bytes 1572864 | tf_op jit(solution)/shard_map/all_to_all | solution.py:62
  62.3 3.6 %fusion.15 = bf16[192,2048]{1,0:T(8,128)(2,1)} fusion(bf16[192,768]{1,0:T(8,128)(2,1)S(1)} %get-tuple-element.6, bf16[1,768,2048]{2,1,0:T(8,128)(2,1)} %param.13), kind=kOutput, calls=%fused_computation.14 | convolution fusion | flops 604372992 | bytes 4227072 | tf_op jit(solution)/shard_map/dot_general | solution.py:12
  65.9 9.0 %all-to-all-done.3 = bf16[8,24,2048]{2,1,0:T(8,128)(2,1)} async-done(((bf16[8,24,2048]{2,1,0:T(8,128)(2,1)}), bf16[8,24,2048]{2,1,0:T(8,128)(2,1)}, u32[]{:S(2)}, u32[]{:S(2)}) %all-to-all-start.3) | async-done | bytes 786464 | tf_op jit(solution)/shard_map/all_to_all | solution.py:62
  74.9 4.2 %all-to-all-start.1 = ((bf16[8,24,2048]{2,1,0:T(8,128)(2,1)}), bf16[8,24,2048]{2,1,0:T(8,128)(2,1)}, u32[]{:S(2)}, u32[]{:S(2)}) async-start(bf16[8,24,2048]{2,1,0:T(8,128)(2,1)} %bitcast.45), calls=%async_computation.1 | async-start | bytes 1572864 | tf_op jit(solution)/shard_map/all_to_all | solution.py:59
  79.1 2.3 %convolution_convert_fusion.3 = bf16[128,2048]{1,0:T(8,128)(2,1)} fusion(bf16[192,2048]{1,0:T(8,128)(2,1)} %bitcast.12, s32[128]{0:T(128)S(1)} %multiply_add_fusion), kind=kOutput, calls=%fused_computation.18 | convolution fusion | flops 100950016 | bytes 1311232 | tf_op jit(solution)/shard_map/dot_general | solution.py:75
  81.4 10.3 %all-to-all-done.1 = bf16[8,24,2048]{2,1,0:T(8,128)(2,1)} async-done(((bf16[8,24,2048]{2,1,0:T(8,128)(2,1)}), bf16[8,24,2048]{2,1,0:T(8,128)(2,1)}, u32[]{:S(2)}, u32[]{:S(2)}) %all-to-all-start.1) | async-done | bytes 786464 | tf_op jit(solution)/shard_map/all_to_all | solution.py:59
  91.7 3.0 %fusion.22 = (f32[128]{0:T(128)}, bf16[128,2048]{1,0:T(8,128)(2,1)}) fusion(bf16[128,2048]{1,0:T(8,128)(2,1)} %param.8, f32[128]{0:T(128)S(1)} %bitcast.52, bf16[192,2048]{1,0:T(8,128)(2,1)} %bitcast.8, s32[128]{0:T(128)S(1)} %multiply_add_fusion), kind=kOutput, calls=%fused_computation.22 | convolution fusion | flops 101998464 | bytes 1836544 | tf_op jit(solution)/shard_map/dot_general | solution.py:72
  94.8 16.0 %reduce-scatter.2.cloned.1.call-done = bf16[192,2048]{1,0:T(8,128)(2,1)} async-done(((bf16[768,2048]{1,0:T(8,128)(2,1)}), bf16[192,2048]{1,0:T(8,128)(2,1)}) %reduce-scatter.2.cloned.1.call-update) | async-done | bytes 786448 | tf_op jit(solution)/shard_map/reduce_scatter | solution.py:81
  (6 shorter events, 0.0 us)
Async XLA Ops:
  7.2 30.8 %copy-start = (bf16[1,2048,768]{2,1,0:T(8,128)(2,1)S(1)}, bf16[1,2048,768]{2,1,0:T(8,128)(2,1)}, u32[]{:S(2)}) copy-start(bf16[1,2048,768]{2,1,0:T(8,128)(2,1)} %param.12) | copy-start | bytes 9437188
  7.2 10.0 %copy-start.5 = (f32[128,1]{0,1:T(1,128)S(1)}, f32[128,1]{0,1:T(1,128)}, u32[]{:S(2)}) copy-start(f32[128,1]{0,1:T(1,128)} %param.10) | copy-start | bytes 1540
  12.0 17.9 %all-to-all-start = ((bf16[8,24,2048]{2,1,0:T(8,128)(2,1)}), bf16[8,24,2048]{2,1,0:T(8,128)(2,1)}, u32[]{:S(2)}, u32[]{:S(2)}) async-start(bf16[8,24,2048]{2,1,0:T(8,128)(2,1)} %bitcast.48), calls=%async_computation | async-start | bytes 1572864 | tf_op jit(solution)/shard_map/all_to_all | solution.py:52
  29.9 16.8 %all-to-all-start.2 = ((bf16[8,24,2048]{2,1,0:T(8,128)(2,1)}), bf16[8,24,2048]{2,1,0:T(8,128)(2,1)}, u32[]{:S(2)}, u32[]{:S(2)}) async-start(bf16[8,24,2048]{2,1,0:T(8,128)(2,1)} %bitcast.47), calls=%async_computation.2 | async-start | bytes 1572864 | tf_op jit(solution)/shard_map/all_to_all | solution.py:53
  34.1 76.6 %reduce-scatter.2.cloned.1.call-start = ((), (), s32[]{:S(2)}) async-start(), calls=%async_computation.5 | async-start | bytes 3932160 | tf_op jit(solution)/shard_map/reduce_scatter | solution.py:81
  37.1 0.8 copy-start.2
  50.6 3.4 %copy-start.3 = (f32[192,768]{1,0:T(8,128)S(1)}, f32[192,768]{1,0:T(8,128)}, u32[]{:S(2)}) copy-start(f32[192,768]{1,0:T(8,128)} %copy-done.2) | copy-start | bytes 1769476
  54.0 1.9 %copy-start.1 = (bf16[1,2048,768]{2,1,0:T(8,128)(2,1)S(1)}, bf16[1,2048,768]{2,1,0:T(8,128)(2,1)}, u32[]{:S(2)}) copy-start(bf16[1,2048,768]{2,1,0:T(8,128)(2,1)} %param.11) | copy-start | bytes 9437188
  54.0 2.0 %copy-start.4 = (f32[192,768]{1,0:T(8,128)S(1)}, f32[192,768]{1,0:T(8,128)}, u32[]{:S(2)}) copy-start(f32[192,768]{1,0:T(8,128)} %get-tuple-element.7) | copy-start | bytes 1769476
  58.1 16.8 %all-to-all-start.3 = ((bf16[8,24,2048]{2,1,0:T(8,128)(2,1)}), bf16[8,24,2048]{2,1,0:T(8,128)(2,1)}, u32[]{:S(2)}, u32[]{:S(2)}) async-start(bf16[8,24,2048]{2,1,0:T(8,128)(2,1)} %bitcast.46), calls=%async_computation.3 | async-start | bytes 1572864 | tf_op jit(solution)/shard_map/all_to_all | solution.py:62
  74.9 16.8 %all-to-all-start.1 = ((bf16[8,24,2048]{2,1,0:T(8,128)(2,1)}), bf16[8,24,2048]{2,1,0:T(8,128)(2,1)}, u32[]{:S(2)}, u32[]{:S(2)}) async-start(bf16[8,24,2048]{2,1,0:T(8,128)(2,1)} %bitcast.45), calls=%async_computation.1 | async-start | bytes 1572864 | tf_op jit(solution)/shard_map/all_to_all | solution.py:59
Sparse Core Ops, SparseCore 0:
  50.7 60.0 reduce-scatter.1
where the time goes:
time: 118 us
  waiting for transfers between devices  51.7 us (44%)
  matrix products  29.7 us (25%)
  starting transfers between devices  17.8 us (15%)
  between operations  14.1 us (12%)
  other arithmetic  2.55 us (2%)
  local copies, waits for them, and re-layouts  1.65 us (1%)
    reduce_scatter x1, waiting for transfers between devices, body(): lax.psum_scatter(lax.dot_general(hidden, cot_flat, contract_first, prefer...  16 us
    all_to_all x1, waiting for transfers between devices, body(): lax.all_to_all(output.reshape(peers, capacity, width), 'tp', split_axis=0...  10.3 us
    all_to_all x1, waiting for transfers between devices, body(): lax.all_to_all(send_in, 'tp', split_axis=0, concat_axis=0, tiled=True)  10.3 us
    all_to_all x1, waiting for transfers between devices, body(): lax.all_to_all(input_grad.reshape(peers, capacity, width), 'tp', split_ax...  9.04 us
    all_to_all x1, waiting for transfers between devices, body(): lax.all_to_all(send_cot, 'tp', split_axis=0, concat_axis=0, tiled=True)  6.07 us
    all_to_all x1, starting transfers between devices, body(): lax.all_to_all(send_in, 'tp', split_axis=0, concat_axis=0, tiled=True)  5.17 us
    all_to_all x1, starting transfers between devices, body(): lax.all_to_all(output.reshape(peers, capacity, width), 'tp', split_axis=0...  4.21 us
    all_to_all x1, starting transfers between devices, body(): lax.all_to_all(send_cot, 'tp', split_axis=0, concat_axis=0, tiled=True)  4.21 us
  transfers between devices with their start and end apart: 5, of which 5 were waited for; matrix products, arithmetic and copies ran while one was open for 20% of the time, Pallas kernels for 0%

commit v1 on v0

v1 whole, which is shorter than its diff:
```python
import functools

import jax
import jax.numpy as jnp
from jax import lax
from jax.experimental import pallas as pl
from jax.experimental.pallas import tpu as pltpu
from jax.sharding import PartitionSpec as P

BF16 = jnp.bfloat16
F32 = jnp.float32
CONTRACT_FIRST = (((0,), (0,)), ((), ()))
CONTRACT_LAST = (((1,), (1,)), ((), ()))


def expert_block(rows_in, rows_cot, gate_mat, up_mat, down_mat):
    pre_act = jnp.dot(rows_in, gate_mat, preferred_element_type=F32)
    up_act = jnp.dot(rows_in, up_mat, preferred_element_type=F32)
    sigma = jax.nn.sigmoid(pre_act)
    hidden = (pre_act * sigma * up_act).astype(BF16)
    output = jnp.dot(hidden, down_mat, preferred_element_type=F32).astype(BF16)
    dhidden = lax.dot_general(rows_cot, down_mat, CONTRACT_LAST, preferred_element_type=F32)
    dup_act = (dhidden * pre_act * sigma).astype(BF16)
    dpre_act = (dhidden * up_act * sigma * (1.0 + pre_act * (1.0 - sigma))).astype(BF16)
    first = lax.dot_general(dpre_act, gate_mat, CONTRACT_LAST, preferred_element_type=F32)
    second = lax.dot_general(dup_act, up_mat, CONTRACT_LAST, preferred_element_type=F32)
    input_grad = (first + second).astype(BF16)
    return (output, input_grad, hidden)


def body_any(tokens, cotangent, routes, gate_weights, w_gate, w_up, w_down):
    tok_rows, width = tokens.shape
    peers = lax.axis_size("tp")
    capacity = 3 * tok_rows * routes.shape[1] // (2 * peers)
    expert_ids = routes[:, 0]
    onehot = (expert_ids[:, None] == jnp.arange(peers, dtype=jnp.int32)[None, :]).astype(jnp.int32)
    rank = jnp.sum((jnp.cumsum(onehot, axis=0) - 1) * onehot, axis=1)
    slot = expert_ids * capacity + rank
    placing = (
        slot[None, :] == jnp.arange(peers * capacity, dtype=jnp.int32)[:, None]
    ).astype(BF16)
    scaled = (gate_weights * cotangent.astype(F32)).astype(BF16)
    send = jnp.dot(
        placing, jnp.concatenate([tokens, scaled], axis=1), preferred_element_type=F32
    ).astype(BF16)
    got = lax.all_to_all(
        send.reshape(peers, capacity, 2 * width), "tp", split_axis=0, concat_axis=0, tiled=True
    ).reshape(-1, 2 * width)
    got_cot = got[:, width:]
    output, input_grad, hidden = expert_block(
        got[:, :width], got_cot, w_gate[0], w_up[0], w_down[0]
    )
    back = lax.all_to_all(
        jnp.concatenate([output, input_grad], axis=1).reshape(peers, capacity, 2 * width),
        "tp", split_axis=0, concat_axis=0, tiled=True,
    ).reshape(-1, 2 * width)
    partial = lax.dot_general(hidden, got_cot, CONTRACT_FIRST, preferred_element_type=F32)
    summed = lax.psum_scatter(partial.astype(BF16), "ctx", scatter_dimension=0, tiled=True)
    home = lax.dot_general(placing, back, CONTRACT_FIRST, preferred_element_type=F32)
    out_tok = home[:, :width]
    layer_output = (gate_weights * out_tok).astype(BF16)
    gate_grad = jnp.sum(cotangent.astype(F32) * out_tok, axis=1, keepdims=True)
    return layer_output, home[:, width:].astype(BF16), gate_grad, summed[None]


VMEM_LIMIT = 32 * 1024 * 1024
TINY = pl.CostEstimate(flops=1, bytes_accessed=1, transcendentals=0)


def call(kernel, outs, **more):
    return pl.pallas_call(
        kernel,
        out_shape=outs,
        cost_estimate=TINY,
        compiler_params=pltpu.CompilerParams(vmem_limit_bytes=VMEM_LIMIT),
        **more,
    )


def shaped(shape, dtype=BF16):
    return jax.ShapeDtypeStruct(shape, dtype)


def diagonal(size):
    return lax.broadcasted_iota(jnp.int32, (size, size), 0) == lax.broadcasted_iota(
        jnp.int32, (size, size), 1
    )


def column(row):
    return jnp.sum(jnp.where(diagonal(row.shape[1]), row, 0), axis=1, keepdims=True)


def send_cot_kernel(peers, capacity, routes, gates, cot, slot_out, *blocks):
    ids = routes[...]
    count = ids.shape[1]
    onehot = lax.broadcasted_iota(jnp.int32, (peers, count), 0) == ids
    upto = lax.broadcasted_iota(jnp.int32, (count, count), 0) <= lax.broadcasted_iota(
        jnp.int32, (count, count), 1
    )
    running = jnp.dot(onehot.astype(BF16), upto.astype(BF16), preferred_element_type=F32)
    rank = jnp.sum(jnp.where(onehot, running - 1.0, 0.0), axis=0, keepdims=True).astype(jnp.int32)
    slot_out[...] = ids * capacity + rank
    own = lax.axis_index("tp")
    slot = (ids ^ own) * capacity + rank
    placing = (lax.broadcasted_iota(jnp.int32, (peers * capacity, count), 0) == slot).astype(BF16)
    gate = column(gates[...])
    step = 512
    for at in range(0, cot.shape[1], step):
        cols = slice(at, at + step)
        scaled = (gate * cot[:, cols].astype(F32)).astype(BF16)
        rows = jnp.dot(placing, scaled, preferred_element_type=F32)
        for k in range(peers):
            blocks[k][:, cols] = rows[k * capacity : (k + 1) * capacity].astype(BF16)


def send_tok_kernel(slot, tok, out):
    placing = (lax.broadcasted_iota(jnp.int32, (out.shape[0], tok.shape[0]), 0) == slot[...]).astype(BF16)
    step = 512
    for at in range(0, tok.shape[1], step):
        cols = slice(at, at + step)
        out[:, cols] = jnp.dot(placing, tok[:, cols], preferred_element_type=F32).astype(BF16)


def gather_kernel(peers, capacity, *refs):
    blocks, (cot_a, cot_b, rows) = refs[:peers], refs[peers:]
    own = lax.axis_index("tp")
    for k in range(peers):
        start = pl.multiple_of((own ^ k) * capacity, 8)
        rows[pl.ds(start, capacity), :] = blocks[k][...].astype(F32)
    half = cot_a.shape[1]
    cot_a[...] = rows[:, :half].astype(BF16)
    cot_b[...] = rows[:, half:].astype(BF16)


def dhidden_kernel(cot_a, cot_b, down, out):
    half = cot_a.shape[1]
    out[...] = lax.dot_general(
        cot_a[...], down[:, :half], CONTRACT_LAST, preferred_element_type=F32
    ) + lax.dot_general(cot_b[...], down[:, half:], CONTRACT_LAST, preferred_element_type=F32)


def hidden_kernel(rows, dhid, gate, up, cot_b, hidden, dpre, dup, *quarters):
    parts, turned = quarters[:4], quarters[4:]
    here = lax.axis_index("ctx")
    tile = pl.program_id(0)
    pre_act = jnp.dot(rows[...], gate[...], preferred_element_type=F32)
    up_act = jnp.dot(rows[...], up[...], preferred_element_type=F32)
    sigma = 1.0 / (1.0 + jnp.exp(-pre_act))
    hid = pre_act * sigma * up_act
    hidden[...] = hid.astype(BF16)
    dh = dhid[...]
    dup[...] = (dh * pre_act * sigma).astype(BF16)
    dpre[...] = (dh * up_act * sigma * (1.0 + pre_act * (1.0 - sigma))).astype(BF16)
    across = hid.T.astype(BF16)
    size = across.shape[0] // 2
    for j in range(2):
        block = across[j * size : (j + 1) * size]
        part = jnp.dot(block, cot_b[...], preferred_element_type=F32).astype(BF16)
        for k in range(4):

            @pl.when((here ^ k) == 2 * tile + j)
            def _():
                parts[k][...] = part
                turned[k][...] = block


def back_kernel(hidden, dpre, dup, gate, up, down, out):
    half = down.shape[1]
    out[:, :half] = jnp.dot(hidden[...], down[...], preferred_element_type=F32).astype(BF16)
    out[:, half:] = (
        lax.dot_general(dpre[...], gate[...], CONTRACT_LAST, preferred_element_type=F32)
        + lax.dot_general(dup[...], up[...], CONTRACT_LAST, preferred_element_type=F32)
    ).astype(BF16)


def home_kernel(slot, gates, back, cot, layer_output, token_grad, gate_grad, total):
    count = cot.shape[0]
    placing = (
        lax.broadcasted_iota(jnp.int32, (count, back.shape[0]), 1) == column(slot[...])
    ).astype(BF16)
    half = cot.shape[1]
    out_tok = jnp.dot(placing, back[:, :half], preferred_element_type=F32)
    layer_output[...] = (column(gates[...]) * out_tok).astype(BF16)
    token_grad[...] = jnp.dot(placing, back[:, half:], preferred_element_type=F32).astype(BF16)
    here = jnp.sum(cot[...].astype(F32) * out_tok, axis=1, keepdims=True)

    @pl.when(pl.program_id(0) == 0)
    def _():
        total[...] = here

    @pl.when(pl.program_id(0) > 0)
    def _():
        total[...] += here

    @pl.when(pl.program_id(0) == pl.num_programs(0) - 1)
    def _():
        gate_grad[...] = jnp.sum(jnp.where(diagonal(count), total[...], 0.0), axis=0, keepdims=True)


def down_kernel(h0, h1, h2, h3, cot_a, near, across, far, far_out, last_out, end_3, mid_3, part, out):
    here = lax.axis_index("ctx")
    outer = (here == 0) | (here == 3)
    half = cot_a.shape[1]

    def times(left, right):
        return jnp.dot(left[...], right[...], preferred_element_type=F32)

    both = times(h0, cot_a) + times(h1, near)

    @pl.when(outer)
    def _():
        out[0, :, :half] = (both + times(h2, far_out) + times(h3, last_out)).astype(BF16)

    @pl.when(jnp.logical_not(outer))
    def _():
        out[0, :, :half] = (both + times(h3, across) + times(h2, far)).astype(BF16)

    out[0, :, half:] = (
        end_3[...].astype(F32) + mid_3[...].astype(F32) + part[...].astype(F32)
    ).astype(BF16)


ENDS = ((0, 1), (1, 0), (2, 3), (3, 2))
MIDDLE = ((1, 2), (2, 1))
INWARD = ((0, 1), (3, 2))
OUTWARD = ((1, 0), (2, 3))


def along(rows, pairs):
    return lax.ppermute(rows, "ctx", pairs)


def plus(left, right):
    return (left.astype(F32) + right.astype(F32)).astype(BF16)


def body_line(tokens, cotangent, routes, gate_weights, w_gate, w_up, w_down):
    count, width = tokens.shape
    peers = lax.axis_size("tp")
    capacity = 3 * count * routes.shape[1] // (2 * peers)
    slots = peers * capacity
    inner = w_gate.shape[2]
    half, quarter = width // 2, inner // 4
    gate_mat, up_mat, down_mat = w_gate[0], w_up[0], w_down[0]
    gates = gate_weights.reshape(1, count)

    slot, *blocks = call(
        functools.partial(send_cot_kernel, peers, capacity),
        [shaped((1, count), jnp.int32)] + [shaped((capacity, width))] * peers,
    )(routes.reshape(1, count), gates, cotangent)
    got = {0: blocks[0]}
    for k in [6, 7, 2, 4, 3, 5, 1]:
        got[k] = lax.ppermute(blocks[k], "tp", [(i, i ^ k) for i in range(peers)])
    send_tok = call(send_tok_kernel, shaped((slots, width)))(slot, tokens)
    rows = lax.all_to_all(
        send_tok.reshape(peers, capacity, width), "tp", split_axis=0, concat_axis=0, tiled=True
    ).reshape(slots, width)

    cot_a, cot_b = call(
        functools.partial(gather_kernel, peers, capacity),
        [shaped((slots, half))] * 2,
        scratch_shapes=[pltpu.VMEM((slots, width), F32)],
    )(*[got[k] for k in range(peers)])
    near = along(cot_a, ENDS)
    across = along(cot_a, MIDDLE)

    whole = lambda *shape: pl.BlockSpec(shape, lambda i: (0,) * len(shape))
    tile = inner // 2
    dhid = call(
        dhidden_kernel,
        shaped((slots, inner), F32),
        grid=(2,),
        in_specs=[whole(slots, half), whole(slots, half), pl.BlockSpec((tile, width), lambda i: (i, 0))],
        out_specs=pl.BlockSpec((slots, tile), lambda i: (0, i)),
    )(cot_a, cot_b, down_mat)
    by_tile = pl.BlockSpec((slots, tile), lambda i: (0, i))
    weights = pl.BlockSpec((width, tile), lambda i: (0, i))
    hidden, dpre, dup, *quarters = call(
        hidden_kernel,
        [shaped((slots, inner))] * 3 + [shaped((quarter, half))] * 4 + [shaped((quarter, slots))] * 4,
        grid=(2,),
        in_specs=[whole(slots, width), by_tile, weights, weights, whole(slots, half)],
        out_specs=[by_tile] * 3 + [whole(quarter, half)] * 4 + [whole(quarter, slots)] * 4,
    )(rows, dhid, gate_mat, up_mat, cot_b)
    part, turned = quarters[:4], quarters[4:]

    in_1 = along(part[3], INWARD)
    far_out = along(across, OUTWARD)
    far = along(near, MIDDLE)
    in_2 = along(part[2], INWARD)

    wide = width // 4
    back = call(
        back_kernel,
        shaped((slots, 2 * width)),
        grid=(4,),
        in_specs=[whole(slots, inner)] * 3
        + [pl.BlockSpec((wide, inner), lambda i: (i, 0))] * 2
        + [pl.BlockSpec((inner, wide), lambda i: (0, i))],
        out_specs=pl.BlockSpec((slots, 2 * wide), lambda i: (0, i)),
    )(hidden, dpre, dup, gate_mat, up_mat, down_mat)
    back = lax.all_to_all(
        back.reshape(peers, capacity, 2 * width), "tp", split_axis=0, concat_axis=0, tiled=True
    ).reshape(slots, 2 * width)

    mid_2 = along(plus(in_1, part[2]), MIDDLE)
    last_out = along(far, OUTWARD)
    turned = [turned[0]] + [
        along(turned[k], tuple((i, i ^ k) for i in range(4))) for k in range(1, 4)
    ]
    end_3 = along(plus(mid_2, part[1]), ENDS)
    mid_3 = along(plus(in_2, part[3]), MIDDLE)

    layer_output, token_grad, gate_grad = call(
        home_kernel,
        [shaped((count, width)), shaped((count, width)), shaped((1, count), F32)],
        grid=(4,),
        in_specs=[
            whole(1, count),
            whole(1, count),
            pl.BlockSpec((slots, 2 * wide), lambda i: (0, i)),
            pl.BlockSpec((count, wide), lambda i: (0, i)),
        ],
        out_specs=[pl.BlockSpec((count, wide), lambda i: (0, i))] * 2 + [whole(1, count)],
        scratch_shapes=[pltpu.VMEM((count, 1), F32)],
    )(slot, gates, back, cotangent)
    down_grad = call(down_kernel, shaped((1, quarter, width)))(
        *turned, cot_a, near, across, far, far_out, last_out, end_3, mid_3, part[0]
    )
    return layer_output, token_grad, gate_grad.reshape(count, 1), down_grad


def solution(mesh):
    rows = P(("ctx", "tp"), None)
    expert = P("tp", None, None)
    line = mesh.shape["ctx"] == 4 and mesh.shape["tp"] == 8
    return jax.shard_map(
        body_line if line else body_any,
        mesh=mesh,
        in_specs=(rows, rows, rows, rows, expert, expert, expert),
        out_specs=(rows, rows, rows, P("tp", "ctx", None)),
        check_vma=False,
    )
```

time: 118 us -> 128 us (1.085)
  starting transfers between devices: 17.8 us -> 48.9 us
  matrix products: 29.7 us -> 0 us
  Pallas kernels: 0 us -> 19 us
  local copies, waits for them, and re-layouts: 1.65 us -> 17 us
  between operations: 14.1 us -> 0.99 us
  waiting for transfers between devices: 51.7 us -> 39.2 us
    ppermute x0 -> x20, starting transfers between devices: none -> 40.1 us  [the longest x13 33.2 us: along(): return lax.ppermute(rows, 'ctx', pairs)]
    ppermute x0 -> x20, waiting for transfers between devices: none -> 39.2 us  [the longest x13 25.4 us: along(): return lax.ppermute(rows, 'ctx', pairs)]
    all_to_all x4 -> x2, waiting for transfers between devices: 35.7 us -> 0.01 us  [the longest x1 0.01 us: body_line(): lax.all_to_all(send_tok.reshape(peers, capacity, width), 'tp', split_axis...]
    dot_general x11 -> x0, matrix products: 29.7 us -> none  [the longest x1 3.8 us: body(): lax.dot_general(hidden, cot_flat, contract_first, preferred_element_type=...]
    pallas_call x0 -> x8, Pallas kernels: none -> 19 us  [the longest x1 5.68 us: body_line(): call(hidden_kernel, [shaped((slots, inner))] * 3 + [shaped((quarter, half...]
    reduce_scatter x1 -> x0, waiting for transfers between devices: 16 us -> none  [body(): lax.psum_scatter(lax.dot_general(hidden, cot_flat, contract_first, prefer...]
    unnamed x12 -> x64, local copies, waits for them, and re-layouts: 1.65 us -> 17 us
    all_to_all x4 -> x2, starting transfers between devices: 17.8 us -> 8.88 us  [the longest x1 5.16 us: body_line(): lax.all_to_all(send_tok.reshape(peers, capacity, width), 'tp', split_axis...]
  transfers between devices with their start and end apart: 5 -> 22, of which waited for: 5 -> 8; matrix products, arithmetic and copies ran while one was open for 20% -> 2% of each run, Pallas kernels for 0% -> 12%
where the time goes in v1:
time: 128 us; the launch traced here: 127 us
  starting transfers between devices  48.9 us (38%)
  waiting for transfers between devices  39.2 us (31%)
  Pallas kernels  19 us (15%)
  local copies, waits for them, and re-layouts  17 us (13%)
  other arithmetic  2.36 us (2%)
    ppermute x13, starting transfers between devices, along(): return lax.ppermute(rows, 'ctx', pairs)  33.2 us
    ppermute x13, waiting for transfers between devices, along(): return lax.ppermute(rows, 'ctx', pairs)  25.4 us
    unnamed x64, local copies, waits for them, and re-layouts  17 us
    ppermute x7, waiting for transfers between devices, body_line(): got[k] = lax.ppermute(blocks[k], 'tp', [(i, i ^ k) for i in range(peers)])  13.8 us
    ppermute x7, starting transfers between devices, body_line(): got[k] = lax.ppermute(blocks[k], 'tp', [(i, i ^ k) for i in range(peers)])  6.81 us
    pallas_call x1, Pallas kernels, body_line(): call(hidden_kernel, [shaped((slots, inner))] * 3 + [shaped((quarter, half...  5.68 us
    all_to_all x1, starting transfers between devices, body_line(): lax.all_to_all(send_tok.reshape(peers, capacity, width), 'tp', split_axis...  5.16 us
    all_to_all x1, starting transfers between devices, body_line(): lax.all_to_all(back.reshape(peers, capacity, 2 * width), 'tp', split_axis...  3.72 us
  transfers between devices with their start and end apart: 22, of which 8 were waited for; matrix products, arithmetic and copies ran while one was open for 2% of the time, Pallas kernels for 12%

profile of v1, /device:TPU:0, one launch (start us, length us, event | category | flops | bytes accessed | tf_op | source)
XLA Modules:
  0.0 127.4 jit_solution(1163739755714116942)
XLA Ops:
  0.7 1.2 copy-done.7
  8.5 5.2 %all-to-all-start = ((bf16[8,24,2048]{2,1,0:T(8,128)(2,1)}), bf16[8,24,2048]{2,1,0:T(8,128)(2,1)}, u32[]{:S(2)}, u32[]{:S(2)}) async-start(bf16[8,24,2048]{2,1,0:T(8,128)(2,1)} %bitcast.18), calls=%async_computation | async-start | bytes 1572864 | tf_op jit(solution)/shard_map/all_to_all | solution.py:256
  14.1 1.7 %collective-permute-start.1 = (bf16[24,2048]{1,0:T(8,128)(2,1)}, bf16[24,2048]{1,0:T(8,128)(2,1)S(1)}, u32[]{:S(2)}, u32[]{:S(2)}) collective-permute-start(bf16[24,2048]{1,0:T(8,128)(2,1)} %copy-done.30), channel_id=1, source_target_pairs={{0,2},{1,3},{2,0},{3,1},{4,6},{5,7},{6,4},{7,5},{8,10},{9,11},{10,... | collective-permute-start | bytes 294920 | tf_op jit(solution)/shard_map/ppermute | solution.py:254
  15.8 1.7 %collective-permute-start.3 = (bf16[24,2048]{1,0:T(8,128)(2,1)S(1)}, bf16[24,2048]{1,0:T(8,128)(2,1)S(1)}, u32[]{:S(2)}, u32[]{:S(2)}) collective-permute-start(bf16[24,2048]{1,0:T(8,128)(2,1)S(1)} %get-tuple-element.34), channel_id=1, source_target_pairs={{0,4},{1,5},{2,6},{3,7},{4,0},{5,1},{6,2},{7,3},{8,12},{9,13},{10,... | collective-permute-start | bytes 294920 | tf_op jit(solution)/shard_map/ppermute | solution.py:254
  17.6 2.6 %collective-permute-start.5 = (bf16[24,2048]{1,0:T(8,128)(2,1)S(1)}, bf16[24,2048]{1,0:T(8,128)(2,1)S(1)}, u32[]{:S(2)}, u32[]{:S(2)}) collective-permute-start(bf16[24,2048]{1,0:T(8,128)(2,1)S(1)} %get-tuple-element.36), channel_id=1, source_target_pairs={{0,6},{1,7},{2,4},{3,5},{4,2},{5,3},{6,0},{7,1},{8,14},{9,15},{10,... | collective-permute-start | bytes 294920 | tf_op jit(solution)/shard_map/ppermute | solution.py:254
  20.2 7.7 %collective-permute-done.1.refs_2_ = bf16[24,2048]{1,0:T(8,128)(2,1)S(1)} collective-permute-done((bf16[24,2048]{1,0:T(8,128)(2,1)}, bf16[24,2048]{1,0:T(8,128)(2,1)S(1)}, u32[]{:S(2)}, u32[]{:S(2)}) %collective-permute-start.1) | collective-permute-done | bytes 98336 | tf_op jit(solution)/shard_map/ppermute | solution.py:254
  29.1 4.0 %collective-permute-done.5.refs_6_ = bf16[24,2048]{1,0:T(8,128)(2,1)S(1)} collective-permute-done((bf16[24,2048]{1,0:T(8,128)(2,1)S(1)}, bf16[24,2048]{1,0:T(8,128)(2,1)S(1)}, u32[]{:S(2)}, u32[]{:S(2)}) %collective-permute-start.5) | collective-permute-done | bytes 98336 | tf_op jit(solution)/shard_map/ppermute | solution.py:254
  33.1 1.2 collective-permute-done.6.refs_7_
  36.0 2.0 %collective-permute-start.10 = (bf16[192,1024]{1,0:T(8,128)(2,1)}, bf16[192,1024]{1,0:T(8,128)(2,1)}, u32[]{:S(2)}, u32[]{:S(2)}) collective-permute-start(bf16[192,1024]{1,0:T(8,128)(2,1)} %get-tuple-element.38.cot_a), channel_id=1, source_target_pairs={{0,8},{8,0},{16,24},{24,16},{1,9},{9,1},{17,25},{25,17},{2,10},{10... | collective-permute-start | bytes 1179656 | tf_op jit(solution)/shard_map/ppermute | solution.py:231
  38.0 2.4 %shard_map.105.dhid = f32[192,768]{1,0:T(8,128)S(1)} custom-call(bf16[192,1024]{1,0:T(8,128)(2,1)} %get-tuple-element.38.cot_a, bf16[192,1024]{1,0:T(8,128)(2,1)S(1)} %get-tuple-element.39.cot_b, bf16[768,2048]{1,0:T(8,128)(2,1)S(1)} %bitcast.10), custom_call_target="tpu_custom_call" | custom-call | flops 1 | bytes 1 | tf_op jit(solution)/shard_map/pallas_call | solution.py:270
  41.3 1.9 %copy-done.1 = bf16[1,2048,768]{2,1,0:T(8,128)(2,1)S(1)} copy-done((bf16[1,2048,768]{2,1,0:T(8,128)(2,1)S(1)}, bf16[1,2048,768]{2,1,0:T(8,128)(2,1)}, u32[]{:S(2)}) %copy-start.1) | copy-done | bytes 3145752
  43.2 1.9 %copy-done.2 = bf16[1,2048,768]{2,1,0:T(8,128)(2,1)S(1)} copy-done((bf16[1,2048,768]{2,1,0:T(8,128)(2,1)S(1)}, bf16[1,2048,768]{2,1,0:T(8,128)(2,1)}, u32[]{:S(2)}) %copy-start.2) | copy-done | bytes 3145752
  45.1 1.1 copy-done.6
  46.1 5.7 %shard_map.106 = (bf16[192,768]{1,0:T(8,128)(2,1)S(1)}, bf16[192,768]{1,0:T(8,128)(2,1)S(1)}, bf16[192,768]{1,0:T(8,128)(2,1)S(1)}, bf16[192,1024]{1,0:T(8,128)(...) custom-call(bf16[192,2048]{1,0:T(8,128)(2,1)} %bitcast.3.rows, ...), custom_call_target="tpu_custom_call" | custom-call | flops 1 | bytes 1 | tf_op jit(solution)/shard_map/pallas_call | solution.py:279
  54.1 2.7 %collective-permute-start.15 = (bf16[192,1024]{1,0:T(8,128)(2,1)}, bf16[192,1024]{1,0:T(8,128)(2,1)}, u32[]{:S(2)}, u32[]{:S(2)}) collective-permute-start(bf16[192,1024]{1,0:T(8,128)(2,1)} %get-tuple-element.50), channel_id=1, source_target_pairs={{0,8},{24,16},{1,9},{25,17},{2,10},{26,18},{3,11},{27,19},{4,12},{... | collective-permute-start | bytes 1179656 | tf_op jit(solution)/shard_map/ppermute | solution.py:231
  56.8 3.6 %shard_map.107 = bf16[192,4096]{1,0:T(8,128)(2,1)S(1)} custom-call(bf16[192,768]{1,0:T(8,128)(2,1)S(1)} %get-tuple-element.40.hidden, bf16[192,768]{1,0:T(8,128)(2,1)S(1)} %get-tuple-element.41.dpre, bf16[192,768]{1,0:T(8,128)(2,1)S(1)} %get-tuple-element.42.dup, bf16[2048,768]{1,0:T(8,128)(2,1)S(1)} %bitcast.13, bf16[2048,768]{1,0:T(8,128)(2,1)S(1)} %bitcast.15, ...), custom_call_target="tpu_custom_call" | custom-call | flops 1 | bytes 1 | tf_op jit(solution)/shard_map/pallas_call | solution.py:294
  60.5 1.2 copy-done.3
  61.7 3.7 %all-to-all-start.1 = ((bf16[8,24,4096]{2,1,0:T(8,128)(2,1)}), bf16[8,24,4096]{2,1,0:T(8,128)(2,1)S(1)}, u32[]{:S(2)}, u32[]{:S(2)}) async-start(bf16[8,24,4096]{2,1,0:T(8,128)(2,1)} %bitcast.17), calls=%async_computation.1 | async-start | bytes 3145728 | tf_op jit(solution)/shard_map/all_to_all | solution.py:303
  66.8 6.2 %collective-permute-start.18 = (bf16[192,1024]{1,0:T(8,128)(2,1)S(1)}, bf16[192,1024]{1,0:T(8,128)(2,1)S(1)}, u32[]{:S(2)}, u32[]{:S(2)}) collective-permute-start(bf16[192,1024]{1,0:T(8,128)(2,1)S(1)} %copy-done.15), channel_id=1, source_target_pairs={{0,8},{24,16},{1,9},{25,17},{2,10},{26,18},{3,11},{27,19},{4,12},{... | collective-permute-start | bytes 1179656 | tf_op jit(solution)/shard_map/ppermute | solution.py:231
  73.0 1.1 add_convert_fusion.2
  74.8 1.3 %collective-permute-start.13 = (bf16[192,1024]{1,0:T(8,128)(2,1)S(1)}, bf16[192,1024]{1,0:T(8,128)(2,1)S(1)}, u32[]{:S(2)}, u32[]{:S(2)}) collective-permute-start(bf16[192,1024]{1,0:T(8,128)(2,1)S(1)} %collective-permute-done.11.across), channel_id=1, source_target_pairs={{8,0},{16,24},{9,1},{17,25},{10,2},{18,26},{11,3},{19,27},{12,4},{... | collective-permute-start | bytes 1179656 | tf_op jit(solution)/shard_map/ppermute | solution.py:231
  76.1 1.3 %collective-permute-start.14 = (bf16[192,1024]{1,0:T(8,128)(2,1)S(1)}, bf16[192,1024]{1,0:T(8,128)(2,1)S(1)}, u32[]{:S(2)}, u32[]{:S(2)}) collective-permute-start(bf16[192,1024]{1,0:T(8,128)(2,1)S(1)} %collective-permute-done.12.far), channel_id=1, source_target_pairs={{8,0},{16,24},{9,1},{17,25},{10,2},{18,26},{11,3},{19,27},{12,4},{... | collective-permute-start | bytes 1179656 | tf_op jit(solution)/shard_map/ppermute | solution.py:231
  77.4 4.1 %collective-permute-done.18 = bf16[192,1024]{1,0:T(8,128)(2,1)S(1)} collective-permute-done((bf16[192,1024]{1,0:T(8,128)(2,1)S(1)}, bf16[192,1024]{1,0:T(8,128)(2,1)S(1)}, u32[]{:S(2)}, u32[]{:S(2)}) %collective-permute-start.18) | collective-permute-done | bytes 393248 | tf_op jit(solution)/shard_map/ppermute | solution.py:231
  81.6 1.1 add_convert_fusion
  83.7 12.6 %collective-permute-start.17 = (bf16[192,1024]{1,0:T(8,128)(2,1)S(1)}, bf16[192,1024]{1,0:T(8,128)(2,1)S(1)}, u32[]{:S(2)}, u32[]{:S(2)}) collective-permute-start(bf16[192,1024]{1,0:T(8,128)(2,1)S(1)} %add_convert_fusion.1), channel_id=1, source_target_pairs={{0,8},{8,0},{16,24},{24,16},{1,9},{9,1},{17,25},{25,17},{2,10},{10... | collective-permute-start | bytes 1179656 | tf_op jit(solution)/shard_map/ppermute | solution.py:231
  96.4 11.9 %collective-permute-done.7.h1 = bf16[192,192]{1,0:T(8,128)(2,1)S(1)} collective-permute-done((bf16[192,192]{1,0:T(8,128)(2,1)S(1)}, bf16[192,192]{1,0:T(8,128)(2,1)S(1)}, u32[]{:S(2)}, u32[]{:S(2)}) %collective-permute-start.7) | collective-permute-done | bytes 73760 | tf_op jit(solution)/shard_map/ppermute | solution.py:231
  108.3 1.6 %collective-permute-start.8 = (bf16[192,192]{1,0:T(8,128)(2,1)S(1)}, bf16[192,192]{1,0:T(8,128)(2,1)S(1)}, u32[]{:S(2)}, u32[]{:S(2)}) collective-permute-start(bf16[192,192]{1,0:T(8,128)(2,1)S(1)} %copy-done.26), channel_id=1, source_target_pairs={{0,16},{8,24},{16,0},{24,8},{1,17},{9,25},{17,1},{25,9},{2,18},{10... | collective-permute-start | bytes 221192 | tf_op jit(solution)/shard_map/ppermute | solution.py:231
  109.9 5.6 %collective-permute-done.8.h2 = bf16[192,192]{1,0:T(8,128)(2,1)S(1)} collective-permute-done((bf16[192,192]{1,0:T(8,128)(2,1)S(1)}, bf16[192,192]{1,0:T(8,128)(2,1)S(1)}, u32[]{:S(2)}, u32[]{:S(2)}) %collective-permute-start.8) | collective-permute-done | bytes 73760 | tf_op jit(solution)/shard_map/ppermute | solution.py:231
  115.4 2.6 %collective-permute-start.9 = (bf16[192,192]{1,0:T(8,128)(2,1)S(1)}, bf16[192,192]{1,0:T(8,128)(2,1)S(1)}, u32[]{:S(2)}, u32[]{:S(2)}) collective-permute-start(bf16[192,192]{1,0:T(8,128)(2,1)S(1)} %copy-done.24), channel_id=1, source_target_pairs={{0,24},{8,16},{16,8},{24,0},{1,25},{9,17},{17,9},{25,1},{2,26},{10... | collective-permute-start | bytes 221192 | tf_op jit(solution)/shard_map/ppermute | solution.py:231
  118.0 3.8 %collective-permute-done.9.h3 = bf16[192,192]{1,0:T(8,128)(2,1)S(1)} collective-permute-done((bf16[192,192]{1,0:T(8,128)(2,1)S(1)}, bf16[192,192]{1,0:T(8,128)(2,1)S(1)}, u32[]{:S(2)}, u32[]{:S(2)}) %collective-permute-start.9) | collective-permute-done | bytes 73760 | tf_op jit(solution)/shard_map/ppermute | solution.py:231
  121.9 2.9 %shard_map.109 = bf16[1,192,2048]{2,1,0:T(8,128)(2,1)} custom-call(bf16[192,192]{1,0:T(8,128)(2,1)S(1)} %copy-done.19, bf16[192,192]{1,0:T(8,128)(2,1)S(1)} %collective-permute-done.7.h1, bf16[192,192]{1,0:T(8,128)(2,1)S(1)} %collective-permute-done.8.h2, bf16[192,192]{1,0:T(8,128)(2,1)S(1)} %collective-permute-done.9.h3, ...), custom_call_target="tpu_custom_call" | custom-call | flops 1 | bytes 1 | tf_op jit(solution)/shard_map/pallas_call | solution.py:328
  124.8 2.7 %shard_map.108 = (bf16[128,2048]{1,0:T(8,128)(2,1)}, bf16[128,2048]{1,0:T(8,128)(2,1)}, f32[1,128]{1,0:T(1,128)}) custom-call(s32[1,128]{1,0:T(1,128)S(1)} %get-tuple-element.29.slot, f32[1,128]{1,0:T(1,128)S(1)} %bitcast.20, bf16[192,4096]{1,0:T(8,128)(2,1)S(1)} %bitcast.16, bf16[128,2048]{1,0:T(8,128)(2,1)S(1)} %copy-done.8), custom_call_target="tpu_custom_call" | custom-call | flops 1 | bytes 1 | tf_op jit(solution)/shard_map/pallas_call | solution.py:315
  (87 shorter events, 16.4 us)
Async XLA Ops:
  0.6 37.4 %copy-start = (bf16[1,768,2048]{2,1,0:T(8,128)(2,1)S(1)}, bf16[1,768,2048]{2,1,0:T(8,128)(2,1)}, u32[]{:S(2)}) copy-start(bf16[1,768,2048]{2,1,0:T(8,128)(2,1)} %param.13) | copy-start | bytes 9437188
  8.5 32.8 %all-to-all-start = ((bf16[8,24,2048]{2,1,0:T(8,128)(2,1)}), bf16[8,24,2048]{2,1,0:T(8,128)(2,1)}, u32[]{:S(2)}, u32[]{:S(2)}) async-start(bf16[8,24,2048]{2,1,0:T(8,128)(2,1)} %bitcast.18), calls=%async_computation | async-start | bytes 1572864 | tf_op jit(solution)/shard_map/all_to_all | solution.py:256
  13.6 4.0 %collective-permute-start = (bf16[24,2048]{1,0:T(8,128)(2,1)}, bf16[24,2048]{1,0:T(8,128)(2,1)S(1)}, u32[]{:S(2)}, u32[]{:S(2)}) collective-permute-start(bf16[24,2048]{1,0:T(8,128)(2,1)} %copy-done.31), channel_id=1, source_target_pairs={{0,1},{1,0},{2,3},{3,2},{4,5},{5,4},{6,7},{7,6},{8,9},{9,8},{10,11... | collective-permute-start | bytes 294920 | tf_op jit(solution)/shard_map/ppermute | solution.py:254
  14.1 13.8 %collective-permute-start.1 = (bf16[24,2048]{1,0:T(8,128)(2,1)}, bf16[24,2048]{1,0:T(8,128)(2,1)S(1)}, u32[]{:S(2)}, u32[]{:S(2)}) collective-permute-start(bf16[24,2048]{1,0:T(8,128)(2,1)} %copy-done.30), channel_id=1, source_target_pairs={{0,2},{1,3},{2,0},{3,1},{4,6},{5,7},{6,4},{7,5},{8,10},{9,11},{10,... | collective-permute-start | bytes 294920 | tf_op jit(solution)/shard_map/ppermute | solution.py:254
  15.8 13.3 %collective-permute-start.2 = (bf16[24,2048]{1,0:T(8,128)(2,1)}, bf16[24,2048]{1,0:T(8,128)(2,1)S(1)}, u32[]{:S(2)}, u32[]{:S(2)}) collective-permute-start(bf16[24,2048]{1,0:T(8,128)(2,1)} %copy-done.29), channel_id=1, source_target_pairs={{0,3},{1,2},{2,1},{3,0},{4,7},{5,6},{6,5},{7,4},{8,11},{9,10},{10,... | collective-permute-start | bytes 294920 | tf_op jit(solution)/shard_map/ppermute | solution.py:254
  15.8 13.3 %collective-permute-start.3 = (bf16[24,2048]{1,0:T(8,128)(2,1)S(1)}, bf16[24,2048]{1,0:T(8,128)(2,1)S(1)}, u32[]{:S(2)}, u32[]{:S(2)}) collective-permute-start(bf16[24,2048]{1,0:T(8,128)(2,1)S(1)} %get-tuple-element.34), channel_id=1, source_target_pairs={{0,4},{1,5},{2,6},{3,7},{4,0},{5,1},{6,2},{7,3},{8,12},{9,13},{10,... | collective-permute-start | bytes 294920 | tf_op jit(solution)/shard_map/ppermute | solution.py:254
  17.5 11.6 %collective-permute-start.4 = (bf16[24,2048]{1,0:T(8,128)(2,1)S(1)}, bf16[24,2048]{1,0:T(8,128)(2,1)S(1)}, u32[]{:S(2)}, u32[]{:S(2)}) collective-permute-start(bf16[24,2048]{1,0:T(8,128)(2,1)S(1)} %get-tuple-element.35), channel_id=1, source_target_pairs={{0,5},{1,4},{2,7},{3,6},{4,1},{5,0},{6,3},{7,2},{8,13},{9,12},{10,... | collective-permute-start | bytes 294920 | tf_op jit(solution)/shard_map/ppermute | solution.py:254
  17.6 15.4 %collective-permute-start.5 = (bf16[24,2048]{1,0:T(8,128)(2,1)S(1)}, bf16[24,2048]{1,0:T(8,128)(2,1)S(1)}, u32[]{:S(2)}, u32[]{:S(2)}) collective-permute-start(bf16[24,2048]{1,0:T(8,128)(2,1)S(1)} %get-tuple-element.36), channel_id=1, source_target_pairs={{0,6},{1,7},{2,4},{3,5},{4,2},{5,3},{6,0},{7,1},{8,14},{9,15},{10,... | collective-permute-start | bytes 294920 | tf_op jit(solution)/shard_map/ppermute | solution.py:254
  28.0 6.3 %collective-permute-start.6 = (bf16[24,2048]{1,0:T(8,128)(2,1)S(1)}, bf16[24,2048]{1,0:T(8,128)(2,1)S(1)}, u32[]{:S(2)}, u32[]{:S(2)}) collective-permute-start(bf16[24,2048]{1,0:T(8,128)(2,1)S(1)} %get-tuple-element.37), channel_id=1, source_target_pairs={{0,7},{1,6},{2,5},{3,4},{4,3},{5,2},{6,1},{7,0},{8,15},{9,14},{10,... | collective-permute-start | bytes 294920 | tf_op jit(solution)/shard_map/ppermute | solution.py:254
  36.0 30.1 %collective-permute-start.10 = (bf16[192,1024]{1,0:T(8,128)(2,1)}, bf16[192,1024]{1,0:T(8,128)(2,1)}, u32[]{:S(2)}, u32[]{:S(2)}) collective-permute-start(bf16[192,1024]{1,0:T(8,128)(2,1)} %get-tuple-element.38.cot_a), channel_id=1, source_target_pairs={{0,8},{8,0},{16,24},{24,16},{1,9},{9,1},{17,25},{25,17},{2,10},{10... | collective-permute-start | bytes 1179656 | tf_op jit(solution)/shard_map/ppermute | solution.py:231
  54.1 6.4 %copy-start.27 = (bf16[192,192]{1,0:T(8,128)(2,1)}, bf16[192,192]{1,0:T(8,128)(2,1)S(1)}, u32[]{:S(2)}) copy-start(bf16[192,192]{1,0:T(8,128)(2,1)S(1)} %get-tuple-element.47) | copy-start | bytes 221188
  54.1 18.9 %collective-permute-start.15 = (bf16[192,1024]{1,0:T(8,128)(2,1)}, bf16[192,1024]{1,0:T(8,128)(2,1)}, u32[]{:S(2)}, u32[]{:S(2)}) collective-permute-start(bf16[192,1024]{1,0:T(8,128)(2,1)} %get-tuple-element.50), channel_id=1, source_target_pairs={{0,8},{24,16},{1,9},{25,17},{2,10},{26,18},{3,11},{27,19},{4,12},{... | collective-permute-start | bytes 1179656 | tf_op jit(solution)/shard_map/ppermute | solution.py:231
  61.6 21.9 %copy-start.13 = (bf16[192,1024]{1,0:T(8,128)(2,1)S(1)}, bf16[192,1024]{1,0:T(8,128)(2,1)}, u32[]{:S(2)}) copy-start(bf16[192,1024]{1,0:T(8,128)(2,1)} %copy-done.12) | copy-start | bytes 1179652
  61.6 34.7 %copy-start.28 = (bf16[192,192]{1,0:T(8,128)(2,1)S(1)}, bf16[192,192]{1,0:T(8,128)(2,1)}, u32[]{:S(2)}) copy-start(bf16[192,192]{1,0:T(8,128)(2,1)} %copy-done.27) | copy-start | bytes 221188
  61.6 46.6 %copy-start.26 = (bf16[192,192]{1,0:T(8,128)(2,1)S(1)}, bf16[192,192]{1,0:T(8,128)(2,1)}, u32[]{:S(2)}) copy-start(bf16[192,192]{1,0:T(8,128)(2,1)} %copy-done.25) | copy-start | bytes 221188
  61.6 53.8 %copy-start.24 = (bf16[192,192]{1,0:T(8,128)(2,1)S(1)}, bf16[192,192]{1,0:T(8,128)(2,1)}, u32[]{:S(2)}) copy-start(bf16[192,192]{1,0:T(8,128)(2,1)} %copy-done.23) | copy-start | bytes 221188
  61.6 60.2 %copy-start.11 = (bf16[192,1024]{1,0:T(8,128)(2,1)S(1)}, bf16[192,1024]{1,0:T(8,128)(2,1)}, u32[]{:S(2)}) copy-start(bf16[192,1024]{1,0:T(8,128)(2,1)} %copy-done.10) | copy-start | bytes 1179652
  61.6 60.2 %copy-start.19 = (bf16[192,192]{1,0:T(8,128)(2,1)S(1)}, bf16[192,192]{1,0:T(8,128)(2,1)}, u32[]{:S(2)}) copy-start(bf16[192,192]{1,0:T(8,128)(2,1)} %copy-done.18) | copy-start | bytes 221188
  61.7 63.1 %all-to-all-start.1 = ((bf16[8,24,4096]{2,1,0:T(8,128)(2,1)}), bf16[8,24,4096]{2,1,0:T(8,128)(2,1)S(1)}, u32[]{:S(2)}, u32[]{:S(2)}) async-start(bf16[8,24,4096]{2,1,0:T(8,128)(2,1)} %bitcast.17), calls=%async_computation.1 | async-start | bytes 3145728 | tf_op jit(solution)/shard_map/all_to_all | solution.py:303
  65.4 9.4 %collective-permute-start.11 = (bf16[192,1024]{1,0:T(8,128)(2,1)}, bf16[192,1024]{1,0:T(8,128)(2,1)S(1)}, u32[]{:S(2)}, u32[]{:S(2)}) collective-permute-start(bf16[192,1024]{1,0:T(8,128)(2,1)} %get-tuple-element.38.cot_a), channel_id=1, source_target_pairs={{8,16},{16,8},{9,17},{17,9},{10,18},{18,10},{11,19},{19,11},{12,20... | collective-permute-start | bytes 1179656 | tf_op jit(solution)/shard_map/ppermute | solution.py:231
  66.1 10.0 %collective-permute-start.12 = (bf16[192,1024]{1,0:T(8,128)(2,1)}, bf16[192,1024]{1,0:T(8,128)(2,1)S(1)}, u32[]{:S(2)}, u32[]{:S(2)}) collective-permute-start(bf16[192,1024]{1,0:T(8,128)(2,1)} %collective-permute-done.10.near), channel_id=1, source_target_pairs={{8,16},{16,8},{9,17},{17,9},{10,18},{18,10},{11,19},{19,11},{12,20... | collective-permute-start | bytes 1179656 | tf_op jit(solution)/shard_map/ppermute | solution.py:231
  66.8 14.8 %collective-permute-start.18 = (bf16[192,1024]{1,0:T(8,128)(2,1)S(1)}, bf16[192,1024]{1,0:T(8,128)(2,1)S(1)}, u32[]{:S(2)}, u32[]{:S(2)}) collective-permute-start(bf16[192,1024]{1,0:T(8,128)(2,1)S(1)} %copy-done.15), channel_id=1, source_target_pairs={{0,8},{24,16},{1,9},{25,17},{2,10},{26,18},{3,11},{27,19},{4,12},{... | collective-permute-start | bytes 1179656 | tf_op jit(solution)/shard_map/ppermute | solution.py:231
  74.1 9.4 %collective-permute-start.16 = (bf16[192,1024]{1,0:T(8,128)(2,1)S(1)}, bf16[192,1024]{1,0:T(8,128)(2,1)S(1)}, u32[]{:S(2)}, u32[]{:S(2)}) collective-permute-start(bf16[192,1024]{1,0:T(8,128)(2,1)S(1)} %add_convert_fusion.2), channel_id=1, source_target_pairs={{8,16},{16,8},{9,17},{17,9},{10,18},{18,10},{11,19},{19,11},{12,20... | collective-permute-start | bytes 1179656 | tf_op jit(solution)/shard_map/ppermute | solution.py:231
  74.8 47.0 %collective-permute-start.13 = (bf16[192,1024]{1,0:T(8,128)(2,1)S(1)}, bf16[192,1024]{1,0:T(8,128)(2,1)S(1)}, u32[]{:S(2)}, u32[]{:S(2)}) collective-permute-start(bf16[192,1024]{1,0:T(8,128)(2,1)S(1)} %collective-permute-done.11.across), channel_id=1, source_target_pairs={{8,0},{16,24},{9,1},{17,25},{10,2},{18,26},{11,3},{19,27},{12,4},{... | collective-permute-start | bytes 1179656 | tf_op jit(solution)/shard_map/ppermute | solution.py:231
  76.1 45.7 %collective-permute-start.14 = (bf16[192,1024]{1,0:T(8,128)(2,1)S(1)}, bf16[192,1024]{1,0:T(8,128)(2,1)S(1)}, u32[]{:S(2)}, u32[]{:S(2)}) collective-permute-start(bf16[192,1024]{1,0:T(8,128)(2,1)S(1)} %collective-permute-done.12.far), channel_id=1, source_target_pairs={{8,0},{16,24},{9,1},{17,25},{10,2},{18,26},{11,3},{19,27},{12,4},{... | collective-permute-start | bytes 1179656 | tf_op jit(solution)/shard_map/ppermute | solution.py:231
  82.7 42.1 %copy-start.8 = (bf16[128,2048]{1,0:T(8,128)(2,1)S(1)}, bf16[128,2048]{1,0:T(8,128)(2,1)}, u32[]{:S(2)}) copy-start(bf16[128,2048]{1,0:T(8,128)(2,1)} %cot.3) | copy-start | bytes 1572868
  82.7 42.1 %copy-start.21 = (f32[128,1]{0,1:T(1,128)S(1)}, f32[128,1]{0,1:T(1,128)}, u32[]{:S(2)}) copy-start(f32[128,1]{0,1:T(1,128)} %param.10) | copy-start | bytes 1540
  82.7 39.2 %collective-permute-start.19 = (bf16[192,1024]{1,0:T(8,128)(2,1)S(1)}, bf16[192,1024]{1,0:T(8,128)(2,1)S(1)}, u32[]{:S(2)}, u32[]{:S(2)}) collective-permute-start(bf16[192,1024]{1,0:T(8,128)(2,1)S(1)} %add_convert_fusion), channel_id=1, source_target_pairs={{8,16},{16,8},{9,17},{17,9},{10,18},{18,10},{11,19},{19,11},{12,20... | collective-permute-start | bytes 1179656 | tf_op jit(solution)/shard_map/ppermute | solution.py:231
  83.7 38.2 %collective-permute-start.17 = (bf16[192,1024]{1,0:T(8,128)(2,1)S(1)}, bf16[192,1024]{1,0:T(8,128)(2,1)S(1)}, u32[]{:S(2)}, u32[]{:S(2)}) collective-permute-start(bf16[192,1024]{1,0:T(8,128)(2,1)S(1)} %add_convert_fusion.1), channel_id=1, source_target_pairs={{0,8},{8,0},{16,24},{24,16},{1,9},{9,1},{17,25},{25,17},{2,10},{10... | collective-permute-start | bytes 1179656 | tf_op jit(solution)/shard_map/ppermute | solution.py:231
  96.3 12.0 %collective-permute-start.7 = (bf16[192,192]{1,0:T(8,128)(2,1)S(1)}, bf16[192,192]{1,0:T(8,128)(2,1)S(1)}, u32[]{:S(2)}, u32[]{:S(2)}) collective-permute-start(bf16[192,192]{1,0:T(8,128)(2,1)S(1)} %copy-done.28), channel_id=1, source_target_pairs={{0,8},{8,0},{16,24},{24,16},{1,9},{9,1},{17,25},{25,17},{2,10},{10... | collective-permute-start | bytes 221192 | tf_op jit(solution)/shard_map/ppermute | solution.py:231
  108.3 7.2 %collective-permute-start.8 = (bf16[192,192]{1,0:T(8,128)(2,1)S(1)}, bf16[192,192]{1,0:T(8,128)(2,1)S(1)}, u32[]{:S(2)}, u32[]{:S(2)}) collective-permute-start(bf16[192,192]{1,0:T(8,128)(2,1)S(1)} %copy-done.26), channel_id=1, source_target_pairs={{0,16},{8,24},{16,0},{24,8},{1,17},{9,25},{17,1},{25,9},{2,18},{10... | collective-permute-start | bytes 221192 | tf_op jit(solution)/shard_map/ppermute | solution.py:231
  115.4 6.4 %collective-permute-start.9 = (bf16[192,192]{1,0:T(8,128)(2,1)S(1)}, bf16[192,192]{1,0:T(8,128)(2,1)S(1)}, u32[]{:S(2)}, u32[]{:S(2)}) collective-permute-start(bf16[192,192]{1,0:T(8,128)(2,1)S(1)} %copy-done.24), channel_id=1, source_target_pairs={{0,24},{8,16},{16,8},{24,0},{1,25},{9,17},{17,9},{25,1},{2,26},{10... | collective-permute-start | bytes 221192 | tf_op jit(solution)/shard_map/ppermute | solution.py:231
  (22 other events, 41.2 us)

commit v2 on v0

v2 whole, which is shorter than its diff:
```python
import functools

import jax
import jax.numpy as jnp
from jax import lax
from jax.experimental import pallas as pl
from jax.experimental.pallas import tpu as pltpu
from jax.sharding import PartitionSpec as P

BF16 = jnp.bfloat16
F32 = jnp.float32
CONTRACT_FIRST = (((0,), (0,)), ((), ()))
CONTRACT_LAST = (((1,), (1,)), ((), ()))


def expert_block(rows_in, rows_cot, gate_mat, up_mat, down_mat):
    pre_act = jnp.dot(rows_in, gate_mat, preferred_element_type=F32)
    up_act = jnp.dot(rows_in, up_mat, preferred_element_type=F32)
    sigma = jax.nn.sigmoid(pre_act)
    hidden = (pre_act * sigma * up_act).astype(BF16)
    output = jnp.dot(hidden, down_mat, preferred_element_type=F32).astype(BF16)
    dhidden = lax.dot_general(rows_cot, down_mat, CONTRACT_LAST, preferred_element_type=F32)
    dup_act = (dhidden * pre_act * sigma).astype(BF16)
    dpre_act = (dhidden * up_act * sigma * (1.0 + pre_act * (1.0 - sigma))).astype(BF16)
    first = lax.dot_general(dpre_act, gate_mat, CONTRACT_LAST, preferred_element_type=F32)
    second = lax.dot_general(dup_act, up_mat, CONTRACT_LAST, preferred_element_type=F32)
    input_grad = (first + second).astype(BF16)
    return (output, input_grad, hidden)


def body_any(tokens, cotangent, routes, gate_weights, w_gate, w_up, w_down):
    tok_rows, width = tokens.shape
    peers = lax.axis_size("tp")
    capacity = 3 * tok_rows * routes.shape[1] // (2 * peers)
    expert_ids = routes[:, 0]
    onehot = (expert_ids[:, None] == jnp.arange(peers, dtype=jnp.int32)[None, :]).astype(jnp.int32)
    rank = jnp.sum((jnp.cumsum(onehot, axis=0) - 1) * onehot, axis=1)
    slot = expert_ids * capacity + rank
    placing = (
        slot[None, :] == jnp.arange(peers * capacity, dtype=jnp.int32)[:, None]
    ).astype(BF16)
    scaled = (gate_weights * cotangent.astype(F32)).astype(BF16)
    send = jnp.dot(
        placing, jnp.concatenate([tokens, scaled], axis=1), preferred_element_type=F32
    ).astype(BF16)
    got = lax.all_to_all(
        send.reshape(peers, capacity, 2 * width), "tp", split_axis=0, concat_axis=0, tiled=True
    ).reshape(-1, 2 * width)
    got_cot = got[:, width:]
    output, input_grad, hidden = expert_block(
        got[:, :width], got_cot, w_gate[0], w_up[0], w_down[0]
    )
    back = lax.all_to_all(
        jnp.concatenate([output, input_grad], axis=1).reshape(peers, capacity, 2 * width),
        "tp", split_axis=0, concat_axis=0, tiled=True,
    ).reshape(-1, 2 * width)
    partial = lax.dot_general(hidden, got_cot, CONTRACT_FIRST, preferred_element_type=F32)
    summed = lax.psum_scatter(partial.astype(BF16), "ctx", scatter_dimension=0, tiled=True)
    home = lax.dot_general(placing, back, CONTRACT_FIRST, preferred_element_type=F32)
    out_tok = home[:, :width]
    layer_output = (gate_weights * out_tok).astype(BF16)
    gate_grad = jnp.sum(cotangent.astype(F32) * out_tok, axis=1, keepdims=True)
    return layer_output, home[:, width:].astype(BF16), gate_grad, summed[None]


VMEM_LIMIT = 24 * 1024 * 1024
TINY = pl.CostEstimate(flops=1, bytes_accessed=1, transcendentals=0)
LONG = pl.CostEstimate(flops=1, bytes_accessed=100_000_000, transcendentals=0)


def call(kernel, outs, cost=TINY, **more):
    return pl.pallas_call(
        kernel,
        out_shape=outs,
        cost_estimate=cost,
        compiler_params=pltpu.CompilerParams(vmem_limit_bytes=VMEM_LIMIT),
        **more,
    )


def shaped(shape, dtype=BF16):
    return jax.ShapeDtypeStruct(shape, dtype)


def in_hbm(array):
    return pltpu.with_memory_space_constraint(array, pltpu.HBM)


def diagonal(size):
    return lax.broadcasted_iota(jnp.int32, (size, size), 0) == lax.broadcasted_iota(
        jnp.int32, (size, size), 1
    )


def column(row):
    return jnp.sum(jnp.where(diagonal(row.shape[1]), row, 0), axis=1, keepdims=True)


def is_outer():
    here = lax.axis_index("ctx")
    return (here == 0) | (here == 3)


def scale_kernel(peers, capacity, routes, gates, cot, slot_out, scaled, to_2, to_3):
    ids = routes[...]
    count, width = cot.shape
    onehot = lax.broadcasted_iota(jnp.int32, (peers, count), 0) == ids
    upto = lax.broadcasted_iota(jnp.int32, (count, count), 0) <= lax.broadcasted_iota(
        jnp.int32, (count, count), 1
    )
    running = jnp.dot(onehot.astype(BF16), upto.astype(BF16), preferred_element_type=F32)
    rank = jnp.sum(jnp.where(onehot, running - 1.0, 0.0), axis=0, keepdims=True).astype(jnp.int32)
    slot = ids * capacity + rank
    slot_out[...] = slot
    scaled[...] = (column(gates[...]) * cot[...].astype(F32)).astype(BF16)
    half = width // 2
    outer = is_outer()

    @pl.when(outer)
    def _():
        to_2[:, :half] = scaled[:, :half]
        to_3[:, :half] = scaled[:, half:]

    @pl.when(jnp.logical_not(outer))
    def _():
        to_2[:, :half] = scaled[:, half:]
        to_3[:, :half] = scaled[:, :half]

    slots = jnp.broadcast_to(column(slot.astype(F32)), (count, to_2.shape[1] - half)).astype(BF16)
    to_2[:, half:] = slots
    to_3[:, half:] = slots


def place(placing, rows, out, at, width):
    step = 512
    for col in range(0, width, step):
        out[:, at + col : at + col + step] = jnp.dot(
            placing, rows[:, col : col + step], preferred_element_type=F32
        ).astype(BF16)


def send_kernel(slot, tok, scaled, out):
    width = tok.shape[1]
    placing = (
        lax.broadcasted_iota(jnp.int32, (out.shape[0], tok.shape[0]), 0) == slot[...]
    ).astype(BF16)
    place(placing, tok, out, 0, width)
    place(placing, scaled, out, width, width)


def remote_kernel(from_2, from_3, out):
    width = out.shape[1] // 2
    count = from_2.shape[0]
    for at, rows in ((0, from_2), (width, from_3)):
        slot = rows[:, width : width + 1].astype(F32).astype(jnp.int32)
        home = (lax.broadcasted_iota(jnp.int32, (count, out.shape[0]), 1) == slot).astype(F32)
        place(home.T.astype(BF16), rows, out, at, width)


def halves_kernel(got, keep, give):
    half = keep.shape[1]
    width = 2 * half
    outer = is_outer()

    @pl.when(outer)
    def _():
        give[...] = got[:, width : width + half]
        keep[...] = got[:, width + half :]

    @pl.when(jnp.logical_not(outer))
    def _():
        keep[...] = got[:, width : width + half]
        give[...] = got[:, width + half :]


def hidden_kernel(got, gate, up, down, hidden, dpre, dup, near, far):
    width = gate.shape[0]
    rows, cot = got.at[:, :width], got.at[:, width:]
    step = 256
    for at in range(0, gate.shape[1], step):
        cols = slice(at, at + step)
        pre_act = jnp.dot(rows[...], gate[:, cols], preferred_element_type=F32)
        up_act = jnp.dot(rows[...], up[:, cols], preferred_element_type=F32)
        dhid = lax.dot_general(cot[...], down[cols, :], CONTRACT_LAST, preferred_element_type=F32)
        sigma = 1.0 / (1.0 + jnp.exp(-pre_act))
        hidden[:, cols] = (pre_act * sigma * up_act).astype(BF16)
        dup[:, cols] = (dhid * pre_act * sigma).astype(BF16)
        dpre[:, cols] = (dhid * up_act * sigma * (1.0 + pre_act * (1.0 - sigma))).astype(BF16)
    half = near.shape[1]
    left, right = hidden[:, :half], hidden[:, half:]
    on_left = lax.axis_index("ctx") < 2

    @pl.when(on_left)
    def _():
        near[...] = left
        far[...] = right

    @pl.when(jnp.logical_not(on_left))
    def _():
        near[...] = right
        far[...] = left


def back_kernel(hidden, dpre, dup, gate, up, down, *refs):
    out = refs[-1]
    width = down.shape[1]
    step = 512
    for at in range(0, width, step):
        cols = slice(at, at + step)
        out[:, cols] = jnp.dot(hidden[...], down[:, cols], preferred_element_type=F32).astype(BF16)
        out[:, width + at : width + at + step] = (
            lax.dot_general(dpre[...], gate[cols, :], CONTRACT_LAST, preferred_element_type=F32)
            + lax.dot_general(dup[...], up[cols, :], CONTRACT_LAST, preferred_element_type=F32)
        ).astype(BF16)


def quarters_kernel(h_own, h_1, h_2, h_3, own, from_1, remote, mine, other):
    half = own.shape[1]
    even = lax.rem(lax.axis_index("ctx"), 2) == 0

    def times(left, right):
        return lax.dot_general(left[...], right, CONTRACT_FIRST, preferred_element_type=F32)

    step = 512
    for at in range(0, half, step):
        cols, later = slice(at, at + step), slice(half + at, half + at + step)
        total = (
            times(h_own, own[:, cols])
            + times(h_1, from_1[:, cols])
            + times(h_2, remote[:, cols])
            + times(h_3, remote[:, later])
        )
        rows = total.shape[0] // 2
        low, high = total[:rows].astype(BF16), total[rows:].astype(BF16)
        mine[:, cols] = jnp.where(even, low, high)
        other[:, cols] = jnp.where(even, high, low)


def home_kernel(slot, gates, back, cot, layer_output, token_grad, gate_grad):
    count, width = cot.shape
    placing = (
        lax.broadcasted_iota(jnp.int32, (count, back.shape[0]), 1) == column(slot[...])
    ).astype(BF16)
    gate = column(gates[...])
    total = jnp.zeros((count, 1), F32)
    step = 512
    for at in range(0, width, step):
        cols = slice(at, at + step)
        out_tok = jnp.dot(placing, back[:, cols], preferred_element_type=F32)
        layer_output[:, cols] = (gate * out_tok).astype(BF16)
        total += jnp.sum(cot[:, cols].astype(F32) * out_tok, axis=1, keepdims=True)
        grad_cols = slice(width + at, width + at + step)
        token_grad[:, cols] = jnp.dot(
            placing, back[:, grad_cols], preferred_element_type=F32
        ).astype(BF16)
    gate_grad[...] = jnp.sum(jnp.where(diagonal(count), total, 0.0), axis=0, keepdims=True)


def join_kernel(mine, got, out):
    half = mine.shape[1]
    outer = is_outer()

    @pl.when(outer)
    def _():
        out[0, :, :half] = got[...]
        out[0, :, half:] = mine[...]

    @pl.when(jnp.logical_not(outer))
    def _():
        out[0, :, :half] = mine[...]
        out[0, :, half:] = got[...]


def along(rows, step):
    return lax.ppermute(rows, "ctx", [(i, i ^ step) for i in range(4)])


def body_line(tokens, cotangent, routes, gate_weights, w_gate, w_up, w_down):
    count, width = tokens.shape
    peers = lax.axis_size("tp")
    capacity = 3 * count * routes.shape[1] // (2 * peers)
    slots = peers * capacity
    inner = w_gate.shape[2]
    quarter = inner // 4
    gates = gate_weights.reshape(1, count)
    whole = pl.BlockSpec()
    after = pl.BlockSpec(memory_space=pl.ANY)

    def over_tp(rows):
        wide = rows.shape[1]
        return lax.all_to_all(
            rows.reshape(peers, capacity, wide), "tp", split_axis=0, concat_axis=0, tiled=True
        ).reshape(slots, wide)

    half = width // 2
    slot, scaled, to_2, to_3 = call(
        functools.partial(scale_kernel, peers, capacity),
        [shaped((1, count), jnp.int32), pltpu.HBM((count, width), BF16)]
        + [pltpu.HBM((count, half + 128), BF16)] * 2,
    )(routes.reshape(1, count), gates, in_hbm(cotangent))
    from_2, from_3 = along(to_2, 2), along(to_3, 3)
    got = over_tp(
        call(send_kernel, pltpu.HBM((slots, 2 * width), BF16), LONG)(
            slot, in_hbm(tokens), in_hbm(scaled)
        )
    )
    remote = over_tp(
        call(remote_kernel, shaped((slots, width)))(from_2, from_3)
    )
    keep, give = call(halves_kernel, [pltpu.HBM((slots, half), BF16)] * 2)(got)
    from_1 = along(give, 1)

    gate_mat, up_mat, down_mat = w_gate[0], w_up[0], w_down[0]
    hidden, dpre, dup, near, far = call(
        hidden_kernel,
        [shaped((slots, inner))] * 3 + [pltpu.HBM((slots, inner // 2), BF16)] * 2,
    )(got, gate_mat, up_mat, down_mat)
    h_1, h_2, h_3 = along(near, 1), along(far, 2), along(far, 3)
    back = over_tp(
        call(
            back_kernel,
            pltpu.HBM((slots, 2 * width), BF16),
        )(hidden, dpre, dup, gate_mat, up_mat, down_mat)
    )

    mine, other = call(
        quarters_kernel, [shaped((quarter, half)), pltpu.HBM((quarter, half), BF16)]
    )(near, h_1, h_2, h_3, keep, from_1, remote)
    swapped = along(other, 1)

    layer_output, token_grad, gate_grad = call(
        home_kernel,
        [shaped((count, width)), shaped((count, width)), shaped((1, count), F32)],
    )(slot, gates, back, in_hbm(cotangent))
    down_grad = call(join_kernel, shaped((1, quarter, width)))(mine, swapped)
    return layer_output, token_grad, gate_grad.reshape(count, 1), down_grad


def solution(mesh):
    rows = P(("ctx", "tp"), None)
    expert = P("tp", None, None)
    line = mesh.shape["ctx"] == 4 and mesh.shape["tp"] == 8
    return jax.shard_map(
        body_line if line else body_any,
        mesh=mesh,
        in_specs=(rows, rows, rows, rows, expert, expert, expert),
        out_specs=(rows, rows, rows, P("tp", "ctx", None)),
        check_vma=False,
    )
```

time: 118 us -> 106 us (0.90)
  matrix products: 29.7 us -> 0 us
  Pallas kernels: 0 us -> 19.9 us
  between operations: 14.1 us -> 0.7 us
  starting transfers between devices: 17.8 us -> 31.1 us
  local copies, waits for them, and re-layouts: 1.65 us -> 8.87 us
  waiting for transfers between devices: 51.7 us -> 44.5 us
  other arithmetic: 2.55 us -> 0 us
    ppermute x0 -> x7, waiting for transfers between devices: none -> 44.5 us  [along(): return lax.ppermute(rows, 'ctx', [(i, i ^ step) for i in range(4)])]
    all_to_all x4 -> x3, waiting for transfers between devices: 35.7 us -> 0.01 us  [over_tp(): lax.all_to_all(rows.reshape(peers, capacity, wide), 'tp', split_axis=0, c...]
    dot_general x11 -> x0, matrix products: 29.7 us -> none  [the longest x1 3.8 us: body(): lax.dot_general(hidden, cot_flat, contract_first, preferred_element_type=...]
    pallas_call x0 -> x9, Pallas kernels: none -> 19.9 us  [the longest x1 4 us: body_line(): call(back_kernel, pltpu.HBM((slots, 2 * width), BF16))]
    ppermute x0 -> x7, starting transfers between devices: none -> 17.5 us  [along(): return lax.ppermute(rows, 'ctx', [(i, i ^ step) for i in range(4)])]
    reduce_scatter x1 -> x0, waiting for transfers between devices: 16 us -> none  [body(): lax.psum_scatter(lax.dot_general(hidden, cot_flat, contract_first, prefer...]
    unnamed x12 -> x26, local copies, waits for them, and re-layouts: 1.65 us -> 8.87 us
    all_to_all x4 -> x3, starting transfers between devices: 17.8 us -> 13.7 us  [over_tp(): lax.all_to_all(rows.reshape(peers, capacity, wide), 'tp', split_axis=0, c...]
  transfers between devices with their start and end apart: 5 -> 10, of which waited for: 5 -> 4; matrix products, arithmetic and copies ran while one was open for 20% -> 0% of each run, Pallas kernels for 0% -> 12%
where the time goes in v2:
time: 106 us; the launch traced here: 105 us
  waiting for transfers between devices  44.5 us (42%)
  starting transfers between devices  31.1 us (29%)
  Pallas kernels  19.9 us (19%)
  local copies, waits for them, and re-layouts  8.87 us (8%)
    ppermute x7, waiting for transfers between devices, along(): return lax.ppermute(rows, 'ctx', [(i, i ^ step) for i in range(4)])  44.5 us
    ppermute x7, starting transfers between devices, along(): return lax.ppermute(rows, 'ctx', [(i, i ^ step) for i in range(4)])  17.5 us
    all_to_all x3, starting transfers between devices, over_tp(): lax.all_to_all(rows.reshape(peers, capacity, wide), 'tp', split_axis=0, c...  13.7 us
    unnamed x26, local copies, waits for them, and re-layouts  8.87 us
    pallas_call x1, Pallas kernels, body_line(): call(back_kernel, pltpu.HBM((slots, 2 * width), BF16))  4 us
    pallas_call x1, Pallas kernels, body_line(): call(hidden_kernel, [shaped((slots, inner))] * 3 + [pltpu.HBM((slots, inn...  3.15 us
    pallas_call x1, Pallas kernels, body_line(): call(send_kernel, pltpu.HBM((slots, 2 * width), BF16), LONG)  2.96 us
    pallas_call x1, Pallas kernels, body_line(): call(home_kernel, [shaped((count, width)), shaped((count, width)), shaped...  2.51 us
  transfers between devices with their start and end apart: 10, of which 4 were waited for; matrix products, arithmetic and copies ran while one was open for 0% of the time, Pallas kernels for 12%

profile of v2, /device:TPU:0, one launch (start us, length us, event | category | flops | bytes accessed | tf_op | source)
XLA Modules:
  0.0 105.1 jit_solution(9129830453436088357)
XLA Ops:
  0.6 0.0 copy-start.7
  0.6 0.6 copy-done.7
  1.3 0.7 copy-done.9
  1.9 2.2 %shard_map.102 = (s32[1,128]{1,0:T(1,128)S(1)}, bf16[128,2048]{1,0:T(8,128)(2,1)}, bf16[128,1152]{1,0:T(8,128)(2,1)}, bf16[128,1152]{1,0:T(8,128)(2,1)}) custom-call(s32[1,128]{1,0:T(1,128)S(1)} %bitcast.24, f32[1,128]{1,0:T(1,128)S(1)} %bitcast.22, bf16[128,2048]{1,0:T(8,128)(2,1)} %cot.3), custom_call_target="tpu_custom_call" | custom-call | flops 1 | bytes 1 | tf_op jit(solution)/shard_map/pallas_call | solution.py:296
  4.2 3.0 %shard_map.103 = bf16[192,4096]{1,0:T(8,128)(2,1)} custom-call(s32[1,128]{1,0:T(1,128)S(1)} %get-tuple-element.20.slot, bf16[128,2048]{1,0:T(8,128)(2,1)} %tok.1, bf16[128,2048]{1,0:T(8,128)(2,1)} %get-tuple-element.21.scaled), custom_call_target="tpu_custom_call" | custom-call | flops 1 | bytes 100000000 | tf_op jit(solution)/shard_map/pallas_call | solution.py:303
  7.1 5.3 %all-to-all-start = ((bf16[8,24,4096]{2,1,0:T(8,128)(2,1)}), bf16[8,24,4096]{2,1,0:T(8,128)(2,1)S(1)}, u32[]{:S(2)}, u32[]{:S(2)}) async-start(bf16[8,24,4096]{2,1,0:T(8,128)(2,1)} %bitcast.25), calls=%async_computation | async-start | bytes 3145728 | tf_op jit(solution)/shard_map/all_to_all | solution.py:291
  12.4 2.7 %collective-permute-start.4 = (bf16[128,1152]{1,0:T(8,128)(2,1)S(1)}, bf16[128,1152]{1,0:T(8,128)(2,1)S(1)}, u32[]{:S(2)}, u32[]{:S(2)}) collective-permute-start(bf16[128,1152]{1,0:T(8,128)(2,1)S(1)} %copy-done.11), channel_id=1, source_target_pairs={{0,16},{8,24},{16,0},{24,8},{1,17},{9,25},{17,1},{25,9},{2,18},{10... | collective-permute-start | bytes 884744 | tf_op jit(solution)/shard_map/ppermute | solution.py:275
  15.1 1.3 %collective-permute-start.5 = (bf16[128,1152]{1,0:T(8,128)(2,1)S(1)}, bf16[128,1152]{1,0:T(8,128)(2,1)S(1)}, u32[]{:S(2)}, u32[]{:S(2)}) collective-permute-start(bf16[128,1152]{1,0:T(8,128)(2,1)S(1)} %copy-done.10), channel_id=1, source_target_pairs={{0,24},{8,16},{16,8},{24,0},{1,25},{9,17},{17,9},{25,1},{2,26},{10... | collective-permute-start | bytes 884744 | tf_op jit(solution)/shard_map/ppermute | solution.py:275
  16.4 19.4 %collective-permute-done.4.from_2 = bf16[128,1152]{1,0:T(8,128)(2,1)S(1)} collective-permute-done((bf16[128,1152]{1,0:T(8,128)(2,1)S(1)}, bf16[128,1152]{1,0:T(8,128)(2,1)S(1)}, u32[]{:S(2)}, u32[]{:S(2)}) %collective-permute-start.4) | collective-permute-done | bytes 294944 | tf_op jit(solution)/shard_map/ppermute | solution.py:275
  35.9 1.4 %shard_map.108 = bf16[192,2048]{1,0:T(8,128)(2,1)} custom-call(bf16[128,1152]{1,0:T(8,128)(2,1)S(1)} %collective-permute-done.4.from_2, bf16[128,1152]{1,0:T(8,128)(2,1)S(1)} %collective-permute-done.5.from_3), custom_call_target="tpu_custom_call" | custom-call | flops 1 | bytes 1 | tf_op jit(solution)/shard_map/pallas_call | solution.py:308
  37.3 4.2 %all-to-all-start.2 = ((bf16[8,24,2048]{2,1,0:T(8,128)(2,1)}), bf16[8,24,2048]{2,1,0:T(8,128)(2,1)S(1)}, u32[]{:S(2)}, u32[]{:S(2)}) async-start(bf16[8,24,2048]{2,1,0:T(8,128)(2,1)} %bitcast.10), calls=%async_computation.2 | async-start | bytes 1572864 | tf_op jit(solution)/shard_map/all_to_all | solution.py:291
  41.4 1.9 %copy-done = bf16[1,2048,768]{2,1,0:T(8,128)(2,1)S(1)} copy-done((bf16[1,2048,768]{2,1,0:T(8,128)(2,1)S(1)}, bf16[1,2048,768]{2,1,0:T(8,128)(2,1)}, u32[]{:S(2)}) %copy-start) | copy-done | bytes 3145752
  43.3 1.9 %copy-done.1 = bf16[1,2048,768]{2,1,0:T(8,128)(2,1)S(1)} copy-done((bf16[1,2048,768]{2,1,0:T(8,128)(2,1)S(1)}, bf16[1,2048,768]{2,1,0:T(8,128)(2,1)}, u32[]{:S(2)}) %copy-start.1) | copy-done | bytes 3145752
  45.2 1.9 %copy-done.2 = bf16[1,768,2048]{2,1,0:T(8,128)(2,1)S(1)} copy-done((bf16[1,768,2048]{2,1,0:T(8,128)(2,1)S(1)}, bf16[1,768,2048]{2,1,0:T(8,128)(2,1)}, u32[]{:S(2)}) %copy-start.2) | copy-done | bytes 3145752
  47.1 3.2 %shard_map.104 = (bf16[192,768]{1,0:T(8,128)(2,1)S(1)}, bf16[192,768]{1,0:T(8,128)(2,1)S(1)}, bf16[192,768]{1,0:T(8,128)(2,1)S(1)}, bf16[192,384]{1,0:T(8,128)(2,1)}, bf16[192,384]{1,0:T(8,128)(2,1)}) custom-call(bf16[192,4096]{1,0:T(8,128)(2,1)S(1)} %bitcast.12, bf16[2048,768]{1,0:T(8,128)(2,1)S(1)} %bitcast.14, bf16[2048,768]{1,0:T(8,128)(2,1)S(1)} %bitcast.16, ...), custom_call_target="tpu_custom_call" | custom-call | flops 1 | bytes 1 | tf_op jit(solution)/shard_map/pallas_call | solution.py:314
  50.3 4.0 %shard_map.105 = bf16[192,4096]{1,0:T(8,128)(2,1)} custom-call(bf16[192,768]{1,0:T(8,128)(2,1)S(1)} %get-tuple-element.22.hidden, bf16[192,768]{1,0:T(8,128)(2,1)S(1)} %get-tuple-element.23.dpre, bf16[192,768]{1,0:T(8,128)(2,1)S(1)} %get-tuple-element.24.dup, bf16[2048,768]{1,0:T(8,128)(2,1)S(1)} %bitcast.15, bf16[2048,768]{1,0:T(8,128)(2,1)S(1)} %bitcast.17, ...), custom_call_target="tpu_custom_call" | custom-call | flops 1 | bytes 1 | tf_op jit(solution)/shard_map/pallas_call | solution.py:320
  54.3 0.9 copy-done.3
  55.1 4.2 %all-to-all-start.1 = ((bf16[8,24,4096]{2,1,0:T(8,128)(2,1)}), bf16[8,24,4096]{2,1,0:T(8,128)(2,1)S(1)}, u32[]{:S(2)}, u32[]{:S(2)}) async-start(bf16[8,24,4096]{2,1,0:T(8,128)(2,1)} %bitcast.26), calls=%async_computation.1 | async-start | bytes 3145728 | tf_op jit(solution)/shard_map/all_to_all | solution.py:291
  59.4 0.0 copy-start.4
  59.4 0.9 shard_map.107
  60.3 6.2 %collective-permute-start.3 = (bf16[192,1024]{1,0:T(8,128)(2,1)}, bf16[192,1024]{1,0:T(8,128)(2,1)S(1)}, u32[]{:S(2)}, u32[]{:S(2)}) collective-permute-start(bf16[192,1024]{1,0:T(8,128)(2,1)} %get-tuple-element.31), channel_id=1, source_target_pairs={{0,8},{8,0},{16,24},{24,16},{1,9},{9,1},{17,25},{25,17},{2,10},{10... | collective-permute-start | bytes 1179656 | tf_op jit(solution)/shard_map/ppermute | solution.py:275
  66.5 0.0 collective-permute-start
  66.6 3.4 %collective-permute-start.2 = (bf16[192,384]{1,0:T(8,128)(2,1)S(1)}, bf16[192,384]{1,0:T(8,128)(2,1)S(1)}, u32[]{:S(2)}, u32[]{:S(2)}) collective-permute-start(bf16[192,384]{1,0:T(8,128)(2,1)S(1)} %copy-done.12), channel_id=1, source_target_pairs={{0,24},{8,16},{16,8},{24,0},{1,25},{9,17},{17,9},{25,1},{2,26},{10... | collective-permute-start | bytes 442376 | tf_op jit(solution)/shard_map/ppermute | solution.py:275
  70.0 0.5 collective-permute-start.1
  70.5 12.8 %collective-permute-done.h_1 = bf16[192,384]{1,0:T(8,128)(2,1)S(1)} collective-permute-done((bf16[192,384]{1,0:T(8,128)(2,1)S(1)}, bf16[192,384]{1,0:T(8,128)(2,1)S(1)}, u32[]{:S(2)}, u32[]{:S(2)}) %collective-permute-start) | collective-permute-done | bytes 147488 | tf_op jit(solution)/shard_map/ppermute | solution.py:275
  83.2 3.1 %collective-permute-done.2.h_3 = bf16[192,384]{1,0:T(8,128)(2,1)S(1)} collective-permute-done((bf16[192,384]{1,0:T(8,128)(2,1)S(1)}, bf16[192,384]{1,0:T(8,128)(2,1)S(1)}, u32[]{:S(2)}, u32[]{:S(2)}) %collective-permute-start.2) | collective-permute-done | bytes 147488 | tf_op jit(solution)/shard_map/ppermute | solution.py:275
  86.4 1.0 copy-done.5
  87.3 1.8 %shard_map.109 = (bf16[192,1024]{1,0:T(8,128)(2,1)S(1)}, bf16[192,1024]{1,0:T(8,128)(2,1)}) custom-call(bf16[192,384]{1,0:T(8,128)(2,1)S(1)} %copy-done.6, bf16[192,384]{1,0:T(8,128)(2,1)S(1)} %collective-permute-done.h_1, bf16[192,384]{1,0:T(8,128)(2,1)S(1)} %collective-permute-done.1.h_2, bf16[192,384]{1,0:T(8,128)(2,1)S(1)} %collective-permute-done.2.h_3, ...), custom_call_target="tpu_custom_call" | custom-call | flops 1 | bytes 1 | tf_op jit(solution)/shard_map/pallas_call | solution.py:326
  89.1 3.3 %collective-permute-start.6 = (bf16[192,1024]{1,0:T(8,128)(2,1)}, bf16[192,1024]{1,0:T(8,128)(2,1)S(1)}, u32[]{:S(2)}, u32[]{:S(2)}) collective-permute-start(bf16[192,1024]{1,0:T(8,128)(2,1)} %get-tuple-element.35), channel_id=1, source_target_pairs={{0,8},{8,0},{16,24},{24,16},{1,9},{9,1},{17,25},{25,17},{2,10},{10... | collective-permute-start | bytes 1179656 | tf_op jit(solution)/shard_map/ppermute | solution.py:275
  92.4 9.2 %collective-permute-done.6.got = bf16[192,1024]{1,0:T(8,128)(2,1)S(1)} collective-permute-done((bf16[192,1024]{1,0:T(8,128)(2,1)}, bf16[192,1024]{1,0:T(8,128)(2,1)S(1)}, u32[]{:S(2)}, u32[]{:S(2)}) %collective-permute-start.6) | collective-permute-done | bytes 393248 | tf_op jit(solution)/shard_map/ppermute | solution.py:275
  101.6 0.9 shard_map.110
  102.6 2.5 %shard_map.106 = (bf16[128,2048]{1,0:T(8,128)(2,1)}, bf16[128,2048]{1,0:T(8,128)(2,1)}, f32[1,128]{1,0:T(1,128)}) custom-call(s32[1,128]{1,0:T(1,128)S(1)} %get-tuple-element.20.slot, f32[1,128]{1,0:T(1,128)S(1)} %bitcast.23, bf16[192,4096]{1,0:T(8,128)(2,1)S(1)} %bitcast.20, bf16[128,2048]{1,0:T(8,128)(2,1)} %cot.3), custom_call_target="tpu_custom_call" | custom-call | flops 1 | bytes 1 | tf_op jit(solution)/shard_map/pallas_call | solution.py:331
  (23 shorter events, 0.0 us)
Async XLA Ops:
  0.6 0.7 copy-start.7
  1.3 0.7 copy-start.9
  7.1 5.3 %copy-start.11 = (bf16[128,1152]{1,0:T(8,128)(2,1)S(1)}, bf16[128,1152]{1,0:T(8,128)(2,1)}, u32[]{:S(2)}) copy-start(bf16[128,1152]{1,0:T(8,128)(2,1)} %get-tuple-element.32) | copy-start | bytes 884740
  7.1 8.0 %copy-start.10 = (bf16[128,1152]{1,0:T(8,128)(2,1)S(1)}, bf16[128,1152]{1,0:T(8,128)(2,1)}, u32[]{:S(2)}) copy-start(bf16[128,1152]{1,0:T(8,128)(2,1)} %get-tuple-element.33) | copy-start | bytes 884740
  7.1 30.1 %all-to-all-start = ((bf16[8,24,4096]{2,1,0:T(8,128)(2,1)}), bf16[8,24,4096]{2,1,0:T(8,128)(2,1)S(1)}, u32[]{:S(2)}, u32[]{:S(2)}) async-start(bf16[8,24,4096]{2,1,0:T(8,128)(2,1)} %bitcast.25), calls=%async_computation | async-start | bytes 3145728 | tf_op jit(solution)/shard_map/all_to_all | solution.py:291
  12.4 23.4 %collective-permute-start.4 = (bf16[128,1152]{1,0:T(8,128)(2,1)S(1)}, bf16[128,1152]{1,0:T(8,128)(2,1)S(1)}, u32[]{:S(2)}, u32[]{:S(2)}) collective-permute-start(bf16[128,1152]{1,0:T(8,128)(2,1)S(1)} %copy-done.11), channel_id=1, source_target_pairs={{0,16},{8,24},{16,0},{24,8},{1,17},{9,25},{17,1},{25,9},{2,18},{10... | collective-permute-start | bytes 884744 | tf_op jit(solution)/shard_map/ppermute | solution.py:275
  15.1 20.8 %collective-permute-start.5 = (bf16[128,1152]{1,0:T(8,128)(2,1)S(1)}, bf16[128,1152]{1,0:T(8,128)(2,1)S(1)}, u32[]{:S(2)}, u32[]{:S(2)}) collective-permute-start(bf16[128,1152]{1,0:T(8,128)(2,1)S(1)} %copy-done.10), channel_id=1, source_target_pairs={{0,24},{8,16},{16,8},{24,0},{1,25},{9,17},{17,9},{25,1},{2,26},{10... | collective-permute-start | bytes 884744 | tf_op jit(solution)/shard_map/ppermute | solution.py:275
  37.3 17.0 %all-to-all-start.2 = ((bf16[8,24,2048]{2,1,0:T(8,128)(2,1)}), bf16[8,24,2048]{2,1,0:T(8,128)(2,1)S(1)}, u32[]{:S(2)}, u32[]{:S(2)}) async-start(bf16[8,24,2048]{2,1,0:T(8,128)(2,1)} %bitcast.10), calls=%async_computation.2 | async-start | bytes 1572864 | tf_op jit(solution)/shard_map/all_to_all | solution.py:291
  41.4 1.9 %copy-start = (bf16[1,2048,768]{2,1,0:T(8,128)(2,1)S(1)}, bf16[1,2048,768]{2,1,0:T(8,128)(2,1)}, u32[]{:S(2)}) copy-start(bf16[1,2048,768]{2,1,0:T(8,128)(2,1)} %param.11) | copy-start | bytes 9437188
  43.3 1.9 %copy-start.1 = (bf16[1,2048,768]{2,1,0:T(8,128)(2,1)S(1)}, bf16[1,2048,768]{2,1,0:T(8,128)(2,1)}, u32[]{:S(2)}) copy-start(bf16[1,2048,768]{2,1,0:T(8,128)(2,1)} %param.12) | copy-start | bytes 9437188
  45.2 1.9 %copy-start.2 = (bf16[1,768,2048]{2,1,0:T(8,128)(2,1)S(1)}, bf16[1,768,2048]{2,1,0:T(8,128)(2,1)}, u32[]{:S(2)}) copy-start(bf16[1,768,2048]{2,1,0:T(8,128)(2,1)} %param.13) | copy-start | bytes 9437188
  54.3 0.9 copy-start.3
  55.1 47.4 %all-to-all-start.1 = ((bf16[8,24,4096]{2,1,0:T(8,128)(2,1)}), bf16[8,24,4096]{2,1,0:T(8,128)(2,1)S(1)}, u32[]{:S(2)}, u32[]{:S(2)}) async-start(bf16[8,24,4096]{2,1,0:T(8,128)(2,1)} %bitcast.26), calls=%async_computation.1 | async-start | bytes 3145728 | tf_op jit(solution)/shard_map/all_to_all | solution.py:291
  59.3 7.2 %copy-start.6 = (bf16[192,384]{1,0:T(8,128)(2,1)S(1)}, bf16[192,384]{1,0:T(8,128)(2,1)}, u32[]{:S(2)}) copy-start(bf16[192,384]{1,0:T(8,128)(2,1)} %get-tuple-element.28.h_own) | copy-start | bytes 442372
  59.3 7.2 %copy-start.12 = (bf16[192,384]{1,0:T(8,128)(2,1)S(1)}, bf16[192,384]{1,0:T(8,128)(2,1)}, u32[]{:S(2)}) copy-start(bf16[192,384]{1,0:T(8,128)(2,1)} %get-tuple-element.29) | copy-start | bytes 442372
  59.4 27.0 %copy-start.4 = (bf16[8,24,2048]{2,1,0:T(8,128)(2,1)S(1)}, bf16[8,24,2048]{2,1,0:T(8,128)(2,1)}, u32[]{:S(2)}) copy-start(bf16[8,24,2048]{2,1,0:T(8,128)(2,1)} %copy-done.3) | copy-start | bytes 2359300
  60.3 26.0 %collective-permute-start.3 = (bf16[192,1024]{1,0:T(8,128)(2,1)}, bf16[192,1024]{1,0:T(8,128)(2,1)S(1)}, u32[]{:S(2)}, u32[]{:S(2)}) collective-permute-start(bf16[192,1024]{1,0:T(8,128)(2,1)} %get-tuple-element.31), channel_id=1, source_target_pairs={{0,8},{8,0},{16,24},{24,16},{1,9},{9,1},{17,25},{25,17},{2,10},{10... | collective-permute-start | bytes 1179656 | tf_op jit(solution)/shard_map/ppermute | solution.py:275
  66.5 16.7 %collective-permute-start = (bf16[192,384]{1,0:T(8,128)(2,1)S(1)}, bf16[192,384]{1,0:T(8,128)(2,1)S(1)}, u32[]{:S(2)}, u32[]{:S(2)}) collective-permute-start(bf16[192,384]{1,0:T(8,128)(2,1)S(1)} %copy-done.6), channel_id=1, source_target_pairs={{0,8},{8,0},{16,24},{24,16},{1,9},{9,1},{17,25},{25,17},{2,10},{10... | collective-permute-start | bytes 442376 | tf_op jit(solution)/shard_map/ppermute | solution.py:275
  66.6 19.8 %collective-permute-start.2 = (bf16[192,384]{1,0:T(8,128)(2,1)S(1)}, bf16[192,384]{1,0:T(8,128)(2,1)S(1)}, u32[]{:S(2)}, u32[]{:S(2)}) collective-permute-start(bf16[192,384]{1,0:T(8,128)(2,1)S(1)} %copy-done.12), channel_id=1, source_target_pairs={{0,24},{8,16},{16,8},{24,0},{1,25},{9,17},{17,9},{25,1},{2,26},{10... | collective-permute-start | bytes 442376 | tf_op jit(solution)/shard_map/ppermute | solution.py:275
  70.0 16.4 %collective-permute-start.1 = (bf16[192,384]{1,0:T(8,128)(2,1)S(1)}, bf16[192,384]{1,0:T(8,128)(2,1)S(1)}, u32[]{:S(2)}, u32[]{:S(2)}) collective-permute-start(bf16[192,384]{1,0:T(8,128)(2,1)S(1)} %copy-done.12), channel_id=1, source_target_pairs={{0,16},{8,24},{16,0},{24,8},{1,17},{9,25},{17,1},{25,9},{2,18},{10... | collective-permute-start | bytes 442376 | tf_op jit(solution)/shard_map/ppermute | solution.py:275
  86.3 1.0 copy-start.5
  87.3 15.2 %copy-start.8 = (f32[128,1]{0,1:T(1,128)S(1)}, f32[128,1]{0,1:T(1,128)}, u32[]{:S(2)}) copy-start(f32[128,1]{0,1:T(1,128)} %param.10) | copy-start | bytes 1540
  89.1 12.5 %collective-permute-start.6 = (bf16[192,1024]{1,0:T(8,128)(2,1)}, bf16[192,1024]{1,0:T(8,128)(2,1)S(1)}, u32[]{:S(2)}, u32[]{:S(2)}) collective-permute-start(bf16[192,1024]{1,0:T(8,128)(2,1)} %get-tuple-element.35), channel_id=1, source_target_pairs={{0,8},{8,0},{16,24},{24,16},{1,9},{9,1},{17,25},{25,17},{2,10},{10... | collective-permute-start | bytes 1179656 | tf_op jit(solution)/shard_map/ppermute | solution.py:275

commit v3 on v2

v3 whole, which is shorter than its diff:
```python
import functools

import jax
import jax.numpy as jnp
from jax import lax
from jax.experimental import pallas as pl
from jax.experimental.pallas import tpu as pltpu
from jax.sharding import PartitionSpec as P

BF16 = jnp.bfloat16
F32 = jnp.float32
CONTRACT_FIRST = (((0,), (0,)), ((), ()))
CONTRACT_LAST = (((1,), (1,)), ((), ()))


def expert_block(rows_in, rows_cot, gate_mat, up_mat, down_mat):
    pre_act = jnp.dot(rows_in, gate_mat, preferred_element_type=F32)
    up_act = jnp.dot(rows_in, up_mat, preferred_element_type=F32)
    sigma = jax.nn.sigmoid(pre_act)
    hidden = (pre_act * sigma * up_act).astype(BF16)
    output = jnp.dot(hidden, down_mat, preferred_element_type=F32).astype(BF16)
    dhidden = lax.dot_general(rows_cot, down_mat, CONTRACT_LAST, preferred_element_type=F32)
    dup_act = (dhidden * pre_act * sigma).astype(BF16)
    dpre_act = (dhidden * up_act * sigma * (1.0 + pre_act * (1.0 - sigma))).astype(BF16)
    first = lax.dot_general(dpre_act, gate_mat, CONTRACT_LAST, preferred_element_type=F32)
    second = lax.dot_general(dup_act, up_mat, CONTRACT_LAST, preferred_element_type=F32)
    input_grad = (first + second).astype(BF16)
    return (output, input_grad, hidden)


def body_any(tokens, cotangent, routes, gate_weights, w_gate, w_up, w_down):
    tok_rows, width = tokens.shape
    peers = lax.axis_size("tp")
    capacity = 3 * tok_rows * routes.shape[1] // (2 * peers)
    expert_ids = routes[:, 0]
    onehot = (expert_ids[:, None] == jnp.arange(peers, dtype=jnp.int32)[None, :]).astype(jnp.int32)
    rank = jnp.sum((jnp.cumsum(onehot, axis=0) - 1) * onehot, axis=1)
    slot = expert_ids * capacity + rank
    placing = (
        slot[None, :] == jnp.arange(peers * capacity, dtype=jnp.int32)[:, None]
    ).astype(BF16)
    scaled = (gate_weights * cotangent.astype(F32)).astype(BF16)
    send = jnp.dot(
        placing, jnp.concatenate([tokens, scaled], axis=1), preferred_element_type=F32
    ).astype(BF16)
    got = lax.all_to_all(
        send.reshape(peers, capacity, 2 * width), "tp", split_axis=0, concat_axis=0, tiled=True
    ).reshape(-1, 2 * width)
    got_cot = got[:, width:]
    output, input_grad, hidden = expert_block(
        got[:, :width], got_cot, w_gate[0], w_up[0], w_down[0]
    )
    back = lax.all_to_all(
        jnp.concatenate([output, input_grad], axis=1).reshape(peers, capacity, 2 * width),
        "tp", split_axis=0, concat_axis=0, tiled=True,
    ).reshape(-1, 2 * width)
    partial = lax.dot_general(hidden, got_cot, CONTRACT_FIRST, preferred_element_type=F32)
    summed = lax.psum_scatter(partial.astype(BF16), "ctx", scatter_dimension=0, tiled=True)
    home = lax.dot_general(placing, back, CONTRACT_FIRST, preferred_element_type=F32)
    out_tok = home[:, :width]
    layer_output = (gate_weights * out_tok).astype(BF16)
    gate_grad = jnp.sum(cotangent.astype(F32) * out_tok, axis=1, keepdims=True)
    return layer_output, home[:, width:].astype(BF16), gate_grad, summed[None]


WIDE = 512
VMEM_LIMIT = 24 * 1024 * 1024
TINY = pl.CostEstimate(flops=1, bytes_accessed=1, transcendentals=0)


def call(kernel, outs, cost=TINY, **more):
    return pl.pallas_call(
        kernel,
        out_shape=outs,
        cost_estimate=cost,
        compiler_params=pltpu.CompilerParams(vmem_limit_bytes=VMEM_LIMIT),
        **more,
    )


def shaped(shape, dtype=BF16):
    return jax.ShapeDtypeStruct(shape, dtype)


def in_hbm(array):
    return pltpu.with_memory_space_constraint(array, pltpu.HBM)


def diagonal(size):
    return lax.broadcasted_iota(jnp.int32, (size, size), 0) == lax.broadcasted_iota(
        jnp.int32, (size, size), 1
    )


def column(row):
    return jnp.sum(jnp.where(diagonal(row.shape[1]), row, 0), axis=1, keepdims=True)


def place(placing, rows, out, at, width):
    step = 512
    for col in range(0, width, step):
        out[:, at + col : at + col + step] = jnp.dot(
            placing, rows[:, col : col + step], preferred_element_type=F32
        ).astype(BF16)


def send_kernel(peers, capacity, routes, gates, tok, cot, slot_out, out, across, scaled):
    ids = routes[...]
    count, width = cot.shape
    onehot = lax.broadcasted_iota(jnp.int32, (peers, count), 0) == ids
    upto = lax.broadcasted_iota(jnp.int32, (count, count), 0) <= lax.broadcasted_iota(
        jnp.int32, (count, count), 1
    )
    running = jnp.dot(onehot.astype(BF16), upto.astype(BF16), preferred_element_type=F32)
    rank = jnp.sum(jnp.where(onehot, running - 1.0, 0.0), axis=0, keepdims=True).astype(jnp.int32)
    slot = ids * capacity + rank
    slot_out[...] = slot
    scaled[...] = (column(gates[...]) * cot[...].astype(F32)).astype(BF16)
    across[:, :width] = scaled[...]
    across[:, width:] = jnp.broadcast_to(
        column(slot.astype(F32)), (count, across.shape[1] - width)
    ).astype(BF16)
    placing = (
        lax.broadcasted_iota(jnp.int32, (peers * capacity, count), 0) == slot
    ).astype(BF16)
    place(placing, tok, out, 0, width)
    place(placing, scaled, out, width, width)


def remote_kernel(after, rows, out):
    count, width = rows.shape[0], out.shape[1]
    slot = rows[:, width : width + 1].astype(F32).astype(jnp.int32)
    home = (lax.broadcasted_iota(jnp.int32, (count, out.shape[0]), 1) == slot).astype(F32)
    place(home.T.astype(BF16), rows, out, 0, width)


def hidden_kernel(got, gate, up, down, hidden, dpre, dup, near, far):
    width = gate.shape[0]
    rows, cot = got.at[:, :width], got.at[:, width:]
    tile = pl.program_id(0)
    pre_act = jnp.dot(rows[...], gate[...], preferred_element_type=F32)
    up_act = jnp.dot(rows[...], up[...], preferred_element_type=F32)
    dhid = lax.dot_general(cot[...], down[...], CONTRACT_LAST, preferred_element_type=F32)
    sigma = 1.0 / (1.0 + jnp.exp(-pre_act))
    hid = (pre_act * sigma * up_act).astype(BF16)
    hidden[...] = hid
    dup[...] = (dhid * pre_act * sigma).astype(BF16)
    dpre[...] = (dhid * up_act * sigma * (1.0 + pre_act * (1.0 - sigma))).astype(BF16)
    size, half = hid.shape[1], near.shape[1]
    on_left = lax.axis_index("ctx") < 2
    for left, right, mine in ((near, far, on_left), (far, near, jnp.logical_not(on_left))):
        for t in range(2 * half // size):
            low, high = t * size, (t + 1) * size
            cut = min(max(half - low, 0), size)

            @pl.when(mine & (tile == t))
            def _():
                if cut > 0:
                    left[:, low : low + cut] = hid[:, :cut]
                if cut < size:
                    right[:, low + cut - half : high - half] = hid[:, cut:]


def back_kernel(hidden, dpre, dup, gate, up, down, out):
    wide = down.shape[1]
    out[:, :wide] = jnp.dot(hidden[...], down[...], preferred_element_type=F32).astype(BF16)
    out[:, wide:] = (
        lax.dot_general(dpre[...], gate[...], CONTRACT_LAST, preferred_element_type=F32)
        + lax.dot_general(dup[...], up[...], CONTRACT_LAST, preferred_element_type=F32)
    ).astype(BF16)


def pass_kernel(*refs):
    pass


def quarters_kernel(h_own, h_remote, got, remote, mine, other):
    width = remote.shape[1]
    even = lax.rem(lax.axis_index("ctx"), 2) == 0

    def times(left, right):
        return lax.dot_general(left[...], right, CONTRACT_FIRST, preferred_element_type=F32)

    step = 512
    for at in range(0, width, step):
        cols = slice(at, at + step)
        total = times(h_own, got[:, width + at : width + at + step]) + times(
            h_remote, remote[:, cols]
        )
        rows = total.shape[0] // 2
        low, high = total[:rows].astype(BF16), total[rows:].astype(BF16)
        mine[:, cols] = jnp.where(even, low, high)
        other[:, cols] = jnp.where(even, high, low)


def home_kernel(slot, gates, back, cot, layer_output, token_grad, gate_grad):
    count, width = cot.shape
    placing = (
        lax.broadcasted_iota(jnp.int32, (count, back.shape[0]), 1) == column(slot[...])
    ).astype(BF16)
    gate = column(gates[...])
    total = jnp.zeros((count, 1), F32)
    step = WIDE
    for at in range(0, width, step):
        cols = slice(at, at + step)
        out_tok = jnp.dot(placing, back[:, 2 * at : 2 * at + step], preferred_element_type=F32)
        layer_output[:, cols] = (gate * out_tok).astype(BF16)
        total += jnp.sum(cot[:, cols].astype(F32) * out_tok, axis=1, keepdims=True)
        grad_cols = slice(2 * at + step, 2 * at + 2 * step)
        token_grad[:, cols] = jnp.dot(
            placing, back[:, grad_cols], preferred_element_type=F32
        ).astype(BF16)
    gate_grad[...] = jnp.sum(jnp.where(diagonal(count), total, 0.0), axis=0, keepdims=True)


def add_kernel(left, right, out):
    out[0] = (left[...].astype(F32) + right[...].astype(F32)).astype(BF16)


def along(rows, step):
    return lax.ppermute(rows, "ctx", [(i, i ^ step) for i in range(4)])


def body_line(tokens, cotangent, routes, gate_weights, w_gate, w_up, w_down):
    count, width = tokens.shape
    peers = lax.axis_size("tp")
    capacity = 3 * count * routes.shape[1] // (2 * peers)
    slots = peers * capacity
    inner = w_gate.shape[2]
    quarter = inner // 4
    gates = gate_weights.reshape(1, count)
    whole = pl.BlockSpec()
    after = pl.BlockSpec(memory_space=pl.ANY)

    def over_tp(rows):
        wide = rows.shape[1]
        return lax.all_to_all(
            rows.reshape(peers, capacity, wide), "tp", split_axis=0, concat_axis=0, tiled=True
        ).reshape(slots, wide)

    slot, send, across = call(
        functools.partial(send_kernel, peers, capacity),
        [shaped((1, count), jnp.int32), pltpu.HBM((slots, 2 * width), BF16)]
        + [pltpu.HBM((count, width + 128), BF16)],
        scratch_shapes=[pltpu.VMEM((count, width), BF16)],
    )(in_hbm(routes.reshape(1, count)), in_hbm(gates), in_hbm(tokens), in_hbm(cotangent))
    rows_across = along(across, 3)
    got = over_tp(send)
    constant = lambda *shape: pl.BlockSpec(shape, lambda i: (0, 0))
    gate_mat, up_mat, down_mat = in_hbm(w_gate[0]), in_hbm(w_up[0]), in_hbm(w_down[0])
    tile = 256
    by_tile = pl.BlockSpec((slots, tile), lambda i: (0, i))
    hidden, dpre, dup, near, far = call(
        hidden_kernel,
        [pltpu.HBM((slots, inner), BF16)] * 3 + [pltpu.HBM((slots, inner // 2), BF16)] * 2,
        grid=(inner // tile,),
        in_specs=[constant(slots, 2 * width)]
        + [pl.BlockSpec((width, tile), lambda i: (0, i))] * 2
        + [pl.BlockSpec((tile, width), lambda i: (i, 0))],
        out_specs=[by_tile] * 3 + [constant(slots, inner // 2)] * 2,
    )(got, gate_mat, up_mat, down_mat)
    far_across = along(far, 3)
    remote = over_tp(
        call(remote_kernel, shaped((slots, width)), in_specs=[after, whole])(near, rows_across)
    )
    back = call(
        back_kernel,
        pltpu.HBM((slots, 2 * width), BF16),
        grid=(width // WIDE,),
        in_specs=[constant(slots, inner)] * 3
        + [pl.BlockSpec((WIDE, inner), lambda i: (i, 0))] * 2
        + [pl.BlockSpec((inner, WIDE), lambda i: (0, i))],
        out_specs=pl.BlockSpec((slots, 2 * WIDE), lambda i: (0, i)),
    )(hidden, dpre, dup, gate_mat, up_mat, down_mat)
    back = over_tp(
        call(
            pass_kernel,
            pltpu.HBM((slots, 2 * width), BF16),
            in_specs=[after] * 2,
            out_specs=after,
            input_output_aliases={0: 0},
        )(back, far_across)
    )

    mine, other = call(
        quarters_kernel, [shaped((quarter, width)), pltpu.HBM((quarter, width), BF16)]
    )(near, far_across, got, remote)
    swapped = along(other, 1)

    layer_output, token_grad, gate_grad = call(
        home_kernel,
        [shaped((count, width)), shaped((count, width)), shaped((1, count), F32)],
    )(slot, gates, back, in_hbm(cotangent))
    down_grad = call(add_kernel, shaped((1, quarter, width)))(mine, swapped)
    return layer_output, token_grad, gate_grad.reshape(count, 1), down_grad


def solution(mesh):
    rows = P(("ctx", "tp"), None)
    expert = P("tp", None, None)
    line = mesh.shape["ctx"] == 4 and mesh.shape["tp"] == 8
    return jax.shard_map(
        body_line if line else body_any,
        mesh=mesh,
        in_specs=(rows, rows, rows, rows, expert, expert, expert),
        out_specs=(rows, rows, rows, P("tp", "ctx", None)),
        check_vma=False,
    )
```

time: 106 us -> 87 us (0.82)
  starting transfers between devices: 31.1 us -> 21.4 us
  waiting for transfers between devices: 44.5 us -> 37.9 us
  local copies, waits for them, and re-layouts: 8.87 us -> 2.94 us
  Pallas kernels: 19.9 us -> 23.5 us
    ppermute x7 -> x3, waiting for transfers between devices: 44.5 us -> 18.5 us  [along(): return lax.ppermute(rows, 'ctx', [(i, i ^ step) for i in range(4)])]
    all_to_all x3, waiting for transfers between devices: 0.01 us -> 19.4 us  [over_tp(): lax.all_to_all(rows.reshape(peers, capacity, wide), 'tp', split_axis=0, c...]
    ppermute x7 -> x3, starting transfers between devices: 17.5 us -> 8.85 us  [along(): return lax.ppermute(rows, 'ctx', [(i, i ^ step) for i in range(4)])]
    unnamed x26 -> x20, local copies, waits for them, and re-layouts: 8.87 us -> 2.94 us
    pallas_call x8 -> x7, Pallas kernels: 17.4 us -> 21 us  [the longest x1 6.88 us: body_line(): call(back_kernel, pltpu.HBM((slots, 2 * width), BF16), grid=(width // WID...]
    all_to_all x3, starting transfers between devices: 13.7 us -> 12.6 us  [over_tp(): lax.all_to_all(rows.reshape(peers, capacity, wide), 'tp', split_axis=0, c...]
  transfers between devices with their start and end apart: 10 -> 6, of which waited for: 4 -> 3; matrix products, arithmetic and copies ran while one was open for 0% -> 0% of each run, Pallas kernels for 12% -> 19%
where the time goes in v3:
time: 87 us; the launch traced here: 86.5 us
  waiting for transfers between devices  37.9 us (44%)
  Pallas kernels  23.5 us (27%)
  starting transfers between devices  21.4 us (25%)
  local copies, waits for them, and re-layouts  2.94 us (3%)
    all_to_all x3, waiting for transfers between devices, over_tp(): lax.all_to_all(rows.reshape(peers, capacity, wide), 'tp', split_axis=0, c...  19.4 us
    ppermute x3, waiting for transfers between devices, along(): return lax.ppermute(rows, 'ctx', [(i, i ^ step) for i in range(4)])  18.5 us
    all_to_all x3, starting transfers between devices, over_tp(): lax.all_to_all(rows.reshape(peers, capacity, wide), 'tp', split_axis=0, c...  12.6 us
    ppermute x3, starting transfers between devices, along(): return lax.ppermute(rows, 'ctx', [(i, i ^ step) for i in range(4)])  8.85 us
    pallas_call x1, Pallas kernels, body_line(): call(back_kernel, pltpu.HBM((slots, 2 * width), BF16), grid=(width // WID...  6.88 us
    pallas_call x1, Pallas kernels, body_line(): call(hidden_kernel, [pltpu.HBM((slots, inner), BF16)] * 3 + [pltpu.HBM((s...  6.73 us
    pallas_call x1, Pallas kernels, body_line(): call(functools.partial(send_kernel, peers, capacity), [shaped((1, count),...  3.1 us
    unnamed x20, local copies, waits for them, and re-layouts  2.94 us
  transfers between devices with their start and end apart: 6, of which 3 were waited for; matrix products, arithmetic and copies ran while one was open for 0% of the time, Pallas kernels for 19%

profile of v3, /device:TPU:0, one launch (start us, length us, event | category | flops | bytes accessed | tf_op | source)
XLA Modules:
  0.0 86.5 jit_solution(4302551614591254718)
XLA Ops:
  0.6 3.1 %shard_map.102 = (s32[1,128]{1,0:T(1,128)S(1)}, bf16[192,4096]{1,0:T(8,128)(2,1)}, bf16[128,2176]{1,0:T(8,128)(2,1)}) custom-call(s32[1,128]{1,0:T(1,128)} %bitcast.26, f32[1,128]{1,0:T(1,128)} %bitcast.16, bf16[128,2048]{1,0:T(8,128)(2,1)} %tok.1, bf16[128,2048]{1,0:T(8,128)(2,1)} %cot.3), custom_call_target="tpu_custom_call" | custom-call | flops 1 | bytes 1 | tf_op jit(solution)/shard_map/pallas_call | solution.py:241
  3.7 0.0 copy-start.8
  3.7 5.3 %all-to-all-start = ((bf16[8,24,4096]{2,1,0:T(8,128)(2,1)}), bf16[8,24,4096]{2,1,0:T(8,128)(2,1)S(1)}, u32[]{:S(2)}, u32[]{:S(2)}) async-start(bf16[8,24,4096]{2,1,0:T(8,128)(2,1)} %bitcast.25), calls=%async_computation | async-start | bytes 3145728 | tf_op jit(solution)/shard_map/all_to_all | solution.py:237
  9.1 0.0 copy-done.8
  9.1 3.6 %collective-permute-start.1 = (bf16[128,2176]{1,0:T(8,128)(2,1)S(1)}, bf16[128,2176]{1,0:T(8,128)(2,1)S(1)}, u32[]{:S(2)}, u32[]{:S(2)}) collective-permute-start(bf16[128,2176]{1,0:T(8,128)(2,1)S(1)} %copy-done.8), channel_id=1, source_target_pairs={{0,24},{8,16},{16,8},{24,0},{1,25},{9,17},{17,9},{25,1},{2,26},{10... | collective-permute-start | bytes 1671176 | tf_op jit(solution)/shard_map/ppermute | solution.py:221
  12.7 17.4 %all-to-all-done = bf16[8,24,4096]{2,1,0:T(8,128)(2,1)S(1)} async-done(((bf16[8,24,4096]{2,1,0:T(8,128)(2,1)}), bf16[8,24,4096]{2,1,0:T(8,128)(2,1)S(1)}, u32[]{:S(2)}, u32[]{:S(2)}) %all-to-all-start) | async-done | bytes 1572896 | tf_op jit(solution)/shard_map/all_to_all | solution.py:237
  30.1 6.7 %shard_map.103 = (bf16[192,768]{1,0:T(8,128)(2,1)}, bf16[192,768]{1,0:T(8,128)(2,1)}, bf16[192,768]{1,0:T(8,128)(2,1)}, bf16[192,384]{1,0:T(8,128)(2,1)}, bf16[192,384]{1,0:T(8,128)(2,1)}) custom-call(bf16[192,4096]{1,0:T(8,128)(2,1)S(1)} %bitcast.12, bf16[2048,768]{1,0:T(8,128)(2,1)} %bitcast.19, bf16[2048,768]{1,0:T(8,128)(2,1)} %bitcast.21, ...), custom_call_target="tpu_custom_call" | custom-call | flops 1 | bytes 1 | tf_op jit(solution)/shard_map/pallas_call | solution.py:253
  36.8 0.0 collective-permute-done.1.rows
  36.8 0.0 copy-start.2
  36.8 0.9 %copy-done.2 = bf16[192,384]{1,0:T(8,128)(2,1)S(1)} copy-done((bf16[192,384]{1,0:T(8,128)(2,1)S(1)}, bf16[192,384]{1,0:T(8,128)(2,1)}, u32[]{:S(2)}) %copy-start.2) | copy-done | bytes 147480
  37.7 1.4 %shard_map.107 = bf16[192,2048]{1,0:T(8,128)(2,1)} custom-call(bf16[192,384]{1,0:T(8,128)(2,1)S(1)} %copy-done.2, bf16[128,2176]{1,0:T(8,128)(2,1)S(1)} %collective-permute-done.1.rows), custom_call_target="tpu_custom_call" | custom-call | flops 1 | bytes 1 | tf_op jit(solution)/shard_map/pallas_call | solution.py:264
  39.1 3.5 %all-to-all-start.2 = ((bf16[8,24,2048]{2,1,0:T(8,128)(2,1)}), bf16[8,24,2048]{2,1,0:T(8,128)(2,1)S(1)}, u32[]{:S(2)}, u32[]{:S(2)}) async-start(bf16[8,24,2048]{2,1,0:T(8,128)(2,1)} %bitcast.10), calls=%async_computation.2 | async-start | bytes 1572864 | tf_op jit(solution)/shard_map/all_to_all | solution.py:237
  42.7 0.0 copy-done.9
  42.7 3.6 %collective-permute-start = (bf16[192,384]{1,0:T(8,128)(2,1)S(1)}, bf16[192,384]{1,0:T(8,128)(2,1)S(1)}, u32[]{:S(2)}, u32[]{:S(2)}) collective-permute-start(bf16[192,384]{1,0:T(8,128)(2,1)S(1)} %copy-done.9), channel_id=1, source_target_pairs={{0,24},{8,16},{16,8},{24,0},{1,25},{9,17},{17,9},{25,1},{2,26},{10... | collective-permute-start | bytes 442376 | tf_op jit(solution)/shard_map/ppermute | solution.py:221
  46.3 0.0 copy-done.4
  46.3 0.0 copy-done.5
  46.3 0.0 copy-done.6
  46.3 6.9 %shard_map.104.refs_0_ = bf16[192,4096]{1,0:T(8,128)(2,1)} custom-call(bf16[192,768]{1,0:T(8,128)(2,1)S(1)} %copy-done.4, bf16[192,768]{1,0:T(8,128)(2,1)S(1)} %copy-done.5, bf16[192,768]{1,0:T(8,128)(2,1)S(1)} %copy-done.6, bf16[2048,768]{1,0:T(8,128)(2,1)} %bitcast.20, bf16[2048,768]{1,0:T(8,128)(2,1)} %bitcast.22, bf16[768,2048]{1,0:T(8,128)(2,1)} %bitcast.24), custom_call_target="tpu_custom_call" | custom-call | flops 1 | bytes 1 | tf_op jit(solution)/shard_map/pallas_call | solution.py:266
  53.2 0.0 collective-permute-done.refs_1_.h_remote
  53.2 2.0 %all-to-all-done.2 = bf16[8,24,2048]{2,1,0:T(8,128)(2,1)S(1)} async-done(((bf16[8,24,2048]{2,1,0:T(8,128)(2,1)}), bf16[8,24,2048]{2,1,0:T(8,128)(2,1)S(1)}, u32[]{:S(2)}, u32[]{:S(2)}) %all-to-all-start.2) | async-done | bytes 786464 | tf_op jit(solution)/shard_map/all_to_all | solution.py:237
  55.2 0.9 %copy-done = bf16[8,24,2048]{2,1,0:T(8,128)(2,1)} copy-done((bf16[8,24,2048]{2,1,0:T(8,128)(2,1)}, bf16[8,24,2048]{2,1,0:T(8,128)(2,1)S(1)}, u32[]{:S(2)}) %copy-start) | copy-done | bytes 786456
  56.1 3.7 %all-to-all-start.1 = ((bf16[8,24,4096]{2,1,0:T(8,128)(2,1)}), bf16[8,24,4096]{2,1,0:T(8,128)(2,1)S(1)}, u32[]{:S(2)}, u32[]{:S(2)}) async-start(bf16[8,24,4096]{2,1,0:T(8,128)(2,1)} %bitcast.18), calls=%async_computation.1 | async-start | bytes 3145728 | tf_op jit(solution)/shard_map/all_to_all | solution.py:237
  59.8 0.0 copy-done.3
  59.8 0.0 copy-start.1
  59.8 1.1 %copy-done.1 = bf16[8,24,2048]{2,1,0:T(8,128)(2,1)S(1)} copy-done((bf16[8,24,2048]{2,1,0:T(8,128)(2,1)S(1)}, bf16[8,24,2048]{2,1,0:T(8,128)(2,1)}, u32[]{:S(2)}) %copy-start.1) | copy-done | bytes 786456
  60.9 1.9 %shard_map.108 = (bf16[192,2048]{1,0:T(8,128)(2,1)S(1)}, bf16[192,2048]{1,0:T(8,128)(2,1)}) custom-call(bf16[192,384]{1,0:T(8,128)(2,1)S(1)} %copy-done.3, bf16[192,384]{1,0:T(8,128)(2,1)S(1)} %collective-permute-done.refs_1_.h_remote, bf16[192,4096]{1,0:T(8,128)(2,1)S(1)} %bitcast.13, bf16[192,2048]{1,0:T(8,128)(2,1)S(1)} %bitcast.15), custom_call_target="tpu_custom_call" | custom-call | flops 1 | bytes 1 | tf_op jit(solution)/shard_map/pallas_call | solution.py:285
  62.8 1.6 %collective-permute-start.2 = (bf16[192,2048]{1,0:T(8,128)(2,1)}, bf16[192,2048]{1,0:T(8,128)(2,1)S(1)}, u32[]{:S(2)}, u32[]{:S(2)}) collective-permute-start(bf16[192,2048]{1,0:T(8,128)(2,1)} %get-tuple-element.29), channel_id=1, source_target_pairs={{0,8},{8,0},{16,24},{24,16},{1,9},{9,1},{17,25},{25,17},{2,10},{10... | collective-permute-start | bytes 2359304 | tf_op jit(solution)/shard_map/ppermute | solution.py:221
  64.4 18.5 %collective-permute-done.2.right = bf16[192,2048]{1,0:T(8,128)(2,1)S(1)} collective-permute-done((bf16[192,2048]{1,0:T(8,128)(2,1)}, bf16[192,2048]{1,0:T(8,128)(2,1)S(1)}, u32[]{:S(2)}, u32[]{:S(2)}) %collective-permute-start.2) | collective-permute-done | bytes 786464 | tf_op jit(solution)/shard_map/ppermute | solution.py:221
  82.9 1.1 %shard_map.109 = bf16[1,192,2048]{2,1,0:T(8,128)(2,1)} custom-call(bf16[192,2048]{1,0:T(8,128)(2,1)S(1)} %get-tuple-element.28.left, bf16[192,2048]{1,0:T(8,128)(2,1)S(1)} %collective-permute-done.2.right), custom_call_target="tpu_custom_call" | custom-call | flops 1 | bytes 1 | tf_op jit(solution)/shard_map/pallas_call | solution.py:294
  84.0 0.0 all-to-all-done.1
  84.0 0.0 copy-done.7
  84.0 2.5 %shard_map.106 = (bf16[128,2048]{1,0:T(8,128)(2,1)}, bf16[128,2048]{1,0:T(8,128)(2,1)}, f32[1,128]{1,0:T(1,128)}) custom-call(s32[1,128]{1,0:T(1,128)S(1)} %get-tuple-element.17.slot, f32[1,128]{1,0:T(1,128)S(1)} %bitcast.17, bf16[192,4096]{1,0:T(8,128)(2,1)S(1)} %bitcast.14, bf16[128,2048]{1,0:T(8,128)(2,1)} %cot.3), custom_call_target="tpu_custom_call" | custom-call | flops 1 | bytes 1 | tf_op jit(solution)/shard_map/pallas_call | solution.py:290
  (8 shorter events, 0.0 us)
Async XLA Ops:
  3.7 5.3 %copy-start.8 = (bf16[128,2176]{1,0:T(8,128)(2,1)S(1)}, bf16[128,2176]{1,0:T(8,128)(2,1)}, u32[]{:S(2)}) copy-start(bf16[128,2176]{1,0:T(8,128)(2,1)} %get-tuple-element.27) | copy-start | bytes 1671172
  3.7 26.4 %all-to-all-start = ((bf16[8,24,4096]{2,1,0:T(8,128)(2,1)}), bf16[8,24,4096]{2,1,0:T(8,128)(2,1)S(1)}, u32[]{:S(2)}, u32[]{:S(2)}) async-start(bf16[8,24,4096]{2,1,0:T(8,128)(2,1)} %bitcast.25), calls=%async_computation | async-start | bytes 3145728 | tf_op jit(solution)/shard_map/all_to_all | solution.py:237
  9.1 27.8 %collective-permute-start.1 = (bf16[128,2176]{1,0:T(8,128)(2,1)S(1)}, bf16[128,2176]{1,0:T(8,128)(2,1)S(1)}, u32[]{:S(2)}, u32[]{:S(2)}) collective-permute-start(bf16[128,2176]{1,0:T(8,128)(2,1)S(1)} %copy-done.8), channel_id=1, source_target_pairs={{0,24},{8,16},{16,8},{24,0},{1,25},{9,17},{17,9},{25,1},{2,26},{10... | collective-permute-start | bytes 1671176 | tf_op jit(solution)/shard_map/ppermute | solution.py:221
  36.8 0.9 %copy-start.2 = (bf16[192,384]{1,0:T(8,128)(2,1)S(1)}, bf16[192,384]{1,0:T(8,128)(2,1)}, u32[]{:S(2)}) copy-start(bf16[192,384]{1,0:T(8,128)(2,1)} %get-tuple-element.26.after.h_own) | copy-start | bytes 442372
  37.7 4.9 %copy-start.9 = (bf16[192,384]{1,0:T(8,128)(2,1)S(1)}, bf16[192,384]{1,0:T(8,128)(2,1)}, u32[]{:S(2)}) copy-start(bf16[192,384]{1,0:T(8,128)(2,1)} %get-tuple-element.22) | copy-start | bytes 442372
  37.7 8.6 %copy-start.4 = (bf16[192,768]{1,0:T(8,128)(2,1)S(1)}, bf16[192,768]{1,0:T(8,128)(2,1)}, u32[]{:S(2)}) copy-start(bf16[192,768]{1,0:T(8,128)(2,1)} %get-tuple-element.19.hidden) | copy-start | bytes 884740
  37.7 8.6 %copy-start.5 = (bf16[192,768]{1,0:T(8,128)(2,1)S(1)}, bf16[192,768]{1,0:T(8,128)(2,1)}, u32[]{:S(2)}) copy-start(bf16[192,768]{1,0:T(8,128)(2,1)} %get-tuple-element.20.dpre) | copy-start | bytes 884740
  37.7 8.6 %copy-start.6 = (bf16[192,768]{1,0:T(8,128)(2,1)S(1)}, bf16[192,768]{1,0:T(8,128)(2,1)}, u32[]{:S(2)}) copy-start(bf16[192,768]{1,0:T(8,128)(2,1)} %get-tuple-element.21.dup) | copy-start | bytes 884740
  39.1 16.1 %all-to-all-start.2 = ((bf16[8,24,2048]{2,1,0:T(8,128)(2,1)}), bf16[8,24,2048]{2,1,0:T(8,128)(2,1)S(1)}, u32[]{:S(2)}, u32[]{:S(2)}) async-start(bf16[8,24,2048]{2,1,0:T(8,128)(2,1)} %bitcast.10), calls=%async_computation.2 | async-start | bytes 1572864 | tf_op jit(solution)/shard_map/all_to_all | solution.py:237
  42.7 10.5 %collective-permute-start = (bf16[192,384]{1,0:T(8,128)(2,1)S(1)}, bf16[192,384]{1,0:T(8,128)(2,1)S(1)}, u32[]{:S(2)}, u32[]{:S(2)}) collective-permute-start(bf16[192,384]{1,0:T(8,128)(2,1)S(1)} %copy-done.9), channel_id=1, source_target_pairs={{0,24},{8,16},{16,8},{24,0},{1,25},{9,17},{17,9},{25,1},{2,26},{10... | collective-permute-start | bytes 442376 | tf_op jit(solution)/shard_map/ppermute | solution.py:221
  55.2 0.9 %copy-start = (bf16[8,24,2048]{2,1,0:T(8,128)(2,1)}, bf16[8,24,2048]{2,1,0:T(8,128)(2,1)S(1)}, u32[]{:S(2)}) copy-start(bf16[8,24,2048]{2,1,0:T(8,128)(2,1)S(1)} %all-to-all-done.2) | copy-start | bytes 2359300
  56.1 3.7 %copy-start.3 = (bf16[192,384]{1,0:T(8,128)(2,1)S(1)}, bf16[192,384]{1,0:T(8,128)(2,1)}, u32[]{:S(2)}) copy-start(bf16[192,384]{1,0:T(8,128)(2,1)} %get-tuple-element.26.after.h_own) | copy-start | bytes 442372
  56.1 27.9 %all-to-all-start.1 = ((bf16[8,24,4096]{2,1,0:T(8,128)(2,1)}), bf16[8,24,4096]{2,1,0:T(8,128)(2,1)S(1)}, u32[]{:S(2)}, u32[]{:S(2)}) async-start(bf16[8,24,4096]{2,1,0:T(8,128)(2,1)} %bitcast.18), calls=%async_computation.1 | async-start | bytes 3145728 | tf_op jit(solution)/shard_map/all_to_all | solution.py:237
  59.8 1.1 %copy-start.1 = (bf16[8,24,2048]{2,1,0:T(8,128)(2,1)S(1)}, bf16[8,24,2048]{2,1,0:T(8,128)(2,1)}, u32[]{:S(2)}) copy-start(bf16[8,24,2048]{2,1,0:T(8,128)(2,1)} %copy-done) | copy-start | bytes 2359300
  62.8 21.2 %copy-start.7 = (f32[128,1]{0,1:T(1,128)S(1)}, f32[128,1]{0,1:T(1,128)}, u32[]{:S(2)}) copy-start(f32[128,1]{0,1:T(1,128)} %param.10) | copy-start | bytes 1540
  62.8 20.1 %collective-permute-start.2 = (bf16[192,2048]{1,0:T(8,128)(2,1)}, bf16[192,2048]{1,0:T(8,128)(2,1)S(1)}, u32[]{:S(2)}, u32[]{:S(2)}) collective-permute-start(bf16[192,2048]{1,0:T(8,128)(2,1)} %get-tuple-element.29), channel_id=1, source_target_pairs={{0,8},{8,0},{16,24},{24,16},{1,9},{9,1},{17,25},{25,17},{2,10},{10... | collective-permute-start | bytes 2359304 | tf_op jit(solution)/shard_map/ppermute | solution.py:221

commit v4 on v3

--- a/solution.py
+++ b/solution.py
@@ -104,7 +104,8 @@
         ).astype(BF16)
 
 
-def send_kernel(peers, capacity, routes, gates, tok, cot, slot_out, out, across, scaled):
+def send_kernel(peers, capacity, routes, gates, tok, cot, slot_out, across, *refs):
+    blocks, scaled = refs[:-1], refs[-1]
     ids = routes[...]
     count, width = cot.shape
     onehot = lax.broadcasted_iota(jnp.int32, (peers, count), 0) == ids
@@ -120,61 +121,114 @@
     across[:, width:] = jnp.broadcast_to(
         column(slot.astype(F32)), (count, across.shape[1] - width)
     ).astype(BF16)
+    slot = (ids ^ lax.axis_index("tp")) * capacity + rank
     placing = (
         lax.broadcasted_iota(jnp.int32, (peers * capacity, count), 0) == slot
     ).astype(BF16)
-    place(placing, tok, out, 0, width)
-    place(placing, scaled, out, width, width)
-
-
-def remote_kernel(after, rows, out):
+    step = 512
+    for at, rows in ((0, tok), (width, scaled)):
+        for col in range(0, width, step):
+            placed = jnp.dot(placing, rows[:, col : col + step], preferred_element_type=F32)
+            for k, block in enumerate(blocks):
+                block[:, at + col : at + col + step] = placed[
+                    k * capacity : (k + 1) * capacity
+                ].astype(BF16)
+
+
+def remote_kernel(rows, *refs):
+    out = refs[-1]
     count, width = rows.shape[0], out.shape[1]
     slot = rows[:, width : width + 1].astype(F32).astype(jnp.int32)
     home = (lax.broadcasted_iota(jnp.int32, (count, out.shape[0]), 1) == slot).astype(F32)
     place(home.T.astype(BF16), rows, out, 0, width)
 
 
-def hidden_kernel(got, gate, up, down, hidden, dpre, dup, near, far):
-    width = gate.shape[0]
-    rows, cot = got.at[:, :width], got.at[:, width:]
-    tile = pl.program_id(0)
-    pre_act = jnp.dot(rows[...], gate[...], preferred_element_type=F32)
-    up_act = jnp.dot(rows[...], up[...], preferred_element_type=F32)
-    dhid = lax.dot_general(cot[...], down[...], CONTRACT_LAST, preferred_element_type=F32)
-    sigma = 1.0 / (1.0 + jnp.exp(-pre_act))
-    hid = (pre_act * sigma * up_act).astype(BF16)
-    hidden[...] = hid
-    dup[...] = (dhid * pre_act * sigma).astype(BF16)
-    dpre[...] = (dhid * up_act * sigma * (1.0 + pre_act * (1.0 - sigma))).astype(BF16)
-    size, half = hid.shape[1], near.shape[1]
+def tile_copies(tiles, sems):
+    copies = [
+        [pltpu.make_async_copy(source, target, sems.at[t, i]) for i, (source, target) in enumerate(pairs)]
+        for t, pairs in enumerate(tiles)
+    ]
+    for tile in copies:
+        for copy in tile:
+            copy.start()
+    return copies
+
+
+def hidden_kernel(peers, *refs):
+    blocks, (gate, up, down, hidden, dpre, dup, near, far, cot) = refs[:peers], refs[peers : peers + 9]
+    gate_in, up_in, down_in, wide, rows, sems = refs[peers + 9 :]
+    width, inner = gate.shape
+    capacity = blocks[0].shape[0]
+    step = inner // sems.shape[0]
+    tiles = [slice(at, at + step) for at in range(0, inner, step)]
+    copies = tile_copies(
+        [
+            (
+                (gate.at[:, t], gate_in.at[:, t]),
+                (up.at[:, t], up_in.at[:, t]),
+                (down.at[t, :], down_in.at[t, :]),
+            )
+            for t in tiles
+        ],
+        sems,
+    )
+    own = lax.axis_index("tp")
+    for k, block in enumerate(blocks):
+        start = pl.multiple_of((own ^ k) * capacity, 8)
+        wide[pl.ds(start, capacity), :] = block[...].astype(F32)
+    rows[...] = wide[...].astype(BF16)
+    cot[...] = rows[:, width:]
+    for t, tile in zip(tiles, copies):
+        for copy in tile:
+            copy.wait()
+        pre_act = jnp.dot(rows[:, :width], gate_in[:, t], preferred_element_type=F32)
+        up_act = jnp.dot(rows[:, :width], up_in[:, t], preferred_element_type=F32)
+        dhid = lax.dot_general(
+            rows[:, width:], down_in[t, :], CONTRACT_LAST, preferred_element_type=F32
+        )
+        sigma = 1.0 / (1.0 + jnp.exp(-pre_act))
+        hidden[:, t] = (pre_act * sigma * up_act).astype(BF16)
+        dup[:, t] = (dhid * pre_act * sigma).astype(BF16)
+        dpre[:, t] = (dhid * up_act * sigma * (1.0 + pre_act * (1.0 - sigma))).astype(BF16)
+    half = near.shape[1]
     on_left = lax.axis_index("ctx") < 2
-    for left, right, mine in ((near, far, on_left), (far, near, jnp.logical_not(on_left))):
-        for t in range(2 * half // size):
-            low, high = t * size, (t + 1) * size
-            cut = min(max(half - low, 0), size)
-
-            @pl.when(mine & (tile == t))
-            def _():
-                if cut > 0:
-                    left[:, low : low + cut] = hid[:, :cut]
-                if cut < size:
-                    right[:, low + cut - half : high - half] = hid[:, cut:]
-
-
-def back_kernel(hidden, dpre, dup, gate, up, down, out):
-    wide = down.shape[1]
-    out[:, :wide] = jnp.dot(hidden[...], down[...], preferred_element_type=F32).astype(BF16)
-    out[:, wide:] = (
-        lax.dot_general(dpre[...], gate[...], CONTRACT_LAST, preferred_element_type=F32)
-        + lax.dot_general(dup[...], up[...], CONTRACT_LAST, preferred_element_type=F32)
-    ).astype(BF16)
+    left, right = hidden[:, :half], hidden[:, half:]
+    near[...] = jnp.where(on_left, left, right)
+    far[...] = jnp.where(on_left, right, left)
+
+
+def back_kernel(hidden, dpre, dup, gate, up, down, out, gate_in, up_in, down_in, sems):
+    width = down.shape[1]
+    tiles = [slice(at, at + WIDE) for at in range(0, width, WIDE)]
+    copies = tile_copies(
+        [
+            (
+                (down.at[:, t], down_in.at[:, t]),
+                (gate.at[t, :], gate_in.at[t, :]),
+                (up.at[t, :], up_in.at[t, :]),
+            )
+            for t in tiles
+        ],
+        sems,
+    )
+    for t, tile in zip(tiles, copies):
+        for copy in tile:
+            copy.wait()
+        at = 2 * t.start
+        out[:, at : at + WIDE] = jnp.dot(
+            hidden[...], down_in[:, t], preferred_element_type=F32
+        ).astype(BF16)
+        out[:, at + WIDE : at + 2 * WIDE] = (
+            lax.dot_general(dpre[...], gate_in[t, :], CONTRACT_LAST, preferred_element_type=F32)
+            + lax.dot_general(dup[...], up_in[t, :], CONTRACT_LAST, preferred_element_type=F32)
+        ).astype(BF16)
 
 
 def pass_kernel(*refs):
     pass
 
 
-def quarters_kernel(h_own, h_remote, got, remote, mine, other):
+def quarters_kernel(h_own, h_remote, own, remote, mine, other):
     width = remote.shape[1]
     even = lax.rem(lax.axis_index("ctx"), 2) == 0
 
@@ -184,7 +238,7 @@
     step = 512
     for at in range(0, width, step):
         cols = slice(at, at + step)
-        total = times(h_own, got[:, width + at : width + at + step]) + times(
+        total = times(h_own, own[:, cols]) + times(
             h_remote, remote[:, cols]
         )
         rows = total.shape[0] // 2
@@ -238,40 +292,45 @@
             rows.reshape(peers, capacity, wide), "tp", split_axis=0, concat_axis=0, tiled=True
         ).reshape(slots, wide)
 
-    slot, send, across = call(
+    slot, across, *blocks = call(
         functools.partial(send_kernel, peers, capacity),
-        [shaped((1, count), jnp.int32), pltpu.HBM((slots, 2 * width), BF16)]
-        + [pltpu.HBM((count, width + 128), BF16)],
+        [shaped((1, count), jnp.int32), pltpu.HBM((count, width + 128), BF16)]
+        + [pltpu.HBM((capacity, 2 * width), BF16)] * peers,
         scratch_shapes=[pltpu.VMEM((count, width), BF16)],
     )(in_hbm(routes.reshape(1, count)), in_hbm(gates), in_hbm(tokens), in_hbm(cotangent))
     rows_across = along(across, 3)
-    got = over_tp(send)
-    constant = lambda *shape: pl.BlockSpec(shape, lambda i: (0, 0))
-    gate_mat, up_mat, down_mat = in_hbm(w_gate[0]), in_hbm(w_up[0]), in_hbm(w_down[0])
-    tile = 256
-    by_tile = pl.BlockSpec((slots, tile), lambda i: (0, i))
-    hidden, dpre, dup, near, far = call(
-        hidden_kernel,
-        [pltpu.HBM((slots, inner), BF16)] * 3 + [pltpu.HBM((slots, inner // 2), BF16)] * 2,
-        grid=(inner // tile,),
-        in_specs=[constant(slots, 2 * width)]
-        + [pl.BlockSpec((width, tile), lambda i: (0, i))] * 2
-        + [pl.BlockSpec((tile, width), lambda i: (i, 0))],
-        out_specs=[by_tile] * 3 + [constant(slots, inner // 2)] * 2,
-    )(got, gate_mat, up_mat, down_mat)
+    got = [in_hbm(blocks[0])] + [
+        lax.ppermute(blocks[k], "tp", [(i, i ^ k) for i in range(peers)]) for k in range(1, peers)
+    ]
+
+    weights = [in_hbm(w[0]) for w in (w_gate, w_up, w_down)]
+    held = [pltpu.VMEM(w.shape, BF16) for w in weights]
+    in_place = pl.BlockSpec(memory_space=pltpu.HBM)
+    hidden, dpre, dup, near, far, cot = call(
+        functools.partial(hidden_kernel, peers),
+        [pltpu.HBM((slots, inner), BF16)] * 3
+        + [pltpu.HBM((slots, inner // 2), BF16)] * 2
+        + [pltpu.HBM((slots, width), BF16)],
+        in_specs=[whole] * peers + [in_place] * 3,
+        scratch_shapes=held
+        + [
+            pltpu.VMEM((slots, 2 * width), F32),
+            pltpu.VMEM((slots, 2 * width), BF16),
+            pltpu.SemaphoreType.DMA((3, 3)),
+        ],
+    )(*got, *weights)
     far_across = along(far, 3)
     remote = over_tp(
-        call(remote_kernel, shaped((slots, width)), in_specs=[after, whole])(near, rows_across)
+        call(
+            remote_kernel, shaped((slots, width)), in_specs=[whole] + [after] * (peers - 1)
+        )(rows_across, *got[1:])
     )
     back = call(
         back_kernel,
         pltpu.HBM((slots, 2 * width), BF16),
-        grid=(width // WIDE,),
-        in_specs=[constant(slots, inner)] * 3
-        + [pl.BlockSpec((WIDE, inner), lambda i: (i, 0))] * 2
-        + [pl.BlockSpec((inner, WIDE), lambda i: (0, i))],
-        out_specs=pl.BlockSpec((slots, 2 * WIDE), lambda i: (0, i)),
-    )(hidden, dpre, dup, gate_mat, up_mat, down_mat)
+        in_specs=[whole] * 3 + [in_place] * 3,
+        scratch_shapes=held + [pltpu.SemaphoreType.DMA((width // WIDE, 3))],
+    )(in_hbm(hidden), in_hbm(dpre), in_hbm(dup), *weights)
     back = over_tp(
         call(
             pass_kernel,
@@ -279,12 +338,12 @@
             in_specs=[after] * 2,
             out_specs=after,
             input_output_aliases={0: 0},
-        )(back, far_across)
+        )(in_hbm(back), far_across)
     )
 
     mine, other = call(
         quarters_kernel, [shaped((quarter, width)), pltpu.HBM((quarter, width), BF16)]
-    )(near, far_across, got, remote)
+    )(in_hbm(near), far_across, in_hbm(cot), remote)
     swapped = along(other, 1)
 
     layer_output, token_grad, gate_grad = call(

time: 87 us -> 81.5 us (0.937)
  waiting for transfers between devices: 37.9 us -> 28.8 us
  starting transfers between devices: 21.4 us -> 26.3 us
  local copies, waits for them, and re-layouts: 2.94 us -> 0.01 us
  Pallas kernels: 23.5 us -> 25.4 us
    ppermute x3, waiting for transfers between devices: 18.5 us -> 2.92 us  [along(): return lax.ppermute(rows, 'ctx', [(i, i ^ step) for i in range(4)])]
    ppermute x0 -> x7, waiting for transfers between devices: none -> 12.1 us  [body_line(): lax.ppermute(blocks[k], 'tp', [(i, i ^ k) for i in range(peers)])]
    ppermute x0 -> x7, starting transfers between devices: none -> 8.88 us  [body_line(): lax.ppermute(blocks[k], 'tp', [(i, i ^ k) for i in range(peers)])]
    all_to_all x3 -> x2, waiting for transfers between devices: 19.4 us -> 13.8 us  [over_tp(): lax.all_to_all(rows.reshape(peers, capacity, wide), 'tp', split_axis=0, c...]
    all_to_all x3 -> x2, starting transfers between devices: 12.6 us -> 7.98 us  [over_tp(): lax.all_to_all(rows.reshape(peers, capacity, wide), 'tp', split_axis=0, c...]
    unnamed x20 -> x2, local copies, waits for them, and re-layouts: 2.94 us -> 0.01 us
    pallas_call x1, Pallas kernels: 1.91 us -> 3.14 us  [body_line(): call(quarters_kernel, [shaped((quarter, width)), pltpu.HBM((quarter, widt...]
  transfers between devices with their start and end apart: 6 -> 12, of which waited for: 3 -> 6; matrix products, arithmetic and copies ran while one was open for 0% -> 0% of each run, Pallas kernels for 19% -> 25%
where the time goes in v4:
time: 81.5 us; the launch traced here: 81.1 us
  waiting for transfers between devices  28.8 us (35%)
  starting transfers between devices  26.3 us (32%)
  Pallas kernels  25.4 us (31%)
    all_to_all x2, waiting for transfers between devices, over_tp(): lax.all_to_all(rows.reshape(peers, capacity, wide), 'tp', split_axis=0, c...  13.8 us
    ppermute x7, waiting for transfers between devices, body_line(): lax.ppermute(blocks[k], 'tp', [(i, i ^ k) for i in range(peers)])  12.1 us
    ppermute x3, starting transfers between devices, along(): return lax.ppermute(rows, 'ctx', [(i, i ^ step) for i in range(4)])  9.44 us
    ppermute x7, starting transfers between devices, body_line(): lax.ppermute(blocks[k], 'tp', [(i, i ^ k) for i in range(peers)])  8.88 us
    all_to_all x2, starting transfers between devices, over_tp(): lax.all_to_all(rows.reshape(peers, capacity, wide), 'tp', split_axis=0, c...  7.98 us
    pallas_call x1, Pallas kernels, body_line(): call(back_kernel, pltpu.HBM((slots, 2 * width), BF16), in_specs=[whole] *...  7.36 us
    pallas_call x1, Pallas kernels, body_line(): call(functools.partial(hidden_kernel, peers), [pltpu.HBM((slots, inner),...  6.97 us
    pallas_call x1, Pallas kernels, body_line(): call(quarters_kernel, [shaped((quarter, width)), pltpu.HBM((quarter, widt...  3.14 us
  transfers between devices with their start and end apart: 12, of which 6 were waited for; matrix products, arithmetic and copies ran while one was open for 0% of the time, Pallas kernels for 25%

profile of v4, /device:TPU:0, one launch (start us, length us, event | category | flops | bytes accessed | tf_op | source)
XLA Modules:
  0.0 81.1 jit_solution(17760132486687942541)
XLA Ops:
  0.6 3.0 %shard_map.102 = (s32[1,128]{1,0:T(1,128)S(1)}, bf16[128,2176]{1,0:T(8,128)(2,1)}, bf16[24,4096]{1,0:T(8,128)(2,1)}, bf16[24,4096]{1,0:T(8,128)(2,1)}, bf16[24,4...) custom-call(s32[1,128]{1,0:T(1,128)} %bitcast.21, ...), custom_call_target="tpu_custom_call" | custom-call | flops 1 | bytes 1 | tf_op jit(solution)/shard_map/pallas_call | solution.py:295
  3.7 5.0 %collective-permute-start.8 = (bf16[128,2176]{1,0:T(8,128)(2,1)}, bf16[128,2176]{1,0:T(8,128)(2,1)S(1)}, u32[]{:S(2)}, u32[]{:S(2)}) collective-permute-start(bf16[128,2176]{1,0:T(8,128)(2,1)} %get-tuple-element.43), channel_id=1, source_target_pairs={{0,24},{8,16},{16,8},{24,0},{1,25},{9,17},{17,9},{25,1},{2,26},{10... | collective-permute-start | bytes 1671176 | tf_op jit(solution)/shard_map/ppermute | solution.py:275
  8.7 0.0 collective-permute-start
  8.7 1.5 %collective-permute-start.1 = (bf16[24,4096]{1,0:T(8,128)(2,1)}, bf16[24,4096]{1,0:T(8,128)(2,1)S(1)}, u32[]{:S(2)}, u32[]{:S(2)}) collective-permute-start(bf16[24,4096]{1,0:T(8,128)(2,1)} %get-tuple-element.28), channel_id=1, source_target_pairs={{0,2},{1,3},{2,0},{3,1},{4,6},{5,7},{6,4},{7,5},{8,10},{9,11},{10,... | collective-permute-start | bytes 589832 | tf_op jit(solution)/shard_map/ppermute | solution.py:303
  10.2 0.4 collective-permute-start.2
  10.6 1.5 %collective-permute-start.3 = (bf16[24,4096]{1,0:T(8,128)(2,1)}, bf16[24,4096]{1,0:T(8,128)(2,1)S(1)}, u32[]{:S(2)}, u32[]{:S(2)}) collective-permute-start(bf16[24,4096]{1,0:T(8,128)(2,1)} %get-tuple-element.30), channel_id=1, source_target_pairs={{0,4},{1,5},{2,6},{3,7},{4,0},{5,1},{6,2},{7,3},{8,12},{9,13},{10,... | collective-permute-start | bytes 589832 | tf_op jit(solution)/shard_map/ppermute | solution.py:303
  12.1 0.0 collective-permute-done.refs_1_.refs_0_
  12.1 0.1 collective-permute-start.4
  12.2 4.4 %collective-permute-done.1.refs_2_.refs_1_ = bf16[24,4096]{1,0:T(8,128)(2,1)S(1)} collective-permute-done((bf16[24,4096]{1,0:T(8,128)(2,1)}, bf16[24,4096]{1,0:T(8,128)(2,1)S(1)}, u32[]{:S(2)}, u32[]{:S(2)}) %collective-permute-start.1) | collective-permute-done | bytes 196640 | tf_op jit(solution)/shard_map/ppermute | solution.py:303
  16.6 2.4 %collective-permute-start.5 = (bf16[24,4096]{1,0:T(8,128)(2,1)}, bf16[24,4096]{1,0:T(8,128)(2,1)S(1)}, u32[]{:S(2)}, u32[]{:S(2)}) collective-permute-start(bf16[24,4096]{1,0:T(8,128)(2,1)} %get-tuple-element.32), channel_id=1, source_target_pairs={{0,6},{1,7},{2,4},{3,5},{4,2},{5,3},{6,0},{7,1},{8,14},{9,15},{10,... | collective-permute-start | bytes 589832 | tf_op jit(solution)/shard_map/ppermute | solution.py:303
  19.1 1.0 %collective-permute-done.2.refs_3_.refs_2_ = bf16[24,4096]{1,0:T(8,128)(2,1)S(1)} collective-permute-done((bf16[24,4096]{1,0:T(8,128)(2,1)}, bf16[24,4096]{1,0:T(8,128)(2,1)S(1)}, u32[]{:S(2)}, u32[]{:S(2)}) %collective-permute-start.2) | collective-permute-done | bytes 196640 | tf_op jit(solution)/shard_map/ppermute | solution.py:303
  20.1 2.9 %collective-permute-start.6 = (bf16[24,4096]{1,0:T(8,128)(2,1)}, bf16[24,4096]{1,0:T(8,128)(2,1)S(1)}, u32[]{:S(2)}, u32[]{:S(2)}) collective-permute-start(bf16[24,4096]{1,0:T(8,128)(2,1)} %get-tuple-element.33), channel_id=1, source_target_pairs={{0,7},{1,6},{2,5},{3,4},{4,3},{5,2},{6,1},{7,0},{8,15},{9,14},{10,... | collective-permute-start | bytes 589832 | tf_op jit(solution)/shard_map/ppermute | solution.py:303
  23.0 0.0 collective-permute-done.3.refs_4_.refs_3_
  23.0 6.6 %collective-permute-done.4.refs_5_.refs_4_ = bf16[24,4096]{1,0:T(8,128)(2,1)S(1)} collective-permute-done((bf16[24,4096]{1,0:T(8,128)(2,1)}, bf16[24,4096]{1,0:T(8,128)(2,1)S(1)}, u32[]{:S(2)}, u32[]{:S(2)}) %collective-permute-start.4) | collective-permute-done | bytes 196640 | tf_op jit(solution)/shard_map/ppermute | solution.py:303
  29.6 0.0 collective-permute-done.5.refs_6_.refs_5_
  29.6 0.0 collective-permute-done.6.refs_7_.refs_6_
  29.7 0.0 collective-permute-done.8.rows
  29.7 1.4 %shard_map.107 = bf16[192,2048]{1,0:T(8,128)(2,1)} custom-call(bf16[128,2176]{1,0:T(8,128)(2,1)S(1)} %collective-permute-done.8.rows, bf16[24,4096]{1,0:T(8,128)(2,1)S(1)} %collective-permute-done.refs_1_.refs_0_, bf16[24,4096]{1,0:T(8,128)(2,1)S(1)} %collective-permute-done.1.refs_2_.refs_1_, bf16[24,4096]{1,0:T(8,128)(2,1)S(1)} %collective-permute-done.2.refs_3_.refs_2_, ...), custom_call_target="tpu_custom_call" | custom-call | flops 1 | bytes 1 | tf_op jit(solution)/shard_map/pallas_call | solution.py:324
  31.0 4.0 %all-to-all-start.1 = ((bf16[8,24,2048]{2,1,0:T(8,128)(2,1)}), bf16[8,24,2048]{2,1,0:T(8,128)(2,1)S(1)}, u32[]{:S(2)}, u32[]{:S(2)}) async-start(bf16[8,24,2048]{2,1,0:T(8,128)(2,1)} %bitcast.8), calls=%async_computation.1 | async-start | bytes 1572864 | tf_op jit(solution)/shard_map/all_to_all | solution.py:291
  35.0 7.0 %shard_map.103 = (bf16[192,768]{1,0:T(8,128)(2,1)}, bf16[192,768]{1,0:T(8,128)(2,1)}, bf16[192,768]{1,0:T(8,128)(2,1)}, bf16[192,384]{1,0:T(8,128)(2,1)}, bf16[1...) custom-call(bf16[24,4096]{1,0:T(8,128)(2,1)} %get-tuple-element.26.refs_0_, ...), custom_call_target="tpu_custom_call" | custom-call | flops 1 | bytes 1 | tf_op jit(solution)/shard_map/pallas_call | solution.py:309
  42.0 0.3 collective-permute-start.7
  42.3 7.4 %shard_map.104.refs_0_ = bf16[192,4096]{1,0:T(8,128)(2,1)} custom-call(bf16[192,768]{1,0:T(8,128)(2,1)} %get-tuple-element.34.hidden, bf16[192,768]{1,0:T(8,128)(2,1)} %get-tuple-element.35.dpre, bf16[192,768]{1,0:T(8,128)(2,1)} %get-tuple-element.36.dup, bf16[2048,768]{1,0:T(8,128)(2,1)} %bitcast.16, bf16[2048,768]{1,0:T(8,128)(2,1)} %bitcast.18, ...), custom_call_target="tpu_custom_call" | custom-call | flops 1 | bytes 1 | tf_op jit(solution)/shard_map/pallas_call | solution.py:328
  49.7 0.8 collective-permute-done.7.refs_1_.h_remote
  50.4 0.0 all-to-all-done.1
  50.4 4.0 %all-to-all-start = ((bf16[8,24,4096]{2,1,0:T(8,128)(2,1)}), bf16[8,24,4096]{2,1,0:T(8,128)(2,1)S(1)}, u32[]{:S(2)}, u32[]{:S(2)}) async-start(bf16[8,24,4096]{2,1,0:T(8,128)(2,1)} %bitcast.14), calls=%async_computation | async-start | bytes 3145728 | tf_op jit(solution)/shard_map/all_to_all | solution.py:291
  54.4 3.1 %shard_map.108 = (bf16[192,2048]{1,0:T(8,128)(2,1)S(1)}, bf16[192,2048]{1,0:T(8,128)(2,1)}) custom-call(bf16[192,384]{1,0:T(8,128)(2,1)} %get-tuple-element.41.h_own, bf16[192,384]{1,0:T(8,128)(2,1)S(1)} %collective-permute-done.7.refs_1_.h_remote, bf16[192,2048]{1,0:T(8,128)(2,1)} %get-tuple-element.42.own, bf16[192,2048]{1,0:T(8,128)(2,1)S(1)} %bitcast.11), custom_call_target="tpu_custom_call" | custom-call | flops 1 | bytes 1 | tf_op jit(solution)/shard_map/pallas_call | solution.py:344
  57.6 4.1 %collective-permute-start.9 = (bf16[192,2048]{1,0:T(8,128)(2,1)}, bf16[192,2048]{1,0:T(8,128)(2,1)S(1)}, u32[]{:S(2)}, u32[]{:S(2)}) collective-permute-start(bf16[192,2048]{1,0:T(8,128)(2,1)} %get-tuple-element.45), channel_id=1, source_target_pairs={{0,8},{8,0},{16,24},{24,16},{1,9},{9,1},{17,25},{25,17},{2,10},{10... | collective-permute-start | bytes 2359304 | tf_op jit(solution)/shard_map/ppermute | solution.py:275
  61.7 13.8 %all-to-all-done = bf16[8,24,4096]{2,1,0:T(8,128)(2,1)S(1)} async-done(((bf16[8,24,4096]{2,1,0:T(8,128)(2,1)}), bf16[8,24,4096]{2,1,0:T(8,128)(2,1)S(1)}, u32[]{:S(2)}, u32[]{:S(2)}) %all-to-all-start) | async-done | bytes 1572896 | tf_op jit(solution)/shard_map/all_to_all | solution.py:291
  75.5 0.0 copy-done
  75.5 2.5 %shard_map.106 = (bf16[128,2048]{1,0:T(8,128)(2,1)}, bf16[128,2048]{1,0:T(8,128)(2,1)}, f32[1,128]{1,0:T(1,128)}) custom-call(s32[1,128]{1,0:T(1,128)S(1)} %get-tuple-element.25.slot, f32[1,128]{1,0:T(1,128)S(1)} %bitcast.13, bf16[192,4096]{1,0:T(8,128)(2,1)S(1)} %bitcast.10, bf16[128,2048]{1,0:T(8,128)(2,1)} %cot.3), custom_call_target="tpu_custom_call" | custom-call | flops 1 | bytes 1 | tf_op jit(solution)/shard_map/pallas_call | solution.py:349
  77.9 2.1 %collective-permute-done.9.right = bf16[192,2048]{1,0:T(8,128)(2,1)S(1)} collective-permute-done((bf16[192,2048]{1,0:T(8,128)(2,1)}, bf16[192,2048]{1,0:T(8,128)(2,1)S(1)}, u32[]{:S(2)}, u32[]{:S(2)}) %collective-permute-start.9) | collective-permute-done | bytes 786464 | tf_op jit(solution)/shard_map/ppermute | solution.py:275
  80.1 1.1 %shard_map.109 = bf16[1,192,2048]{2,1,0:T(8,128)(2,1)} custom-call(bf16[192,2048]{1,0:T(8,128)(2,1)S(1)} %get-tuple-element.44.left, bf16[192,2048]{1,0:T(8,128)(2,1)S(1)} %collective-permute-done.9.right), custom_call_target="tpu_custom_call" | custom-call | flops 1 | bytes 1 | tf_op jit(solution)/shard_map/pallas_call | solution.py:353
  (2 shorter events, 0.0 us)
Async XLA Ops:
  3.7 26.0 %collective-permute-start.8 = (bf16[128,2176]{1,0:T(8,128)(2,1)}, bf16[128,2176]{1,0:T(8,128)(2,1)S(1)}, u32[]{:S(2)}, u32[]{:S(2)}) collective-permute-start(bf16[128,2176]{1,0:T(8,128)(2,1)} %get-tuple-element.43), channel_id=1, source_target_pairs={{0,24},{8,16},{16,8},{24,0},{1,25},{9,17},{17,9},{25,1},{2,26},{10... | collective-permute-start | bytes 1671176 | tf_op jit(solution)/shard_map/ppermute | solution.py:275
  8.7 3.4 %collective-permute-start = (bf16[24,4096]{1,0:T(8,128)(2,1)}, bf16[24,4096]{1,0:T(8,128)(2,1)S(1)}, u32[]{:S(2)}, u32[]{:S(2)}) collective-permute-start(bf16[24,4096]{1,0:T(8,128)(2,1)} %get-tuple-element.27), channel_id=1, source_target_pairs={{0,1},{1,0},{2,3},{3,2},{4,5},{5,4},{6,7},{7,6},{8,9},{9,8},{10,11... | collective-permute-start | bytes 589832 | tf_op jit(solution)/shard_map/ppermute | solution.py:303
  8.7 7.9 %collective-permute-start.1 = (bf16[24,4096]{1,0:T(8,128)(2,1)}, bf16[24,4096]{1,0:T(8,128)(2,1)S(1)}, u32[]{:S(2)}, u32[]{:S(2)}) collective-permute-start(bf16[24,4096]{1,0:T(8,128)(2,1)} %get-tuple-element.28), channel_id=1, source_target_pairs={{0,2},{1,3},{2,0},{3,1},{4,6},{5,7},{6,4},{7,5},{8,10},{9,11},{10,... | collective-permute-start | bytes 589832 | tf_op jit(solution)/shard_map/ppermute | solution.py:303
  10.2 9.9 %collective-permute-start.2 = (bf16[24,4096]{1,0:T(8,128)(2,1)}, bf16[24,4096]{1,0:T(8,128)(2,1)S(1)}, u32[]{:S(2)}, u32[]{:S(2)}) collective-permute-start(bf16[24,4096]{1,0:T(8,128)(2,1)} %get-tuple-element.29), channel_id=1, source_target_pairs={{0,3},{1,2},{2,1},{3,0},{4,7},{5,6},{6,5},{7,4},{8,11},{9,10},{10,... | collective-permute-start | bytes 589832 | tf_op jit(solution)/shard_map/ppermute | solution.py:303
  10.6 12.4 %collective-permute-start.3 = (bf16[24,4096]{1,0:T(8,128)(2,1)}, bf16[24,4096]{1,0:T(8,128)(2,1)S(1)}, u32[]{:S(2)}, u32[]{:S(2)}) collective-permute-start(bf16[24,4096]{1,0:T(8,128)(2,1)} %get-tuple-element.30), channel_id=1, source_target_pairs={{0,4},{1,5},{2,6},{3,7},{4,0},{5,1},{6,2},{7,3},{8,12},{9,13},{10,... | collective-permute-start | bytes 589832 | tf_op jit(solution)/shard_map/ppermute | solution.py:303
  12.1 17.6 %collective-permute-start.4 = (bf16[24,4096]{1,0:T(8,128)(2,1)}, bf16[24,4096]{1,0:T(8,128)(2,1)S(1)}, u32[]{:S(2)}, u32[]{:S(2)}) collective-permute-start(bf16[24,4096]{1,0:T(8,128)(2,1)} %get-tuple-element.31), channel_id=1, source_target_pairs={{0,5},{1,4},{2,7},{3,6},{4,1},{5,0},{6,3},{7,2},{8,13},{9,12},{10,... | collective-permute-start | bytes 589832 | tf_op jit(solution)/shard_map/ppermute | solution.py:303
  16.6 13.0 %collective-permute-start.5 = (bf16[24,4096]{1,0:T(8,128)(2,1)}, bf16[24,4096]{1,0:T(8,128)(2,1)S(1)}, u32[]{:S(2)}, u32[]{:S(2)}) collective-permute-start(bf16[24,4096]{1,0:T(8,128)(2,1)} %get-tuple-element.32), channel_id=1, source_target_pairs={{0,6},{1,7},{2,4},{3,5},{4,2},{5,3},{6,0},{7,1},{8,14},{9,15},{10,... | collective-permute-start | bytes 589832 | tf_op jit(solution)/shard_map/ppermute | solution.py:303
  20.1 9.6 %collective-permute-start.6 = (bf16[24,4096]{1,0:T(8,128)(2,1)}, bf16[24,4096]{1,0:T(8,128)(2,1)S(1)}, u32[]{:S(2)}, u32[]{:S(2)}) collective-permute-start(bf16[24,4096]{1,0:T(8,128)(2,1)} %get-tuple-element.33), channel_id=1, source_target_pairs={{0,7},{1,6},{2,5},{3,4},{4,3},{5,2},{6,1},{7,0},{8,15},{9,14},{10,... | collective-permute-start | bytes 589832 | tf_op jit(solution)/shard_map/ppermute | solution.py:303
  31.0 19.4 %all-to-all-start.1 = ((bf16[8,24,2048]{2,1,0:T(8,128)(2,1)}), bf16[8,24,2048]{2,1,0:T(8,128)(2,1)S(1)}, u32[]{:S(2)}, u32[]{:S(2)}) async-start(bf16[8,24,2048]{2,1,0:T(8,128)(2,1)} %bitcast.8), calls=%async_computation.1 | async-start | bytes 1572864 | tf_op jit(solution)/shard_map/all_to_all | solution.py:291
  42.0 8.4 %collective-permute-start.7 = (bf16[192,384]{1,0:T(8,128)(2,1)}, bf16[192,384]{1,0:T(8,128)(2,1)S(1)}, u32[]{:S(2)}, u32[]{:S(2)}) collective-permute-start(bf16[192,384]{1,0:T(8,128)(2,1)} %get-tuple-element.37), channel_id=1, source_target_pairs={{0,24},{8,16},{16,8},{24,0},{1,25},{9,17},{17,9},{25,1},{2,26},{10... | collective-permute-start | bytes 442376 | tf_op jit(solution)/shard_map/ppermute | solution.py:275
  50.4 25.0 %copy-start = (f32[128,1]{0,1:T(1,128)S(1)}, f32[128,1]{0,1:T(1,128)}, u32[]{:S(2)}) copy-start(f32[128,1]{0,1:T(1,128)} %param.10) | copy-start | bytes 1540
  50.4 25.0 %all-to-all-start = ((bf16[8,24,4096]{2,1,0:T(8,128)(2,1)}), bf16[8,24,4096]{2,1,0:T(8,128)(2,1)S(1)}, u32[]{:S(2)}, u32[]{:S(2)}) async-start(bf16[8,24,4096]{2,1,0:T(8,128)(2,1)} %bitcast.14), calls=%async_computation | async-start | bytes 3145728 | tf_op jit(solution)/shard_map/all_to_all | solution.py:291
  57.6 22.5 %collective-permute-start.9 = (bf16[192,2048]{1,0:T(8,128)(2,1)}, bf16[192,2048]{1,0:T(8,128)(2,1)S(1)}, u32[]{:S(2)}, u32[]{:S(2)}) collective-permute-start(bf16[192,2048]{1,0:T(8,128)(2,1)} %get-tuple-element.45), channel_id=1, source_target_pairs={{0,8},{8,0},{16,24},{24,16},{1,9},{9,1},{17,25},{25,17},{2,10},{10... | collective-permute-start | bytes 2359304 | tf_op jit(solution)/shard_map/ppermute | solution.py:275

commit v5 on v4

--- a/solution.py
+++ b/solution.py
@@ -63,6 +63,9 @@
     return layer_output, home[:, width:].astype(BF16), gate_grad, summed[None]
 
 
+LANES = 128
+TILES = 3
+TAIL = 16
 WIDE = 512
 VMEM_LIMIT = 24 * 1024 * 1024
 TINY = pl.CostEstimate(flops=1, bytes_accessed=1, transcendentals=0)
@@ -117,10 +120,10 @@
     slot = ids * capacity + rank
     slot_out[...] = slot
     scaled[...] = (column(gates[...]) * cot[...].astype(F32)).astype(BF16)
-    across[:, :width] = scaled[...]
-    across[:, width:] = jnp.broadcast_to(
-        column(slot.astype(F32)), (count, across.shape[1] - width)
-    ).astype(BF16)
+    chunks = width // LANES
+    for c in range(chunks):
+        across[c * count : (c + 1) * count] = scaled[:, c * LANES : (c + 1) * LANES]
+    across[chunks * count :] = jnp.broadcast_to(slot.astype(F32), (TAIL, count)).astype(BF16)
     slot = (ids ^ lax.axis_index("tp")) * capacity + rank
     placing = (
         lax.broadcasted_iota(jnp.int32, (peers * capacity, count), 0) == slot
@@ -137,59 +140,69 @@
 
 def remote_kernel(rows, *refs):
     out = refs[-1]
-    count, width = rows.shape[0], out.shape[1]
-    slot = rows[:, width : width + 1].astype(F32).astype(jnp.int32)
-    home = (lax.broadcasted_iota(jnp.int32, (count, out.shape[0]), 1) == slot).astype(F32)
-    place(home.T.astype(BF16), rows, out, 0, width)
-
-
-def tile_copies(tiles, sems):
-    copies = [
-        [pltpu.make_async_copy(source, target, sems.at[t, i]) for i, (source, target) in enumerate(pairs)]
-        for t, pairs in enumerate(tiles)
-    ]
-    for tile in copies:
-        for copy in tile:
+    count, chunks = LANES, out.shape[1] // LANES
+    slot = rows[chunks * count : chunks * count + 8].astype(F32)[:1].astype(jnp.int32)
+    placing = (
+        lax.broadcasted_iota(jnp.int32, (out.shape[0], count), 0) == slot
+    ).astype(BF16)
+    group = WIDE // LANES
+    for c in range(0, chunks, group):
+        some = [rows[i * count : (i + 1) * count] for i in range(c, c + group)]
+        out[:, c * LANES : (c + group) * LANES] = jnp.dot(
+            placing, jnp.concatenate(some, axis=1), preferred_element_type=F32
+        ).astype(BF16)
+
+
+def staged(stages, sems, ahead=3):
+    copies, used = [], 0
+    for pairs in stages:
+        copies.append(
+            [pltpu.make_async_copy(source, target, sems.at[used + i]) for i, (source, target) in enumerate(pairs)]
+        )
+        used += len(pairs)
+    for stage in copies[:ahead]:
+        for copy in stage:
             copy.start()
-    return copies
-
-
-def hidden_kernel(peers, *refs):
-    blocks, (gate, up, down, hidden, dpre, dup, near, far, cot) = refs[:peers], refs[peers : peers + 9]
-    gate_in, up_in, down_in, wide, rows, sems = refs[peers + 9 :]
+    left = list(range(len(copies)))
+
+    def arrive():
+        now = left.pop(0)
+        for copy in copies[now]:
+            copy.wait()
+        if now + ahead < len(copies):
+            for copy in copies[now + ahead]:
+                copy.start()
+
+    return arrive
+
+
+def hidden_kernel(order, *refs):
+    peers = len(order)
+    blocks, (gate, up, hidden, by_up, by_pre, near, far, cot, same) = refs[:peers], refs[peers : peers + 9]
+    gate_in, up_in, wide, rows, sems = refs[peers + 9 :]
     width, inner = gate.shape
     capacity = blocks[0].shape[0]
-    step = inner // sems.shape[0]
+    step = inner // TILES
     tiles = [slice(at, at + step) for at in range(0, inner, step)]
-    copies = tile_copies(
-        [
-            (
-                (gate.at[:, t], gate_in.at[:, t]),
-                (up.at[:, t], up_in.at[:, t]),
-                (down.at[t, :], down_in.at[t, :]),
-            )
-            for t in tiles
-        ],
-        sems,
+    arrive = staged(
+        [((gate.at[:, t], gate_in.at[:, t]), (up.at[:, t], up_in.at[:, t])) for t in tiles], sems
     )
     own = lax.axis_index("tp")
-    for k, block in enumerate(blocks):
+    for k, block in zip(order, blocks):
         start = pl.multiple_of((own ^ k) * capacity, 8)
         wide[pl.ds(start, capacity), :] = block[...].astype(F32)
-    rows[...] = wide[...].astype(BF16)
-    cot[...] = rows[:, width:]
-    for t, tile in zip(tiles, copies):
-        for copy in tile:
-            copy.wait()
-        pre_act = jnp.dot(rows[:, :width], gate_in[:, t], preferred_element_type=F32)
-        up_act = jnp.dot(rows[:, :width], up_in[:, t], preferred_element_type=F32)
-        dhid = lax.dot_general(
-            rows[:, width:], down_in[t, :], CONTRACT_LAST, preferred_element_type=F32
-        )
-        sigma = 1.0 / (1.0 + jnp.exp(-pre_act))
-        hidden[:, t] = (pre_act * sigma * up_act).astype(BF16)
-        dup[:, t] = (dhid * pre_act * sigma).astype(BF16)
-        dpre[:, t] = (dhid * up_act * sigma * (1.0 + pre_act * (1.0 - sigma))).astype(BF16)
+    rows[...] = wide[:, :width].astype(BF16)
+    cot[...] = wide[:, width:].astype(BF16)
+    same[...] = cot[...]
+    for t in tiles:
+        arrive()
+        pre = jnp.dot(rows[...], gate_in[:, t], preferred_element_type=F32)
+        up_act = jnp.dot(rows[...], up_in[:, t], preferred_element_type=F32)
+        sigma = 1.0 / (1.0 + jnp.exp(-pre))
+        silu = pre * sigma
+        hidden[:, t] = (silu * up_act).astype(BF16)
+        by_up[:, t] = silu.astype(BF16)
+        by_pre[:, t] = (up_act * sigma * (1.0 + pre * (1.0 - sigma))).astype(BF16)
     half = near.shape[1]
     on_left = lax.axis_index("ctx") < 2
     left, right = hidden[:, :half], hidden[:, half:]
@@ -197,54 +210,74 @@
     far[...] = jnp.where(on_left, right, left)
 
 
-def back_kernel(hidden, dpre, dup, gate, up, down, out, gate_in, up_in, down_in, sems):
-    width = down.shape[1]
+def back_kernel(
+    hidden, by_up, by_pre, cot, gate, up, down, out,
+    gate_in, up_in, down_in, dpre, dup, stage, sems, out_sems,
+):
+    inner, width = down.shape
+    step = inner // TILES
+    inner_tiles = [slice(at, at + step) for at in range(0, inner, step)]
     tiles = [slice(at, at + WIDE) for at in range(0, width, WIDE)]
-    copies = tile_copies(
-        [
-            (
-                (down.at[:, t], down_in.at[:, t]),
-                (gate.at[t, :], gate_in.at[t, :]),
-                (up.at[t, :], up_in.at[t, :]),
-            )
-            for t in tiles
-        ],
-        sems,
-    )
-    for t, tile in zip(tiles, copies):
-        for copy in tile:
-            copy.wait()
+    stages = [[(down.at[t, :], down_in.at[t, :])] for t in inner_tiles]
+    stages += [[(gate.at[t, :], gate_in.at[t, :]), (up.at[t, :], up_in.at[t, :])] for t in tiles]
+    arrive = staged(stages, sems)
+    for t in inner_tiles:
+        arrive()
+        dhid = lax.dot_general(cot[...], down_in[t, :], CONTRACT_LAST, preferred_element_type=F32)
+        dup[:, t] = (dhid * by_up[:, t].astype(F32)).astype(BF16)
+        dpre[:, t] = (dhid * by_pre[:, t].astype(F32)).astype(BF16)
+    leaving = []
+    for i, t in enumerate(tiles):
         at = 2 * t.start
-        out[:, at : at + WIDE] = jnp.dot(
+        both = slice(at, at + 2 * WIDE)
+        stage[:, at : at + WIDE] = jnp.dot(
             hidden[...], down_in[:, t], preferred_element_type=F32
         ).astype(BF16)
-        out[:, at + WIDE : at + 2 * WIDE] = (
+        arrive()
+        stage[:, at + WIDE : at + 2 * WIDE] = (
             lax.dot_general(dpre[...], gate_in[t, :], CONTRACT_LAST, preferred_element_type=F32)
             + lax.dot_general(dup[...], up_in[t, :], CONTRACT_LAST, preferred_element_type=F32)
         ).astype(BF16)
+        leave = pltpu.make_async_copy(stage.at[:, both], out.at[:, both], out_sems.at[i])
+        leave.start()
+        leaving.append(leave)
+    for leave in leaving:
+        leave.wait()
 
 
 def pass_kernel(*refs):
     pass
 
 
-def quarters_kernel(h_own, h_remote, own, remote, mine, other):
+def quarters_kernel(h_own, h_remote, own, remote, mine, other, stage, sems):
     width = remote.shape[1]
     even = lax.rem(lax.axis_index("ctx"), 2) == 0
-
-    def times(left, right):
-        return lax.dot_general(left[...], right, CONTRACT_FIRST, preferred_element_type=F32)
-
-    step = 512
-    for at in range(0, width, step):
-        cols = slice(at, at + step)
-        total = times(h_own, own[:, cols]) + times(
-            h_remote, remote[:, cols]
-        )
-        rows = total.shape[0] // 2
-        low, high = total[:rows].astype(BF16), total[rows:].astype(BF16)
-        mine[:, cols] = jnp.where(even, low, high)
-        other[:, cols] = jnp.where(even, high, low)
+    left, right = h_own[...].astype(F32).T, h_remote[...].astype(F32).T
+    size = left.shape[0] // 2
+
+    def halves(turned):
+        low, high = turned[:size].astype(BF16), turned[size:].astype(BF16)
+        return jnp.where(even, low, high), jnp.where(even, high, low)
+
+    (own_mine, own_other), (remote_mine, remote_other) = halves(left), halves(right)
+    leaving = []
+    for i, at in enumerate(range(0, width, WIDE)):
+        cols = slice(at, at + WIDE)
+        stage[:, cols] = (
+            jnp.dot(own_other, own[:, cols], preferred_element_type=F32)
+            + jnp.dot(remote_other, remote[:, cols], preferred_element_type=F32)
+        ).astype(BF16)
+        leave = pltpu.make_async_copy(stage.at[:, cols], other.at[:, cols], sems.at[i])
+        leave.start()
+        leaving.append(leave)
+    for at in range(0, width, WIDE):
+        cols = slice(at, at + WIDE)
+        mine[:, cols] = (
+            jnp.dot(own_mine, own[:, cols], preferred_element_type=F32)
+            + jnp.dot(remote_mine, remote[:, cols], preferred_element_type=F32)
+        ).astype(BF16)
+    for leave in leaving:
+        leave.wait()
 
 
 def home_kernel(slot, gates, back, cot, layer_output, token_grad, gate_grad):
@@ -283,7 +316,7 @@
     inner = w_gate.shape[2]
     quarter = inner // 4
     gates = gate_weights.reshape(1, count)
-    whole = pl.BlockSpec()
+    whole, in_place = pl.BlockSpec(), pl.BlockSpec(memory_space=pltpu.HBM)
     after = pl.BlockSpec(memory_space=pl.ANY)
 
     def over_tp(rows):
@@ -294,43 +327,54 @@
 
     slot, across, *blocks = call(
         functools.partial(send_kernel, peers, capacity),
-        [shaped((1, count), jnp.int32), pltpu.HBM((count, width + 128), BF16)]
+        [
+            shaped((1, count), jnp.int32),
+            pltpu.HBM((width // LANES * count + TAIL, LANES), BF16),
+        ]
         + [pltpu.HBM((capacity, 2 * width), BF16)] * peers,
         scratch_shapes=[pltpu.VMEM((count, width), BF16)],
     )(in_hbm(routes.reshape(1, count)), in_hbm(gates), in_hbm(tokens), in_hbm(cotangent))
     rows_across = along(across, 3)
-    got = [in_hbm(blocks[0])] + [
-        lax.ppermute(blocks[k], "tp", [(i, i ^ k) for i in range(peers)]) for k in range(1, peers)
-    ]
-
-    weights = [in_hbm(w[0]) for w in (w_gate, w_up, w_down)]
-    held = [pltpu.VMEM(w.shape, BF16) for w in weights]
-    in_place = pl.BlockSpec(memory_space=pltpu.HBM)
-    hidden, dpre, dup, near, far, cot = call(
-        functools.partial(hidden_kernel, peers),
-        [pltpu.HBM((slots, inner), BF16)] * 3
+    got = {0: in_hbm(blocks[0])}
+    for k in range(1, peers):
+        got[k] = lax.ppermute(blocks[k], "tp", [(i, i ^ k) for i in range(peers)])
+    order = (6, 7, 4, 5, 2, 3, 1, 0)
+    got = [got[k] for k in order]
+
+    gate_mat, up_mat, down_mat = [in_hbm(w[0]) for w in (w_gate, w_up, w_down)]
+    held = [pltpu.VMEM((width, inner), BF16)] * 2
+    dma = pltpu.SemaphoreType.DMA
+    hidden, by_up, by_pre, near, far, cot, same = call(
+        functools.partial(hidden_kernel, order),
+        [shaped((slots, inner))] * 3
         + [pltpu.HBM((slots, inner // 2), BF16)] * 2
-        + [pltpu.HBM((slots, width), BF16)],
-        in_specs=[whole] * peers + [in_place] * 3,
+        + [shaped((slots, width)), pltpu.HBM((slots, width), BF16)],
+        in_specs=[whole] * peers + [in_place] * 2,
         scratch_shapes=held
         + [
             pltpu.VMEM((slots, 2 * width), F32),
-            pltpu.VMEM((slots, 2 * width), BF16),
-            pltpu.SemaphoreType.DMA((3, 3)),
+            pltpu.VMEM((slots, width), BF16),
+            dma((2 * TILES,)),
         ],
-    )(*got, *weights)
+    )(*got, gate_mat, up_mat)
+    near, same = in_hbm(near), in_hbm(same)
     far_across = along(far, 3)
     remote = over_tp(
         call(
             remote_kernel, shaped((slots, width)), in_specs=[whole] + [after] * (peers - 1)
-        )(rows_across, *got[1:])
-    )
+        )(rows_across, *[g for k, g in zip(order, got) if k])
+    )
+    tiles = width // WIDE
     back = call(
         back_kernel,
         pltpu.HBM((slots, 2 * width), BF16),
-        in_specs=[whole] * 3 + [in_place] * 3,
-        scratch_shapes=held + [pltpu.SemaphoreType.DMA((width // WIDE, 3))],
-    )(in_hbm(hidden), in_hbm(dpre), in_hbm(dup), *weights)
+        in_specs=[whole] * 4 + [in_place] * 3,
+        out_specs=in_place,
+        scratch_shapes=held
+        + [pltpu.VMEM((inner, width), BF16)]
+        + [pltpu.VMEM((slots, inner), BF16)] * 2
+        + [pltpu.VMEM((slots, 2 * width), BF16), dma((TILES + 2 * tiles,)), dma((tiles,))],
+    )(hidden, by_up, by_pre, cot, gate_mat, up_mat, down_mat)
     back = over_tp(
         call(
             pass_kernel,
@@ -342,8 +386,14 @@
     )
 
     mine, other = call(
-        quarters_kernel, [shaped((quarter, width)), pltpu.HBM((quarter, width), BF16)]
-    )(in_hbm(near), far_across, in_hbm(cot), remote)
+        quarters_kernel,
+        [shaped((quarter, width)), pltpu.HBM((quarter, width), BF16)],
+        out_specs=[whole, in_place],
+        scratch_shapes=[
+            pltpu.VMEM((quarter, width), BF16),
+            pltpu.SemaphoreType.DMA((width // WIDE,)),
+        ],
+    )(near, far_across, same, remote)
     swapped = along(other, 1)
 
     layer_output, token_grad, gate_grad = call(

time: 81.5 us -> 79.2 us (0.972)
  Pallas kernels: 25.4 us -> 24.2 us
  waiting for transfers between devices: 28.8 us -> 27.7 us
    pallas_call x1, Pallas kernels: 6.97 us -> 5.52 us  [body_line(): call(functools.partial(hidden_kernel, order), [shaped((slots, inner))] *...]
    ppermute x3, waiting for transfers between devices: 2.92 us -> 1.99 us  [along(): return lax.ppermute(rows, 'ctx', [(i, i ^ step) for i in range(4)])]
    pallas_call x1, Pallas kernels: 7.36 us -> 8.19 us  [body_line(): call(back_kernel, pltpu.HBM((slots, 2 * width), BF16), in_specs=[whole] *...]
  transfers between devices with their start and end apart: 12 -> 12, of which waited for: 6 -> 6; matrix products, arithmetic and copies ran while one was open for 0% -> 0% of each run, Pallas kernels for 25% -> 24%
where the time goes in v5:
time: 79.2 us; the launch traced here: 78.8 us
  waiting for transfers between devices  27.7 us (35%)
  starting transfers between devices  26.1 us (33%)
  Pallas kernels  24.2 us (31%)
    all_to_all x2, waiting for transfers between devices, over_tp(): lax.all_to_all(rows.reshape(peers, capacity, wide), 'tp', split_axis=0, c...  14 us
    ppermute x7, waiting for transfers between devices, body_line(): got[k] = lax.ppermute(blocks[k], 'tp', [(i, i ^ k) for i in range(peers)])  11.8 us
    ppermute x3, starting transfers between devices, along(): return lax.ppermute(rows, 'ctx', [(i, i ^ step) for i in range(4)])  9.86 us
    ppermute x7, starting transfers between devices, body_line(): got[k] = lax.ppermute(blocks[k], 'tp', [(i, i ^ k) for i in range(peers)])  8.29 us
    pallas_call x1, Pallas kernels, body_line(): call(back_kernel, pltpu.HBM((slots, 2 * width), BF16), in_specs=[whole] *...  8.19 us
    all_to_all x2, starting transfers between devices, over_tp(): lax.all_to_all(rows.reshape(peers, capacity, wide), 'tp', split_axis=0, c...  7.96 us
    pallas_call x1, Pallas kernels, body_line(): call(functools.partial(hidden_kernel, order), [shaped((slots, inner))] *...  5.52 us
    pallas_call x1, Pallas kernels, body_line(): call(functools.partial(send_kernel, peers, capacity), [shaped((1, count),...  3.13 us
  transfers between devices with their start and end apart: 12, of which 6 were waited for; matrix products, arithmetic and copies ran while one was open for 0% of the time, Pallas kernels for 24%

profile of v5, /device:TPU:0, one launch (start us, length us, event | category | flops | bytes accessed | tf_op | source)
XLA Modules:
  0.0 78.8 jit_solution(17174199582473456777)
XLA Ops:
  0.6 3.1 %shard_map.102 = (s32[1,128]{1,0:T(1,128)S(1)}, bf16[2064,128]{1,0:T(8,128)(2,1)}, bf16[24,4096]{1,0:T(8,128)(2,1)}, bf16[24,4096]{1,0:T(8,128)(2,1)}, bf16[24,4...) custom-call(s32[1,128]{1,0:T(1,128)} %bitcast.20, ...), custom_call_target="tpu_custom_call" | custom-call | flops 1 | bytes 1 | tf_op jit(solution)/shard_map/pallas_call | solution.py:328
  3.8 5.0 %collective-permute-start.8 = (bf16[2064,128]{1,0:T(8,128)(2,1)}, bf16[2064,128]{1,0:T(8,128)(2,1)S(1)}, u32[]{:S(2)}, u32[]{:S(2)}) collective-permute-start(bf16[2064,128]{1,0:T(8,128)(2,1)} %get-tuple-element.45), channel_id=1, source_target_pairs={{0,24},{8,16},{16,8},{24,0},{1,25},{9,17},{17,9},{25,1},{2,26},{10... | collective-permute-start | bytes 1585160 | tf_op jit(solution)/shard_map/ppermute | solution.py:308
  8.8 2.4 %collective-permute-start = (bf16[24,4096]{1,0:T(8,128)(2,1)}, bf16[24,4096]{1,0:T(8,128)(2,1)S(1)}, u32[]{:S(2)}, u32[]{:S(2)}) collective-permute-start(bf16[24,4096]{1,0:T(8,128)(2,1)} %get-tuple-element.27), channel_id=1, source_target_pairs={{0,6},{1,7},{2,4},{3,5},{4,2},{5,3},{6,0},{7,1},{8,14},{9,15},{10,... | collective-permute-start | bytes 589832 | tf_op jit(solution)/shard_map/ppermute | solution.py:340
  11.3 0.0 collective-permute-start.1
  11.3 0.9 %collective-permute-start.2 = (bf16[24,4096]{1,0:T(8,128)(2,1)}, bf16[24,4096]{1,0:T(8,128)(2,1)S(1)}, u32[]{:S(2)}, u32[]{:S(2)}) collective-permute-start(bf16[24,4096]{1,0:T(8,128)(2,1)} %get-tuple-element.29), channel_id=1, source_target_pairs={{0,4},{1,5},{2,6},{3,7},{4,0},{5,1},{6,2},{7,3},{8,12},{9,13},{10,... | collective-permute-start | bytes 589832 | tf_op jit(solution)/shard_map/ppermute | solution.py:340
  12.1 1.1 %collective-permute-start.3 = (bf16[24,4096]{1,0:T(8,128)(2,1)}, bf16[24,4096]{1,0:T(8,128)(2,1)S(1)}, u32[]{:S(2)}, u32[]{:S(2)}) collective-permute-start(bf16[24,4096]{1,0:T(8,128)(2,1)} %get-tuple-element.30), channel_id=1, source_target_pairs={{0,5},{1,4},{2,7},{3,6},{4,1},{5,0},{6,3},{7,2},{8,13},{9,12},{10,... | collective-permute-start | bytes 589832 | tf_op jit(solution)/shard_map/ppermute | solution.py:340
  13.2 4.0 %collective-permute-done.refs_0_ = bf16[24,4096]{1,0:T(8,128)(2,1)S(1)} collective-permute-done((bf16[24,4096]{1,0:T(8,128)(2,1)}, bf16[24,4096]{1,0:T(8,128)(2,1)S(1)}, u32[]{:S(2)}, u32[]{:S(2)}) %collective-permute-start) | collective-permute-done | bytes 196640 | tf_op jit(solution)/shard_map/ppermute | solution.py:340
  17.2 2.1 %collective-permute-start.4 = (bf16[24,4096]{1,0:T(8,128)(2,1)}, bf16[24,4096]{1,0:T(8,128)(2,1)S(1)}, u32[]{:S(2)}, u32[]{:S(2)}) collective-permute-start(bf16[24,4096]{1,0:T(8,128)(2,1)} %get-tuple-element.31), channel_id=1, source_target_pairs={{0,2},{1,3},{2,0},{3,1},{4,6},{5,7},{6,4},{7,5},{8,10},{9,11},{10,... | collective-permute-start | bytes 589832 | tf_op jit(solution)/shard_map/ppermute | solution.py:340
  19.3 1.8 %collective-permute-done.1.refs_1_ = bf16[24,4096]{1,0:T(8,128)(2,1)S(1)} collective-permute-done((bf16[24,4096]{1,0:T(8,128)(2,1)}, bf16[24,4096]{1,0:T(8,128)(2,1)S(1)}, u32[]{:S(2)}, u32[]{:S(2)}) %collective-permute-start.1) | collective-permute-done | bytes 196640 | tf_op jit(solution)/shard_map/ppermute | solution.py:340
  21.2 1.7 %collective-permute-start.5 = (bf16[24,4096]{1,0:T(8,128)(2,1)}, bf16[24,4096]{1,0:T(8,128)(2,1)S(1)}, u32[]{:S(2)}, u32[]{:S(2)}) collective-permute-start(bf16[24,4096]{1,0:T(8,128)(2,1)} %get-tuple-element.32), channel_id=1, source_target_pairs={{0,3},{1,2},{2,1},{3,0},{4,7},{5,6},{6,5},{7,4},{8,11},{9,10},{10,... | collective-permute-start | bytes 589832 | tf_op jit(solution)/shard_map/ppermute | solution.py:340
  22.9 1.8 %collective-permute-done.2.refs_2_ = bf16[24,4096]{1,0:T(8,128)(2,1)S(1)} collective-permute-done((bf16[24,4096]{1,0:T(8,128)(2,1)}, bf16[24,4096]{1,0:T(8,128)(2,1)S(1)}, u32[]{:S(2)}, u32[]{:S(2)}) %collective-permute-start.2) | collective-permute-done | bytes 196640 | tf_op jit(solution)/shard_map/ppermute | solution.py:340
  24.7 0.1 collective-permute-start.6
  24.8 4.1 %collective-permute-done.3.refs_3_ = bf16[24,4096]{1,0:T(8,128)(2,1)S(1)} collective-permute-done((bf16[24,4096]{1,0:T(8,128)(2,1)}, bf16[24,4096]{1,0:T(8,128)(2,1)S(1)}, u32[]{:S(2)}, u32[]{:S(2)}) %collective-permute-start.3) | collective-permute-done | bytes 196640 | tf_op jit(solution)/shard_map/ppermute | solution.py:340
  28.9 0.0 collective-permute-done.4.refs_4_
  28.9 0.0 collective-permute-done.5.refs_5_
  28.9 0.0 collective-permute-done.6.refs_6_
  28.9 0.0 collective-permute-done.8.rows
  28.9 1.2 %shard_map.107 = bf16[192,2048]{1,0:T(8,128)(2,1)} custom-call(bf16[2064,128]{1,0:T(8,128)(2,1)S(1)} %collective-permute-done.8.rows, bf16[24,4096]{1,0:T(8,128)(2,1)S(1)} %collective-permute-done.refs_0_, bf16[24,4096]{1,0:T(8,128)(2,1)S(1)} %collective-permute-done.1.refs_1_, bf16[24,4096]{1,0:T(8,128)(2,1)S(1)} %collective-permute-done.2.refs_2_, ...), custom_call_target="tpu_custom_call" | custom-call | flops 1 | bytes 1 | tf_op jit(solution)/shard_map/pallas_call | solution.py:363
  30.1 3.8 %all-to-all-start.1 = ((bf16[8,24,2048]{2,1,0:T(8,128)(2,1)}), bf16[8,24,2048]{2,1,0:T(8,128)(2,1)S(1)}, u32[]{:S(2)}, u32[]{:S(2)}) async-start(bf16[8,24,2048]{2,1,0:T(8,128)(2,1)} %bitcast.8), calls=%async_computation.1 | async-start | bytes 1572864 | tf_op jit(solution)/shard_map/all_to_all | solution.py:324
  33.9 5.5 %shard_map.103 = (bf16[192,768]{1,0:T(8,128)(2,1)S(1)}, bf16[192,768]{1,0:T(8,128)(2,1)S(1)}, bf16[192,768]{1,0:T(8,128)(2,1)S(1)}, bf16[192,384]{1,0:T(8,128)(2...) custom-call(bf16[24,4096]{1,0:T(8,128)(2,1)S(1)} %collective-permute-done.refs_0_, ...), custom_call_target="tpu_custom_call" | custom-call | flops 1 | bytes 1 | tf_op jit(solution)/shard_map/pallas_call | solution.py:347
  39.4 0.4 collective-permute-start.7
  39.8 8.2 %shard_map.104.refs_0_ = bf16[192,4096]{1,0:T(8,128)(2,1)} custom-call(bf16[192,768]{1,0:T(8,128)(2,1)S(1)} %get-tuple-element.35.hidden, bf16[192,768]{1,0:T(8,128)(2,1)S(1)} %get-tuple-element.36.by_up, bf16[192,768]{1,0:T(8,128)(2,1)S(1)} %get-tuple-element.37.by_pre, bf16[192,2048]{1,0:T(8,128)(2,1)S(1)} %get-tuple-element.38.cot, ...), custom_call_target="tpu_custom_call" | custom-call | flops 1 | bytes 1 | tf_op jit(solution)/shard_map/pallas_call | solution.py:368
  48.0 0.0 collective-permute-done.7.refs_1_.h_remote
  48.0 0.0 copy-start
  48.0 0.0 all-to-all-done.1
  48.0 4.2 %all-to-all-start = ((bf16[8,24,4096]{2,1,0:T(8,128)(2,1)}), bf16[8,24,4096]{2,1,0:T(8,128)(2,1)S(1)}, u32[]{:S(2)}, u32[]{:S(2)}) async-start(bf16[8,24,4096]{2,1,0:T(8,128)(2,1)} %bitcast.14), calls=%async_computation | async-start | bytes 3145728 | tf_op jit(solution)/shard_map/all_to_all | solution.py:324
  52.2 2.6 %shard_map.108 = (bf16[192,2048]{1,0:T(8,128)(2,1)S(1)}, bf16[192,2048]{1,0:T(8,128)(2,1)}) custom-call(bf16[192,384]{1,0:T(8,128)(2,1)} %get-tuple-element.43.h_own, bf16[192,384]{1,0:T(8,128)(2,1)S(1)} %collective-permute-done.7.refs_1_.h_remote, bf16[192,2048]{1,0:T(8,128)(2,1)} %get-tuple-element.44.own, bf16[192,2048]{1,0:T(8,128)(2,1)S(1)} %bitcast.11), custom_call_target="tpu_custom_call" | custom-call | flops 1 | bytes 1 | tf_op jit(solution)/shard_map/pallas_call | solution.py:388
  54.8 4.5 %collective-permute-start.9 = (bf16[192,2048]{1,0:T(8,128)(2,1)}, bf16[192,2048]{1,0:T(8,128)(2,1)S(1)}, u32[]{:S(2)}, u32[]{:S(2)}) collective-permute-start(bf16[192,2048]{1,0:T(8,128)(2,1)} %get-tuple-element.47), channel_id=1, source_target_pairs={{0,8},{8,0},{16,24},{24,16},{1,9},{9,1},{17,25},{25,17},{2,10},{10... | collective-permute-start | bytes 2359304 | tf_op jit(solution)/shard_map/ppermute | solution.py:308
  59.3 14.0 %all-to-all-done = bf16[8,24,4096]{2,1,0:T(8,128)(2,1)S(1)} async-done(((bf16[8,24,4096]{2,1,0:T(8,128)(2,1)}), bf16[8,24,4096]{2,1,0:T(8,128)(2,1)S(1)}, u32[]{:S(2)}, u32[]{:S(2)}) %all-to-all-start) | async-done | bytes 1572896 | tf_op jit(solution)/shard_map/all_to_all | solution.py:324
  73.3 2.5 %shard_map.106 = (bf16[128,2048]{1,0:T(8,128)(2,1)}, bf16[128,2048]{1,0:T(8,128)(2,1)}, f32[1,128]{1,0:T(1,128)}) custom-call(s32[1,128]{1,0:T(1,128)S(1)} %get-tuple-element.26.slot, f32[1,128]{1,0:T(1,128)S(1)} %bitcast.13, bf16[192,4096]{1,0:T(8,128)(2,1)S(1)} %bitcast.10, bf16[128,2048]{1,0:T(8,128)(2,1)} %cot.3), custom_call_target="tpu_custom_call" | custom-call | flops 1 | bytes 1 | tf_op jit(solution)/shard_map/pallas_call | solution.py:399
  75.7 2.0 %collective-permute-done.9.right = bf16[192,2048]{1,0:T(8,128)(2,1)S(1)} collective-permute-done((bf16[192,2048]{1,0:T(8,128)(2,1)}, bf16[192,2048]{1,0:T(8,128)(2,1)S(1)}, u32[]{:S(2)}, u32[]{:S(2)}) %collective-permute-start.9) | collective-permute-done | bytes 786464 | tf_op jit(solution)/shard_map/ppermute | solution.py:308
  77.7 1.1 %shard_map.109 = bf16[1,192,2048]{2,1,0:T(8,128)(2,1)} custom-call(bf16[192,2048]{1,0:T(8,128)(2,1)S(1)} %get-tuple-element.46.left, bf16[192,2048]{1,0:T(8,128)(2,1)S(1)} %collective-permute-done.9.right), custom_call_target="tpu_custom_call" | custom-call | flops 1 | bytes 1 | tf_op jit(solution)/shard_map/pallas_call | solution.py:403
  (2 shorter events, 0.0 us)
Async XLA Ops:
  3.8 25.1 %collective-permute-start.8 = (bf16[2064,128]{1,0:T(8,128)(2,1)}, bf16[2064,128]{1,0:T(8,128)(2,1)S(1)}, u32[]{:S(2)}, u32[]{:S(2)}) collective-permute-start(bf16[2064,128]{1,0:T(8,128)(2,1)} %get-tuple-element.45), channel_id=1, source_target_pairs={{0,24},{8,16},{16,8},{24,0},{1,25},{9,17},{17,9},{25,1},{2,26},{10... | collective-permute-start | bytes 1585160 | tf_op jit(solution)/shard_map/ppermute | solution.py:308
  8.8 8.4 %collective-permute-start = (bf16[24,4096]{1,0:T(8,128)(2,1)}, bf16[24,4096]{1,0:T(8,128)(2,1)S(1)}, u32[]{:S(2)}, u32[]{:S(2)}) collective-permute-start(bf16[24,4096]{1,0:T(8,128)(2,1)} %get-tuple-element.27), channel_id=1, source_target_pairs={{0,6},{1,7},{2,4},{3,5},{4,2},{5,3},{6,0},{7,1},{8,14},{9,15},{10,... | collective-permute-start | bytes 589832 | tf_op jit(solution)/shard_map/ppermute | solution.py:340
  11.3 9.9 %collective-permute-start.1 = (bf16[24,4096]{1,0:T(8,128)(2,1)}, bf16[24,4096]{1,0:T(8,128)(2,1)S(1)}, u32[]{:S(2)}, u32[]{:S(2)}) collective-permute-start(bf16[24,4096]{1,0:T(8,128)(2,1)} %get-tuple-element.28), channel_id=1, source_target_pairs={{0,7},{1,6},{2,5},{3,4},{4,3},{5,2},{6,1},{7,0},{8,15},{9,14},{10,... | collective-permute-start | bytes 589832 | tf_op jit(solution)/shard_map/ppermute | solution.py:340
  11.3 13.5 %collective-permute-start.2 = (bf16[24,4096]{1,0:T(8,128)(2,1)}, bf16[24,4096]{1,0:T(8,128)(2,1)S(1)}, u32[]{:S(2)}, u32[]{:S(2)}) collective-permute-start(bf16[24,4096]{1,0:T(8,128)(2,1)} %get-tuple-element.29), channel_id=1, source_target_pairs={{0,4},{1,5},{2,6},{3,7},{4,0},{5,1},{6,2},{7,3},{8,12},{9,13},{10,... | collective-permute-start | bytes 589832 | tf_op jit(solution)/shard_map/ppermute | solution.py:340
  12.1 16.7 %collective-permute-start.3 = (bf16[24,4096]{1,0:T(8,128)(2,1)}, bf16[24,4096]{1,0:T(8,128)(2,1)S(1)}, u32[]{:S(2)}, u32[]{:S(2)}) collective-permute-start(bf16[24,4096]{1,0:T(8,128)(2,1)} %get-tuple-element.30), channel_id=1, source_target_pairs={{0,5},{1,4},{2,7},{3,6},{4,1},{5,0},{6,3},{7,2},{8,13},{9,12},{10,... | collective-permute-start | bytes 589832 | tf_op jit(solution)/shard_map/ppermute | solution.py:340
  17.2 11.7 %collective-permute-start.4 = (bf16[24,4096]{1,0:T(8,128)(2,1)}, bf16[24,4096]{1,0:T(8,128)(2,1)S(1)}, u32[]{:S(2)}, u32[]{:S(2)}) collective-permute-start(bf16[24,4096]{1,0:T(8,128)(2,1)} %get-tuple-element.31), channel_id=1, source_target_pairs={{0,2},{1,3},{2,0},{3,1},{4,6},{5,7},{6,4},{7,5},{8,10},{9,11},{10,... | collective-permute-start | bytes 589832 | tf_op jit(solution)/shard_map/ppermute | solution.py:340
  21.2 7.7 %collective-permute-start.5 = (bf16[24,4096]{1,0:T(8,128)(2,1)}, bf16[24,4096]{1,0:T(8,128)(2,1)S(1)}, u32[]{:S(2)}, u32[]{:S(2)}) collective-permute-start(bf16[24,4096]{1,0:T(8,128)(2,1)} %get-tuple-element.32), channel_id=1, source_target_pairs={{0,3},{1,2},{2,1},{3,0},{4,7},{5,6},{6,5},{7,4},{8,11},{9,10},{10,... | collective-permute-start | bytes 589832 | tf_op jit(solution)/shard_map/ppermute | solution.py:340
  24.7 4.2 %collective-permute-start.6 = (bf16[24,4096]{1,0:T(8,128)(2,1)}, bf16[24,4096]{1,0:T(8,128)(2,1)S(1)}, u32[]{:S(2)}, u32[]{:S(2)}) collective-permute-start(bf16[24,4096]{1,0:T(8,128)(2,1)} %get-tuple-element.33), channel_id=1, source_target_pairs={{0,1},{1,0},{2,3},{3,2},{4,5},{5,4},{6,7},{7,6},{8,9},{9,8},{10,11... | collective-permute-start | bytes 589832 | tf_op jit(solution)/shard_map/ppermute | solution.py:340
  30.1 17.9 %all-to-all-start.1 = ((bf16[8,24,2048]{2,1,0:T(8,128)(2,1)}), bf16[8,24,2048]{2,1,0:T(8,128)(2,1)S(1)}, u32[]{:S(2)}, u32[]{:S(2)}) async-start(bf16[8,24,2048]{2,1,0:T(8,128)(2,1)} %bitcast.8), calls=%async_computation.1 | async-start | bytes 1572864 | tf_op jit(solution)/shard_map/all_to_all | solution.py:324
  39.4 8.5 %collective-permute-start.7 = (bf16[192,384]{1,0:T(8,128)(2,1)}, bf16[192,384]{1,0:T(8,128)(2,1)S(1)}, u32[]{:S(2)}, u32[]{:S(2)}) collective-permute-start(bf16[192,384]{1,0:T(8,128)(2,1)} %get-tuple-element.39), channel_id=1, source_target_pairs={{0,24},{8,16},{16,8},{24,0},{1,25},{9,17},{17,9},{25,1},{2,26},{10... | collective-permute-start | bytes 442376 | tf_op jit(solution)/shard_map/ppermute | solution.py:308
  48.0 25.3 %copy-start = (f32[128,1]{0,1:T(1,128)S(1)}, f32[128,1]{0,1:T(1,128)}, u32[]{:S(2)}) copy-start(f32[128,1]{0,1:T(1,128)} %param.10) | copy-start | bytes 1540
  48.0 25.2 %all-to-all-start = ((bf16[8,24,4096]{2,1,0:T(8,128)(2,1)}), bf16[8,24,4096]{2,1,0:T(8,128)(2,1)S(1)}, u32[]{:S(2)}, u32[]{:S(2)}) async-start(bf16[8,24,4096]{2,1,0:T(8,128)(2,1)} %bitcast.14), calls=%async_computation | async-start | bytes 3145728 | tf_op jit(solution)/shard_map/all_to_all | solution.py:324
  54.8 22.9 %collective-permute-start.9 = (bf16[192,2048]{1,0:T(8,128)(2,1)}, bf16[192,2048]{1,0:T(8,128)(2,1)S(1)}, u32[]{:S(2)}, u32[]{:S(2)}) collective-permute-start(bf16[192,2048]{1,0:T(8,128)(2,1)} %get-tuple-element.47), channel_id=1, source_target_pairs={{0,8},{8,0},{16,24},{24,16},{1,9},{9,1},{17,25},{25,17},{2,10},{10... | collective-permute-start | bytes 2359304 | tf_op jit(solution)/shard_map/ppermute | solution.py:308

commit v6 on v5

--- a/solution.py
+++ b/solution.py
@@ -64,9 +64,9 @@
 
 
 LANES = 128
-TILES = 3
+TILES, BACK_TILES = 3, 2
 TAIL = 16
-WIDE = 512
+WIDE = 1024
 VMEM_LIMIT = 24 * 1024 * 1024
 TINY = pl.CostEstimate(flops=1, bytes_accessed=1, transcendentals=0)
 
@@ -215,7 +215,7 @@
     gate_in, up_in, down_in, dpre, dup, stage, sems, out_sems,
 ):
     inner, width = down.shape
-    step = inner // TILES
+    step = inner // BACK_TILES
     inner_tiles = [slice(at, at + step) for at in range(0, inner, step)]
     tiles = [slice(at, at + WIDE) for at in range(0, width, WIDE)]
     stages = [[(down.at[t, :], down_in.at[t, :])] for t in inner_tiles]
@@ -373,7 +373,7 @@
         scratch_shapes=held
         + [pltpu.VMEM((inner, width), BF16)]
         + [pltpu.VMEM((slots, inner), BF16)] * 2
-        + [pltpu.VMEM((slots, 2 * width), BF16), dma((TILES + 2 * tiles,)), dma((tiles,))],
+        + [pltpu.VMEM((slots, 2 * width), BF16), dma((BACK_TILES + 2 * tiles,)), dma((tiles,))],
     )(hidden, by_up, by_pre, cot, gate_mat, up_mat, down_mat)
     back = over_tp(
         call(

time: 79.2 us -> 78 us (0.985)
  Pallas kernels: 24.2 us -> 23 us
  waiting for transfers between devices: 27.7 us -> 28.9 us
  starting transfers between devices: 26.1 us -> 25.1 us
    pallas_call x1, Pallas kernels: 8.19 us -> 6.85 us  [body_line(): call(back_kernel, pltpu.HBM((slots, 2 * width), BF16), in_specs=[whole] *...]
    ppermute x3, starting transfers between devices: 9.86 us -> 9.07 us  [along(): return lax.ppermute(rows, 'ctx', [(i, i ^ step) for i in range(4)])]
  transfers between devices with their start and end apart: 12 -> 12, of which waited for: 6 -> 7; matrix products, arithmetic and copies ran while one was open for 0% -> 0% of each run, Pallas kernels for 24% -> 23%
where the time goes in v6:
time: 78 us; the launch traced here: 77.7 us
  waiting for transfers between devices  28.9 us (37%)
  starting transfers between devices  25.1 us (32%)
  Pallas kernels  23 us (29%)
    all_to_all x2, waiting for transfers between devices, over_tp(): lax.all_to_all(rows.reshape(peers, capacity, wide), 'tp', split_axis=0, c...  14.7 us
    ppermute x7, waiting for transfers between devices, body_line(): got[k] = lax.ppermute(blocks[k], 'tp', [(i, i ^ k) for i in range(peers)])  11.8 us
    ppermute x3, starting transfers between devices, along(): return lax.ppermute(rows, 'ctx', [(i, i ^ step) for i in range(4)])  9.07 us
    ppermute x7, starting transfers between devices, body_line(): got[k] = lax.ppermute(blocks[k], 'tp', [(i, i ^ k) for i in range(peers)])  8.29 us
    all_to_all x2, starting transfers between devices, over_tp(): lax.all_to_all(rows.reshape(peers, capacity, wide), 'tp', split_axis=0, c...  7.73 us
    pallas_call x1, Pallas kernels, body_line(): call(back_kernel, pltpu.HBM((slots, 2 * width), BF16), in_specs=[whole] *...  6.85 us
    pallas_call x1, Pallas kernels, body_line(): call(functools.partial(hidden_kernel, order), [shaped((slots, inner))] *...  5.52 us
    pallas_call x1, Pallas kernels, body_line(): call(functools.partial(send_kernel, peers, capacity), [shaped((1, count),...  3.13 us
  transfers between devices with their start and end apart: 12, of which 7 were waited for; matrix products, arithmetic and copies ran while one was open for 0% of the time, Pallas kernels for 23%

profile of v6, /device:TPU:0, one launch (start us, length us, event | category | flops | bytes accessed | tf_op | source)
XLA Modules:
  0.0 77.7 jit_solution(16549393360431515943)
XLA Ops:
  0.6 3.1 %shard_map.102 = (s32[1,128]{1,0:T(1,128)S(1)}, bf16[2064,128]{1,0:T(8,128)(2,1)}, bf16[24,4096]{1,0:T(8,128)(2,1)}, bf16[24,4096]{1,0:T(8,128)(2,1)}, bf16[24,4...) custom-call(s32[1,128]{1,0:T(1,128)} %bitcast.20, ...), custom_call_target="tpu_custom_call" | custom-call | flops 1 | bytes 1 | tf_op jit(solution)/shard_map/pallas_call | solution.py:328
  3.8 5.0 %collective-permute-start.8 = (bf16[2064,128]{1,0:T(8,128)(2,1)}, bf16[2064,128]{1,0:T(8,128)(2,1)S(1)}, u32[]{:S(2)}, u32[]{:S(2)}) collective-permute-start(bf16[2064,128]{1,0:T(8,128)(2,1)} %get-tuple-element.45), channel_id=1, source_target_pairs={{0,24},{8,16},{16,8},{24,0},{1,25},{9,17},{17,9},{25,1},{2,26},{10... | collective-permute-start | bytes 1585160 | tf_op jit(solution)/shard_map/ppermute | solution.py:308
  8.8 2.4 %collective-permute-start = (bf16[24,4096]{1,0:T(8,128)(2,1)}, bf16[24,4096]{1,0:T(8,128)(2,1)S(1)}, u32[]{:S(2)}, u32[]{:S(2)}) collective-permute-start(bf16[24,4096]{1,0:T(8,128)(2,1)} %get-tuple-element.27), channel_id=1, source_target_pairs={{0,6},{1,7},{2,4},{3,5},{4,2},{5,3},{6,0},{7,1},{8,14},{9,15},{10,... | collective-permute-start | bytes 589832 | tf_op jit(solution)/shard_map/ppermute | solution.py:340
  11.3 0.0 collective-permute-start.1
  11.3 0.9 %collective-permute-start.2 = (bf16[24,4096]{1,0:T(8,128)(2,1)}, bf16[24,4096]{1,0:T(8,128)(2,1)S(1)}, u32[]{:S(2)}, u32[]{:S(2)}) collective-permute-start(bf16[24,4096]{1,0:T(8,128)(2,1)} %get-tuple-element.29), channel_id=1, source_target_pairs={{0,4},{1,5},{2,6},{3,7},{4,0},{5,1},{6,2},{7,3},{8,12},{9,13},{10,... | collective-permute-start | bytes 589832 | tf_op jit(solution)/shard_map/ppermute | solution.py:340
  12.1 1.1 %collective-permute-start.3 = (bf16[24,4096]{1,0:T(8,128)(2,1)}, bf16[24,4096]{1,0:T(8,128)(2,1)S(1)}, u32[]{:S(2)}, u32[]{:S(2)}) collective-permute-start(bf16[24,4096]{1,0:T(8,128)(2,1)} %get-tuple-element.30), channel_id=1, source_target_pairs={{0,5},{1,4},{2,7},{3,6},{4,1},{5,0},{6,3},{7,2},{8,13},{9,12},{10,... | collective-permute-start | bytes 589832 | tf_op jit(solution)/shard_map/ppermute | solution.py:340
  13.2 4.0 %collective-permute-done.refs_0_ = bf16[24,4096]{1,0:T(8,128)(2,1)S(1)} collective-permute-done((bf16[24,4096]{1,0:T(8,128)(2,1)}, bf16[24,4096]{1,0:T(8,128)(2,1)S(1)}, u32[]{:S(2)}, u32[]{:S(2)}) %collective-permute-start) | collective-permute-done | bytes 196640 | tf_op jit(solution)/shard_map/ppermute | solution.py:340
  17.2 2.1 %collective-permute-start.4 = (bf16[24,4096]{1,0:T(8,128)(2,1)}, bf16[24,4096]{1,0:T(8,128)(2,1)S(1)}, u32[]{:S(2)}, u32[]{:S(2)}) collective-permute-start(bf16[24,4096]{1,0:T(8,128)(2,1)} %get-tuple-element.31), channel_id=1, source_target_pairs={{0,2},{1,3},{2,0},{3,1},{4,6},{5,7},{6,4},{7,5},{8,10},{9,11},{10,... | collective-permute-start | bytes 589832 | tf_op jit(solution)/shard_map/ppermute | solution.py:340
  19.3 1.8 %collective-permute-done.1.refs_1_ = bf16[24,4096]{1,0:T(8,128)(2,1)S(1)} collective-permute-done((bf16[24,4096]{1,0:T(8,128)(2,1)}, bf16[24,4096]{1,0:T(8,128)(2,1)S(1)}, u32[]{:S(2)}, u32[]{:S(2)}) %collective-permute-start.1) | collective-permute-done | bytes 196640 | tf_op jit(solution)/shard_map/ppermute | solution.py:340
  21.2 1.7 %collective-permute-start.5 = (bf16[24,4096]{1,0:T(8,128)(2,1)}, bf16[24,4096]{1,0:T(8,128)(2,1)S(1)}, u32[]{:S(2)}, u32[]{:S(2)}) collective-permute-start(bf16[24,4096]{1,0:T(8,128)(2,1)} %get-tuple-element.32), channel_id=1, source_target_pairs={{0,3},{1,2},{2,1},{3,0},{4,7},{5,6},{6,5},{7,4},{8,11},{9,10},{10,... | collective-permute-start | bytes 589832 | tf_op jit(solution)/shard_map/ppermute | solution.py:340
  22.9 1.8 %collective-permute-done.2.refs_2_ = bf16[24,4096]{1,0:T(8,128)(2,1)S(1)} collective-permute-done((bf16[24,4096]{1,0:T(8,128)(2,1)}, bf16[24,4096]{1,0:T(8,128)(2,1)S(1)}, u32[]{:S(2)}, u32[]{:S(2)}) %collective-permute-start.2) | collective-permute-done | bytes 196640 | tf_op jit(solution)/shard_map/ppermute | solution.py:340
  24.7 0.1 collective-permute-start.6
  24.8 4.1 %collective-permute-done.3.refs_3_ = bf16[24,4096]{1,0:T(8,128)(2,1)S(1)} collective-permute-done((bf16[24,4096]{1,0:T(8,128)(2,1)}, bf16[24,4096]{1,0:T(8,128)(2,1)S(1)}, u32[]{:S(2)}, u32[]{:S(2)}) %collective-permute-start.3) | collective-permute-done | bytes 196640 | tf_op jit(solution)/shard_map/ppermute | solution.py:340
  28.9 0.0 collective-permute-done.4.refs_4_
  28.9 0.0 collective-permute-done.5.refs_5_
  28.9 0.0 collective-permute-done.6.refs_6_
  28.9 0.0 collective-permute-done.8.rows
  28.9 1.2 %shard_map.107 = bf16[192,2048]{1,0:T(8,128)(2,1)} custom-call(bf16[2064,128]{1,0:T(8,128)(2,1)S(1)} %collective-permute-done.8.rows, bf16[24,4096]{1,0:T(8,128)(2,1)S(1)} %collective-permute-done.refs_0_, bf16[24,4096]{1,0:T(8,128)(2,1)S(1)} %collective-permute-done.1.refs_1_, bf16[24,4096]{1,0:T(8,128)(2,1)S(1)} %collective-permute-done.2.refs_2_, ...), custom_call_target="tpu_custom_call" | custom-call | flops 1 | bytes 1 | tf_op jit(solution)/shard_map/pallas_call | solution.py:363
  30.1 3.8 %all-to-all-start.1 = ((bf16[8,24,2048]{2,1,0:T(8,128)(2,1)}), bf16[8,24,2048]{2,1,0:T(8,128)(2,1)S(1)}, u32[]{:S(2)}, u32[]{:S(2)}) async-start(bf16[8,24,2048]{2,1,0:T(8,128)(2,1)} %bitcast.8), calls=%async_computation.1 | async-start | bytes 1572864 | tf_op jit(solution)/shard_map/all_to_all | solution.py:324
  33.9 5.5 %shard_map.103 = (bf16[192,768]{1,0:T(8,128)(2,1)S(1)}, bf16[192,768]{1,0:T(8,128)(2,1)S(1)}, bf16[192,768]{1,0:T(8,128)(2,1)S(1)}, bf16[192,384]{1,0:T(8,128)(2...) custom-call(bf16[24,4096]{1,0:T(8,128)(2,1)S(1)} %collective-permute-done.refs_0_, ...), custom_call_target="tpu_custom_call" | custom-call | flops 1 | bytes 1 | tf_op jit(solution)/shard_map/pallas_call | solution.py:347
  39.4 0.4 collective-permute-start.7
  39.8 6.9 %shard_map.104.refs_0_ = bf16[192,4096]{1,0:T(8,128)(2,1)} custom-call(bf16[192,768]{1,0:T(8,128)(2,1)S(1)} %get-tuple-element.35.hidden, bf16[192,768]{1,0:T(8,128)(2,1)S(1)} %get-tuple-element.36.by_up, bf16[192,768]{1,0:T(8,128)(2,1)S(1)} %get-tuple-element.37.by_pre, bf16[192,2048]{1,0:T(8,128)(2,1)S(1)} %get-tuple-element.38.cot, ...), custom_call_target="tpu_custom_call" | custom-call | flops 1 | bytes 1 | tf_op jit(solution)/shard_map/pallas_call | solution.py:368
  46.6 1.2 %collective-permute-done.7.refs_1_.h_remote = bf16[192,384]{1,0:T(8,128)(2,1)S(1)} collective-permute-done((bf16[192,384]{1,0:T(8,128)(2,1)}, bf16[192,384]{1,0:T(8,128)(2,1)S(1)}, u32[]{:S(2)}, u32[]{:S(2)}) %collective-permute-start.7) | collective-permute-done | bytes 147488 | tf_op jit(solution)/shard_map/ppermute | solution.py:308
  47.9 0.0 all-to-all-done.1
  47.9 4.0 %all-to-all-start = ((bf16[8,24,4096]{2,1,0:T(8,128)(2,1)}), bf16[8,24,4096]{2,1,0:T(8,128)(2,1)S(1)}, u32[]{:S(2)}, u32[]{:S(2)}) async-start(bf16[8,24,4096]{2,1,0:T(8,128)(2,1)} %bitcast.14), calls=%async_computation | async-start | bytes 3145728 | tf_op jit(solution)/shard_map/all_to_all | solution.py:324
  51.8 2.6 %shard_map.108 = (bf16[192,2048]{1,0:T(8,128)(2,1)S(1)}, bf16[192,2048]{1,0:T(8,128)(2,1)}) custom-call(bf16[192,384]{1,0:T(8,128)(2,1)} %get-tuple-element.43.h_own, bf16[192,384]{1,0:T(8,128)(2,1)S(1)} %collective-permute-done.7.refs_1_.h_remote, bf16[192,2048]{1,0:T(8,128)(2,1)} %get-tuple-element.44.own, bf16[192,2048]{1,0:T(8,128)(2,1)S(1)} %bitcast.11), custom_call_target="tpu_custom_call" | custom-call | flops 1 | bytes 1 | tf_op jit(solution)/shard_map/pallas_call | solution.py:388
  54.5 3.7 %collective-permute-start.9 = (bf16[192,2048]{1,0:T(8,128)(2,1)}, bf16[192,2048]{1,0:T(8,128)(2,1)S(1)}, u32[]{:S(2)}, u32[]{:S(2)}) collective-permute-start(bf16[192,2048]{1,0:T(8,128)(2,1)} %get-tuple-element.47), channel_id=1, source_target_pairs={{0,8},{8,0},{16,24},{24,16},{1,9},{9,1},{17,25},{25,17},{2,10},{10... | collective-permute-start | bytes 2359304 | tf_op jit(solution)/shard_map/ppermute | solution.py:308
  58.2 14.7 %all-to-all-done = bf16[8,24,4096]{2,1,0:T(8,128)(2,1)S(1)} async-done(((bf16[8,24,4096]{2,1,0:T(8,128)(2,1)}), bf16[8,24,4096]{2,1,0:T(8,128)(2,1)S(1)}, u32[]{:S(2)}, u32[]{:S(2)}) %all-to-all-start) | async-done | bytes 1572896 | tf_op jit(solution)/shard_map/all_to_all | solution.py:324
  72.9 0.0 copy-done
  72.9 2.5 %shard_map.106 = (bf16[128,2048]{1,0:T(8,128)(2,1)}, bf16[128,2048]{1,0:T(8,128)(2,1)}, f32[1,128]{1,0:T(1,128)}) custom-call(s32[1,128]{1,0:T(1,128)S(1)} %get-tuple-element.26.slot, f32[1,128]{1,0:T(1,128)S(1)} %bitcast.13, bf16[192,4096]{1,0:T(8,128)(2,1)S(1)} %bitcast.10, bf16[128,2048]{1,0:T(8,128)(2,1)} %cot.3), custom_call_target="tpu_custom_call" | custom-call | flops 1 | bytes 1 | tf_op jit(solution)/shard_map/pallas_call | solution.py:399
  75.4 1.2 %collective-permute-done.9.right = bf16[192,2048]{1,0:T(8,128)(2,1)S(1)} collective-permute-done((bf16[192,2048]{1,0:T(8,128)(2,1)}, bf16[192,2048]{1,0:T(8,128)(2,1)S(1)}, u32[]{:S(2)}, u32[]{:S(2)}) %collective-permute-start.9) | collective-permute-done | bytes 786464 | tf_op jit(solution)/shard_map/ppermute | solution.py:308
  76.6 1.1 %shard_map.109 = bf16[1,192,2048]{2,1,0:T(8,128)(2,1)} custom-call(bf16[192,2048]{1,0:T(8,128)(2,1)S(1)} %get-tuple-element.46.left, bf16[192,2048]{1,0:T(8,128)(2,1)S(1)} %collective-permute-done.9.right), custom_call_target="tpu_custom_call" | custom-call | flops 1 | bytes 1 | tf_op jit(solution)/shard_map/pallas_call | solution.py:403
  (2 shorter events, 0.0 us)
Async XLA Ops:
  3.8 25.1 %collective-permute-start.8 = (bf16[2064,128]{1,0:T(8,128)(2,1)}, bf16[2064,128]{1,0:T(8,128)(2,1)S(1)}, u32[]{:S(2)}, u32[]{:S(2)}) collective-permute-start(bf16[2064,128]{1,0:T(8,128)(2,1)} %get-tuple-element.45), channel_id=1, source_target_pairs={{0,24},{8,16},{16,8},{24,0},{1,25},{9,17},{17,9},{25,1},{2,26},{10... | collective-permute-start | bytes 1585160 | tf_op jit(solution)/shard_map/ppermute | solution.py:308
  8.8 8.4 %collective-permute-start = (bf16[24,4096]{1,0:T(8,128)(2,1)}, bf16[24,4096]{1,0:T(8,128)(2,1)S(1)}, u32[]{:S(2)}, u32[]{:S(2)}) collective-permute-start(bf16[24,4096]{1,0:T(8,128)(2,1)} %get-tuple-element.27), channel_id=1, source_target_pairs={{0,6},{1,7},{2,4},{3,5},{4,2},{5,3},{6,0},{7,1},{8,14},{9,15},{10,... | collective-permute-start | bytes 589832 | tf_op jit(solution)/shard_map/ppermute | solution.py:340
  11.3 9.9 %collective-permute-start.1 = (bf16[24,4096]{1,0:T(8,128)(2,1)}, bf16[24,4096]{1,0:T(8,128)(2,1)S(1)}, u32[]{:S(2)}, u32[]{:S(2)}) collective-permute-start(bf16[24,4096]{1,0:T(8,128)(2,1)} %get-tuple-element.28), channel_id=1, source_target_pairs={{0,7},{1,6},{2,5},{3,4},{4,3},{5,2},{6,1},{7,0},{8,15},{9,14},{10,... | collective-permute-start | bytes 589832 | tf_op jit(solution)/shard_map/ppermute | solution.py:340
  11.3 13.5 %collective-permute-start.2 = (bf16[24,4096]{1,0:T(8,128)(2,1)}, bf16[24,4096]{1,0:T(8,128)(2,1)S(1)}, u32[]{:S(2)}, u32[]{:S(2)}) collective-permute-start(bf16[24,4096]{1,0:T(8,128)(2,1)} %get-tuple-element.29), channel_id=1, source_target_pairs={{0,4},{1,5},{2,6},{3,7},{4,0},{5,1},{6,2},{7,3},{8,12},{9,13},{10,... | collective-permute-start | bytes 589832 | tf_op jit(solution)/shard_map/ppermute | solution.py:340
  12.1 16.7 %collective-permute-start.3 = (bf16[24,4096]{1,0:T(8,128)(2,1)}, bf16[24,4096]{1,0:T(8,128)(2,1)S(1)}, u32[]{:S(2)}, u32[]{:S(2)}) collective-permute-start(bf16[24,4096]{1,0:T(8,128)(2,1)} %get-tuple-element.30), channel_id=1, source_target_pairs={{0,5},{1,4},{2,7},{3,6},{4,1},{5,0},{6,3},{7,2},{8,13},{9,12},{10,... | collective-permute-start | bytes 589832 | tf_op jit(solution)/shard_map/ppermute | solution.py:340
  17.2 11.7 %collective-permute-start.4 = (bf16[24,4096]{1,0:T(8,128)(2,1)}, bf16[24,4096]{1,0:T(8,128)(2,1)S(1)}, u32[]{:S(2)}, u32[]{:S(2)}) collective-permute-start(bf16[24,4096]{1,0:T(8,128)(2,1)} %get-tuple-element.31), channel_id=1, source_target_pairs={{0,2},{1,3},{2,0},{3,1},{4,6},{5,7},{6,4},{7,5},{8,10},{9,11},{10,... | collective-permute-start | bytes 589832 | tf_op jit(solution)/shard_map/ppermute | solution.py:340
  21.2 7.7 %collective-permute-start.5 = (bf16[24,4096]{1,0:T(8,128)(2,1)}, bf16[24,4096]{1,0:T(8,128)(2,1)S(1)}, u32[]{:S(2)}, u32[]{:S(2)}) collective-permute-start(bf16[24,4096]{1,0:T(8,128)(2,1)} %get-tuple-element.32), channel_id=1, source_target_pairs={{0,3},{1,2},{2,1},{3,0},{4,7},{5,6},{6,5},{7,4},{8,11},{9,10},{10,... | collective-permute-start | bytes 589832 | tf_op jit(solution)/shard_map/ppermute | solution.py:340
  24.7 4.2 %collective-permute-start.6 = (bf16[24,4096]{1,0:T(8,128)(2,1)}, bf16[24,4096]{1,0:T(8,128)(2,1)S(1)}, u32[]{:S(2)}, u32[]{:S(2)}) collective-permute-start(bf16[24,4096]{1,0:T(8,128)(2,1)} %get-tuple-element.33), channel_id=1, source_target_pairs={{0,1},{1,0},{2,3},{3,2},{4,5},{5,4},{6,7},{7,6},{8,9},{9,8},{10,11... | collective-permute-start | bytes 589832 | tf_op jit(solution)/shard_map/ppermute | solution.py:340
  30.1 17.7 %all-to-all-start.1 = ((bf16[8,24,2048]{2,1,0:T(8,128)(2,1)}), bf16[8,24,2048]{2,1,0:T(8,128)(2,1)S(1)}, u32[]{:S(2)}, u32[]{:S(2)}) async-start(bf16[8,24,2048]{2,1,0:T(8,128)(2,1)} %bitcast.8), calls=%async_computation.1 | async-start | bytes 1572864 | tf_op jit(solution)/shard_map/all_to_all | solution.py:324
  39.4 8.4 %collective-permute-start.7 = (bf16[192,384]{1,0:T(8,128)(2,1)}, bf16[192,384]{1,0:T(8,128)(2,1)S(1)}, u32[]{:S(2)}, u32[]{:S(2)}) collective-permute-start(bf16[192,384]{1,0:T(8,128)(2,1)} %get-tuple-element.39), channel_id=1, source_target_pairs={{0,24},{8,16},{16,8},{24,0},{1,25},{9,17},{17,9},{25,1},{2,26},{10... | collective-permute-start | bytes 442376 | tf_op jit(solution)/shard_map/ppermute | solution.py:308
  47.9 25.0 %copy-start = (f32[128,1]{0,1:T(1,128)S(1)}, f32[128,1]{0,1:T(1,128)}, u32[]{:S(2)}) copy-start(f32[128,1]{0,1:T(1,128)} %param.10) | copy-start | bytes 1540
  47.9 25.0 %all-to-all-start = ((bf16[8,24,4096]{2,1,0:T(8,128)(2,1)}), bf16[8,24,4096]{2,1,0:T(8,128)(2,1)S(1)}, u32[]{:S(2)}, u32[]{:S(2)}) async-start(bf16[8,24,4096]{2,1,0:T(8,128)(2,1)} %bitcast.14), calls=%async_computation | async-start | bytes 3145728 | tf_op jit(solution)/shard_map/all_to_all | solution.py:324
  54.5 22.1 %collective-permute-start.9 = (bf16[192,2048]{1,0:T(8,128)(2,1)}, bf16[192,2048]{1,0:T(8,128)(2,1)S(1)}, u32[]{:S(2)}, u32[]{:S(2)}) collective-permute-start(bf16[192,2048]{1,0:T(8,128)(2,1)} %get-tuple-element.47), channel_id=1, source_target_pairs={{0,8},{8,0},{16,24},{24,16},{1,9},{9,1},{17,25},{25,17},{2,10},{10... | collective-permute-start | bytes 2359304 | tf_op jit(solution)/shard_map/ppermute | solution.py:308

commit v7 on v6

--- a/solution.py
+++ b/solution.py
@@ -118,13 +118,14 @@
     running = jnp.dot(onehot.astype(BF16), upto.astype(BF16), preferred_element_type=F32)
     rank = jnp.sum(jnp.where(onehot, running - 1.0, 0.0), axis=0, keepdims=True).astype(jnp.int32)
     slot = ids * capacity + rank
-    slot_out[...] = slot
+    slot_out[0:1] = slot
     scaled[...] = (column(gates[...]) * cot[...].astype(F32)).astype(BF16)
     chunks = width // LANES
     for c in range(chunks):
         across[c * count : (c + 1) * count] = scaled[:, c * LANES : (c + 1) * LANES]
     across[chunks * count :] = jnp.broadcast_to(slot.astype(F32), (TAIL, count)).astype(BF16)
     slot = (ids ^ lax.axis_index("tp")) * capacity + rank
+    slot_out[1:2] = slot
     placing = (
         lax.broadcasted_iota(jnp.int32, (peers * capacity, count), 0) == slot
     ).astype(BF16)
@@ -187,10 +188,8 @@
     arrive = staged(
         [((gate.at[:, t], gate_in.at[:, t]), (up.at[:, t], up_in.at[:, t])) for t in tiles], sems
     )
-    own = lax.axis_index("tp")
     for k, block in zip(order, blocks):
-        start = pl.multiple_of((own ^ k) * capacity, 8)
-        wide[pl.ds(start, capacity), :] = block[...].astype(F32)
+        wide[k * capacity : (k + 1) * capacity, :] = block[...].astype(F32)
     rows[...] = wide[:, :width].astype(BF16)
     cot[...] = wide[:, width:].astype(BF16)
     same[...] = cot[...]
@@ -207,13 +206,19 @@
     on_left = lax.axis_index("ctx") < 2
     left, right = hidden[:, :half], hidden[:, half:]
     near[...] = jnp.where(on_left, left, right)
-    far[...] = jnp.where(on_left, right, left)
+    gone = jnp.where(on_left, right, left).astype(F32)
+    own = lax.axis_index("tp")
+    for k in range(peers):
+        start = pl.multiple_of((own ^ k) * capacity, 8)
+        wide[pl.ds(start, capacity), :half] = gone[k * capacity : (k + 1) * capacity]
+    far[...] = wide[:, :half].astype(BF16)
 
 
 def back_kernel(
-    hidden, by_up, by_pre, cot, gate, up, down, out,
-    gate_in, up_in, down_in, dpre, dup, stage, sems, out_sems,
+    hidden, by_up, by_pre, cot, gate, up, down, *refs,
 ):
+    blocks, (gate_in, up_in, down_in, dpre, dup, sems) = refs[:-6], refs[-6:]
+    capacity = blocks[0].shape[0]
     inner, width = down.shape
     step = inner // BACK_TILES
     inner_tiles = [slice(at, at + step) for at in range(0, inner, step)]
@@ -226,30 +231,22 @@
         dhid = lax.dot_general(cot[...], down_in[t, :], CONTRACT_LAST, preferred_element_type=F32)
         dup[:, t] = (dhid * by_up[:, t].astype(F32)).astype(BF16)
         dpre[:, t] = (dhid * by_pre[:, t].astype(F32)).astype(BF16)
-    leaving = []
-    for i, t in enumerate(tiles):
-        at = 2 * t.start
-        both = slice(at, at + 2 * WIDE)
-        stage[:, at : at + WIDE] = jnp.dot(
-            hidden[...], down_in[:, t], preferred_element_type=F32
-        ).astype(BF16)
+
+    def leave(at, rows):
+        for i, block in enumerate(blocks):
+            block[:, at : at + WIDE] = rows[i * capacity : (i + 1) * capacity].astype(BF16)
+
+    for t in tiles:
+        leave(t.start, jnp.dot(hidden[...], down_in[:, t], preferred_element_type=F32))
         arrive()
-        stage[:, at + WIDE : at + 2 * WIDE] = (
+        leave(
+            width + t.start,
             lax.dot_general(dpre[...], gate_in[t, :], CONTRACT_LAST, preferred_element_type=F32)
-            + lax.dot_general(dup[...], up_in[t, :], CONTRACT_LAST, preferred_element_type=F32)
-        ).astype(BF16)
-        leave = pltpu.make_async_copy(stage.at[:, both], out.at[:, both], out_sems.at[i])
-        leave.start()
-        leaving.append(leave)
-    for leave in leaving:
-        leave.wait()
-
-
-def pass_kernel(*refs):
-    pass
-
-
-def quarters_kernel(h_own, h_remote, own, remote, mine, other, stage, sems):
+            + lax.dot_general(dup[...], up_in[t, :], CONTRACT_LAST, preferred_element_type=F32),
+        )
+
+
+def quarters_kernel(after, h_own, h_remote, own, remote, mine, other, stage, sems):
     width = remote.shape[1]
     even = lax.rem(lax.axis_index("ctx"), 2) == 0
     left, right = h_own[...].astype(F32).T, h_remote[...].astype(F32).T
@@ -280,22 +277,26 @@
         leave.wait()
 
 
-def home_kernel(slot, gates, back, cot, layer_output, token_grad, gate_grad):
+def home_kernel(order, after, slot, gates, cot, *refs):
+    peers = len(order)
+    blocks, (layer_output, token_grad, gate_grad, wide) = refs[:peers], refs[peers:]
     count, width = cot.shape
+    capacity = blocks[0].shape[0]
+    for k, block in zip(order, blocks):
+        wide[k * capacity : (k + 1) * capacity, :] = block[...].astype(F32)
     placing = (
-        lax.broadcasted_iota(jnp.int32, (count, back.shape[0]), 1) == column(slot[...])
+        lax.broadcasted_iota(jnp.int32, (count, wide.shape[0]), 1) == column(slot[1:2])
     ).astype(BF16)
     gate = column(gates[...])
     total = jnp.zeros((count, 1), F32)
-    step = WIDE
+    step = 512
     for at in range(0, width, step):
-        cols = slice(at, at + step)
-        out_tok = jnp.dot(placing, back[:, 2 * at : 2 * at + step], preferred_element_type=F32)
+        cols, later = slice(at, at + step), slice(width + at, width + at + step)
+        out_tok = jnp.dot(placing, wide[:, cols].astype(BF16), preferred_element_type=F32)
         layer_output[:, cols] = (gate * out_tok).astype(BF16)
         total += jnp.sum(cot[:, cols].astype(F32) * out_tok, axis=1, keepdims=True)
-        grad_cols = slice(2 * at + step, 2 * at + 2 * step)
         token_grad[:, cols] = jnp.dot(
-            placing, back[:, grad_cols], preferred_element_type=F32
+            placing, wide[:, later].astype(BF16), preferred_element_type=F32
         ).astype(BF16)
     gate_grad[...] = jnp.sum(jnp.where(diagonal(count), total, 0.0), axis=0, keepdims=True)
 
@@ -328,7 +329,7 @@
     slot, across, *blocks = call(
         functools.partial(send_kernel, peers, capacity),
         [
-            shaped((1, count), jnp.int32),
+            shaped((2, count), jnp.int32),
             pltpu.HBM((width // LANES * count + TAIL, LANES), BF16),
         ]
         + [pltpu.HBM((capacity, 2 * width), BF16)] * peers,
@@ -338,7 +339,7 @@
     got = {0: in_hbm(blocks[0])}
     for k in range(1, peers):
         got[k] = lax.ppermute(blocks[k], "tp", [(i, i ^ k) for i in range(peers)])
-    order = (6, 7, 4, 5, 2, 3, 1, 0)
+    order = (6, 7, 2, 4, 3, 5, 1, 0)
     got = [got[k] for k in order]
 
     gate_mat, up_mat, down_mat = [in_hbm(w[0]) for w in (w_gate, w_up, w_down)]
@@ -364,43 +365,39 @@
             remote_kernel, shaped((slots, width)), in_specs=[whole] + [after] * (peers - 1)
         )(rows_across, *[g for k, g in zip(order, got) if k])
     )
-    tiles = width // WIDE
     back = call(
         back_kernel,
-        pltpu.HBM((slots, 2 * width), BF16),
+        [pltpu.HBM((capacity, 2 * width), BF16)] * peers,
         in_specs=[whole] * 4 + [in_place] * 3,
-        out_specs=in_place,
         scratch_shapes=held
         + [pltpu.VMEM((inner, width), BF16)]
         + [pltpu.VMEM((slots, inner), BF16)] * 2
-        + [pltpu.VMEM((slots, 2 * width), BF16), dma((BACK_TILES + 2 * tiles,)), dma((tiles,))],
+        + [dma((BACK_TILES + 2 * (width // WIDE),))],
     )(hidden, by_up, by_pre, cot, gate_mat, up_mat, down_mat)
-    back = over_tp(
-        call(
-            pass_kernel,
-            pltpu.HBM((slots, 2 * width), BF16),
-            in_specs=[after] * 2,
-            out_specs=after,
-            input_output_aliases={0: 0},
-        )(in_hbm(back), far_across)
-    )
+    home = [
+        lax.ppermute(back[k], "tp", [(i, i ^ k) for i in range(peers)]) if k else in_hbm(back[0])
+        for k in order
+    ]
 
     mine, other = call(
         quarters_kernel,
         [shaped((quarter, width)), pltpu.HBM((quarter, width), BF16)],
+        in_specs=[after] + [whole] * 4,
         out_specs=[whole, in_place],
         scratch_shapes=[
             pltpu.VMEM((quarter, width), BF16),
-            pltpu.SemaphoreType.DMA((width // WIDE,)),
+            dma((width // WIDE,)),
         ],
-    )(near, far_across, same, remote)
+    )(in_hbm(back[0]), near, far_across, same, remote)
     swapped = along(other, 1)
 
+    down_grad = call(add_kernel, shaped((1, quarter, width)))(mine, swapped)
     layer_output, token_grad, gate_grad = call(
-        home_kernel,
+        functools.partial(home_kernel, order),
         [shaped((count, width)), shaped((count, width)), shaped((1, count), F32)],
-    )(slot, gates, back, in_hbm(cotangent))
-    down_grad = call(add_kernel, shaped((1, quarter, width)))(mine, swapped)
+        in_specs=[after] + [whole] * (3 + peers),
+        scratch_shapes=[pltpu.VMEM((slots, 2 * width), F32)],
+    )(in_hbm(down_grad), slot, gates, cotangent, *home)
     return layer_output, token_grad, gate_grad.reshape(count, 1), down_grad
 
 

time: 78 us -> 77.1 us (0.988)
  waiting for transfers between devices: 28.9 us -> 27.1 us
  starting transfers between devices: 25.1 us -> 26.1 us
    all_to_all x2 -> x1, waiting for transfers between devices: 14.7 us -> 0.01 us  [over_tp(): lax.all_to_all(rows.reshape(peers, capacity, wide), 'tp', split_axis=0, c...]
    ppermute x0 -> x7, waiting for transfers between devices: none -> 8.8 us  [body_line(): lax.ppermute(back[k], 'tp', [(i, i ^ k) for i in range(peers)])]
    ppermute x0 -> x7, starting transfers between devices: none -> 7.13 us  [body_line(): lax.ppermute(back[k], 'tp', [(i, i ^ k) for i in range(peers)])]
    all_to_all x2 -> x1, starting transfers between devices: 7.73 us -> 3.55 us  [over_tp(): lax.all_to_all(rows.reshape(peers, capacity, wide), 'tp', split_axis=0, c...]
    ppermute x3, waiting for transfers between devices: 2.43 us -> 4.77 us  [along(): return lax.ppermute(rows, 'ctx', [(i, i ^ step) for i in range(4)])]
    ppermute x7, waiting for transfers between devices: 11.8 us -> 13.5 us  [body_line(): got[k] = lax.ppermute(blocks[k], 'tp', [(i, i ^ k) for i in range(peers)])]
    ppermute x7, starting transfers between devices: 8.29 us -> 6.58 us  [body_line(): got[k] = lax.ppermute(blocks[k], 'tp', [(i, i ^ k) for i in range(peers)])]
    pallas_call x4 -> x3, Pallas kernels: 12.5 us -> 12.5 us  [the longest x1 6.98 us: body_line(): call(back_kernel, [pltpu.HBM((capacity, 2 * width), BF16)] * peers, in_sp...]
  transfers between devices with their start and end apart: 12 -> 18, of which waited for: 7 -> 11; matrix products, arithmetic and copies ran while one was open for 0% -> 0% of each run, Pallas kernels for 23% -> 18%
where the time goes in v7:
time: 77.1 us; the launch traced here: 76.9 us
  waiting for transfers between devices  27.1 us (35%)
  starting transfers between devices  26.1 us (34%)
  Pallas kernels  23 us (30%)
    ppermute x7, waiting for transfers between devices, body_line(): got[k] = lax.ppermute(blocks[k], 'tp', [(i, i ^ k) for i in range(peers)])  13.5 us
    ppermute x3, starting transfers between devices, along(): return lax.ppermute(rows, 'ctx', [(i, i ^ step) for i in range(4)])  8.82 us
    ppermute x7, waiting for transfers between devices, body_line(): lax.ppermute(back[k], 'tp', [(i, i ^ k) for i in range(peers)])  8.8 us
    ppermute x7, starting transfers between devices, body_line(): lax.ppermute(back[k], 'tp', [(i, i ^ k) for i in range(peers)])  7.13 us
    pallas_call x1, Pallas kernels, body_line(): call(back_kernel, [pltpu.HBM((capacity, 2 * width), BF16)] * peers, in_sp...  6.98 us
    ppermute x7, starting transfers between devices, body_line(): got[k] = lax.ppermute(blocks[k], 'tp', [(i, i ^ k) for i in range(peers)])  6.58 us
    pallas_call x1, Pallas kernels, body_line(): call(functools.partial(hidden_kernel, order), [shaped((slots, inner))] *...  5.53 us
    ppermute x3, waiting for transfers between devices, along(): return lax.ppermute(rows, 'ctx', [(i, i ^ step) for i in range(4)])  4.77 us
  transfers between devices with their start and end apart: 18, of which 11 were waited for; matrix products, arithmetic and copies ran while one was open for 0% of the time, Pallas kernels for 18%

profile of v7, /device:TPU:0, one launch (start us, length us, event | category | flops | bytes accessed | tf_op | source)
XLA Modules:
  0.0 76.9 jit_solution(15962768501954370611)
XLA Ops:
  0.6 3.1 %shard_map.102 = (s32[2,128]{1,0:T(2,128)S(1)}, bf16[2064,128]{1,0:T(8,128)(2,1)}, bf16[24,4096]{1,0:T(8,128)(2,1)}, bf16[24,4096]{1,0:T(8,128)(2,1)}, bf16[24,4...) custom-call(s32[1,128]{1,0:T(1,128)} %bitcast.16, ...), custom_call_target="tpu_custom_call" | custom-call | flops 1 | bytes 1 | tf_op jit(solution)/shard_map/pallas_call | solution.py:329
  3.8 5.0 %collective-permute-start.8 = (bf16[2064,128]{1,0:T(8,128)(2,1)}, bf16[2064,128]{1,0:T(8,128)(2,1)S(1)}, u32[]{:S(2)}, u32[]{:S(2)}) collective-permute-start(bf16[2064,128]{1,0:T(8,128)(2,1)} %get-tuple-element.50), channel_id=1, source_target_pairs={{0,24},{8,16},{16,8},{24,0},{1,25},{9,17},{17,9},{25,1},{2,26},{10... | collective-permute-start | bytes 1585160 | tf_op jit(solution)/shard_map/ppermute | solution.py:309
  8.8 2.4 %collective-permute-start = (bf16[24,4096]{1,0:T(8,128)(2,1)}, bf16[24,4096]{1,0:T(8,128)(2,1)S(1)}, u32[]{:S(2)}, u32[]{:S(2)}) collective-permute-start(bf16[24,4096]{1,0:T(8,128)(2,1)} %get-tuple-element.34), channel_id=1, source_target_pairs={{0,6},{1,7},{2,4},{3,5},{4,2},{5,3},{6,0},{7,1},{8,14},{9,15},{10,... | collective-permute-start | bytes 589832 | tf_op jit(solution)/shard_map/ppermute | solution.py:341
  11.3 0.8 %collective-permute-start.2 = (bf16[24,4096]{1,0:T(8,128)(2,1)}, bf16[24,4096]{1,0:T(8,128)(2,1)S(1)}, u32[]{:S(2)}, u32[]{:S(2)}) collective-permute-start(bf16[24,4096]{1,0:T(8,128)(2,1)} %get-tuple-element.36), channel_id=1, source_target_pairs={{0,2},{1,3},{2,0},{3,1},{4,6},{5,7},{6,4},{7,5},{8,10},{9,11},{10,... | collective-permute-start | bytes 589832 | tf_op jit(solution)/shard_map/ppermute | solution.py:341
  12.1 1.5 %collective-permute-start.3 = (bf16[24,4096]{1,0:T(8,128)(2,1)}, bf16[24,4096]{1,0:T(8,128)(2,1)S(1)}, u32[]{:S(2)}, u32[]{:S(2)}) collective-permute-start(bf16[24,4096]{1,0:T(8,128)(2,1)} %get-tuple-element.37), channel_id=1, source_target_pairs={{0,4},{1,5},{2,6},{3,7},{4,0},{5,1},{6,2},{7,3},{8,12},{9,13},{10,... | collective-permute-start | bytes 589832 | tf_op jit(solution)/shard_map/ppermute | solution.py:341
  13.6 3.6 %collective-permute-done.refs_0_ = bf16[24,4096]{1,0:T(8,128)(2,1)S(1)} collective-permute-done((bf16[24,4096]{1,0:T(8,128)(2,1)}, bf16[24,4096]{1,0:T(8,128)(2,1)S(1)}, u32[]{:S(2)}, u32[]{:S(2)}) %collective-permute-start) | collective-permute-done | bytes 196640 | tf_op jit(solution)/shard_map/ppermute | solution.py:341
  17.2 3.9 %collective-permute-done.1.refs_1_ = bf16[24,4096]{1,0:T(8,128)(2,1)S(1)} collective-permute-done((bf16[24,4096]{1,0:T(8,128)(2,1)}, bf16[24,4096]{1,0:T(8,128)(2,1)S(1)}, u32[]{:S(2)}, u32[]{:S(2)}) %collective-permute-start.1) | collective-permute-done | bytes 196640 | tf_op jit(solution)/shard_map/ppermute | solution.py:341
  21.2 1.8 %collective-permute-start.5 = (bf16[24,4096]{1,0:T(8,128)(2,1)}, bf16[24,4096]{1,0:T(8,128)(2,1)S(1)}, u32[]{:S(2)}, u32[]{:S(2)}) collective-permute-start(bf16[24,4096]{1,0:T(8,128)(2,1)} %get-tuple-element.39), channel_id=1, source_target_pairs={{0,5},{1,4},{2,7},{3,6},{4,1},{5,0},{6,3},{7,2},{8,13},{9,12},{10,... | collective-permute-start | bytes 589832 | tf_op jit(solution)/shard_map/ppermute | solution.py:341
  22.9 3.3 %collective-permute-done.2.refs_2_ = bf16[24,4096]{1,0:T(8,128)(2,1)S(1)} collective-permute-done((bf16[24,4096]{1,0:T(8,128)(2,1)}, bf16[24,4096]{1,0:T(8,128)(2,1)S(1)}, u32[]{:S(2)}, u32[]{:S(2)}) %collective-permute-start.2) | collective-permute-done | bytes 196640 | tf_op jit(solution)/shard_map/ppermute | solution.py:341
  26.3 1.9 %collective-permute-done.4.refs_4_ = bf16[24,4096]{1,0:T(8,128)(2,1)S(1)} collective-permute-done((bf16[24,4096]{1,0:T(8,128)(2,1)}, bf16[24,4096]{1,0:T(8,128)(2,1)S(1)}, u32[]{:S(2)}, u32[]{:S(2)}) %collective-permute-start.4) | collective-permute-done | bytes 196640 | tf_op jit(solution)/shard_map/ppermute | solution.py:341
  28.1 0.8 %collective-permute-done.5.refs_5_ = bf16[24,4096]{1,0:T(8,128)(2,1)S(1)} collective-permute-done((bf16[24,4096]{1,0:T(8,128)(2,1)}, bf16[24,4096]{1,0:T(8,128)(2,1)S(1)}, u32[]{:S(2)}, u32[]{:S(2)}) %collective-permute-start.5) | collective-permute-done | bytes 196640 | tf_op jit(solution)/shard_map/ppermute | solution.py:341
  28.9 1.2 %shard_map.105 = bf16[192,2048]{1,0:T(8,128)(2,1)} custom-call(bf16[2064,128]{1,0:T(8,128)(2,1)S(1)} %collective-permute-done.8.rows, bf16[24,4096]{1,0:T(8,128)(2,1)S(1)} %collective-permute-done.refs_0_, bf16[24,4096]{1,0:T(8,128)(2,1)S(1)} %collective-permute-done.1.refs_1_, bf16[24,4096]{1,0:T(8,128)(2,1)S(1)} %collective-permute-done.2.refs_2_, ...), custom_call_target="tpu_custom_call" | custom-call | flops 1 | bytes 1 | tf_op jit(solution)/shard_map/pallas_call | solution.py:364
  30.2 3.5 %all-to-all-start = ((bf16[8,24,2048]{2,1,0:T(8,128)(2,1)}), bf16[8,24,2048]{2,1,0:T(8,128)(2,1)S(1)}, u32[]{:S(2)}, u32[]{:S(2)}) async-start(bf16[8,24,2048]{2,1,0:T(8,128)(2,1)} %bitcast.5), calls=%async_computation | async-start | bytes 1572864 | tf_op jit(solution)/shard_map/all_to_all | solution.py:325
  33.7 5.5 %shard_map.103 = (bf16[192,768]{1,0:T(8,128)(2,1)S(1)}, bf16[192,768]{1,0:T(8,128)(2,1)S(1)}, bf16[192,768]{1,0:T(8,128)(2,1)S(1)}, bf16[192,384]{1,0:T(8,128)(2...) custom-call(bf16[24,4096]{1,0:T(8,128)(2,1)S(1)} %collective-permute-done.refs_0_, ...), custom_call_target="tpu_custom_call" | custom-call | flops 1 | bytes 1 | tf_op jit(solution)/shard_map/pallas_call | solution.py:348
  39.2 0.1 collective-permute-start.7
  39.3 7.0 %shard_map.104 = (bf16[24,4096]{1,0:T(8,128)(2,1)}, bf16[24,4096]{1,0:T(8,128)(2,1)}, bf16[24,4096]{1,0:T(8,128)(2,1)}, bf16[24,4096]{1,0:T(8,128)(2,1)}, bf16[2...) custom-call(bf16[192,768]{1,0:T(8,128)(2,1)S(1)} %get-tuple-element.42.hidde, ...), custom_call_target="tpu_custom_call" | custom-call | flops 1 | bytes 1 | tf_op jit(solution)/shard_map/pallas_call | solution.py:368
  46.3 0.0 copy-start
  46.3 0.0 copy-start.1
  46.3 1.3 %collective-permute-done.7.h_remote = bf16[192,384]{1,0:T(8,128)(2,1)S(1)} collective-permute-done((bf16[192,384]{1,0:T(8,128)(2,1)}, bf16[192,384]{1,0:T(8,128)(2,1)S(1)}, u32[]{:S(2)}, u32[]{:S(2)}) %collective-permute-start.7) | collective-permute-done | bytes 147488 | tf_op jit(solution)/shard_map/ppermute | solution.py:309
  47.6 2.6 %shard_map.106 = (bf16[192,2048]{1,0:T(8,128)(2,1)S(1)}, bf16[192,2048]{1,0:T(8,128)(2,1)}) custom-call(bf16[24,4096]{1,0:T(8,128)(2,1)} %get-tuple-element.46.after.refs_7_, bf16[192,384]{1,0:T(8,128)(2,1)} %get-tuple-element.47.h_own, bf16[192,384]{1,0:T(8,128)(2,1)S(1)} %collective-permute-done.7.h_remote, bf16[192,2048]{1,0:T(8,128)(2,1)} %get-tuple-element.49.own, ...), custom_call_target="tpu_custom_call" | custom-call | flops 1 | bytes 1 | tf_op jit(solution)/shard_map/pallas_call | solution.py:382
  50.2 3.7 %collective-permute-start.9 = (bf16[192,2048]{1,0:T(8,128)(2,1)}, bf16[192,2048]{1,0:T(8,128)(2,1)S(1)}, u32[]{:S(2)}, u32[]{:S(2)}) collective-permute-start(bf16[192,2048]{1,0:T(8,128)(2,1)} %get-tuple-element.52), channel_id=1, source_target_pairs={{0,8},{8,0},{16,24},{24,16},{1,9},{9,1},{17,25},{25,17},{2,10},{10... | collective-permute-start | bytes 2359304 | tf_op jit(solution)/shard_map/ppermute | solution.py:309
  54.0 2.9 %collective-permute-start.10 = (bf16[24,4096]{1,0:T(8,128)(2,1)}, bf16[24,4096]{1,0:T(8,128)(2,1)S(1)}, u32[]{:S(2)}, u32[]{:S(2)}) collective-permute-start(bf16[24,4096]{1,0:T(8,128)(2,1)} %get-tuple-element.54), channel_id=1, source_target_pairs={{0,6},{1,7},{2,4},{3,5},{4,2},{5,3},{6,0},{7,1},{8,14},{9,15},{10,... | collective-permute-start | bytes 589832 | tf_op jit(solution)/shard_map/ppermute | solution.py:378
  56.9 0.9 %collective-permute-start.12 = (bf16[24,4096]{1,0:T(8,128)(2,1)}, bf16[24,4096]{1,0:T(8,128)(2,1)S(1)}, u32[]{:S(2)}, u32[]{:S(2)}) collective-permute-start(bf16[24,4096]{1,0:T(8,128)(2,1)} %get-tuple-element.56), channel_id=1, source_target_pairs={{0,2},{1,3},{2,0},{3,1},{4,6},{5,7},{6,4},{7,5},{8,10},{9,11},{10,... | collective-permute-start | bytes 589832 | tf_op jit(solution)/shard_map/ppermute | solution.py:378
  57.8 1.5 %collective-permute-start.13 = (bf16[24,4096]{1,0:T(8,128)(2,1)}, bf16[24,4096]{1,0:T(8,128)(2,1)S(1)}, u32[]{:S(2)}, u32[]{:S(2)}) collective-permute-start(bf16[24,4096]{1,0:T(8,128)(2,1)} %get-tuple-element.57), channel_id=1, source_target_pairs={{0,4},{1,5},{2,6},{3,7},{4,0},{5,1},{6,2},{7,3},{8,12},{9,13},{10,... | collective-permute-start | bytes 589832 | tf_op jit(solution)/shard_map/ppermute | solution.py:378
  59.3 3.4 %collective-permute-done.10.refs_0_ = bf16[24,4096]{1,0:T(8,128)(2,1)S(1)} collective-permute-done((bf16[24,4096]{1,0:T(8,128)(2,1)}, bf16[24,4096]{1,0:T(8,128)(2,1)S(1)}, u32[]{:S(2)}, u32[]{:S(2)}) %collective-permute-start.10) | collective-permute-done | bytes 196640 | tf_op jit(solution)/shard_map/ppermute | solution.py:378
  62.7 4.1 %collective-permute-done.11.refs_1_ = bf16[24,4096]{1,0:T(8,128)(2,1)S(1)} collective-permute-done((bf16[24,4096]{1,0:T(8,128)(2,1)}, bf16[24,4096]{1,0:T(8,128)(2,1)S(1)}, u32[]{:S(2)}, u32[]{:S(2)}) %collective-permute-start.11) | collective-permute-done | bytes 196640 | tf_op jit(solution)/shard_map/ppermute | solution.py:378
  66.8 1.8 %collective-permute-start.15 = (bf16[24,4096]{1,0:T(8,128)(2,1)}, bf16[24,4096]{1,0:T(8,128)(2,1)S(1)}, u32[]{:S(2)}, u32[]{:S(2)}) collective-permute-start(bf16[24,4096]{1,0:T(8,128)(2,1)} %get-tuple-element.59), channel_id=1, source_target_pairs={{0,5},{1,4},{2,7},{3,6},{4,1},{5,0},{6,3},{7,2},{8,13},{9,12},{10,... | collective-permute-start | bytes 589832 | tf_op jit(solution)/shard_map/ppermute | solution.py:378
  68.6 3.5 %collective-permute-done.9.right = bf16[192,2048]{1,0:T(8,128)(2,1)S(1)} collective-permute-done((bf16[192,2048]{1,0:T(8,128)(2,1)}, bf16[192,2048]{1,0:T(8,128)(2,1)S(1)}, u32[]{:S(2)}, u32[]{:S(2)}) %collective-permute-start.9) | collective-permute-done | bytes 786464 | tf_op jit(solution)/shard_map/ppermute | solution.py:309
  72.1 1.1 %shard_map.107.after = bf16[1,192,2048]{2,1,0:T(8,128)(2,1)} custom-call(bf16[192,2048]{1,0:T(8,128)(2,1)S(1)} %get-tuple-element.51.left, bf16[192,2048]{1,0:T(8,128)(2,1)S(1)} %collective-permute-done.9.right), custom_call_target="tpu_custom_call" | custom-call | flops 1 | bytes 1 | tf_op jit(solution)/shard_map/pallas_call | solution.py:394
  73.2 0.6 collective-permute-done.14.refs_4_
  73.8 0.7 collective-permute-done.15.refs_5_
  74.5 2.4 %shard_map.108 = (bf16[128,2048]{1,0:T(8,128)(2,1)}, bf16[128,2048]{1,0:T(8,128)(2,1)}, f32[1,128]{1,0:T(1,128)}) custom-call(bf16[1,192,2048]{2,1,0:T(8,128)(2,1)} %shard_map.107.after, s32[2,128]{1,0:T(2,128)S(1)} %get-tuple-element.53.slot, f32[1,128]{1,0:T(1,128)S(1)} %bitcast.10, bf16[128,2048]{1,0:T(8,128)(2,1)S(1)} %copy-done, ...), custom_call_target="tpu_custom_call" | custom-call | flops 1 | bytes 1 | tf_op jit(solution)/shard_map/pallas_call | solution.py:395
  (15 shorter events, 0.0 us)
Async XLA Ops:
  3.8 25.2 %collective-permute-start.8 = (bf16[2064,128]{1,0:T(8,128)(2,1)}, bf16[2064,128]{1,0:T(8,128)(2,1)S(1)}, u32[]{:S(2)}, u32[]{:S(2)}) collective-permute-start(bf16[2064,128]{1,0:T(8,128)(2,1)} %get-tuple-element.50), channel_id=1, source_target_pairs={{0,24},{8,16},{16,8},{24,0},{1,25},{9,17},{17,9},{25,1},{2,26},{10... | collective-permute-start | bytes 1585160 | tf_op jit(solution)/shard_map/ppermute | solution.py:309
  8.8 8.4 %collective-permute-start = (bf16[24,4096]{1,0:T(8,128)(2,1)}, bf16[24,4096]{1,0:T(8,128)(2,1)S(1)}, u32[]{:S(2)}, u32[]{:S(2)}) collective-permute-start(bf16[24,4096]{1,0:T(8,128)(2,1)} %get-tuple-element.34), channel_id=1, source_target_pairs={{0,6},{1,7},{2,4},{3,5},{4,2},{5,3},{6,0},{7,1},{8,14},{9,15},{10,... | collective-permute-start | bytes 589832 | tf_op jit(solution)/shard_map/ppermute | solution.py:341
  11.2 9.9 %collective-permute-start.1 = (bf16[24,4096]{1,0:T(8,128)(2,1)}, bf16[24,4096]{1,0:T(8,128)(2,1)S(1)}, u32[]{:S(2)}, u32[]{:S(2)}) collective-permute-start(bf16[24,4096]{1,0:T(8,128)(2,1)} %get-tuple-element.35), channel_id=1, source_target_pairs={{0,7},{1,6},{2,5},{3,4},{4,3},{5,2},{6,1},{7,0},{8,15},{9,14},{10,... | collective-permute-start | bytes 589832 | tf_op jit(solution)/shard_map/ppermute | solution.py:341
  11.3 15.0 %collective-permute-start.2 = (bf16[24,4096]{1,0:T(8,128)(2,1)}, bf16[24,4096]{1,0:T(8,128)(2,1)S(1)}, u32[]{:S(2)}, u32[]{:S(2)}) collective-permute-start(bf16[24,4096]{1,0:T(8,128)(2,1)} %get-tuple-element.36), channel_id=1, source_target_pairs={{0,2},{1,3},{2,0},{3,1},{4,6},{5,7},{6,4},{7,5},{8,10},{9,11},{10,... | collective-permute-start | bytes 589832 | tf_op jit(solution)/shard_map/ppermute | solution.py:341
  12.1 14.2 %collective-permute-start.3 = (bf16[24,4096]{1,0:T(8,128)(2,1)}, bf16[24,4096]{1,0:T(8,128)(2,1)S(1)}, u32[]{:S(2)}, u32[]{:S(2)}) collective-permute-start(bf16[24,4096]{1,0:T(8,128)(2,1)} %get-tuple-element.37), channel_id=1, source_target_pairs={{0,4},{1,5},{2,6},{3,7},{4,0},{5,1},{6,2},{7,3},{8,12},{9,13},{10,... | collective-permute-start | bytes 589832 | tf_op jit(solution)/shard_map/ppermute | solution.py:341
  17.2 10.9 %collective-permute-start.4 = (bf16[24,4096]{1,0:T(8,128)(2,1)}, bf16[24,4096]{1,0:T(8,128)(2,1)S(1)}, u32[]{:S(2)}, u32[]{:S(2)}) collective-permute-start(bf16[24,4096]{1,0:T(8,128)(2,1)} %get-tuple-element.38), channel_id=1, source_target_pairs={{0,3},{1,2},{2,1},{3,0},{4,7},{5,6},{6,5},{7,4},{8,11},{9,10},{10,... | collective-permute-start | bytes 589832 | tf_op jit(solution)/shard_map/ppermute | solution.py:341
  21.2 7.7 %collective-permute-start.5 = (bf16[24,4096]{1,0:T(8,128)(2,1)}, bf16[24,4096]{1,0:T(8,128)(2,1)S(1)}, u32[]{:S(2)}, u32[]{:S(2)}) collective-permute-start(bf16[24,4096]{1,0:T(8,128)(2,1)} %get-tuple-element.39), channel_id=1, source_target_pairs={{0,5},{1,4},{2,7},{3,6},{4,1},{5,0},{6,3},{7,2},{8,13},{9,12},{10,... | collective-permute-start | bytes 589832 | tf_op jit(solution)/shard_map/ppermute | solution.py:341
  26.3 2.7 %collective-permute-start.6 = (bf16[24,4096]{1,0:T(8,128)(2,1)}, bf16[24,4096]{1,0:T(8,128)(2,1)S(1)}, u32[]{:S(2)}, u32[]{:S(2)}) collective-permute-start(bf16[24,4096]{1,0:T(8,128)(2,1)} %get-tuple-element.40), channel_id=1, source_target_pairs={{0,1},{1,0},{2,3},{3,2},{4,5},{5,4},{6,7},{7,6},{8,9},{9,8},{10,11... | collective-permute-start | bytes 589832 | tf_op jit(solution)/shard_map/ppermute | solution.py:341
  30.2 17.5 %all-to-all-start = ((bf16[8,24,2048]{2,1,0:T(8,128)(2,1)}), bf16[8,24,2048]{2,1,0:T(8,128)(2,1)S(1)}, u32[]{:S(2)}, u32[]{:S(2)}) async-start(bf16[8,24,2048]{2,1,0:T(8,128)(2,1)} %bitcast.5), calls=%async_computation | async-start | bytes 1572864 | tf_op jit(solution)/shard_map/all_to_all | solution.py:325
  39.2 8.4 %collective-permute-start.7 = (bf16[192,384]{1,0:T(8,128)(2,1)}, bf16[192,384]{1,0:T(8,128)(2,1)S(1)}, u32[]{:S(2)}, u32[]{:S(2)}) collective-permute-start(bf16[192,384]{1,0:T(8,128)(2,1)} %get-tuple-element.48), channel_id=1, source_target_pairs={{0,24},{8,16},{16,8},{24,0},{1,25},{9,17},{17,9},{25,1},{2,26},{10... | collective-permute-start | bytes 442376 | tf_op jit(solution)/shard_map/ppermute | solution.py:309
  46.3 28.2 %copy-start = (bf16[128,2048]{1,0:T(8,128)(2,1)S(1)}, bf16[128,2048]{1,0:T(8,128)(2,1)}, u32[]{:S(2)}) copy-start(bf16[128,2048]{1,0:T(8,128)(2,1)} %cot.3) | copy-start | bytes 1572868
  46.3 28.1 %copy-start.1 = (f32[128,1]{0,1:T(1,128)S(1)}, f32[128,1]{0,1:T(1,128)}, u32[]{:S(2)}) copy-start(f32[128,1]{0,1:T(1,128)} %param.10) | copy-start | bytes 1540
  50.2 21.8 %collective-permute-start.9 = (bf16[192,2048]{1,0:T(8,128)(2,1)}, bf16[192,2048]{1,0:T(8,128)(2,1)S(1)}, u32[]{:S(2)}, u32[]{:S(2)}) collective-permute-start(bf16[192,2048]{1,0:T(8,128)(2,1)} %get-tuple-element.52), channel_id=1, source_target_pairs={{0,8},{8,0},{16,24},{24,16},{1,9},{9,1},{17,25},{25,17},{2,10},{10... | collective-permute-start | bytes 2359304 | tf_op jit(solution)/shard_map/ppermute | solution.py:309
  54.0 8.7 %collective-permute-start.10 = (bf16[24,4096]{1,0:T(8,128)(2,1)}, bf16[24,4096]{1,0:T(8,128)(2,1)S(1)}, u32[]{:S(2)}, u32[]{:S(2)}) collective-permute-start(bf16[24,4096]{1,0:T(8,128)(2,1)} %get-tuple-element.54), channel_id=1, source_target_pairs={{0,6},{1,7},{2,4},{3,5},{4,2},{5,3},{6,0},{7,1},{8,14},{9,15},{10,... | collective-permute-start | bytes 589832 | tf_op jit(solution)/shard_map/ppermute | solution.py:378
  56.9 9.9 %collective-permute-start.11 = (bf16[24,4096]{1,0:T(8,128)(2,1)}, bf16[24,4096]{1,0:T(8,128)(2,1)S(1)}, u32[]{:S(2)}, u32[]{:S(2)}) collective-permute-start(bf16[24,4096]{1,0:T(8,128)(2,1)} %get-tuple-element.55), channel_id=1, source_target_pairs={{0,7},{1,6},{2,5},{3,4},{4,3},{5,2},{6,1},{7,0},{8,15},{9,14},{10,... | collective-permute-start | bytes 589832 | tf_op jit(solution)/shard_map/ppermute | solution.py:378
  56.9 16.3 %collective-permute-start.12 = (bf16[24,4096]{1,0:T(8,128)(2,1)}, bf16[24,4096]{1,0:T(8,128)(2,1)S(1)}, u32[]{:S(2)}, u32[]{:S(2)}) collective-permute-start(bf16[24,4096]{1,0:T(8,128)(2,1)} %get-tuple-element.56), channel_id=1, source_target_pairs={{0,2},{1,3},{2,0},{3,1},{4,6},{5,7},{6,4},{7,5},{8,10},{9,11},{10,... | collective-permute-start | bytes 589832 | tf_op jit(solution)/shard_map/ppermute | solution.py:378
  57.8 15.3 %collective-permute-start.13 = (bf16[24,4096]{1,0:T(8,128)(2,1)}, bf16[24,4096]{1,0:T(8,128)(2,1)S(1)}, u32[]{:S(2)}, u32[]{:S(2)}) collective-permute-start(bf16[24,4096]{1,0:T(8,128)(2,1)} %get-tuple-element.57), channel_id=1, source_target_pairs={{0,4},{1,5},{2,6},{3,7},{4,0},{5,1},{6,2},{7,3},{8,12},{9,13},{10,... | collective-permute-start | bytes 589832 | tf_op jit(solution)/shard_map/ppermute | solution.py:378
  62.7 11.1 %collective-permute-start.14 = (bf16[24,4096]{1,0:T(8,128)(2,1)}, bf16[24,4096]{1,0:T(8,128)(2,1)S(1)}, u32[]{:S(2)}, u32[]{:S(2)}) collective-permute-start(bf16[24,4096]{1,0:T(8,128)(2,1)} %get-tuple-element.58), channel_id=1, source_target_pairs={{0,3},{1,2},{2,1},{3,0},{4,7},{5,6},{6,5},{7,4},{8,11},{9,10},{10,... | collective-permute-start | bytes 589832 | tf_op jit(solution)/shard_map/ppermute | solution.py:378
  66.8 7.7 %collective-permute-start.15 = (bf16[24,4096]{1,0:T(8,128)(2,1)}, bf16[24,4096]{1,0:T(8,128)(2,1)S(1)}, u32[]{:S(2)}, u32[]{:S(2)}) collective-permute-start(bf16[24,4096]{1,0:T(8,128)(2,1)} %get-tuple-element.59), channel_id=1, source_target_pairs={{0,5},{1,4},{2,7},{3,6},{4,1},{5,0},{6,3},{7,2},{8,13},{9,12},{10,... | collective-permute-start | bytes 589832 | tf_op jit(solution)/shard_map/ppermute | solution.py:378
  72.1 2.4 %collective-permute-start.16 = (bf16[24,4096]{1,0:T(8,128)(2,1)}, bf16[24,4096]{1,0:T(8,128)(2,1)S(1)}, u32[]{:S(2)}, u32[]{:S(2)}) collective-permute-start(bf16[24,4096]{1,0:T(8,128)(2,1)} %get-tuple-element.60), channel_id=1, source_target_pairs={{0,1},{1,0},{2,3},{3,2},{4,5},{5,4},{6,7},{7,6},{8,9},{9,8},{10,11... | collective-permute-start | bytes 589832 | tf_op jit(solution)/shard_map/ppermute | solution.py:378

commit v8 on v7

--- a/solution.py
+++ b/solution.py
@@ -179,8 +179,8 @@
 
 def hidden_kernel(order, *refs):
     peers = len(order)
-    blocks, (gate, up, hidden, by_up, by_pre, near, far, cot, same) = refs[:peers], refs[peers : peers + 9]
-    gate_in, up_in, wide, rows, sems = refs[peers + 9 :]
+    blocks, (gate, up, hidden, by_up, by_pre, near, far, cot) = refs[:peers], refs[peers : peers + 8]
+    gate_in, up_in, wide, rows, sems = refs[peers + 8 :]
     width, inner = gate.shape
     capacity = blocks[0].shape[0]
     step = inner // TILES
@@ -189,10 +189,9 @@
         [((gate.at[:, t], gate_in.at[:, t]), (up.at[:, t], up_in.at[:, t])) for t in tiles], sems
     )
     for k, block in zip(order, blocks):
-        wide[k * capacity : (k + 1) * capacity, :] = block[...].astype(F32)
-    rows[...] = wide[:, :width].astype(BF16)
-    cot[...] = wide[:, width:].astype(BF16)
-    same[...] = cot[...]
+        at = slice(k * capacity, (k + 1) * capacity)
+        rows[at] = block[:, :width]
+        cot[at] = block[:, width:]
     for t in tiles:
         arrive()
         pre = jnp.dot(rows[...], gate_in[:, t], preferred_element_type=F32)
@@ -210,8 +209,8 @@
     own = lax.axis_index("tp")
     for k in range(peers):
         start = pl.multiple_of((own ^ k) * capacity, 8)
-        wide[pl.ds(start, capacity), :half] = gone[k * capacity : (k + 1) * capacity]
-    far[...] = wide[:, :half].astype(BF16)
+        wide[pl.ds(start, capacity), :] = gone[k * capacity : (k + 1) * capacity]
+    far[...] = wide[...].astype(BF16)
 
 
 def back_kernel(
@@ -283,7 +282,7 @@
     count, width = cot.shape
     capacity = blocks[0].shape[0]
     for k, block in zip(order, blocks):
-        wide[k * capacity : (k + 1) * capacity, :] = block[...].astype(F32)
+        wide[k * capacity : (k + 1) * capacity, :] = block[...]
     placing = (
         lax.broadcasted_iota(jnp.int32, (count, wide.shape[0]), 1) == column(slot[1:2])
     ).astype(BF16)
@@ -292,11 +291,11 @@
     step = 512
     for at in range(0, width, step):
         cols, later = slice(at, at + step), slice(width + at, width + at + step)
-        out_tok = jnp.dot(placing, wide[:, cols].astype(BF16), preferred_element_type=F32)
+        out_tok = jnp.dot(placing, wide[:, cols], preferred_element_type=F32)
         layer_output[:, cols] = (gate * out_tok).astype(BF16)
         total += jnp.sum(cot[:, cols].astype(F32) * out_tok, axis=1, keepdims=True)
         token_grad[:, cols] = jnp.dot(
-            placing, wide[:, later].astype(BF16), preferred_element_type=F32
+            placing, wide[:, later], preferred_element_type=F32
         ).astype(BF16)
     gate_grad[...] = jnp.sum(jnp.where(diagonal(count), total, 0.0), axis=0, keepdims=True)
 
@@ -345,20 +344,19 @@
     gate_mat, up_mat, down_mat = [in_hbm(w[0]) for w in (w_gate, w_up, w_down)]
     held = [pltpu.VMEM((width, inner), BF16)] * 2
     dma = pltpu.SemaphoreType.DMA
-    hidden, by_up, by_pre, near, far, cot, same = call(
+    hidden, by_up, by_pre, near, far, cot = call(
         functools.partial(hidden_kernel, order),
         [shaped((slots, inner))] * 3
-        + [pltpu.HBM((slots, inner // 2), BF16)] * 2
-        + [shaped((slots, width)), pltpu.HBM((slots, width), BF16)],
+        + [shaped((slots, inner // 2)), pltpu.HBM((slots, inner // 2), BF16)]
+        + [shaped((slots, width))],
         in_specs=[whole] * peers + [in_place] * 2,
         scratch_shapes=held
         + [
-            pltpu.VMEM((slots, 2 * width), F32),
+            pltpu.VMEM((slots, inner // 2), F32),
             pltpu.VMEM((slots, width), BF16),
             dma((2 * TILES,)),
         ],
     )(*got, gate_mat, up_mat)
-    near, same = in_hbm(near), in_hbm(same)
     far_across = along(far, 3)
     remote = over_tp(
         call(
@@ -388,7 +386,7 @@
             pltpu.VMEM((quarter, width), BF16),
             dma((width // WIDE,)),
         ],
-    )(in_hbm(back[0]), near, far_across, same, remote)
+    )(in_hbm(back[0]), near, far_across, cot, remote)
     swapped = along(other, 1)
 
     down_grad = call(add_kernel, shaped((1, quarter, width)))(mine, swapped)
@@ -396,17 +394,27 @@
         functools.partial(home_kernel, order),
         [shaped((count, width)), shaped((count, width)), shaped((1, count), F32)],
         in_specs=[after] + [whole] * (3 + peers),
-        scratch_shapes=[pltpu.VMEM((slots, 2 * width), F32)],
+        scratch_shapes=[pltpu.VMEM((slots, 2 * width), BF16)],
     )(in_hbm(down_grad), slot, gates, cotangent, *home)
     return layer_output, token_grad, gate_grad.reshape(count, 1), down_grad
+
+
+def body(tokens, cotangent, routes, gate_weights, w_gate, w_up, w_down):
+    count, width = tokens.shape
+    peers, inner = lax.axis_size("tp"), w_gate.shape[2]
+    capacity = 3 * count * routes.shape[1] // (2 * peers)
+    on_line = lax.axis_size("ctx") == 4 and peers == 8
+    even = count == LANES and capacity % 8 == 0 and peers * capacity <= 256
+    tiled = width % (2 * WIDE) == 0 and inner % (2 * TILES * LANES) == 0 and w_gate.shape[0] == 1
+    chosen = body_line if on_line and even and tiled else body_any
+    return chosen(tokens, cotangent, routes, gate_weights, w_gate, w_up, w_down)
 
 
 def solution(mesh):
     rows = P(("ctx", "tp"), None)
     expert = P("tp", None, None)
-    line = mesh.shape["ctx"] == 4 and mesh.shape["tp"] == 8
     return jax.shard_map(
-        body_line if line else body_any,
+        body,
         mesh=mesh,
         in_specs=(rows, rows, rows, rows, expert, expert, expert),
         out_specs=(rows, rows, rows, P("tp", "ctx", None)),

time: 77.1 us -> 75.6 us (0.981)
  Pallas kernels: 23 us -> 21.4 us
    pallas_call x1, Pallas kernels: 2.63 us -> 1.41 us  [body_line(): call(quarters_kernel, [shaped((quarter, width)), pltpu.HBM((quarter, widt...]
where the time goes in v8:
time: 75.6 us; the launch traced here: 75.3 us
  waiting for transfers between devices  27.1 us (36%)
  starting transfers between devices  26 us (34%)
  Pallas kernels  21.4 us (28%)
    ppermute x7, waiting for transfers between devices, body_line(): got[k] = lax.ppermute(blocks[k], 'tp', [(i, i ^ k) for i in range(peers)])  13.5 us
    ppermute x3, starting transfers between devices, along(): return lax.ppermute(rows, 'ctx', [(i, i ^ step) for i in range(4)])  8.8 us
    ppermute x7, waiting for transfers between devices, body_line(): lax.ppermute(back[k], 'tp', [(i, i ^ k) for i in range(peers)])  8.8 us
    ppermute x7, starting transfers between devices, body_line(): lax.ppermute(back[k], 'tp', [(i, i ^ k) for i in range(peers)])  7.1 us
    pallas_call x1, Pallas kernels, body_line(): call(back_kernel, [pltpu.HBM((capacity, 2 * width), BF16)] * peers, in_sp...  6.97 us
    ppermute x7, starting transfers between devices, body_line(): got[k] = lax.ppermute(blocks[k], 'tp', [(i, i ^ k) for i in range(peers)])  6.58 us
    pallas_call x1, Pallas kernels, body_line(): call(functools.partial(hidden_kernel, order), [shaped((slots, inner))] *...  5.23 us
    ppermute x3, waiting for transfers between devices, along(): return lax.ppermute(rows, 'ctx', [(i, i ^ step) for i in range(4)])  4.78 us
  transfers between devices with their start and end apart: 18, of which 11 were waited for; matrix products, arithmetic and copies ran while one was open for 0% of the time, Pallas kernels for 18%

profile of v8, /device:TPU:0, one launch (start us, length us, event | category | flops | bytes accessed | tf_op | source)
XLA Modules:
  0.0 75.3 jit_solution(3677317520069732003)
XLA Ops:
  0.6 3.1 %shard_map.102 = (s32[2,128]{1,0:T(2,128)S(1)}, bf16[2064,128]{1,0:T(8,128)(2,1)}, bf16[24,4096]{1,0:T(8,128)(2,1)}, bf16[24,4096]{1,0:T(8,128)(2,1)}, bf16[24,4...) custom-call(s32[1,128]{1,0:T(1,128)} %bitcast.16, ...), custom_call_target="tpu_custom_call" | custom-call | flops 1 | bytes 1 | tf_op jit(solution)/shard_map/pallas_call | solution.py:328
  3.8 5.0 %collective-permute-start.8 = (bf16[2064,128]{1,0:T(8,128)(2,1)}, bf16[2064,128]{1,0:T(8,128)(2,1)S(1)}, u32[]{:S(2)}, u32[]{:S(2)}) collective-permute-start(bf16[2064,128]{1,0:T(8,128)(2,1)} %get-tuple-element.48), channel_id=1, source_target_pairs={{0,24},{8,16},{16,8},{24,0},{1,25},{9,17},{17,9},{25,1},{2,26},{10... | collective-permute-start | bytes 1585160 | tf_op jit(solution)/shard_map/ppermute | solution.py:308
  8.8 2.4 %collective-permute-start = (bf16[24,4096]{1,0:T(8,128)(2,1)}, bf16[24,4096]{1,0:T(8,128)(2,1)S(1)}, u32[]{:S(2)}, u32[]{:S(2)}) collective-permute-start(bf16[24,4096]{1,0:T(8,128)(2,1)} %get-tuple-element.33), channel_id=1, source_target_pairs={{0,6},{1,7},{2,4},{3,5},{4,2},{5,3},{6,0},{7,1},{8,14},{9,15},{10,... | collective-permute-start | bytes 589832 | tf_op jit(solution)/shard_map/ppermute | solution.py:340
  11.3 0.8 %collective-permute-start.2 = (bf16[24,4096]{1,0:T(8,128)(2,1)}, bf16[24,4096]{1,0:T(8,128)(2,1)S(1)}, u32[]{:S(2)}, u32[]{:S(2)}) collective-permute-start(bf16[24,4096]{1,0:T(8,128)(2,1)} %get-tuple-element.35), channel_id=1, source_target_pairs={{0,2},{1,3},{2,0},{3,1},{4,6},{5,7},{6,4},{7,5},{8,10},{9,11},{10,... | collective-permute-start | bytes 589832 | tf_op jit(solution)/shard_map/ppermute | solution.py:340
  12.1 1.5 %collective-permute-start.3 = (bf16[24,4096]{1,0:T(8,128)(2,1)}, bf16[24,4096]{1,0:T(8,128)(2,1)S(1)}, u32[]{:S(2)}, u32[]{:S(2)}) collective-permute-start(bf16[24,4096]{1,0:T(8,128)(2,1)} %get-tuple-element.36), channel_id=1, source_target_pairs={{0,4},{1,5},{2,6},{3,7},{4,0},{5,1},{6,2},{7,3},{8,12},{9,13},{10,... | collective-permute-start | bytes 589832 | tf_op jit(solution)/shard_map/ppermute | solution.py:340
  13.6 3.6 %collective-permute-done.refs_0_ = bf16[24,4096]{1,0:T(8,128)(2,1)S(1)} collective-permute-done((bf16[24,4096]{1,0:T(8,128)(2,1)}, bf16[24,4096]{1,0:T(8,128)(2,1)S(1)}, u32[]{:S(2)}, u32[]{:S(2)}) %collective-permute-start) | collective-permute-done | bytes 196640 | tf_op jit(solution)/shard_map/ppermute | solution.py:340
  17.2 3.9 %collective-permute-done.1.refs_1_ = bf16[24,4096]{1,0:T(8,128)(2,1)S(1)} collective-permute-done((bf16[24,4096]{1,0:T(8,128)(2,1)}, bf16[24,4096]{1,0:T(8,128)(2,1)S(1)}, u32[]{:S(2)}, u32[]{:S(2)}) %collective-permute-start.1) | collective-permute-done | bytes 196640 | tf_op jit(solution)/shard_map/ppermute | solution.py:340
  21.2 1.8 %collective-permute-start.5 = (bf16[24,4096]{1,0:T(8,128)(2,1)}, bf16[24,4096]{1,0:T(8,128)(2,1)S(1)}, u32[]{:S(2)}, u32[]{:S(2)}) collective-permute-start(bf16[24,4096]{1,0:T(8,128)(2,1)} %get-tuple-element.38), channel_id=1, source_target_pairs={{0,5},{1,4},{2,7},{3,6},{4,1},{5,0},{6,3},{7,2},{8,13},{9,12},{10,... | collective-permute-start | bytes 589832 | tf_op jit(solution)/shard_map/ppermute | solution.py:340
  22.9 3.3 %collective-permute-done.2.refs_2_ = bf16[24,4096]{1,0:T(8,128)(2,1)S(1)} collective-permute-done((bf16[24,4096]{1,0:T(8,128)(2,1)}, bf16[24,4096]{1,0:T(8,128)(2,1)S(1)}, u32[]{:S(2)}, u32[]{:S(2)}) %collective-permute-start.2) | collective-permute-done | bytes 196640 | tf_op jit(solution)/shard_map/ppermute | solution.py:340
  26.3 1.9 %collective-permute-done.4.refs_4_ = bf16[24,4096]{1,0:T(8,128)(2,1)S(1)} collective-permute-done((bf16[24,4096]{1,0:T(8,128)(2,1)}, bf16[24,4096]{1,0:T(8,128)(2,1)S(1)}, u32[]{:S(2)}, u32[]{:S(2)}) %collective-permute-start.4) | collective-permute-done | bytes 196640 | tf_op jit(solution)/shard_map/ppermute | solution.py:340
  28.1 0.8 %collective-permute-done.5.refs_5_ = bf16[24,4096]{1,0:T(8,128)(2,1)S(1)} collective-permute-done((bf16[24,4096]{1,0:T(8,128)(2,1)}, bf16[24,4096]{1,0:T(8,128)(2,1)S(1)}, u32[]{:S(2)}, u32[]{:S(2)}) %collective-permute-start.5) | collective-permute-done | bytes 196640 | tf_op jit(solution)/shard_map/ppermute | solution.py:340
  28.9 1.2 %shard_map.105 = bf16[192,2048]{1,0:T(8,128)(2,1)} custom-call(bf16[2064,128]{1,0:T(8,128)(2,1)S(1)} %collective-permute-done.8.rows, bf16[24,4096]{1,0:T(8,128)(2,1)S(1)} %collective-permute-done.refs_0_, bf16[24,4096]{1,0:T(8,128)(2,1)S(1)} %collective-permute-done.1.refs_1_, bf16[24,4096]{1,0:T(8,128)(2,1)S(1)} %collective-permute-done.2.refs_2_, ...), custom_call_target="tpu_custom_call" | custom-call | flops 1 | bytes 1 | tf_op jit(solution)/shard_map/pallas_call | solution.py:362
  30.2 3.5 %all-to-all-start = ((bf16[8,24,2048]{2,1,0:T(8,128)(2,1)}), bf16[8,24,2048]{2,1,0:T(8,128)(2,1)S(1)}, u32[]{:S(2)}, u32[]{:S(2)}) async-start(bf16[8,24,2048]{2,1,0:T(8,128)(2,1)} %bitcast.5), calls=%async_computation | async-start | bytes 1572864 | tf_op jit(solution)/shard_map/all_to_all | solution.py:324
  33.7 5.2 %shard_map.103 = (bf16[192,768]{1,0:T(8,128)(2,1)S(1)}, bf16[192,768]{1,0:T(8,128)(2,1)S(1)}, bf16[192,768]{1,0:T(8,128)(2,1)S(1)}, bf16[192,384]{1,0:T(8,128)(2...) custom-call(bf16[24,4096]{1,0:T(8,128)(2,1)S(1)} %collective-permute-done.refs_0_, ...), custom_call_target="tpu_custom_call" | custom-call | flops 1 | bytes 1 | tf_op jit(solution)/shard_map/pallas_call | solution.py:347
  38.9 0.1 collective-permute-start.7
  39.0 7.0 %shard_map.104 = (bf16[24,4096]{1,0:T(8,128)(2,1)}, bf16[24,4096]{1,0:T(8,128)(2,1)}, bf16[24,4096]{1,0:T(8,128)(2,1)}, bf16[24,4096]{1,0:T(8,128)(2,1)}, bf16[2...) custom-call(bf16[192,768]{1,0:T(8,128)(2,1)S(1)} %get-tuple-element.41.hidde, ...), custom_call_target="tpu_custom_call" | custom-call | flops 1 | bytes 1 | tf_op jit(solution)/shard_map/pallas_call | solution.py:366
  46.0 0.0 copy-start
  46.0 0.0 copy-start.1
  46.0 1.3 %collective-permute-done.7.h_remote = bf16[192,384]{1,0:T(8,128)(2,1)S(1)} collective-permute-done((bf16[192,384]{1,0:T(8,128)(2,1)}, bf16[192,384]{1,0:T(8,128)(2,1)S(1)}, u32[]{:S(2)}, u32[]{:S(2)}) %collective-permute-start.7) | collective-permute-done | bytes 147488 | tf_op jit(solution)/shard_map/ppermute | solution.py:308
  47.3 1.4 %shard_map.106 = (bf16[192,2048]{1,0:T(8,128)(2,1)S(1)}, bf16[192,2048]{1,0:T(8,128)(2,1)}) custom-call(bf16[24,4096]{1,0:T(8,128)(2,1)} %get-tuple-element.45.after.refs_7_, bf16[192,384]{1,0:T(8,128)(2,1)S(1)} %get-tuple-element.46.h_own, bf16[192,384]{1,0:T(8,128)(2,1)S(1)} %collective-permute-done.7.h_remote, ...), custom_call_target="tpu_custom_call" | custom-call | flops 1 | bytes 1 | tf_op jit(solution)/shard_map/pallas_call | solution.py:380
  48.7 3.7 %collective-permute-start.9 = (bf16[192,2048]{1,0:T(8,128)(2,1)}, bf16[192,2048]{1,0:T(8,128)(2,1)S(1)}, u32[]{:S(2)}, u32[]{:S(2)}) collective-permute-start(bf16[192,2048]{1,0:T(8,128)(2,1)} %get-tuple-element.50), channel_id=1, source_target_pairs={{0,8},{8,0},{16,24},{24,16},{1,9},{9,1},{17,25},{25,17},{2,10},{10... | collective-permute-start | bytes 2359304 | tf_op jit(solution)/shard_map/ppermute | solution.py:308
  52.4 2.9 %collective-permute-start.10 = (bf16[24,4096]{1,0:T(8,128)(2,1)}, bf16[24,4096]{1,0:T(8,128)(2,1)S(1)}, u32[]{:S(2)}, u32[]{:S(2)}) collective-permute-start(bf16[24,4096]{1,0:T(8,128)(2,1)} %get-tuple-element.52), channel_id=1, source_target_pairs={{0,6},{1,7},{2,4},{3,5},{4,2},{5,3},{6,0},{7,1},{8,14},{9,15},{10,... | collective-permute-start | bytes 589832 | tf_op jit(solution)/shard_map/ppermute | solution.py:376
  55.3 0.9 %collective-permute-start.12 = (bf16[24,4096]{1,0:T(8,128)(2,1)}, bf16[24,4096]{1,0:T(8,128)(2,1)S(1)}, u32[]{:S(2)}, u32[]{:S(2)}) collective-permute-start(bf16[24,4096]{1,0:T(8,128)(2,1)} %get-tuple-element.54), channel_id=1, source_target_pairs={{0,2},{1,3},{2,0},{3,1},{4,6},{5,7},{6,4},{7,5},{8,10},{9,11},{10,... | collective-permute-start | bytes 589832 | tf_op jit(solution)/shard_map/ppermute | solution.py:376
  56.3 1.5 %collective-permute-start.13 = (bf16[24,4096]{1,0:T(8,128)(2,1)}, bf16[24,4096]{1,0:T(8,128)(2,1)S(1)}, u32[]{:S(2)}, u32[]{:S(2)}) collective-permute-start(bf16[24,4096]{1,0:T(8,128)(2,1)} %get-tuple-element.55), channel_id=1, source_target_pairs={{0,4},{1,5},{2,6},{3,7},{4,0},{5,1},{6,2},{7,3},{8,12},{9,13},{10,... | collective-permute-start | bytes 589832 | tf_op jit(solution)/shard_map/ppermute | solution.py:376
  57.7 3.4 %collective-permute-done.10.refs_0_ = bf16[24,4096]{1,0:T(8,128)(2,1)S(1)} collective-permute-done((bf16[24,4096]{1,0:T(8,128)(2,1)}, bf16[24,4096]{1,0:T(8,128)(2,1)S(1)}, u32[]{:S(2)}, u32[]{:S(2)}) %collective-permute-start.10) | collective-permute-done | bytes 196640 | tf_op jit(solution)/shard_map/ppermute | solution.py:376
  61.1 4.1 %collective-permute-done.11.refs_1_ = bf16[24,4096]{1,0:T(8,128)(2,1)S(1)} collective-permute-done((bf16[24,4096]{1,0:T(8,128)(2,1)}, bf16[24,4096]{1,0:T(8,128)(2,1)S(1)}, u32[]{:S(2)}, u32[]{:S(2)}) %collective-permute-start.11) | collective-permute-done | bytes 196640 | tf_op jit(solution)/shard_map/ppermute | solution.py:376
  65.2 1.8 %collective-permute-start.15 = (bf16[24,4096]{1,0:T(8,128)(2,1)}, bf16[24,4096]{1,0:T(8,128)(2,1)S(1)}, u32[]{:S(2)}, u32[]{:S(2)}) collective-permute-start(bf16[24,4096]{1,0:T(8,128)(2,1)} %get-tuple-element.57), channel_id=1, source_target_pairs={{0,5},{1,4},{2,7},{3,6},{4,1},{5,0},{6,3},{7,2},{8,13},{9,12},{10,... | collective-permute-start | bytes 589832 | tf_op jit(solution)/shard_map/ppermute | solution.py:376
  67.0 3.5 %collective-permute-done.9.right = bf16[192,2048]{1,0:T(8,128)(2,1)S(1)} collective-permute-done((bf16[192,2048]{1,0:T(8,128)(2,1)}, bf16[192,2048]{1,0:T(8,128)(2,1)S(1)}, u32[]{:S(2)}, u32[]{:S(2)}) %collective-permute-start.9) | collective-permute-done | bytes 786464 | tf_op jit(solution)/shard_map/ppermute | solution.py:308
  70.5 1.1 %shard_map.107.after = bf16[1,192,2048]{2,1,0:T(8,128)(2,1)} custom-call(bf16[192,2048]{1,0:T(8,128)(2,1)S(1)} %get-tuple-element.49.left, bf16[192,2048]{1,0:T(8,128)(2,1)S(1)} %collective-permute-done.9.right), custom_call_target="tpu_custom_call" | custom-call | flops 1 | bytes 1 | tf_op jit(solution)/shard_map/pallas_call | solution.py:392
  71.6 0.6 collective-permute-done.14.refs_4_
  72.2 0.7 collective-permute-done.15.refs_5_
  72.9 2.4 %shard_map.108 = (bf16[128,2048]{1,0:T(8,128)(2,1)}, bf16[128,2048]{1,0:T(8,128)(2,1)}, f32[1,128]{1,0:T(1,128)}) custom-call(bf16[1,192,2048]{2,1,0:T(8,128)(2,1)} %shard_map.107.after, s32[2,128]{1,0:T(2,128)S(1)} %get-tuple-element.51.slot, f32[1,128]{1,0:T(1,128)S(1)} %bitcast.10, bf16[128,2048]{1,0:T(8,128)(2,1)S(1)} %copy-done, ...), custom_call_target="tpu_custom_call" | custom-call | flops 1 | bytes 1 | tf_op jit(solution)/shard_map/pallas_call | solution.py:393
  (15 shorter events, 0.0 us)
Async XLA Ops:
  3.8 25.2 %collective-permute-start.8 = (bf16[2064,128]{1,0:T(8,128)(2,1)}, bf16[2064,128]{1,0:T(8,128)(2,1)S(1)}, u32[]{:S(2)}, u32[]{:S(2)}) collective-permute-start(bf16[2064,128]{1,0:T(8,128)(2,1)} %get-tuple-element.48), channel_id=1, source_target_pairs={{0,24},{8,16},{16,8},{24,0},{1,25},{9,17},{17,9},{25,1},{2,26},{10... | collective-permute-start | bytes 1585160 | tf_op jit(solution)/shard_map/ppermute | solution.py:308
  8.8 8.4 %collective-permute-start = (bf16[24,4096]{1,0:T(8,128)(2,1)}, bf16[24,4096]{1,0:T(8,128)(2,1)S(1)}, u32[]{:S(2)}, u32[]{:S(2)}) collective-permute-start(bf16[24,4096]{1,0:T(8,128)(2,1)} %get-tuple-element.33), channel_id=1, source_target_pairs={{0,6},{1,7},{2,4},{3,5},{4,2},{5,3},{6,0},{7,1},{8,14},{9,15},{10,... | collective-permute-start | bytes 589832 | tf_op jit(solution)/shard_map/ppermute | solution.py:340
  11.2 9.9 %collective-permute-start.1 = (bf16[24,4096]{1,0:T(8,128)(2,1)}, bf16[24,4096]{1,0:T(8,128)(2,1)S(1)}, u32[]{:S(2)}, u32[]{:S(2)}) collective-permute-start(bf16[24,4096]{1,0:T(8,128)(2,1)} %get-tuple-element.34), channel_id=1, source_target_pairs={{0,7},{1,6},{2,5},{3,4},{4,3},{5,2},{6,1},{7,0},{8,15},{9,14},{10,... | collective-permute-start | bytes 589832 | tf_op jit(solution)/shard_map/ppermute | solution.py:340
  11.3 15.0 %collective-permute-start.2 = (bf16[24,4096]{1,0:T(8,128)(2,1)}, bf16[24,4096]{1,0:T(8,128)(2,1)S(1)}, u32[]{:S(2)}, u32[]{:S(2)}) collective-permute-start(bf16[24,4096]{1,0:T(8,128)(2,1)} %get-tuple-element.35), channel_id=1, source_target_pairs={{0,2},{1,3},{2,0},{3,1},{4,6},{5,7},{6,4},{7,5},{8,10},{9,11},{10,... | collective-permute-start | bytes 589832 | tf_op jit(solution)/shard_map/ppermute | solution.py:340
  12.1 14.2 %collective-permute-start.3 = (bf16[24,4096]{1,0:T(8,128)(2,1)}, bf16[24,4096]{1,0:T(8,128)(2,1)S(1)}, u32[]{:S(2)}, u32[]{:S(2)}) collective-permute-start(bf16[24,4096]{1,0:T(8,128)(2,1)} %get-tuple-element.36), channel_id=1, source_target_pairs={{0,4},{1,5},{2,6},{3,7},{4,0},{5,1},{6,2},{7,3},{8,12},{9,13},{10,... | collective-permute-start | bytes 589832 | tf_op jit(solution)/shard_map/ppermute | solution.py:340
  17.2 10.9 %collective-permute-start.4 = (bf16[24,4096]{1,0:T(8,128)(2,1)}, bf16[24,4096]{1,0:T(8,128)(2,1)S(1)}, u32[]{:S(2)}, u32[]{:S(2)}) collective-permute-start(bf16[24,4096]{1,0:T(8,128)(2,1)} %get-tuple-element.37), channel_id=1, source_target_pairs={{0,3},{1,2},{2,1},{3,0},{4,7},{5,6},{6,5},{7,4},{8,11},{9,10},{10,... | collective-permute-start | bytes 589832 | tf_op jit(solution)/shard_map/ppermute | solution.py:340
  21.2 7.7 %collective-permute-start.5 = (bf16[24,4096]{1,0:T(8,128)(2,1)}, bf16[24,4096]{1,0:T(8,128)(2,1)S(1)}, u32[]{:S(2)}, u32[]{:S(2)}) collective-permute-start(bf16[24,4096]{1,0:T(8,128)(2,1)} %get-tuple-element.38), channel_id=1, source_target_pairs={{0,5},{1,4},{2,7},{3,6},{4,1},{5,0},{6,3},{7,2},{8,13},{9,12},{10,... | collective-permute-start | bytes 589832 | tf_op jit(solution)/shard_map/ppermute | solution.py:340
  26.3 2.7 %collective-permute-start.6 = (bf16[24,4096]{1,0:T(8,128)(2,1)}, bf16[24,4096]{1,0:T(8,128)(2,1)S(1)}, u32[]{:S(2)}, u32[]{:S(2)}) collective-permute-start(bf16[24,4096]{1,0:T(8,128)(2,1)} %get-tuple-element.39), channel_id=1, source_target_pairs={{0,1},{1,0},{2,3},{3,2},{4,5},{5,4},{6,7},{7,6},{8,9},{9,8},{10,11... | collective-permute-start | bytes 589832 | tf_op jit(solution)/shard_map/ppermute | solution.py:340
  30.2 17.2 %all-to-all-start = ((bf16[8,24,2048]{2,1,0:T(8,128)(2,1)}), bf16[8,24,2048]{2,1,0:T(8,128)(2,1)S(1)}, u32[]{:S(2)}, u32[]{:S(2)}) async-start(bf16[8,24,2048]{2,1,0:T(8,128)(2,1)} %bitcast.5), calls=%async_computation | async-start | bytes 1572864 | tf_op jit(solution)/shard_map/all_to_all | solution.py:324
  38.9 8.4 %collective-permute-start.7 = (bf16[192,384]{1,0:T(8,128)(2,1)}, bf16[192,384]{1,0:T(8,128)(2,1)S(1)}, u32[]{:S(2)}, u32[]{:S(2)}) collective-permute-start(bf16[192,384]{1,0:T(8,128)(2,1)} %get-tuple-element.47), channel_id=1, source_target_pairs={{0,24},{8,16},{16,8},{24,0},{1,25},{9,17},{17,9},{25,1},{2,26},{10... | collective-permute-start | bytes 442376 | tf_op jit(solution)/shard_map/ppermute | solution.py:308
  46.0 26.9 %copy-start = (bf16[128,2048]{1,0:T(8,128)(2,1)S(1)}, bf16[128,2048]{1,0:T(8,128)(2,1)}, u32[]{:S(2)}) copy-start(bf16[128,2048]{1,0:T(8,128)(2,1)} %cot.3) | copy-start | bytes 1572868
  46.0 26.9 %copy-start.1 = (f32[128,1]{0,1:T(1,128)S(1)}, f32[128,1]{0,1:T(1,128)}, u32[]{:S(2)}) copy-start(f32[128,1]{0,1:T(1,128)} %param.10) | copy-start | bytes 1540
  48.7 21.8 %collective-permute-start.9 = (bf16[192,2048]{1,0:T(8,128)(2,1)}, bf16[192,2048]{1,0:T(8,128)(2,1)S(1)}, u32[]{:S(2)}, u32[]{:S(2)}) collective-permute-start(bf16[192,2048]{1,0:T(8,128)(2,1)} %get-tuple-element.50), channel_id=1, source_target_pairs={{0,8},{8,0},{16,24},{24,16},{1,9},{9,1},{17,25},{25,17},{2,10},{10... | collective-permute-start | bytes 2359304 | tf_op jit(solution)/shard_map/ppermute | solution.py:308
  52.4 8.7 %collective-permute-start.10 = (bf16[24,4096]{1,0:T(8,128)(2,1)}, bf16[24,4096]{1,0:T(8,128)(2,1)S(1)}, u32[]{:S(2)}, u32[]{:S(2)}) collective-permute-start(bf16[24,4096]{1,0:T(8,128)(2,1)} %get-tuple-element.52), channel_id=1, source_target_pairs={{0,6},{1,7},{2,4},{3,5},{4,2},{5,3},{6,0},{7,1},{8,14},{9,15},{10,... | collective-permute-start | bytes 589832 | tf_op jit(solution)/shard_map/ppermute | solution.py:376
  55.3 9.9 %collective-permute-start.11 = (bf16[24,4096]{1,0:T(8,128)(2,1)}, bf16[24,4096]{1,0:T(8,128)(2,1)S(1)}, u32[]{:S(2)}, u32[]{:S(2)}) collective-permute-start(bf16[24,4096]{1,0:T(8,128)(2,1)} %get-tuple-element.53), channel_id=1, source_target_pairs={{0,7},{1,6},{2,5},{3,4},{4,3},{5,2},{6,1},{7,0},{8,15},{9,14},{10,... | collective-permute-start | bytes 589832 | tf_op jit(solution)/shard_map/ppermute | solution.py:376
  55.3 16.3 %collective-permute-start.12 = (bf16[24,4096]{1,0:T(8,128)(2,1)}, bf16[24,4096]{1,0:T(8,128)(2,1)S(1)}, u32[]{:S(2)}, u32[]{:S(2)}) collective-permute-start(bf16[24,4096]{1,0:T(8,128)(2,1)} %get-tuple-element.54), channel_id=1, source_target_pairs={{0,2},{1,3},{2,0},{3,1},{4,6},{5,7},{6,4},{7,5},{8,10},{9,11},{10,... | collective-permute-start | bytes 589832 | tf_op jit(solution)/shard_map/ppermute | solution.py:376
  56.3 15.3 %collective-permute-start.13 = (bf16[24,4096]{1,0:T(8,128)(2,1)}, bf16[24,4096]{1,0:T(8,128)(2,1)S(1)}, u32[]{:S(2)}, u32[]{:S(2)}) collective-permute-start(bf16[24,4096]{1,0:T(8,128)(2,1)} %get-tuple-element.55), channel_id=1, source_target_pairs={{0,4},{1,5},{2,6},{3,7},{4,0},{5,1},{6,2},{7,3},{8,12},{9,13},{10,... | collective-permute-start | bytes 589832 | tf_op jit(solution)/shard_map/ppermute | solution.py:376
  61.1 11.1 %collective-permute-start.14 = (bf16[24,4096]{1,0:T(8,128)(2,1)}, bf16[24,4096]{1,0:T(8,128)(2,1)S(1)}, u32[]{:S(2)}, u32[]{:S(2)}) collective-permute-start(bf16[24,4096]{1,0:T(8,128)(2,1)} %get-tuple-element.56), channel_id=1, source_target_pairs={{0,3},{1,2},{2,1},{3,0},{4,7},{5,6},{6,5},{7,4},{8,11},{9,10},{10,... | collective-permute-start | bytes 589832 | tf_op jit(solution)/shard_map/ppermute | solution.py:376
  65.2 7.7 %collective-permute-start.15 = (bf16[24,4096]{1,0:T(8,128)(2,1)}, bf16[24,4096]{1,0:T(8,128)(2,1)S(1)}, u32[]{:S(2)}, u32[]{:S(2)}) collective-permute-start(bf16[24,4096]{1,0:T(8,128)(2,1)} %get-tuple-element.57), channel_id=1, source_target_pairs={{0,5},{1,4},{2,7},{3,6},{4,1},{5,0},{6,3},{7,2},{8,13},{9,12},{10,... | collective-permute-start | bytes 589832 | tf_op jit(solution)/shard_map/ppermute | solution.py:376
  70.5 2.4 %collective-permute-start.16 = (bf16[24,4096]{1,0:T(8,128)(2,1)}, bf16[24,4096]{1,0:T(8,128)(2,1)S(1)}, u32[]{:S(2)}, u32[]{:S(2)}) collective-permute-start(bf16[24,4096]{1,0:T(8,128)(2,1)} %get-tuple-element.58), channel_id=1, source_target_pairs={{0,1},{1,0},{2,3},{3,2},{4,5},{5,4},{6,7},{7,6},{8,9},{9,8},{10,11... | collective-permute-start | bytes 589832 | tf_op jit(solution)/shard_map/ppermute | solution.py:376

commit v9 on v8

--- a/solution.py
+++ b/solution.py
@@ -331,11 +331,12 @@
             shaped((2, count), jnp.int32),
             pltpu.HBM((width // LANES * count + TAIL, LANES), BF16),
         ]
-        + [pltpu.HBM((capacity, 2 * width), BF16)] * peers,
+        + [shaped((capacity, 2 * width))]
+        + [pltpu.HBM((capacity, 2 * width), BF16)] * (peers - 1),
         scratch_shapes=[pltpu.VMEM((count, width), BF16)],
     )(in_hbm(routes.reshape(1, count)), in_hbm(gates), in_hbm(tokens), in_hbm(cotangent))
     rows_across = along(across, 3)
-    got = {0: in_hbm(blocks[0])}
+    got = {0: blocks[0]}
     for k in range(1, peers):
         got[k] = lax.ppermute(blocks[k], "tp", [(i, i ^ k) for i in range(peers)])
     order = (6, 7, 2, 4, 3, 5, 1, 0)
@@ -365,7 +366,7 @@
     )
     back = call(
         back_kernel,
-        [pltpu.HBM((capacity, 2 * width), BF16)] * peers,
+        [shaped((capacity, 2 * width))] + [pltpu.HBM((capacity, 2 * width), BF16)] * (peers - 1),
         in_specs=[whole] * 4 + [in_place] * 3,
         scratch_shapes=held
         + [pltpu.VMEM((inner, width), BF16)]
@@ -373,7 +374,7 @@
         + [dma((BACK_TILES + 2 * (width // WIDE),))],
     )(hidden, by_up, by_pre, cot, gate_mat, up_mat, down_mat)
     home = [
-        lax.ppermute(back[k], "tp", [(i, i ^ k) for i in range(peers)]) if k else in_hbm(back[0])
+        lax.ppermute(back[k], "tp", [(i, i ^ k) for i in range(peers)]) if k else back[0]
         for k in order
     ]
 
@@ -386,7 +387,7 @@
             pltpu.VMEM((quarter, width), BF16),
             dma((width // WIDE,)),
         ],
-    )(in_hbm(back[0]), near, far_across, cot, remote)
+    )(in_hbm(back[1]), near, far_across, cot, remote)
     swapped = along(other, 1)
 
     down_grad = call(add_kernel, shaped((1, quarter, width)))(mine, swapped)

time: 75.6 us -> 73.5 us (0.972)
  Pallas kernels: 21.4 us -> 19.4 us
    pallas_call x1, Pallas kernels: 2.39 us -> 1.45 us  [body_line(): call(functools.partial(home_kernel, order), [shaped((count, width)), shap...]
    pallas_call x1, Pallas kernels: 5.23 us -> 4.31 us  [body_line(): call(functools.partial(hidden_kernel, order), [shaped((slots, inner))] *...]
  transfers between devices with their start and end apart: 18 -> 18, of which waited for: 11 -> 11; matrix products, arithmetic and copies ran while one was open for 0% -> 0% of each run, Pallas kernels for 18% -> 17%
where the time goes in v9:
time: 73.5 us; the launch traced here: 73.3 us
  waiting for transfers between devices  27.2 us (37%)
  starting transfers between devices  26 us (35%)
  Pallas kernels  19.4 us (26%)
    ppermute x7, waiting for transfers between devices, body_line(): got[k] = lax.ppermute(blocks[k], 'tp', [(i, i ^ k) for i in range(peers)])  13.5 us
    ppermute x7, waiting for transfers between devices, body_line(): lax.ppermute(back[k], 'tp', [(i, i ^ k) for i in range(peers)])  8.8 us
    ppermute x3, starting transfers between devices, along(): return lax.ppermute(rows, 'ctx', [(i, i ^ step) for i in range(4)])  8.78 us
    ppermute x7, starting transfers between devices, body_line(): lax.ppermute(back[k], 'tp', [(i, i ^ k) for i in range(peers)])  7.04 us
    pallas_call x1, Pallas kernels, body_line(): call(back_kernel, [shaped((capacity, 2 * width))] + [pltpu.HBM((capacity,...  6.91 us
    ppermute x7, starting transfers between devices, body_line(): got[k] = lax.ppermute(blocks[k], 'tp', [(i, i ^ k) for i in range(peers)])  6.58 us
    ppermute x3, waiting for transfers between devices, along(): return lax.ppermute(rows, 'ctx', [(i, i ^ step) for i in range(4)])  4.85 us
    pallas_call x1, Pallas kernels, body_line(): call(functools.partial(hidden_kernel, order), [shaped((slots, inner))] *...  4.31 us
  transfers between devices with their start and end apart: 18, of which 11 were waited for; matrix products, arithmetic and copies ran while one was open for 0% of the time, Pallas kernels for 17%

profile of v9, /device:TPU:0, one launch (start us, length us, event | category | flops | bytes accessed | tf_op | source)
XLA Modules:
  0.0 73.3 jit_solution(1174651468844935248)
XLA Ops:
  0.6 3.1 %shard_map.102 = (s32[2,128]{1,0:T(2,128)S(1)}, bf16[2064,128]{1,0:T(8,128)(2,1)}, bf16[24,4096]{1,0:T(8,128)(2,1)S(1)}, bf16[24,4096]{1,0:T(8,128)(2,1)}, bf16[...) custom-call(s32[1,128]{1,0:T(1,128)} %bitcast.16, ...), custom_call_target="tpu_custom_call" | custom-call | flops 1 | bytes 1 | tf_op jit(solution)/shard_map/pallas_call | solution.py:328
  3.7 5.0 %collective-permute-start.8 = (bf16[2064,128]{1,0:T(8,128)(2,1)}, bf16[2064,128]{1,0:T(8,128)(2,1)S(1)}, u32[]{:S(2)}, u32[]{:S(2)}) collective-permute-start(bf16[2064,128]{1,0:T(8,128)(2,1)} %get-tuple-element.48), channel_id=1, source_target_pairs={{0,24},{8,16},{16,8},{24,0},{1,25},{9,17},{17,9},{25,1},{2,26},{10... | collective-permute-start | bytes 1585160 | tf_op jit(solution)/shard_map/ppermute | solution.py:308
  8.7 2.5 %collective-permute-start = (bf16[24,4096]{1,0:T(8,128)(2,1)}, bf16[24,4096]{1,0:T(8,128)(2,1)S(1)}, u32[]{:S(2)}, u32[]{:S(2)}) collective-permute-start(bf16[24,4096]{1,0:T(8,128)(2,1)} %get-tuple-element.33), channel_id=1, source_target_pairs={{0,6},{1,7},{2,4},{3,5},{4,2},{5,3},{6,0},{7,1},{8,14},{9,15},{10,... | collective-permute-start | bytes 589832 | tf_op jit(solution)/shard_map/ppermute | solution.py:341
  11.2 0.8 %collective-permute-start.2 = (bf16[24,4096]{1,0:T(8,128)(2,1)}, bf16[24,4096]{1,0:T(8,128)(2,1)S(1)}, u32[]{:S(2)}, u32[]{:S(2)}) collective-permute-start(bf16[24,4096]{1,0:T(8,128)(2,1)} %get-tuple-element.35), channel_id=1, source_target_pairs={{0,2},{1,3},{2,0},{3,1},{4,6},{5,7},{6,4},{7,5},{8,10},{9,11},{10,... | collective-permute-start | bytes 589832 | tf_op jit(solution)/shard_map/ppermute | solution.py:341
  12.0 1.5 %collective-permute-start.3 = (bf16[24,4096]{1,0:T(8,128)(2,1)}, bf16[24,4096]{1,0:T(8,128)(2,1)S(1)}, u32[]{:S(2)}, u32[]{:S(2)}) collective-permute-start(bf16[24,4096]{1,0:T(8,128)(2,1)} %get-tuple-element.36), channel_id=1, source_target_pairs={{0,4},{1,5},{2,6},{3,7},{4,0},{5,1},{6,2},{7,3},{8,12},{9,13},{10,... | collective-permute-start | bytes 589832 | tf_op jit(solution)/shard_map/ppermute | solution.py:341
  13.5 3.6 %collective-permute-done.refs_0_ = bf16[24,4096]{1,0:T(8,128)(2,1)S(1)} collective-permute-done((bf16[24,4096]{1,0:T(8,128)(2,1)}, bf16[24,4096]{1,0:T(8,128)(2,1)S(1)}, u32[]{:S(2)}, u32[]{:S(2)}) %collective-permute-start) | collective-permute-done | bytes 196640 | tf_op jit(solution)/shard_map/ppermute | solution.py:341
  17.2 3.9 %collective-permute-done.1.refs_1_ = bf16[24,4096]{1,0:T(8,128)(2,1)S(1)} collective-permute-done((bf16[24,4096]{1,0:T(8,128)(2,1)}, bf16[24,4096]{1,0:T(8,128)(2,1)S(1)}, u32[]{:S(2)}, u32[]{:S(2)}) %collective-permute-start.1) | collective-permute-done | bytes 196640 | tf_op jit(solution)/shard_map/ppermute | solution.py:341
  21.1 1.8 %collective-permute-start.5 = (bf16[24,4096]{1,0:T(8,128)(2,1)}, bf16[24,4096]{1,0:T(8,128)(2,1)S(1)}, u32[]{:S(2)}, u32[]{:S(2)}) collective-permute-start(bf16[24,4096]{1,0:T(8,128)(2,1)} %get-tuple-element.38), channel_id=1, source_target_pairs={{0,5},{1,4},{2,7},{3,6},{4,1},{5,0},{6,3},{7,2},{8,13},{9,12},{10,... | collective-permute-start | bytes 589832 | tf_op jit(solution)/shard_map/ppermute | solution.py:341
  22.9 3.3 %collective-permute-done.2.refs_2_ = bf16[24,4096]{1,0:T(8,128)(2,1)S(1)} collective-permute-done((bf16[24,4096]{1,0:T(8,128)(2,1)}, bf16[24,4096]{1,0:T(8,128)(2,1)S(1)}, u32[]{:S(2)}, u32[]{:S(2)}) %collective-permute-start.2) | collective-permute-done | bytes 196640 | tf_op jit(solution)/shard_map/ppermute | solution.py:341
  26.2 1.9 %collective-permute-done.4.refs_4_ = bf16[24,4096]{1,0:T(8,128)(2,1)S(1)} collective-permute-done((bf16[24,4096]{1,0:T(8,128)(2,1)}, bf16[24,4096]{1,0:T(8,128)(2,1)S(1)}, u32[]{:S(2)}, u32[]{:S(2)}) %collective-permute-start.4) | collective-permute-done | bytes 196640 | tf_op jit(solution)/shard_map/ppermute | solution.py:341
  28.0 0.8 %collective-permute-done.5.refs_5_ = bf16[24,4096]{1,0:T(8,128)(2,1)S(1)} collective-permute-done((bf16[24,4096]{1,0:T(8,128)(2,1)}, bf16[24,4096]{1,0:T(8,128)(2,1)S(1)}, u32[]{:S(2)}, u32[]{:S(2)}) %collective-permute-start.5) | collective-permute-done | bytes 196640 | tf_op jit(solution)/shard_map/ppermute | solution.py:341
  28.8 1.2 %shard_map.105 = bf16[192,2048]{1,0:T(8,128)(2,1)} custom-call(bf16[2064,128]{1,0:T(8,128)(2,1)S(1)} %collective-permute-done.8.rows, bf16[24,4096]{1,0:T(8,128)(2,1)S(1)} %collective-permute-done.refs_0_, bf16[24,4096]{1,0:T(8,128)(2,1)S(1)} %collective-permute-done.1.refs_1_, bf16[24,4096]{1,0:T(8,128)(2,1)S(1)} %collective-permute-done.2.refs_2_, ...), custom_call_target="tpu_custom_call" | custom-call | flops 1 | bytes 1 | tf_op jit(solution)/shard_map/pallas_call | solution.py:363
  30.1 3.5 %all-to-all-start = ((bf16[8,24,2048]{2,1,0:T(8,128)(2,1)}), bf16[8,24,2048]{2,1,0:T(8,128)(2,1)S(1)}, u32[]{:S(2)}, u32[]{:S(2)}) async-start(bf16[8,24,2048]{2,1,0:T(8,128)(2,1)} %bitcast.5), calls=%async_computation | async-start | bytes 1572864 | tf_op jit(solution)/shard_map/all_to_all | solution.py:324
  33.6 4.3 %shard_map.103 = (bf16[192,768]{1,0:T(8,128)(2,1)S(1)}, bf16[192,768]{1,0:T(8,128)(2,1)S(1)}, bf16[192,768]{1,0:T(8,128)(2,1)S(1)}, bf16[192,384]{1,0:T(8,128)(2...) custom-call(bf16[24,4096]{1,0:T(8,128)(2,1)S(1)} %collective-permute-done.refs_0_, ...), custom_call_target="tpu_custom_call" | custom-call | flops 1 | bytes 1 | tf_op jit(solution)/shard_map/pallas_call | solution.py:348
  38.0 0.1 collective-permute-start.7
  38.0 6.9 %shard_map.104 = (bf16[24,4096]{1,0:T(8,128)(2,1)S(1)}, bf16[24,4096]{1,0:T(8,128)(2,1)}, bf16[24,4096]{1,0:T(8,128)(2,1)}, bf16[24,4096]{1,0:T(8,128)(2,1)}, bf...) custom-call(bf16[192,768]{1,0:T(8,128)(2,1)S(1)} %get-tuple-element.41.h, ...), custom_call_target="tpu_custom_call" | custom-call | flops 1 | bytes 1 | tf_op jit(solution)/shard_map/pallas_call | solution.py:367
  45.0 0.0 copy-start
  45.0 0.0 copy-start.1
  45.0 1.3 %collective-permute-done.7.h_remote = bf16[192,384]{1,0:T(8,128)(2,1)S(1)} collective-permute-done((bf16[192,384]{1,0:T(8,128)(2,1)}, bf16[192,384]{1,0:T(8,128)(2,1)S(1)}, u32[]{:S(2)}, u32[]{:S(2)}) %collective-permute-start.7) | collective-permute-done | bytes 147488 | tf_op jit(solution)/shard_map/ppermute | solution.py:308
  46.3 1.4 %shard_map.106 = (bf16[192,2048]{1,0:T(8,128)(2,1)S(1)}, bf16[192,2048]{1,0:T(8,128)(2,1)}) custom-call(bf16[24,4096]{1,0:T(8,128)(2,1)} %get-tuple-element.45.after, bf16[192,384]{1,0:T(8,128)(2,1)S(1)} %get-tuple-element.46.h_own, bf16[192,384]{1,0:T(8,128)(2,1)S(1)} %collective-permute-done.7.h_remote, bf16[192,2048]{1,0:T(8,128)(2,1)S(1)} %get-tuple-element.44.cot.own, ...), custom_call_target="tpu_custom_call" | custom-call | flops 1 | bytes 1 | tf_op jit(solution)/shard_map/pallas_call | solution.py:381
  47.7 3.7 %collective-permute-start.9 = (bf16[192,2048]{1,0:T(8,128)(2,1)}, bf16[192,2048]{1,0:T(8,128)(2,1)S(1)}, u32[]{:S(2)}, u32[]{:S(2)}) collective-permute-start(bf16[192,2048]{1,0:T(8,128)(2,1)} %get-tuple-element.50), channel_id=1, source_target_pairs={{0,8},{8,0},{16,24},{24,16},{1,9},{9,1},{17,25},{25,17},{2,10},{10... | collective-permute-start | bytes 2359304 | tf_op jit(solution)/shard_map/ppermute | solution.py:308
  51.4 2.8 %collective-permute-start.10 = (bf16[24,4096]{1,0:T(8,128)(2,1)}, bf16[24,4096]{1,0:T(8,128)(2,1)S(1)}, u32[]{:S(2)}, u32[]{:S(2)}) collective-permute-start(bf16[24,4096]{1,0:T(8,128)(2,1)} %get-tuple-element.52), channel_id=1, source_target_pairs={{0,6},{1,7},{2,4},{3,5},{4,2},{5,3},{6,0},{7,1},{8,14},{9,15},{10,... | collective-permute-start | bytes 589832 | tf_op jit(solution)/shard_map/ppermute | solution.py:377
  54.3 0.9 %collective-permute-start.12 = (bf16[24,4096]{1,0:T(8,128)(2,1)}, bf16[24,4096]{1,0:T(8,128)(2,1)S(1)}, u32[]{:S(2)}, u32[]{:S(2)}) collective-permute-start(bf16[24,4096]{1,0:T(8,128)(2,1)} %get-tuple-element.54), channel_id=1, source_target_pairs={{0,2},{1,3},{2,0},{3,1},{4,6},{5,7},{6,4},{7,5},{8,10},{9,11},{10,... | collective-permute-start | bytes 589832 | tf_op jit(solution)/shard_map/ppermute | solution.py:377
  55.2 1.5 %collective-permute-start.13 = (bf16[24,4096]{1,0:T(8,128)(2,1)}, bf16[24,4096]{1,0:T(8,128)(2,1)S(1)}, u32[]{:S(2)}, u32[]{:S(2)}) collective-permute-start(bf16[24,4096]{1,0:T(8,128)(2,1)} %get-tuple-element.55), channel_id=1, source_target_pairs={{0,4},{1,5},{2,6},{3,7},{4,0},{5,1},{6,2},{7,3},{8,12},{9,13},{10,... | collective-permute-start | bytes 589832 | tf_op jit(solution)/shard_map/ppermute | solution.py:377
  56.7 3.4 %collective-permute-done.10.refs_0_ = bf16[24,4096]{1,0:T(8,128)(2,1)S(1)} collective-permute-done((bf16[24,4096]{1,0:T(8,128)(2,1)}, bf16[24,4096]{1,0:T(8,128)(2,1)S(1)}, u32[]{:S(2)}, u32[]{:S(2)}) %collective-permute-start.10) | collective-permute-done | bytes 196640 | tf_op jit(solution)/shard_map/ppermute | solution.py:377
  60.1 4.1 %collective-permute-done.11.refs_1_ = bf16[24,4096]{1,0:T(8,128)(2,1)S(1)} collective-permute-done((bf16[24,4096]{1,0:T(8,128)(2,1)}, bf16[24,4096]{1,0:T(8,128)(2,1)S(1)}, u32[]{:S(2)}, u32[]{:S(2)}) %collective-permute-start.11) | collective-permute-done | bytes 196640 | tf_op jit(solution)/shard_map/ppermute | solution.py:377
  64.2 1.8 %collective-permute-start.15 = (bf16[24,4096]{1,0:T(8,128)(2,1)}, bf16[24,4096]{1,0:T(8,128)(2,1)S(1)}, u32[]{:S(2)}, u32[]{:S(2)}) collective-permute-start(bf16[24,4096]{1,0:T(8,128)(2,1)} %get-tuple-element.57), channel_id=1, source_target_pairs={{0,5},{1,4},{2,7},{3,6},{4,1},{5,0},{6,3},{7,2},{8,13},{9,12},{10,... | collective-permute-start | bytes 589832 | tf_op jit(solution)/shard_map/ppermute | solution.py:377
  66.0 3.5 %collective-permute-done.9.right = bf16[192,2048]{1,0:T(8,128)(2,1)S(1)} collective-permute-done((bf16[192,2048]{1,0:T(8,128)(2,1)}, bf16[192,2048]{1,0:T(8,128)(2,1)S(1)}, u32[]{:S(2)}, u32[]{:S(2)}) %collective-permute-start.9) | collective-permute-done | bytes 786464 | tf_op jit(solution)/shard_map/ppermute | solution.py:308
  69.5 1.1 %shard_map.107.after = bf16[1,192,2048]{2,1,0:T(8,128)(2,1)} custom-call(bf16[192,2048]{1,0:T(8,128)(2,1)S(1)} %get-tuple-element.49.left, bf16[192,2048]{1,0:T(8,128)(2,1)S(1)} %collective-permute-done.9.right), custom_call_target="tpu_custom_call" | custom-call | flops 1 | bytes 1 | tf_op jit(solution)/shard_map/pallas_call | solution.py:393
  70.5 0.6 collective-permute-done.14.refs_4_
  71.2 0.7 collective-permute-done.15.refs_5_
  71.8 1.4 %shard_map.108 = (bf16[128,2048]{1,0:T(8,128)(2,1)}, bf16[128,2048]{1,0:T(8,128)(2,1)}, f32[1,128]{1,0:T(1,128)}) custom-call(bf16[1,192,2048]{2,1,0:T(8,128)(2,1)} %shard_map.107.after, s32[2,128]{1,0:T(2,128)S(1)} %get-tuple-element.51.slot, f32[1,128]{1,0:T(1,128)S(1)} %bitcast.10, bf16[128,2048]{1,0:T(8,128)(2,1)S(1)} %copy-done, ...), custom_call_target="tpu_custom_call" | custom-call | flops 1 | bytes 1 | tf_op jit(solution)/shard_map/pallas_call | solution.py:394
  (15 shorter events, 0.0 us)
Async XLA Ops:
  3.7 25.2 %collective-permute-start.8 = (bf16[2064,128]{1,0:T(8,128)(2,1)}, bf16[2064,128]{1,0:T(8,128)(2,1)S(1)}, u32[]{:S(2)}, u32[]{:S(2)}) collective-permute-start(bf16[2064,128]{1,0:T(8,128)(2,1)} %get-tuple-element.48), channel_id=1, source_target_pairs={{0,24},{8,16},{16,8},{24,0},{1,25},{9,17},{17,9},{25,1},{2,26},{10... | collective-permute-start | bytes 1585160 | tf_op jit(solution)/shard_map/ppermute | solution.py:308
  8.7 8.4 %collective-permute-start = (bf16[24,4096]{1,0:T(8,128)(2,1)}, bf16[24,4096]{1,0:T(8,128)(2,1)S(1)}, u32[]{:S(2)}, u32[]{:S(2)}) collective-permute-start(bf16[24,4096]{1,0:T(8,128)(2,1)} %get-tuple-element.33), channel_id=1, source_target_pairs={{0,6},{1,7},{2,4},{3,5},{4,2},{5,3},{6,0},{7,1},{8,14},{9,15},{10,... | collective-permute-start | bytes 589832 | tf_op jit(solution)/shard_map/ppermute | solution.py:341
  11.2 9.9 %collective-permute-start.1 = (bf16[24,4096]{1,0:T(8,128)(2,1)}, bf16[24,4096]{1,0:T(8,128)(2,1)S(1)}, u32[]{:S(2)}, u32[]{:S(2)}) collective-permute-start(bf16[24,4096]{1,0:T(8,128)(2,1)} %get-tuple-element.34), channel_id=1, source_target_pairs={{0,7},{1,6},{2,5},{3,4},{4,3},{5,2},{6,1},{7,0},{8,15},{9,14},{10,... | collective-permute-start | bytes 589832 | tf_op jit(solution)/shard_map/ppermute | solution.py:341
  11.2 15.0 %collective-permute-start.2 = (bf16[24,4096]{1,0:T(8,128)(2,1)}, bf16[24,4096]{1,0:T(8,128)(2,1)S(1)}, u32[]{:S(2)}, u32[]{:S(2)}) collective-permute-start(bf16[24,4096]{1,0:T(8,128)(2,1)} %get-tuple-element.35), channel_id=1, source_target_pairs={{0,2},{1,3},{2,0},{3,1},{4,6},{5,7},{6,4},{7,5},{8,10},{9,11},{10,... | collective-permute-start | bytes 589832 | tf_op jit(solution)/shard_map/ppermute | solution.py:341
  12.0 14.2 %collective-permute-start.3 = (bf16[24,4096]{1,0:T(8,128)(2,1)}, bf16[24,4096]{1,0:T(8,128)(2,1)S(1)}, u32[]{:S(2)}, u32[]{:S(2)}) collective-permute-start(bf16[24,4096]{1,0:T(8,128)(2,1)} %get-tuple-element.36), channel_id=1, source_target_pairs={{0,4},{1,5},{2,6},{3,7},{4,0},{5,1},{6,2},{7,3},{8,12},{9,13},{10,... | collective-permute-start | bytes 589832 | tf_op jit(solution)/shard_map/ppermute | solution.py:341
  17.2 10.9 %collective-permute-start.4 = (bf16[24,4096]{1,0:T(8,128)(2,1)}, bf16[24,4096]{1,0:T(8,128)(2,1)S(1)}, u32[]{:S(2)}, u32[]{:S(2)}) collective-permute-start(bf16[24,4096]{1,0:T(8,128)(2,1)} %get-tuple-element.37), channel_id=1, source_target_pairs={{0,3},{1,2},{2,1},{3,0},{4,7},{5,6},{6,5},{7,4},{8,11},{9,10},{10,... | collective-permute-start | bytes 589832 | tf_op jit(solution)/shard_map/ppermute | solution.py:341
  21.1 7.7 %collective-permute-start.5 = (bf16[24,4096]{1,0:T(8,128)(2,1)}, bf16[24,4096]{1,0:T(8,128)(2,1)S(1)}, u32[]{:S(2)}, u32[]{:S(2)}) collective-permute-start(bf16[24,4096]{1,0:T(8,128)(2,1)} %get-tuple-element.38), channel_id=1, source_target_pairs={{0,5},{1,4},{2,7},{3,6},{4,1},{5,0},{6,3},{7,2},{8,13},{9,12},{10,... | collective-permute-start | bytes 589832 | tf_op jit(solution)/shard_map/ppermute | solution.py:341
  26.2 2.7 %collective-permute-start.6 = (bf16[24,4096]{1,0:T(8,128)(2,1)}, bf16[24,4096]{1,0:T(8,128)(2,1)S(1)}, u32[]{:S(2)}, u32[]{:S(2)}) collective-permute-start(bf16[24,4096]{1,0:T(8,128)(2,1)} %get-tuple-element.39), channel_id=1, source_target_pairs={{0,1},{1,0},{2,3},{3,2},{4,5},{5,4},{6,7},{7,6},{8,9},{9,8},{10,11... | collective-permute-start | bytes 589832 | tf_op jit(solution)/shard_map/ppermute | solution.py:341
  30.1 16.2 %all-to-all-start = ((bf16[8,24,2048]{2,1,0:T(8,128)(2,1)}), bf16[8,24,2048]{2,1,0:T(8,128)(2,1)S(1)}, u32[]{:S(2)}, u32[]{:S(2)}) async-start(bf16[8,24,2048]{2,1,0:T(8,128)(2,1)} %bitcast.5), calls=%async_computation | async-start | bytes 1572864 | tf_op jit(solution)/shard_map/all_to_all | solution.py:324
  38.0 8.4 %collective-permute-start.7 = (bf16[192,384]{1,0:T(8,128)(2,1)}, bf16[192,384]{1,0:T(8,128)(2,1)S(1)}, u32[]{:S(2)}, u32[]{:S(2)}) collective-permute-start(bf16[192,384]{1,0:T(8,128)(2,1)} %get-tuple-element.47), channel_id=1, source_target_pairs={{0,24},{8,16},{16,8},{24,0},{1,25},{9,17},{17,9},{25,1},{2,26},{10... | collective-permute-start | bytes 442376 | tf_op jit(solution)/shard_map/ppermute | solution.py:308
  45.0 26.9 %copy-start = (bf16[128,2048]{1,0:T(8,128)(2,1)S(1)}, bf16[128,2048]{1,0:T(8,128)(2,1)}, u32[]{:S(2)}) copy-start(bf16[128,2048]{1,0:T(8,128)(2,1)} %cot.3) | copy-start | bytes 1572868
  45.0 26.9 %copy-start.1 = (f32[128,1]{0,1:T(1,128)S(1)}, f32[128,1]{0,1:T(1,128)}, u32[]{:S(2)}) copy-start(f32[128,1]{0,1:T(1,128)} %param.10) | copy-start | bytes 1540
  47.7 21.7 %collective-permute-start.9 = (bf16[192,2048]{1,0:T(8,128)(2,1)}, bf16[192,2048]{1,0:T(8,128)(2,1)S(1)}, u32[]{:S(2)}, u32[]{:S(2)}) collective-permute-start(bf16[192,2048]{1,0:T(8,128)(2,1)} %get-tuple-element.50), channel_id=1, source_target_pairs={{0,8},{8,0},{16,24},{24,16},{1,9},{9,1},{17,25},{25,17},{2,10},{10... | collective-permute-start | bytes 2359304 | tf_op jit(solution)/shard_map/ppermute | solution.py:308
  51.4 8.6 %collective-permute-start.10 = (bf16[24,4096]{1,0:T(8,128)(2,1)}, bf16[24,4096]{1,0:T(8,128)(2,1)S(1)}, u32[]{:S(2)}, u32[]{:S(2)}) collective-permute-start(bf16[24,4096]{1,0:T(8,128)(2,1)} %get-tuple-element.52), channel_id=1, source_target_pairs={{0,6},{1,7},{2,4},{3,5},{4,2},{5,3},{6,0},{7,1},{8,14},{9,15},{10,... | collective-permute-start | bytes 589832 | tf_op jit(solution)/shard_map/ppermute | solution.py:377
  54.3 9.9 %collective-permute-start.11 = (bf16[24,4096]{1,0:T(8,128)(2,1)}, bf16[24,4096]{1,0:T(8,128)(2,1)S(1)}, u32[]{:S(2)}, u32[]{:S(2)}) collective-permute-start(bf16[24,4096]{1,0:T(8,128)(2,1)} %get-tuple-element.53), channel_id=1, source_target_pairs={{0,7},{1,6},{2,5},{3,4},{4,3},{5,2},{6,1},{7,0},{8,15},{9,14},{10,... | collective-permute-start | bytes 589832 | tf_op jit(solution)/shard_map/ppermute | solution.py:377
  54.3 16.3 %collective-permute-start.12 = (bf16[24,4096]{1,0:T(8,128)(2,1)}, bf16[24,4096]{1,0:T(8,128)(2,1)S(1)}, u32[]{:S(2)}, u32[]{:S(2)}) collective-permute-start(bf16[24,4096]{1,0:T(8,128)(2,1)} %get-tuple-element.54), channel_id=1, source_target_pairs={{0,2},{1,3},{2,0},{3,1},{4,6},{5,7},{6,4},{7,5},{8,10},{9,11},{10,... | collective-permute-start | bytes 589832 | tf_op jit(solution)/shard_map/ppermute | solution.py:377
  55.2 15.3 %collective-permute-start.13 = (bf16[24,4096]{1,0:T(8,128)(2,1)}, bf16[24,4096]{1,0:T(8,128)(2,1)S(1)}, u32[]{:S(2)}, u32[]{:S(2)}) collective-permute-start(bf16[24,4096]{1,0:T(8,128)(2,1)} %get-tuple-element.55), channel_id=1, source_target_pairs={{0,4},{1,5},{2,6},{3,7},{4,0},{5,1},{6,2},{7,3},{8,12},{9,13},{10,... | collective-permute-start | bytes 589832 | tf_op jit(solution)/shard_map/ppermute | solution.py:377
  60.1 11.1 %collective-permute-start.14 = (bf16[24,4096]{1,0:T(8,128)(2,1)}, bf16[24,4096]{1,0:T(8,128)(2,1)S(1)}, u32[]{:S(2)}, u32[]{:S(2)}) collective-permute-start(bf16[24,4096]{1,0:T(8,128)(2,1)} %get-tuple-element.56), channel_id=1, source_target_pairs={{0,3},{1,2},{2,1},{3,0},{4,7},{5,6},{6,5},{7,4},{8,11},{9,10},{10,... | collective-permute-start | bytes 589832 | tf_op jit(solution)/shard_map/ppermute | solution.py:377
  64.2 7.7 %collective-permute-start.15 = (bf16[24,4096]{1,0:T(8,128)(2,1)}, bf16[24,4096]{1,0:T(8,128)(2,1)S(1)}, u32[]{:S(2)}, u32[]{:S(2)}) collective-permute-start(bf16[24,4096]{1,0:T(8,128)(2,1)} %get-tuple-element.57), channel_id=1, source_target_pairs={{0,5},{1,4},{2,7},{3,6},{4,1},{5,0},{6,3},{7,2},{8,13},{9,12},{10,... | collective-permute-start | bytes 589832 | tf_op jit(solution)/shard_map/ppermute | solution.py:377
  69.5 2.4 %collective-permute-start.16 = (bf16[24,4096]{1,0:T(8,128)(2,1)}, bf16[24,4096]{1,0:T(8,128)(2,1)S(1)}, u32[]{:S(2)}, u32[]{:S(2)}) collective-permute-start(bf16[24,4096]{1,0:T(8,128)(2,1)} %get-tuple-element.45.after), channel_id=1, source_target_pairs={{0,1},{1,0},{2,3},{3,2},{4,5},{5,4},{6,7},{7,6},{8,9},{9,8},{10,11... | collective-permute-start | bytes 589832 | tf_op jit(solution)/shard_map/ppermute | solution.py:377

commit v10 on v9

--- a/solution.py
+++ b/solution.py
@@ -245,7 +245,7 @@
         )
 
 
-def quarters_kernel(after, h_own, h_remote, own, remote, mine, other, stage, sems):
+def quarters_kernel(after, h_own, h_remote, own, remote, mine, other):
     width = remote.shape[1]
     even = lax.rem(lax.axis_index("ctx"), 2) == 0
     left, right = h_own[...].astype(F32).T, h_remote[...].astype(F32).T
@@ -256,24 +256,13 @@
         return jnp.where(even, low, high), jnp.where(even, high, low)
 
     (own_mine, own_other), (remote_mine, remote_other) = halves(left), halves(right)
-    leaving = []
-    for i, at in enumerate(range(0, width, WIDE)):
-        cols = slice(at, at + WIDE)
-        stage[:, cols] = (
-            jnp.dot(own_other, own[:, cols], preferred_element_type=F32)
-            + jnp.dot(remote_other, remote[:, cols], preferred_element_type=F32)
-        ).astype(BF16)
-        leave = pltpu.make_async_copy(stage.at[:, cols], other.at[:, cols], sems.at[i])
-        leave.start()
-        leaving.append(leave)
     for at in range(0, width, WIDE):
         cols = slice(at, at + WIDE)
-        mine[:, cols] = (
-            jnp.dot(own_mine, own[:, cols], preferred_element_type=F32)
-            + jnp.dot(remote_mine, remote[:, cols], preferred_element_type=F32)
-        ).astype(BF16)
-    for leave in leaving:
-        leave.wait()
+        for out, left, right in ((other, own_other, remote_other), (mine, own_mine, remote_mine)):
+            out[:, cols] = (
+                jnp.dot(left, own[:, cols], preferred_element_type=F32)
+                + jnp.dot(right, remote[:, cols], preferred_element_type=F32)
+            ).astype(BF16)
 
 
 def home_kernel(order, after, slot, gates, cot, *refs):
@@ -329,7 +318,7 @@
         functools.partial(send_kernel, peers, capacity),
         [
             shaped((2, count), jnp.int32),
-            pltpu.HBM((width // LANES * count + TAIL, LANES), BF16),
+            shaped((width // LANES * count + TAIL, LANES)),
         ]
         + [shaped((capacity, 2 * width))]
         + [pltpu.HBM((capacity, 2 * width), BF16)] * (peers - 1),
@@ -348,7 +337,7 @@
     hidden, by_up, by_pre, near, far, cot = call(
         functools.partial(hidden_kernel, order),
         [shaped((slots, inner))] * 3
-        + [shaped((slots, inner // 2)), pltpu.HBM((slots, inner // 2), BF16)]
+        + [shaped((slots, inner // 2))] * 2
         + [shaped((slots, width))],
         in_specs=[whole] * peers + [in_place] * 2,
         scratch_shapes=held
@@ -380,13 +369,8 @@
 
     mine, other = call(
         quarters_kernel,
-        [shaped((quarter, width)), pltpu.HBM((quarter, width), BF16)],
+        [shaped((quarter, width))] * 2,
         in_specs=[after] + [whole] * 4,
-        out_specs=[whole, in_place],
-        scratch_shapes=[
-            pltpu.VMEM((quarter, width), BF16),
-            dma((width // WIDE,)),
-        ],
     )(in_hbm(back[1]), near, far_across, cot, remote)
     swapped = along(other, 1)
 

time: 73.5 us -> 72.3 us (0.984)
  Pallas kernels: 19.4 us -> 18.4 us
  starting transfers between devices: 26 us -> 25.2 us
  transfers between devices with their start and end apart: 18 -> 18, of which waited for: 11 -> 12; matrix products, arithmetic and copies ran while one was open for 0% -> 0% of each run, Pallas kernels for 17% -> 16%
where the time goes in v10:
time: 72.3 us; the launch traced here: 72.1 us
  waiting for transfers between devices  27.7 us (38%)
  starting transfers between devices  25.2 us (35%)
  Pallas kernels  18.4 us (25%)
    ppermute x7, waiting for transfers between devices, body_line(): got[k] = lax.ppermute(blocks[k], 'tp', [(i, i ^ k) for i in range(peers)])  13.5 us
    ppermute x7, waiting for transfers between devices, body_line(): lax.ppermute(back[k], 'tp', [(i, i ^ k) for i in range(peers)])  9.01 us
    ppermute x3, starting transfers between devices, along(): return lax.ppermute(rows, 'ctx', [(i, i ^ step) for i in range(4)])  8.34 us
    pallas_call x1, Pallas kernels, body_line(): call(back_kernel, [shaped((capacity, 2 * width))] + [pltpu.HBM((capacity,...  6.91 us
    ppermute x7, starting transfers between devices, body_line(): lax.ppermute(back[k], 'tp', [(i, i ^ k) for i in range(peers)])  6.75 us
    ppermute x7, starting transfers between devices, body_line(): got[k] = lax.ppermute(blocks[k], 'tp', [(i, i ^ k) for i in range(peers)])  6.59 us
    ppermute x3, waiting for transfers between devices, along(): return lax.ppermute(rows, 'ctx', [(i, i ^ step) for i in range(4)])  4.43 us
    pallas_call x1, Pallas kernels, body_line(): call(functools.partial(hidden_kernel, order), [shaped((slots, inner))] *...  3.64 us
  transfers between devices with their start and end apart: 18, of which 12 were waited for; matrix products, arithmetic and copies ran while one was open for 0% of the time, Pallas kernels for 16%

profile of v10, /device:TPU:0, one launch (start us, length us, event | category | flops | bytes accessed | tf_op | source)
XLA Modules:
  0.0 72.1 jit_solution(6680700969083964509)
XLA Ops:
  0.6 3.1 %shard_map.102 = (s32[2,128]{1,0:T(2,128)S(1)}, bf16[2064,128]{1,0:T(8,128)(2,1)S(1)}, bf16[24,4096]{1,0:T(8,128)(2,1)S(1)}, bf16[24,4096]{1,0:T(8,128)(2,1)}, b...) custom-call(s32[1,128]{1,0:T(1,128)} %bitcast.16, ...), custom_call_target="tpu_custom_call" | custom-call | flops 1 | bytes 1 | tf_op jit(solution)/shard_map/pallas_call | solution.py:317
  3.7 5.0 %collective-permute-start.8 = (bf16[2064,128]{1,0:T(8,128)(2,1)S(1)}, bf16[2064,128]{1,0:T(8,128)(2,1)S(1)}, u32[]{:S(2)}, u32[]{:S(2)}) collective-permute-start(bf16[2064,128]{1,0:T(8,128)(2,1)S(1)} %get-tuple-element.48), channel_id=1, source_target_pairs={{0,24},{8,16},{16,8},{24,0},{1,25},{9,17},{17,9},{25,1},{2,26},{10... | collective-permute-start | bytes 1585160 | tf_op jit(solution)/shard_map/ppermute | solution.py:297
  8.7 2.4 %collective-permute-start = (bf16[24,4096]{1,0:T(8,128)(2,1)}, bf16[24,4096]{1,0:T(8,128)(2,1)S(1)}, u32[]{:S(2)}, u32[]{:S(2)}) collective-permute-start(bf16[24,4096]{1,0:T(8,128)(2,1)} %get-tuple-element.33), channel_id=1, source_target_pairs={{0,6},{1,7},{2,4},{3,5},{4,2},{5,3},{6,0},{7,1},{8,14},{9,15},{10,... | collective-permute-start | bytes 589832 | tf_op jit(solution)/shard_map/ppermute | solution.py:330
  11.2 0.8 %collective-permute-start.2 = (bf16[24,4096]{1,0:T(8,128)(2,1)}, bf16[24,4096]{1,0:T(8,128)(2,1)S(1)}, u32[]{:S(2)}, u32[]{:S(2)}) collective-permute-start(bf16[24,4096]{1,0:T(8,128)(2,1)} %get-tuple-element.35), channel_id=1, source_target_pairs={{0,2},{1,3},{2,0},{3,1},{4,6},{5,7},{6,4},{7,5},{8,10},{9,11},{10,... | collective-permute-start | bytes 589832 | tf_op jit(solution)/shard_map/ppermute | solution.py:330
  12.0 1.5 %collective-permute-start.3 = (bf16[24,4096]{1,0:T(8,128)(2,1)}, bf16[24,4096]{1,0:T(8,128)(2,1)S(1)}, u32[]{:S(2)}, u32[]{:S(2)}) collective-permute-start(bf16[24,4096]{1,0:T(8,128)(2,1)} %get-tuple-element.36), channel_id=1, source_target_pairs={{0,4},{1,5},{2,6},{3,7},{4,0},{5,1},{6,2},{7,3},{8,12},{9,13},{10,... | collective-permute-start | bytes 589832 | tf_op jit(solution)/shard_map/ppermute | solution.py:330
  13.6 3.6 %collective-permute-done.refs_0_ = bf16[24,4096]{1,0:T(8,128)(2,1)S(1)} collective-permute-done((bf16[24,4096]{1,0:T(8,128)(2,1)}, bf16[24,4096]{1,0:T(8,128)(2,1)S(1)}, u32[]{:S(2)}, u32[]{:S(2)}) %collective-permute-start) | collective-permute-done | bytes 196640 | tf_op jit(solution)/shard_map/ppermute | solution.py:330
  17.2 3.9 %collective-permute-done.1.refs_1_ = bf16[24,4096]{1,0:T(8,128)(2,1)S(1)} collective-permute-done((bf16[24,4096]{1,0:T(8,128)(2,1)}, bf16[24,4096]{1,0:T(8,128)(2,1)S(1)}, u32[]{:S(2)}, u32[]{:S(2)}) %collective-permute-start.1) | collective-permute-done | bytes 196640 | tf_op jit(solution)/shard_map/ppermute | solution.py:330
  21.1 1.8 %collective-permute-start.5 = (bf16[24,4096]{1,0:T(8,128)(2,1)}, bf16[24,4096]{1,0:T(8,128)(2,1)S(1)}, u32[]{:S(2)}, u32[]{:S(2)}) collective-permute-start(bf16[24,4096]{1,0:T(8,128)(2,1)} %get-tuple-element.38), channel_id=1, source_target_pairs={{0,5},{1,4},{2,7},{3,6},{4,1},{5,0},{6,3},{7,2},{8,13},{9,12},{10,... | collective-permute-start | bytes 589832 | tf_op jit(solution)/shard_map/ppermute | solution.py:330
  22.9 3.3 %collective-permute-done.2.refs_2_ = bf16[24,4096]{1,0:T(8,128)(2,1)S(1)} collective-permute-done((bf16[24,4096]{1,0:T(8,128)(2,1)}, bf16[24,4096]{1,0:T(8,128)(2,1)S(1)}, u32[]{:S(2)}, u32[]{:S(2)}) %collective-permute-start.2) | collective-permute-done | bytes 196640 | tf_op jit(solution)/shard_map/ppermute | solution.py:330
  26.2 1.9 %collective-permute-done.4.refs_4_ = bf16[24,4096]{1,0:T(8,128)(2,1)S(1)} collective-permute-done((bf16[24,4096]{1,0:T(8,128)(2,1)}, bf16[24,4096]{1,0:T(8,128)(2,1)S(1)}, u32[]{:S(2)}, u32[]{:S(2)}) %collective-permute-start.4) | collective-permute-done | bytes 196640 | tf_op jit(solution)/shard_map/ppermute | solution.py:330
  28.1 0.8 %collective-permute-done.5.refs_5_ = bf16[24,4096]{1,0:T(8,128)(2,1)S(1)} collective-permute-done((bf16[24,4096]{1,0:T(8,128)(2,1)}, bf16[24,4096]{1,0:T(8,128)(2,1)S(1)}, u32[]{:S(2)}, u32[]{:S(2)}) %collective-permute-start.5) | collective-permute-done | bytes 196640 | tf_op jit(solution)/shard_map/ppermute | solution.py:330
  28.9 1.2 %shard_map.105 = bf16[192,2048]{1,0:T(8,128)(2,1)} custom-call(bf16[2064,128]{1,0:T(8,128)(2,1)S(1)} %collective-permute-done.8.rows, bf16[24,4096]{1,0:T(8,128)(2,1)S(1)} %collective-permute-done.refs_0_, bf16[24,4096]{1,0:T(8,128)(2,1)S(1)} %collective-permute-done.1.refs_1_, bf16[24,4096]{1,0:T(8,128)(2,1)S(1)} %collective-permute-done.2.refs_2_, ...), custom_call_target="tpu_custom_call" | custom-call | flops 1 | bytes 1 | tf_op jit(solution)/shard_map/pallas_call | solution.py:352
  30.1 3.5 %all-to-all-start = ((bf16[8,24,2048]{2,1,0:T(8,128)(2,1)}), bf16[8,24,2048]{2,1,0:T(8,128)(2,1)S(1)}, u32[]{:S(2)}, u32[]{:S(2)}) async-start(bf16[8,24,2048]{2,1,0:T(8,128)(2,1)} %bitcast.5), calls=%async_computation | async-start | bytes 1572864 | tf_op jit(solution)/shard_map/all_to_all | solution.py:313
  33.6 3.6 %shard_map.103 = (bf16[192,768]{1,0:T(8,128)(2,1)S(1)}, bf16[192,768]{1,0:T(8,128)(2,1)S(1)}, bf16[192,768]{1,0:T(8,128)(2,1)S(1)}, bf16[192,384]{1,0:T(8,128)(2...) custom-call(bf16[24,4096]{1,0:T(8,128)(2,1)S(1)} %collective-permute-done.refs_0_, ...), custom_call_target="tpu_custom_call" | custom-call | flops 1 | bytes 1 | tf_op jit(solution)/shard_map/pallas_call | solution.py:337
  37.3 0.1 collective-permute-start.7
  37.4 6.9 %shard_map.104 = (bf16[24,4096]{1,0:T(8,128)(2,1)S(1)}, bf16[24,4096]{1,0:T(8,128)(2,1)}, bf16[24,4096]{1,0:T(8,128)(2,1)}, bf16[24,4096]{1,0:T(8,128)(2,1)}, bf...) custom-call(bf16[192,768]{1,0:T(8,128)(2,1)S(1)} %get-tuple-element.41.h, ...), custom_call_target="tpu_custom_call" | custom-call | flops 1 | bytes 1 | tf_op jit(solution)/shard_map/pallas_call | solution.py:356
  44.3 0.0 copy-start
  44.3 1.1 %collective-permute-done.7.h_remote = bf16[192,384]{1,0:T(8,128)(2,1)S(1)} collective-permute-done((bf16[192,384]{1,0:T(8,128)(2,1)S(1)}, bf16[192,384]{1,0:T(8,128)(2,1)S(1)}, u32[]{:S(2)}, u32[]{:S(2)}) %collective-permute-start.7) | collective-permute-done | bytes 147488 | tf_op jit(solution)/shard_map/ppermute | solution.py:297
  45.5 0.7 %all-to-all-done = bf16[8,24,2048]{2,1,0:T(8,128)(2,1)S(1)} async-done(((bf16[8,24,2048]{2,1,0:T(8,128)(2,1)}), bf16[8,24,2048]{2,1,0:T(8,128)(2,1)S(1)}, u32[]{:S(2)}, u32[]{:S(2)}) %all-to-all-start) | async-done | bytes 786464 | tf_op jit(solution)/shard_map/all_to_all | solution.py:313
  46.2 1.1 %shard_map.106 = (bf16[192,2048]{1,0:T(8,128)(2,1)S(1)}, bf16[192,2048]{1,0:T(8,128)(2,1)S(1)}) custom-call(bf16[24,4096]{1,0:T(8,128)(2,1)} %get-tuple-element.45.after, bf16[192,384]{1,0:T(8,128)(2,1)S(1)} %get-tuple-element.46.h_own, bf16[192,384]{1,0:T(8,128)(2,1)S(1)} %collective-permute-done.7.h_remote, ...), custom_call_target="tpu_custom_call" | custom-call | flops 1 | bytes 1 | tf_op jit(solution)/shard_map/pallas_call | solution.py:370
  47.3 3.2 %collective-permute-start.9 = (bf16[192,2048]{1,0:T(8,128)(2,1)S(1)}, bf16[192,2048]{1,0:T(8,128)(2,1)S(1)}, u32[]{:S(2)}, u32[]{:S(2)}) collective-permute-start(bf16[192,2048]{1,0:T(8,128)(2,1)S(1)} %get-tuple-element.50), channel_id=1, source_target_pairs={{0,8},{8,0},{16,24},{24,16},{1,9},{9,1},{17,25},{25,17},{2,10},{10... | collective-permute-start | bytes 2359304 | tf_op jit(solution)/shard_map/ppermute | solution.py:297
  50.5 2.5 %collective-permute-start.10 = (bf16[24,4096]{1,0:T(8,128)(2,1)}, bf16[24,4096]{1,0:T(8,128)(2,1)S(1)}, u32[]{:S(2)}, u32[]{:S(2)}) collective-permute-start(bf16[24,4096]{1,0:T(8,128)(2,1)} %get-tuple-element.52), channel_id=1, source_target_pairs={{0,6},{1,7},{2,4},{3,5},{4,2},{5,3},{6,0},{7,1},{8,14},{9,15},{10,... | collective-permute-start | bytes 589832 | tf_op jit(solution)/shard_map/ppermute | solution.py:366
  53.0 0.9 %collective-permute-start.12 = (bf16[24,4096]{1,0:T(8,128)(2,1)}, bf16[24,4096]{1,0:T(8,128)(2,1)S(1)}, u32[]{:S(2)}, u32[]{:S(2)}) collective-permute-start(bf16[24,4096]{1,0:T(8,128)(2,1)} %get-tuple-element.54), channel_id=1, source_target_pairs={{0,2},{1,3},{2,0},{3,1},{4,6},{5,7},{6,4},{7,5},{8,10},{9,11},{10,... | collective-permute-start | bytes 589832 | tf_op jit(solution)/shard_map/ppermute | solution.py:366
  54.0 1.5 %collective-permute-start.13 = (bf16[24,4096]{1,0:T(8,128)(2,1)}, bf16[24,4096]{1,0:T(8,128)(2,1)S(1)}, u32[]{:S(2)}, u32[]{:S(2)}) collective-permute-start(bf16[24,4096]{1,0:T(8,128)(2,1)} %get-tuple-element.55), channel_id=1, source_target_pairs={{0,4},{1,5},{2,6},{3,7},{4,0},{5,1},{6,2},{7,3},{8,12},{9,13},{10,... | collective-permute-start | bytes 589832 | tf_op jit(solution)/shard_map/ppermute | solution.py:366
  55.4 3.4 %collective-permute-done.10.refs_0_ = bf16[24,4096]{1,0:T(8,128)(2,1)S(1)} collective-permute-done((bf16[24,4096]{1,0:T(8,128)(2,1)}, bf16[24,4096]{1,0:T(8,128)(2,1)S(1)}, u32[]{:S(2)}, u32[]{:S(2)}) %collective-permute-start.10) | collective-permute-done | bytes 196640 | tf_op jit(solution)/shard_map/ppermute | solution.py:366
  58.8 4.1 %collective-permute-done.11.refs_1_ = bf16[24,4096]{1,0:T(8,128)(2,1)S(1)} collective-permute-done((bf16[24,4096]{1,0:T(8,128)(2,1)}, bf16[24,4096]{1,0:T(8,128)(2,1)S(1)}, u32[]{:S(2)}, u32[]{:S(2)}) %collective-permute-start.11) | collective-permute-done | bytes 196640 | tf_op jit(solution)/shard_map/ppermute | solution.py:366
  63.0 1.8 %collective-permute-start.15 = (bf16[24,4096]{1,0:T(8,128)(2,1)}, bf16[24,4096]{1,0:T(8,128)(2,1)S(1)}, u32[]{:S(2)}, u32[]{:S(2)}) collective-permute-start(bf16[24,4096]{1,0:T(8,128)(2,1)} %get-tuple-element.57), channel_id=1, source_target_pairs={{0,5},{1,4},{2,7},{3,6},{4,1},{5,0},{6,3},{7,2},{8,13},{9,12},{10,... | collective-permute-start | bytes 589832 | tf_op jit(solution)/shard_map/ppermute | solution.py:366
  64.7 3.3 %collective-permute-done.9.right = bf16[192,2048]{1,0:T(8,128)(2,1)S(1)} collective-permute-done((bf16[192,2048]{1,0:T(8,128)(2,1)S(1)}, bf16[192,2048]{1,0:T(8,128)(2,1)S(1)}, u32[]{:S(2)}, u32[]{:S(2)}) %collective-permute-start.9) | collective-permute-done | bytes 786464 | tf_op jit(solution)/shard_map/ppermute | solution.py:297
  68.0 1.1 %shard_map.107.after = bf16[1,192,2048]{2,1,0:T(8,128)(2,1)} custom-call(bf16[192,2048]{1,0:T(8,128)(2,1)S(1)} %get-tuple-element.49.left, bf16[192,2048]{1,0:T(8,128)(2,1)S(1)} %collective-permute-done.9.right), custom_call_target="tpu_custom_call" | custom-call | flops 1 | bytes 1 | tf_op jit(solution)/shard_map/pallas_call | solution.py:377
  69.1 0.8 %collective-permute-done.14.refs_4_ = bf16[24,4096]{1,0:T(8,128)(2,1)S(1)} collective-permute-done((bf16[24,4096]{1,0:T(8,128)(2,1)}, bf16[24,4096]{1,0:T(8,128)(2,1)S(1)}, u32[]{:S(2)}, u32[]{:S(2)}) %collective-permute-start.14) | collective-permute-done | bytes 196640 | tf_op jit(solution)/shard_map/ppermute | solution.py:366
  70.0 0.7 collective-permute-done.15.refs_5_
  70.6 1.5 %shard_map.108 = (bf16[128,2048]{1,0:T(8,128)(2,1)}, bf16[128,2048]{1,0:T(8,128)(2,1)}, f32[1,128]{1,0:T(1,128)}) custom-call(bf16[1,192,2048]{2,1,0:T(8,128)(2,1)} %shard_map.107.after, s32[2,128]{1,0:T(2,128)S(1)} %get-tuple-element.51.slot, f32[1,128]{1,0:T(1,128)S(1)} %bitcast.10, bf16[128,2048]{1,0:T(8,128)(2,1)S(1)} %copy-done, ...), custom_call_target="tpu_custom_call" | custom-call | flops 1 | bytes 1 | tf_op jit(solution)/shard_map/pallas_call | solution.py:378
  (15 shorter events, 0.0 us)
Async XLA Ops:
  3.7 25.2 %collective-permute-start.8 = (bf16[2064,128]{1,0:T(8,128)(2,1)S(1)}, bf16[2064,128]{1,0:T(8,128)(2,1)S(1)}, u32[]{:S(2)}, u32[]{:S(2)}) collective-permute-start(bf16[2064,128]{1,0:T(8,128)(2,1)S(1)} %get-tuple-element.48), channel_id=1, source_target_pairs={{0,24},{8,16},{16,8},{24,0},{1,25},{9,17},{17,9},{25,1},{2,26},{10... | collective-permute-start | bytes 1585160 | tf_op jit(solution)/shard_map/ppermute | solution.py:297
  8.7 8.4 %collective-permute-start = (bf16[24,4096]{1,0:T(8,128)(2,1)}, bf16[24,4096]{1,0:T(8,128)(2,1)S(1)}, u32[]{:S(2)}, u32[]{:S(2)}) collective-permute-start(bf16[24,4096]{1,0:T(8,128)(2,1)} %get-tuple-element.33), channel_id=1, source_target_pairs={{0,6},{1,7},{2,4},{3,5},{4,2},{5,3},{6,0},{7,1},{8,14},{9,15},{10,... | collective-permute-start | bytes 589832 | tf_op jit(solution)/shard_map/ppermute | solution.py:330
  11.2 9.9 %collective-permute-start.1 = (bf16[24,4096]{1,0:T(8,128)(2,1)}, bf16[24,4096]{1,0:T(8,128)(2,1)S(1)}, u32[]{:S(2)}, u32[]{:S(2)}) collective-permute-start(bf16[24,4096]{1,0:T(8,128)(2,1)} %get-tuple-element.34), channel_id=1, source_target_pairs={{0,7},{1,6},{2,5},{3,4},{4,3},{5,2},{6,1},{7,0},{8,15},{9,14},{10,... | collective-permute-start | bytes 589832 | tf_op jit(solution)/shard_map/ppermute | solution.py:330
  11.2 15.0 %collective-permute-start.2 = (bf16[24,4096]{1,0:T(8,128)(2,1)}, bf16[24,4096]{1,0:T(8,128)(2,1)S(1)}, u32[]{:S(2)}, u32[]{:S(2)}) collective-permute-start(bf16[24,4096]{1,0:T(8,128)(2,1)} %get-tuple-element.35), channel_id=1, source_target_pairs={{0,2},{1,3},{2,0},{3,1},{4,6},{5,7},{6,4},{7,5},{8,10},{9,11},{10,... | collective-permute-start | bytes 589832 | tf_op jit(solution)/shard_map/ppermute | solution.py:330
  12.0 14.2 %collective-permute-start.3 = (bf16[24,4096]{1,0:T(8,128)(2,1)}, bf16[24,4096]{1,0:T(8,128)(2,1)S(1)}, u32[]{:S(2)}, u32[]{:S(2)}) collective-permute-start(bf16[24,4096]{1,0:T(8,128)(2,1)} %get-tuple-element.36), channel_id=1, source_target_pairs={{0,4},{1,5},{2,6},{3,7},{4,0},{5,1},{6,2},{7,3},{8,12},{9,13},{10,... | collective-permute-start | bytes 589832 | tf_op jit(solution)/shard_map/ppermute | solution.py:330
  17.2 10.9 %collective-permute-start.4 = (bf16[24,4096]{1,0:T(8,128)(2,1)}, bf16[24,4096]{1,0:T(8,128)(2,1)S(1)}, u32[]{:S(2)}, u32[]{:S(2)}) collective-permute-start(bf16[24,4096]{1,0:T(8,128)(2,1)} %get-tuple-element.37), channel_id=1, source_target_pairs={{0,3},{1,2},{2,1},{3,0},{4,7},{5,6},{6,5},{7,4},{8,11},{9,10},{10,... | collective-permute-start | bytes 589832 | tf_op jit(solution)/shard_map/ppermute | solution.py:330
  21.1 7.8 %collective-permute-start.5 = (bf16[24,4096]{1,0:T(8,128)(2,1)}, bf16[24,4096]{1,0:T(8,128)(2,1)S(1)}, u32[]{:S(2)}, u32[]{:S(2)}) collective-permute-start(bf16[24,4096]{1,0:T(8,128)(2,1)} %get-tuple-element.38), channel_id=1, source_target_pairs={{0,5},{1,4},{2,7},{3,6},{4,1},{5,0},{6,3},{7,2},{8,13},{9,12},{10,... | collective-permute-start | bytes 589832 | tf_op jit(solution)/shard_map/ppermute | solution.py:330
  26.2 2.7 %collective-permute-start.6 = (bf16[24,4096]{1,0:T(8,128)(2,1)}, bf16[24,4096]{1,0:T(8,128)(2,1)S(1)}, u32[]{:S(2)}, u32[]{:S(2)}) collective-permute-start(bf16[24,4096]{1,0:T(8,128)(2,1)} %get-tuple-element.39), channel_id=1, source_target_pairs={{0,1},{1,0},{2,3},{3,2},{4,5},{5,4},{6,7},{7,6},{8,9},{9,8},{10,11... | collective-permute-start | bytes 589832 | tf_op jit(solution)/shard_map/ppermute | solution.py:330
  30.1 16.1 %all-to-all-start = ((bf16[8,24,2048]{2,1,0:T(8,128)(2,1)}), bf16[8,24,2048]{2,1,0:T(8,128)(2,1)S(1)}, u32[]{:S(2)}, u32[]{:S(2)}) async-start(bf16[8,24,2048]{2,1,0:T(8,128)(2,1)} %bitcast.5), calls=%async_computation | async-start | bytes 1572864 | tf_op jit(solution)/shard_map/all_to_all | solution.py:313
  37.3 8.1 %collective-permute-start.7 = (bf16[192,384]{1,0:T(8,128)(2,1)S(1)}, bf16[192,384]{1,0:T(8,128)(2,1)S(1)}, u32[]{:S(2)}, u32[]{:S(2)}) collective-permute-start(bf16[192,384]{1,0:T(8,128)(2,1)S(1)} %get-tuple-element.47), channel_id=1, source_target_pairs={{0,24},{8,16},{16,8},{24,0},{1,25},{9,17},{17,9},{25,1},{2,26},{10... | collective-permute-start | bytes 442376 | tf_op jit(solution)/shard_map/ppermute | solution.py:297
  44.3 26.3 %copy-start = (bf16[128,2048]{1,0:T(8,128)(2,1)S(1)}, bf16[128,2048]{1,0:T(8,128)(2,1)}, u32[]{:S(2)}) copy-start(bf16[128,2048]{1,0:T(8,128)(2,1)} %cot.3) | copy-start | bytes 1572868
  44.3 26.3 %copy-start.1 = (f32[128,1]{0,1:T(1,128)S(1)}, f32[128,1]{0,1:T(1,128)}, u32[]{:S(2)}) copy-start(f32[128,1]{0,1:T(1,128)} %param.10) | copy-start | bytes 1540
  47.3 20.8 %collective-permute-start.9 = (bf16[192,2048]{1,0:T(8,128)(2,1)S(1)}, bf16[192,2048]{1,0:T(8,128)(2,1)S(1)}, u32[]{:S(2)}, u32[]{:S(2)}) collective-permute-start(bf16[192,2048]{1,0:T(8,128)(2,1)S(1)} %get-tuple-element.50), channel_id=1, source_target_pairs={{0,8},{8,0},{16,24},{24,16},{1,9},{9,1},{17,25},{25,17},{2,10},{10... | collective-permute-start | bytes 2359304 | tf_op jit(solution)/shard_map/ppermute | solution.py:297
  50.5 8.4 %collective-permute-start.10 = (bf16[24,4096]{1,0:T(8,128)(2,1)}, bf16[24,4096]{1,0:T(8,128)(2,1)S(1)}, u32[]{:S(2)}, u32[]{:S(2)}) collective-permute-start(bf16[24,4096]{1,0:T(8,128)(2,1)} %get-tuple-element.52), channel_id=1, source_target_pairs={{0,6},{1,7},{2,4},{3,5},{4,2},{5,3},{6,0},{7,1},{8,14},{9,15},{10,... | collective-permute-start | bytes 589832 | tf_op jit(solution)/shard_map/ppermute | solution.py:366
  53.0 9.9 %collective-permute-start.11 = (bf16[24,4096]{1,0:T(8,128)(2,1)}, bf16[24,4096]{1,0:T(8,128)(2,1)S(1)}, u32[]{:S(2)}, u32[]{:S(2)}) collective-permute-start(bf16[24,4096]{1,0:T(8,128)(2,1)} %get-tuple-element.53), channel_id=1, source_target_pairs={{0,7},{1,6},{2,5},{3,4},{4,3},{5,2},{6,1},{7,0},{8,15},{9,14},{10,... | collective-permute-start | bytes 589832 | tf_op jit(solution)/shard_map/ppermute | solution.py:366
  53.0 16.1 %collective-permute-start.12 = (bf16[24,4096]{1,0:T(8,128)(2,1)}, bf16[24,4096]{1,0:T(8,128)(2,1)S(1)}, u32[]{:S(2)}, u32[]{:S(2)}) collective-permute-start(bf16[24,4096]{1,0:T(8,128)(2,1)} %get-tuple-element.54), channel_id=1, source_target_pairs={{0,2},{1,3},{2,0},{3,1},{4,6},{5,7},{6,4},{7,5},{8,10},{9,11},{10,... | collective-permute-start | bytes 589832 | tf_op jit(solution)/shard_map/ppermute | solution.py:366
  54.0 15.1 %collective-permute-start.13 = (bf16[24,4096]{1,0:T(8,128)(2,1)}, bf16[24,4096]{1,0:T(8,128)(2,1)S(1)}, u32[]{:S(2)}, u32[]{:S(2)}) collective-permute-start(bf16[24,4096]{1,0:T(8,128)(2,1)} %get-tuple-element.55), channel_id=1, source_target_pairs={{0,4},{1,5},{2,6},{3,7},{4,0},{5,1},{6,2},{7,3},{8,12},{9,13},{10,... | collective-permute-start | bytes 589832 | tf_op jit(solution)/shard_map/ppermute | solution.py:366
  58.8 11.1 %collective-permute-start.14 = (bf16[24,4096]{1,0:T(8,128)(2,1)}, bf16[24,4096]{1,0:T(8,128)(2,1)S(1)}, u32[]{:S(2)}, u32[]{:S(2)}) collective-permute-start(bf16[24,4096]{1,0:T(8,128)(2,1)} %get-tuple-element.56), channel_id=1, source_target_pairs={{0,3},{1,2},{2,1},{3,0},{4,7},{5,6},{6,5},{7,4},{8,11},{9,10},{10,... | collective-permute-start | bytes 589832 | tf_op jit(solution)/shard_map/ppermute | solution.py:366
  63.0 7.7 %collective-permute-start.15 = (bf16[24,4096]{1,0:T(8,128)(2,1)}, bf16[24,4096]{1,0:T(8,128)(2,1)S(1)}, u32[]{:S(2)}, u32[]{:S(2)}) collective-permute-start(bf16[24,4096]{1,0:T(8,128)(2,1)} %get-tuple-element.57), channel_id=1, source_target_pairs={{0,5},{1,4},{2,7},{3,6},{4,1},{5,0},{6,3},{7,2},{8,13},{9,12},{10,... | collective-permute-start | bytes 589832 | tf_op jit(solution)/shard_map/ppermute | solution.py:366
  68.0 2.6 %collective-permute-start.16 = (bf16[24,4096]{1,0:T(8,128)(2,1)}, bf16[24,4096]{1,0:T(8,128)(2,1)S(1)}, u32[]{:S(2)}, u32[]{:S(2)}) collective-permute-start(bf16[24,4096]{1,0:T(8,128)(2,1)} %get-tuple-element.45.after), channel_id=1, source_target_pairs={{0,1},{1,0},{2,3},{3,2},{4,5},{5,4},{6,7},{7,6},{8,9},{9,8},{10,11... | collective-permute-start | bytes 589832 | tf_op jit(solution)/shard_map/ppermute | solution.py:366

commit v11 on v10

--- a/solution.py
+++ b/solution.py
@@ -245,24 +245,20 @@
         )
 
 
-def quarters_kernel(after, h_own, h_remote, own, remote, mine, other):
-    width = remote.shape[1]
-    even = lax.rem(lax.axis_index("ctx"), 2) == 0
-    left, right = h_own[...].astype(F32).T, h_remote[...].astype(F32).T
-    size = left.shape[0] // 2
-
-    def halves(turned):
-        low, high = turned[:size].astype(BF16), turned[size:].astype(BF16)
-        return jnp.where(even, low, high), jnp.where(even, high, low)
-
-    (own_mine, own_other), (remote_mine, remote_other) = halves(left), halves(right)
-    for at in range(0, width, WIDE):
+def turned(hid, away):
+    low = (lax.rem(lax.axis_index("ctx"), 2) == 0) != away
+    size = hid.shape[1] // 2
+    return jnp.where(low, hid[:, :size], hid[:, size:]).astype(F32).T.astype(BF16)
+
+
+def quarters_kernel(after, h_own, h_remote, own, remote, other):
+    left, right = turned(h_own, True), turned(h_remote, True)
+    for at in range(0, remote.shape[1], WIDE):
         cols = slice(at, at + WIDE)
-        for out, left, right in ((other, own_other, remote_other), (mine, own_mine, remote_mine)):
-            out[:, cols] = (
-                jnp.dot(left, own[:, cols], preferred_element_type=F32)
-                + jnp.dot(right, remote[:, cols], preferred_element_type=F32)
-            ).astype(BF16)
+        other[:, cols] = (
+            jnp.dot(left, own[:, cols], preferred_element_type=F32)
+            + jnp.dot(right, remote[:, cols], preferred_element_type=F32)
+        ).astype(BF16)
 
 
 def home_kernel(order, after, slot, gates, cot, *refs):
@@ -289,8 +285,14 @@
     gate_grad[...] = jnp.sum(jnp.where(diagonal(count), total, 0.0), axis=0, keepdims=True)
 
 
-def add_kernel(left, right, out):
-    out[0] = (left[...].astype(F32) + right[...].astype(F32)).astype(BF16)
+def add_kernel(h_own, h_remote, own, remote, got, out):
+    left, right = turned(h_own, False), turned(h_remote, False)
+    for at in range(0, remote.shape[1], WIDE):
+        cols = slice(at, at + WIDE)
+        mine = jnp.dot(left, own[:, cols], preferred_element_type=F32) + jnp.dot(
+            right, remote[:, cols], preferred_element_type=F32
+        )
+        out[0, :, cols] = (mine + got[:, cols].astype(F32)).astype(BF16)
 
 
 def along(rows, step):
@@ -367,14 +369,16 @@
         for k in order
     ]
 
-    mine, other = call(
+    other = call(
         quarters_kernel,
-        [shaped((quarter, width))] * 2,
+        shaped((quarter, width)),
         in_specs=[after] + [whole] * 4,
     )(in_hbm(back[1]), near, far_across, cot, remote)
     swapped = along(other, 1)
 
-    down_grad = call(add_kernel, shaped((1, quarter, width)))(mine, swapped)
+    down_grad = call(add_kernel, shaped((1, quarter, width)))(
+        near, far_across, cot, remote, swapped
+    )
     layer_output, token_grad, gate_grad = call(
         functools.partial(home_kernel, order),
         [shaped((count, width)), shaped((count, width)), shaped((1, count), F32)],

time: 72.3 us -> 72.1 us (level)
  transfers between devices with their start and end apart: 18 -> 18, of which waited for: 12 -> 12; matrix products, arithmetic and copies ran while one was open for 0% -> 0% of each run, Pallas kernels for 16% -> 17%
where the time goes in v11:
time: 72.1 us; the launch traced here: 71.9 us
  waiting for transfers between devices  27.1 us (38%)
  starting transfers between devices  25.2 us (35%)
  Pallas kernels  18.8 us (26%)
    ppermute x7, waiting for transfers between devices, body_line(): got[k] = lax.ppermute(blocks[k], 'tp', [(i, i ^ k) for i in range(peers)])  13.5 us
    ppermute x7, waiting for transfers between devices, body_line(): lax.ppermute(back[k], 'tp', [(i, i ^ k) for i in range(peers)])  8.4 us
    ppermute x3, starting transfers between devices, along(): return lax.ppermute(rows, 'ctx', [(i, i ^ step) for i in range(4)])  8.34 us
    pallas_call x1, Pallas kernels, body_line(): call(back_kernel, [shaped((capacity, 2 * width))] + [pltpu.HBM((capacity,...  6.9 us
    ppermute x7, starting transfers between devices, body_line(): lax.ppermute(back[k], 'tp', [(i, i ^ k) for i in range(peers)])  6.77 us
    ppermute x7, starting transfers between devices, body_line(): got[k] = lax.ppermute(blocks[k], 'tp', [(i, i ^ k) for i in range(peers)])  6.59 us
    ppermute x3, waiting for transfers between devices, along(): return lax.ppermute(rows, 'ctx', [(i, i ^ step) for i in range(4)])  4.46 us
    pallas_call x1, Pallas kernels, body_line(): call(functools.partial(hidden_kernel, order), [shaped((slots, inner))] *...  3.64 us
  transfers between devices with their start and end apart: 18, of which 12 were waited for; matrix products, arithmetic and copies ran while one was open for 0% of the time, Pallas kernels for 17%

profile of v11, /device:TPU:0, one launch (start us, length us, event | category | flops | bytes accessed | tf_op | source)
XLA Modules:
  0.0 71.9 jit_solution(15988447885621110562)
XLA Ops:
  0.6 3.1 %shard_map.102 = (s32[2,128]{1,0:T(2,128)S(1)}, bf16[2064,128]{1,0:T(8,128)(2,1)S(1)}, bf16[24,4096]{1,0:T(8,128)(2,1)S(1)}, bf16[24,4096]{1,0:T(8,128)(2,1)}, b...) custom-call(s32[1,128]{1,0:T(1,128)} %bitcast.17, ...), custom_call_target="tpu_custom_call" | custom-call | flops 1 | bytes 1 | tf_op jit(solution)/shard_map/pallas_call | solution.py:319
  3.7 5.0 %collective-permute-start.8 = (bf16[2064,128]{1,0:T(8,128)(2,1)S(1)}, bf16[2064,128]{1,0:T(8,128)(2,1)S(1)}, u32[]{:S(2)}, u32[]{:S(2)}) collective-permute-start(bf16[2064,128]{1,0:T(8,128)(2,1)S(1)} %get-tuple-element.42), channel_id=1, source_target_pairs={{0,24},{8,16},{16,8},{24,0},{1,25},{9,17},{17,9},{25,1},{2,26},{10... | collective-permute-start | bytes 1585160 | tf_op jit(solution)/shard_map/ppermute | solution.py:299
  8.7 2.4 %collective-permute-start = (bf16[24,4096]{1,0:T(8,128)(2,1)}, bf16[24,4096]{1,0:T(8,128)(2,1)S(1)}, u32[]{:S(2)}, u32[]{:S(2)}) collective-permute-start(bf16[24,4096]{1,0:T(8,128)(2,1)} %get-tuple-element.31), channel_id=1, source_target_pairs={{0,6},{1,7},{2,4},{3,5},{4,2},{5,3},{6,0},{7,1},{8,14},{9,15},{10,... | collective-permute-start | bytes 589832 | tf_op jit(solution)/shard_map/ppermute | solution.py:332
  11.2 0.8 %collective-permute-start.2 = (bf16[24,4096]{1,0:T(8,128)(2,1)}, bf16[24,4096]{1,0:T(8,128)(2,1)S(1)}, u32[]{:S(2)}, u32[]{:S(2)}) collective-permute-start(bf16[24,4096]{1,0:T(8,128)(2,1)} %get-tuple-element.33), channel_id=1, source_target_pairs={{0,2},{1,3},{2,0},{3,1},{4,6},{5,7},{6,4},{7,5},{8,10},{9,11},{10,... | collective-permute-start | bytes 589832 | tf_op jit(solution)/shard_map/ppermute | solution.py:332
  12.0 1.5 %collective-permute-start.3 = (bf16[24,4096]{1,0:T(8,128)(2,1)}, bf16[24,4096]{1,0:T(8,128)(2,1)S(1)}, u32[]{:S(2)}, u32[]{:S(2)}) collective-permute-start(bf16[24,4096]{1,0:T(8,128)(2,1)} %get-tuple-element.34), channel_id=1, source_target_pairs={{0,4},{1,5},{2,6},{3,7},{4,0},{5,1},{6,2},{7,3},{8,12},{9,13},{10,... | collective-permute-start | bytes 589832 | tf_op jit(solution)/shard_map/ppermute | solution.py:332
  13.6 3.6 %collective-permute-done.refs_0_ = bf16[24,4096]{1,0:T(8,128)(2,1)S(1)} collective-permute-done((bf16[24,4096]{1,0:T(8,128)(2,1)}, bf16[24,4096]{1,0:T(8,128)(2,1)S(1)}, u32[]{:S(2)}, u32[]{:S(2)}) %collective-permute-start) | collective-permute-done | bytes 196640 | tf_op jit(solution)/shard_map/ppermute | solution.py:332
  17.2 0.0 collective-permute-start.4
  17.2 3.9 %collective-permute-done.1.refs_1_ = bf16[24,4096]{1,0:T(8,128)(2,1)S(1)} collective-permute-done((bf16[24,4096]{1,0:T(8,128)(2,1)}, bf16[24,4096]{1,0:T(8,128)(2,1)S(1)}, u32[]{:S(2)}, u32[]{:S(2)}) %collective-permute-start.1) | collective-permute-done | bytes 196640 | tf_op jit(solution)/shard_map/ppermute | solution.py:332
  21.1 1.8 %collective-permute-start.5 = (bf16[24,4096]{1,0:T(8,128)(2,1)}, bf16[24,4096]{1,0:T(8,128)(2,1)S(1)}, u32[]{:S(2)}, u32[]{:S(2)}) collective-permute-start(bf16[24,4096]{1,0:T(8,128)(2,1)} %get-tuple-element.36), channel_id=1, source_target_pairs={{0,5},{1,4},{2,7},{3,6},{4,1},{5,0},{6,3},{7,2},{8,13},{9,12},{10,... | collective-permute-start | bytes 589832 | tf_op jit(solution)/shard_map/ppermute | solution.py:332
  22.9 3.3 %collective-permute-done.2.refs_2_ = bf16[24,4096]{1,0:T(8,128)(2,1)S(1)} collective-permute-done((bf16[24,4096]{1,0:T(8,128)(2,1)}, bf16[24,4096]{1,0:T(8,128)(2,1)S(1)}, u32[]{:S(2)}, u32[]{:S(2)}) %collective-permute-start.2) | collective-permute-done | bytes 196640 | tf_op jit(solution)/shard_map/ppermute | solution.py:332
  26.2 1.9 %collective-permute-done.4.refs_4_ = bf16[24,4096]{1,0:T(8,128)(2,1)S(1)} collective-permute-done((bf16[24,4096]{1,0:T(8,128)(2,1)}, bf16[24,4096]{1,0:T(8,128)(2,1)S(1)}, u32[]{:S(2)}, u32[]{:S(2)}) %collective-permute-start.4) | collective-permute-done | bytes 196640 | tf_op jit(solution)/shard_map/ppermute | solution.py:332
  28.1 0.8 %collective-permute-done.5.refs_5_ = bf16[24,4096]{1,0:T(8,128)(2,1)S(1)} collective-permute-done((bf16[24,4096]{1,0:T(8,128)(2,1)}, bf16[24,4096]{1,0:T(8,128)(2,1)S(1)}, u32[]{:S(2)}, u32[]{:S(2)}) %collective-permute-start.5) | collective-permute-done | bytes 196640 | tf_op jit(solution)/shard_map/ppermute | solution.py:332
  28.9 1.2 %shard_map.104 = bf16[192,2048]{1,0:T(8,128)(2,1)} custom-call(bf16[2064,128]{1,0:T(8,128)(2,1)S(1)} %collective-permute-done.8.rows, bf16[24,4096]{1,0:T(8,128)(2,1)S(1)} %collective-permute-done.refs_0_, bf16[24,4096]{1,0:T(8,128)(2,1)S(1)} %collective-permute-done.1.refs_1_, bf16[24,4096]{1,0:T(8,128)(2,1)S(1)} %collective-permute-done.2.refs_2_, ...), custom_call_target="tpu_custom_call" | custom-call | flops 1 | bytes 1 | tf_op jit(solution)/shard_map/pallas_call | solution.py:354
  30.1 3.5 %all-to-all-start = ((bf16[8,24,2048]{2,1,0:T(8,128)(2,1)}), bf16[8,24,2048]{2,1,0:T(8,128)(2,1)S(1)}, u32[]{:S(2)}, u32[]{:S(2)}) async-start(bf16[8,24,2048]{2,1,0:T(8,128)(2,1)} %bitcast.4), calls=%async_computation | async-start | bytes 1572864 | tf_op jit(solution)/shard_map/all_to_all | solution.py:315
  33.6 3.6 %shard_map.103 = (bf16[192,768]{1,0:T(8,128)(2,1)S(1)}, bf16[192,768]{1,0:T(8,128)(2,1)S(1)}, bf16[192,768]{1,0:T(8,128)(2,1)S(1)}, bf16[192,384]{1,0:T(8,128)(2...) custom-call(bf16[24,4096]{1,0:T(8,128)(2,1)S(1)} %collective-permute-done.refs_0_, ...), custom_call_target="tpu_custom_call" | custom-call | flops 1 | bytes 1 | tf_op jit(solution)/shard_map/pallas_call | solution.py:339
  37.3 0.1 collective-permute-start.7
  37.4 6.9 %shard_map.105 = (bf16[24,4096]{1,0:T(8,128)(2,1)S(1)}, bf16[24,4096]{1,0:T(8,128)(2,1)}, bf16[24,4096]{1,0:T(8,128)(2,1)}, bf16[24,4096]{1,0:T(8,128)(2,1)}, bf...) custom-call(bf16[192,768]{1,0:T(8,128)(2,1)S(1)} %get-tuple-element.43.h, ...), custom_call_target="tpu_custom_call" | custom-call | flops 1 | bytes 1 | tf_op jit(solution)/shard_map/pallas_call | solution.py:358
  44.3 1.2 %collective-permute-done.7.h_remote = bf16[192,384]{1,0:T(8,128)(2,1)S(1)} collective-permute-done((bf16[192,384]{1,0:T(8,128)(2,1)S(1)}, bf16[192,384]{1,0:T(8,128)(2,1)S(1)}, u32[]{:S(2)}, u32[]{:S(2)}) %collective-permute-start.7) | collective-permute-done | bytes 147488 | tf_op jit(solution)/shard_map/ppermute | solution.py:299
  45.5 0.7 %all-to-all-done = bf16[8,24,2048]{2,1,0:T(8,128)(2,1)S(1)} async-done(((bf16[8,24,2048]{2,1,0:T(8,128)(2,1)}), bf16[8,24,2048]{2,1,0:T(8,128)(2,1)S(1)}, u32[]{:S(2)}, u32[]{:S(2)}) %all-to-all-start) | async-done | bytes 786464 | tf_op jit(solution)/shard_map/all_to_all | solution.py:315
  46.2 0.8 %shard_map.106 = bf16[192,2048]{1,0:T(8,128)(2,1)S(1)} custom-call(bf16[24,4096]{1,0:T(8,128)(2,1)} %get-tuple-element.46.after, bf16[192,384]{1,0:T(8,128)(2,1)S(1)} %get-tuple-element.39.h_own, bf16[192,384]{1,0:T(8,128)(2,1)S(1)} %collective-permute-done.7.h_remote, bf16[192,2048]{1,0:T(8,128)(2,1)S(1)} %get-tuple-element.41.cot.own, ...), custom_call_target="tpu_custom_call" | custom-call | flops 1 | bytes 1 | tf_op jit(solution)/shard_map/pallas_call | solution.py:372
  47.0 3.2 %collective-permute-start.9 = (bf16[192,2048]{1,0:T(8,128)(2,1)S(1)}, bf16[192,2048]{1,0:T(8,128)(2,1)S(1)}, u32[]{:S(2)}, u32[]{:S(2)}) collective-permute-start(bf16[192,2048]{1,0:T(8,128)(2,1)S(1)} %shard_map.106), channel_id=1, source_target_pairs={{0,8},{8,0},{16,24},{24,16},{1,9},{9,1},{17,25},{25,17},{2,10},{10... | collective-permute-start | bytes 2359304 | tf_op jit(solution)/shard_map/ppermute | solution.py:299
  50.3 2.6 %collective-permute-start.10 = (bf16[24,4096]{1,0:T(8,128)(2,1)}, bf16[24,4096]{1,0:T(8,128)(2,1)S(1)}, u32[]{:S(2)}, u32[]{:S(2)}) collective-permute-start(bf16[24,4096]{1,0:T(8,128)(2,1)} %get-tuple-element.48), channel_id=1, source_target_pairs={{0,6},{1,7},{2,4},{3,5},{4,2},{5,3},{6,0},{7,1},{8,14},{9,15},{10,... | collective-permute-start | bytes 589832 | tf_op jit(solution)/shard_map/ppermute | solution.py:368
  52.8 0.9 %collective-permute-start.12 = (bf16[24,4096]{1,0:T(8,128)(2,1)}, bf16[24,4096]{1,0:T(8,128)(2,1)S(1)}, u32[]{:S(2)}, u32[]{:S(2)}) collective-permute-start(bf16[24,4096]{1,0:T(8,128)(2,1)} %get-tuple-element.50), channel_id=1, source_target_pairs={{0,2},{1,3},{2,0},{3,1},{4,6},{5,7},{6,4},{7,5},{8,10},{9,11},{10,... | collective-permute-start | bytes 589832 | tf_op jit(solution)/shard_map/ppermute | solution.py:368
  53.8 1.5 %collective-permute-start.13 = (bf16[24,4096]{1,0:T(8,128)(2,1)}, bf16[24,4096]{1,0:T(8,128)(2,1)S(1)}, u32[]{:S(2)}, u32[]{:S(2)}) collective-permute-start(bf16[24,4096]{1,0:T(8,128)(2,1)} %get-tuple-element.51), channel_id=1, source_target_pairs={{0,4},{1,5},{2,6},{3,7},{4,0},{5,1},{6,2},{7,3},{8,12},{9,13},{10,... | collective-permute-start | bytes 589832 | tf_op jit(solution)/shard_map/ppermute | solution.py:368
  55.2 3.4 %collective-permute-done.10.refs_0_ = bf16[24,4096]{1,0:T(8,128)(2,1)S(1)} collective-permute-done((bf16[24,4096]{1,0:T(8,128)(2,1)}, bf16[24,4096]{1,0:T(8,128)(2,1)S(1)}, u32[]{:S(2)}, u32[]{:S(2)}) %collective-permute-start.10) | collective-permute-done | bytes 196640 | tf_op jit(solution)/shard_map/ppermute | solution.py:368
  58.6 4.1 %collective-permute-done.11.refs_1_ = bf16[24,4096]{1,0:T(8,128)(2,1)S(1)} collective-permute-done((bf16[24,4096]{1,0:T(8,128)(2,1)}, bf16[24,4096]{1,0:T(8,128)(2,1)S(1)}, u32[]{:S(2)}, u32[]{:S(2)}) %collective-permute-start.11) | collective-permute-done | bytes 196640 | tf_op jit(solution)/shard_map/ppermute | solution.py:368
  62.7 1.8 %collective-permute-start.15 = (bf16[24,4096]{1,0:T(8,128)(2,1)}, bf16[24,4096]{1,0:T(8,128)(2,1)S(1)}, u32[]{:S(2)}, u32[]{:S(2)}) collective-permute-start(bf16[24,4096]{1,0:T(8,128)(2,1)} %get-tuple-element.53), channel_id=1, source_target_pairs={{0,5},{1,4},{2,7},{3,6},{4,1},{5,0},{6,3},{7,2},{8,13},{9,12},{10,... | collective-permute-start | bytes 589832 | tf_op jit(solution)/shard_map/ppermute | solution.py:368
  64.5 3.3 %collective-permute-done.9.got = bf16[192,2048]{1,0:T(8,128)(2,1)S(1)} collective-permute-done((bf16[192,2048]{1,0:T(8,128)(2,1)S(1)}, bf16[192,2048]{1,0:T(8,128)(2,1)S(1)}, u32[]{:S(2)}, u32[]{:S(2)}) %collective-permute-start.9) | collective-permute-done | bytes 786464 | tf_op jit(solution)/shard_map/ppermute | solution.py:299
  67.8 1.7 %shard_map.107.after = bf16[1,192,2048]{2,1,0:T(8,128)(2,1)} custom-call(bf16[192,384]{1,0:T(8,128)(2,1)S(1)} %get-tuple-element.39.h_own, bf16[192,384]{1,0:T(8,128)(2,1)S(1)} %collective-permute-done.7.h_remote, bf16[192,2048]{1,0:T(8,128)(2,1)S(1)} %get-tuple-element.41.cot.own, bf16[192,2048]{1,0:T(8,128)(2,1)S(1)} %bitcast.9, ...), custom_call_target="tpu_custom_call" | custom-call | flops 1 | bytes 1 | tf_op jit(solution)/shard_map/pallas_call | solution.py:379
  69.5 0.2 collective-permute-done.14.refs_4_
  69.7 0.7 collective-permute-done.15.refs_5_
  70.4 1.5 %shard_map.108 = (bf16[128,2048]{1,0:T(8,128)(2,1)}, bf16[128,2048]{1,0:T(8,128)(2,1)}, f32[1,128]{1,0:T(1,128)}) custom-call(bf16[1,192,2048]{2,1,0:T(8,128)(2,1)} %shard_map.107.after, s32[2,128]{1,0:T(2,128)S(1)} %get-tuple-element.47.slot, f32[1,128]{1,0:T(1,128)S(1)} %bitcast.11, bf16[128,2048]{1,0:T(8,128)(2,1)S(1)} %copy-done, ...), custom_call_target="tpu_custom_call" | custom-call | flops 1 | bytes 1 | tf_op jit(solution)/shard_map/pallas_call | solution.py:382
  (15 shorter events, 0.0 us)
Async XLA Ops:
  3.7 25.2 %collective-permute-start.8 = (bf16[2064,128]{1,0:T(8,128)(2,1)S(1)}, bf16[2064,128]{1,0:T(8,128)(2,1)S(1)}, u32[]{:S(2)}, u32[]{:S(2)}) collective-permute-start(bf16[2064,128]{1,0:T(8,128)(2,1)S(1)} %get-tuple-element.42), channel_id=1, source_target_pairs={{0,24},{8,16},{16,8},{24,0},{1,25},{9,17},{17,9},{25,1},{2,26},{10... | collective-permute-start | bytes 1585160 | tf_op jit(solution)/shard_map/ppermute | solution.py:299
  8.7 8.4 %collective-permute-start = (bf16[24,4096]{1,0:T(8,128)(2,1)}, bf16[24,4096]{1,0:T(8,128)(2,1)S(1)}, u32[]{:S(2)}, u32[]{:S(2)}) collective-permute-start(bf16[24,4096]{1,0:T(8,128)(2,1)} %get-tuple-element.31), channel_id=1, source_target_pairs={{0,6},{1,7},{2,4},{3,5},{4,2},{5,3},{6,0},{7,1},{8,14},{9,15},{10,... | collective-permute-start | bytes 589832 | tf_op jit(solution)/shard_map/ppermute | solution.py:332
  11.2 9.9 %collective-permute-start.1 = (bf16[24,4096]{1,0:T(8,128)(2,1)}, bf16[24,4096]{1,0:T(8,128)(2,1)S(1)}, u32[]{:S(2)}, u32[]{:S(2)}) collective-permute-start(bf16[24,4096]{1,0:T(8,128)(2,1)} %get-tuple-element.32), channel_id=1, source_target_pairs={{0,7},{1,6},{2,5},{3,4},{4,3},{5,2},{6,1},{7,0},{8,15},{9,14},{10,... | collective-permute-start | bytes 589832 | tf_op jit(solution)/shard_map/ppermute | solution.py:332
  11.2 15.0 %collective-permute-start.2 = (bf16[24,4096]{1,0:T(8,128)(2,1)}, bf16[24,4096]{1,0:T(8,128)(2,1)S(1)}, u32[]{:S(2)}, u32[]{:S(2)}) collective-permute-start(bf16[24,4096]{1,0:T(8,128)(2,1)} %get-tuple-element.33), channel_id=1, source_target_pairs={{0,2},{1,3},{2,0},{3,1},{4,6},{5,7},{6,4},{7,5},{8,10},{9,11},{10,... | collective-permute-start | bytes 589832 | tf_op jit(solution)/shard_map/ppermute | solution.py:332
  12.0 14.2 %collective-permute-start.3 = (bf16[24,4096]{1,0:T(8,128)(2,1)}, bf16[24,4096]{1,0:T(8,128)(2,1)S(1)}, u32[]{:S(2)}, u32[]{:S(2)}) collective-permute-start(bf16[24,4096]{1,0:T(8,128)(2,1)} %get-tuple-element.34), channel_id=1, source_target_pairs={{0,4},{1,5},{2,6},{3,7},{4,0},{5,1},{6,2},{7,3},{8,12},{9,13},{10,... | collective-permute-start | bytes 589832 | tf_op jit(solution)/shard_map/ppermute | solution.py:332
  17.2 10.9 %collective-permute-start.4 = (bf16[24,4096]{1,0:T(8,128)(2,1)}, bf16[24,4096]{1,0:T(8,128)(2,1)S(1)}, u32[]{:S(2)}, u32[]{:S(2)}) collective-permute-start(bf16[24,4096]{1,0:T(8,128)(2,1)} %get-tuple-element.35), channel_id=1, source_target_pairs={{0,3},{1,2},{2,1},{3,0},{4,7},{5,6},{6,5},{7,4},{8,11},{9,10},{10,... | collective-permute-start | bytes 589832 | tf_op jit(solution)/shard_map/ppermute | solution.py:332
  21.1 7.8 %collective-permute-start.5 = (bf16[24,4096]{1,0:T(8,128)(2,1)}, bf16[24,4096]{1,0:T(8,128)(2,1)S(1)}, u32[]{:S(2)}, u32[]{:S(2)}) collective-permute-start(bf16[24,4096]{1,0:T(8,128)(2,1)} %get-tuple-element.36), channel_id=1, source_target_pairs={{0,5},{1,4},{2,7},{3,6},{4,1},{5,0},{6,3},{7,2},{8,13},{9,12},{10,... | collective-permute-start | bytes 589832 | tf_op jit(solution)/shard_map/ppermute | solution.py:332
  26.2 2.7 %collective-permute-start.6 = (bf16[24,4096]{1,0:T(8,128)(2,1)}, bf16[24,4096]{1,0:T(8,128)(2,1)S(1)}, u32[]{:S(2)}, u32[]{:S(2)}) collective-permute-start(bf16[24,4096]{1,0:T(8,128)(2,1)} %get-tuple-element.37), channel_id=1, source_target_pairs={{0,1},{1,0},{2,3},{3,2},{4,5},{5,4},{6,7},{7,6},{8,9},{9,8},{10,11... | collective-permute-start | bytes 589832 | tf_op jit(solution)/shard_map/ppermute | solution.py:332
  30.1 16.1 %all-to-all-start = ((bf16[8,24,2048]{2,1,0:T(8,128)(2,1)}), bf16[8,24,2048]{2,1,0:T(8,128)(2,1)S(1)}, u32[]{:S(2)}, u32[]{:S(2)}) async-start(bf16[8,24,2048]{2,1,0:T(8,128)(2,1)} %bitcast.4), calls=%async_computation | async-start | bytes 1572864 | tf_op jit(solution)/shard_map/all_to_all | solution.py:315
  37.3 8.1 %collective-permute-start.7 = (bf16[192,384]{1,0:T(8,128)(2,1)S(1)}, bf16[192,384]{1,0:T(8,128)(2,1)S(1)}, u32[]{:S(2)}, u32[]{:S(2)}) collective-permute-start(bf16[192,384]{1,0:T(8,128)(2,1)S(1)} %get-tuple-element.40), channel_id=1, source_target_pairs={{0,24},{8,16},{16,8},{24,0},{1,25},{9,17},{17,9},{25,1},{2,26},{10... | collective-permute-start | bytes 442376 | tf_op jit(solution)/shard_map/ppermute | solution.py:299
  46.2 24.2 %copy-start = (bf16[128,2048]{1,0:T(8,128)(2,1)S(1)}, bf16[128,2048]{1,0:T(8,128)(2,1)}, u32[]{:S(2)}) copy-start(bf16[128,2048]{1,0:T(8,128)(2,1)} %cot.3) | copy-start | bytes 1572868
  46.2 24.2 %copy-start.1 = (f32[128,1]{0,1:T(1,128)S(1)}, f32[128,1]{0,1:T(1,128)}, u32[]{:S(2)}) copy-start(f32[128,1]{0,1:T(1,128)} %param.10) | copy-start | bytes 1540
  47.0 20.8 %collective-permute-start.9 = (bf16[192,2048]{1,0:T(8,128)(2,1)S(1)}, bf16[192,2048]{1,0:T(8,128)(2,1)S(1)}, u32[]{:S(2)}, u32[]{:S(2)}) collective-permute-start(bf16[192,2048]{1,0:T(8,128)(2,1)S(1)} %shard_map.106), channel_id=1, source_target_pairs={{0,8},{8,0},{16,24},{24,16},{1,9},{9,1},{17,25},{25,17},{2,10},{10... | collective-permute-start | bytes 2359304 | tf_op jit(solution)/shard_map/ppermute | solution.py:299
  50.3 8.4 %collective-permute-start.10 = (bf16[24,4096]{1,0:T(8,128)(2,1)}, bf16[24,4096]{1,0:T(8,128)(2,1)S(1)}, u32[]{:S(2)}, u32[]{:S(2)}) collective-permute-start(bf16[24,4096]{1,0:T(8,128)(2,1)} %get-tuple-element.48), channel_id=1, source_target_pairs={{0,6},{1,7},{2,4},{3,5},{4,2},{5,3},{6,0},{7,1},{8,14},{9,15},{10,... | collective-permute-start | bytes 589832 | tf_op jit(solution)/shard_map/ppermute | solution.py:368
  52.8 9.9 %collective-permute-start.11 = (bf16[24,4096]{1,0:T(8,128)(2,1)}, bf16[24,4096]{1,0:T(8,128)(2,1)S(1)}, u32[]{:S(2)}, u32[]{:S(2)}) collective-permute-start(bf16[24,4096]{1,0:T(8,128)(2,1)} %get-tuple-element.49), channel_id=1, source_target_pairs={{0,7},{1,6},{2,5},{3,4},{4,3},{5,2},{6,1},{7,0},{8,15},{9,14},{10,... | collective-permute-start | bytes 589832 | tf_op jit(solution)/shard_map/ppermute | solution.py:368
  52.8 16.7 %collective-permute-start.12 = (bf16[24,4096]{1,0:T(8,128)(2,1)}, bf16[24,4096]{1,0:T(8,128)(2,1)S(1)}, u32[]{:S(2)}, u32[]{:S(2)}) collective-permute-start(bf16[24,4096]{1,0:T(8,128)(2,1)} %get-tuple-element.50), channel_id=1, source_target_pairs={{0,2},{1,3},{2,0},{3,1},{4,6},{5,7},{6,4},{7,5},{8,10},{9,11},{10,... | collective-permute-start | bytes 589832 | tf_op jit(solution)/shard_map/ppermute | solution.py:368
  53.8 15.7 %collective-permute-start.13 = (bf16[24,4096]{1,0:T(8,128)(2,1)}, bf16[24,4096]{1,0:T(8,128)(2,1)S(1)}, u32[]{:S(2)}, u32[]{:S(2)}) collective-permute-start(bf16[24,4096]{1,0:T(8,128)(2,1)} %get-tuple-element.51), channel_id=1, source_target_pairs={{0,4},{1,5},{2,6},{3,7},{4,0},{5,1},{6,2},{7,3},{8,12},{9,13},{10,... | collective-permute-start | bytes 589832 | tf_op jit(solution)/shard_map/ppermute | solution.py:368
  58.6 11.1 %collective-permute-start.14 = (bf16[24,4096]{1,0:T(8,128)(2,1)}, bf16[24,4096]{1,0:T(8,128)(2,1)S(1)}, u32[]{:S(2)}, u32[]{:S(2)}) collective-permute-start(bf16[24,4096]{1,0:T(8,128)(2,1)} %get-tuple-element.52), channel_id=1, source_target_pairs={{0,3},{1,2},{2,1},{3,0},{4,7},{5,6},{6,5},{7,4},{8,11},{9,10},{10,... | collective-permute-start | bytes 589832 | tf_op jit(solution)/shard_map/ppermute | solution.py:368
  62.7 7.7 %collective-permute-start.15 = (bf16[24,4096]{1,0:T(8,128)(2,1)}, bf16[24,4096]{1,0:T(8,128)(2,1)S(1)}, u32[]{:S(2)}, u32[]{:S(2)}) collective-permute-start(bf16[24,4096]{1,0:T(8,128)(2,1)} %get-tuple-element.53), channel_id=1, source_target_pairs={{0,5},{1,4},{2,7},{3,6},{4,1},{5,0},{6,3},{7,2},{8,13},{9,12},{10,... | collective-permute-start | bytes 589832 | tf_op jit(solution)/shard_map/ppermute | solution.py:368
  67.8 2.6 %collective-permute-start.16 = (bf16[24,4096]{1,0:T(8,128)(2,1)}, bf16[24,4096]{1,0:T(8,128)(2,1)S(1)}, u32[]{:S(2)}, u32[]{:S(2)}) collective-permute-start(bf16[24,4096]{1,0:T(8,128)(2,1)} %get-tuple-element.46.after), channel_id=1, source_target_pairs={{0,1},{1,0},{2,3},{3,2},{4,5},{5,4},{6,7},{7,6},{8,9},{9,8},{10,11... | collective-permute-start | bytes 589832 | tf_op jit(solution)/shard_map/ppermute | solution.py:368
